TPU v7x, 32 devices: a whole 2x2x4 slice. The times are simulated.
32 devices in a mesh: dp: 16 (over z, y, x), tensor: 2 (over core).
Axes of the slice: x: 2, y: 2, z: 4, core: 2. Of those that a mesh axis runs over, the one named last changes fastest.
Arguments:
- inputs: float32 [16384, 1280], P(('dp', 'tensor')), may hold values from -6 to 6
- cotangent: float32 [16384, 1280], P(('dp', 'tensor')), may hold values from -6 to 6
- query_weight: bfloat16 [2, 1280, 1280], P(None, 'dp', 'tensor'), may hold values from -0.15625 to 0.15625
- key_weight: bfloat16 [2, 1280, 1280], P(None, 'dp', 'tensor'), may hold values from -0.15625 to 0.15625
- value_weight: bfloat16 [2, 1280, 1280], P(None, 'dp', 'tensor'), may hold values from -0.15625 to 0.15625
- output_weight: bfloat16 [2, 1280, 1280], P(None, 'tensor', 'dp'), may hold values from -2.5 to 2.5
- up_weight: bfloat16 [2, 1280, 1280], P(None, 'dp', 'tensor'), may hold values from -0.15625 to 0.15625
- down_weight: bfloat16 [2, 1280, 1280], P(None, 'tensor', 'dp'), may hold values from -0.15625 to 0.15625
- attention_gain: float32 [2, 1280], replicated, may hold values from 0.1 to 1.9
- feed_gain: float32 [2, 1280], replicated, may hold values from 0.1 to 1.9
- query_scale: float32 [2, 80], replicated, may hold values from -0.5 to 1.5
- cont_lengths: int32 [16, 4], P('dp'), may hold values from 1 to 192, 512 in all within a row
Outputs:
- block_output: float32 [16384, 1280], P(('dp', 'tensor'))
- input_grad: float32 [16384, 1280], P(('dp', 'tensor'))
- grad_query: float32 [2, 1280, 1280], P(None, 'dp', 'tensor')
- grad_key: float32 [2, 1280, 1280], P(None, 'dp', 'tensor')
- grad_value: float32 [2, 1280, 1280], P(None, 'dp', 'tensor')
- grad_output: float32 [2, 1280, 1280], P(None, 'tensor', 'dp')
- grad_up: float32 [2, 1280, 1280], P(None, 'dp', 'tensor')
- grad_down: float32 [2, 1280, 1280], P(None, 'tensor', 'dp')
- grad_attention: float32 [2, 1280], replicated
- grad_feed: float32 [2, 1280], replicated
- grad_scale: float32 [2, 80], replicated
Inputs may be any that keep to these rules, and one draw needn't show every extreme that they name: `cont_lengths`: each row holds the lengths of one dp index's 4 continuations in order; they sum to 512 and the largest is 192.
All inputs are finite; a program needn't handle non-finite values.
Results may differ from a plain program's by a relative error of at most 0.038.
Values may be sent and summed in bfloat16 or wider, within the bound.
No kernel may reach another device: no remote copies, remote signals or barrier semaphores. Data moves between devices by JAX's collectives and lax.ppermute only.
A program may use at most 256 MiB of HBM per device.

v0:
```python
from functools import partial
import math

import jax
import jax.numpy as jnp
from jax import lax
from jax.sharding import PartitionSpec as P

HD = 80
LAYERS = 2
PROMPT_DEV = 512


EPSILON = 1e-06
LOG_TWO_E = 1.4426950408889634
NEGATIVE = -1e30


def from_partner(shard, axis, distance):
    return lax.ppermute(shard, axis, [(i, i ^ 1 << distance) for i in range(lax.axis_size(axis))])


def lowered(values):
    return values.astype(jnp.bfloat16)


def matmul(former, latter):
    return jnp.dot(former, latter, preferred_element_type=jnp.float32)


def inner_rows(former, latter):
    return lax.dot_general(
        former, latter, (((0,), (0,)), ((), ())), preferred_element_type=jnp.float32
    )


def inner_columns(former, latter):
    return lax.dot_general(
        former, latter, (((1,), (1,)), ((), ())), preferred_element_type=jnp.float32
    )


def inverse_root(source):
    return lax.rsqrt(jnp.mean(source * source, axis=1, keepdims=True) + EPSILON)


def softplus(values):
    return jnp.log1p(jnp.exp(values))


def split_heads(values):
    row_count = values.shape[0]
    return values.reshape(row_count, values.shape[1] // HD, HD).transpose(1, 0, 2)


def merge_heads(values):
    return values.transpose(1, 0, 2).reshape(values.shape[1], values.shape[0] * values.shape[2])


def norm_backward(source, inverse, gain_row, incoming):
    unit_rows = source * inverse
    gain_grad = jnp.sum(incoming * unit_rows, axis=0)
    scaled = incoming * gain_row
    return (
        gain_grad,
        inverse * (scaled - unit_rows * jnp.mean(scaled * unit_rows, axis=1, keepdims=True)),
    )


def segment_ids(lengths_row, total_rows):
    offsets = jnp.arange(total_rows, dtype=jnp.int32) - PROMPT_DEV
    bounds = jnp.cumsum(lengths_row)
    passed = jnp.sum((offsets[:, None] >= bounds[None, :]).astype(jnp.int32), axis=1)
    return jnp.where(offsets < 0, 0, 1 + passed)


def gather_rows(local_rows):
    return lax.all_gather(local_rows, "tensor", axis=0, tiled=True)


def gather_grads(local_rows):
    return lax.all_gather(local_rows, "tensor", axis=0, tiled=True)


def reduce_rows(values, weight):

    def partial_term(offset, amount):
        return matmul(values, weight)

    return lax.psum_scatter(
        partial_term(
            jnp.int32(0), values.shape[0] // lax.axis_size("tensor") * lax.axis_size("tensor")
        ).astype(jnp.bfloat16),
        "tensor",
        scatter_dimension=0,
        tiled=True,
    ).astype(jnp.float32)


def reduce_back(values, weight):

    def partial_term(offset, amount):
        return inner_columns(values, weight)

    return lax.psum_scatter(
        partial_term(
            jnp.int32(0), values.shape[0] // lax.axis_size("tensor") * lax.axis_size("tensor")
        ).astype(jnp.bfloat16),
        "tensor",
        scatter_dimension=0,
        tiled=True,
    ).astype(jnp.float32)


def head_forward(allowed, operands):
    query_rows, key_rows, value_rows = operands
    scores = jnp.where(allowed, inner_columns(query_rows, key_rows), NEGATIVE)
    highest = jnp.max(scores, axis=1, keepdims=True)
    weights = jnp.exp(scores - highest)
    totals = jnp.sum(weights, axis=1, keepdims=True)
    shares_low = lowered(weights / totals)
    return (matmul(shares_low, value_rows), (highest + jnp.log(totals))[:, 0])


def head_backward(allowed, operands):
    query_rows, key_rows, value_rows, log_totals, grad_rows = operands
    scores = inner_columns(query_rows, key_rows)
    shares = jnp.exp(jnp.where(allowed, scores - log_totals[:, None], NEGATIVE))
    grad_shares = lowered(inner_columns(grad_rows, value_rows)).astype(jnp.float32)
    deltas = jnp.sum(shares * grad_shares, axis=1, keepdims=True)
    grad_scores = lowered(shares * (grad_shares - deltas))
    return (
        matmul(grad_scores, key_rows),
        inner_rows(grad_scores, query_rows),
        inner_rows(lowered(shares), grad_rows),
    )


def body(
    inputs,
    cotangent,
    query_weight,
    key_weight,
    value_weight,
    output_weight,
    up_weight,
    down_weight,
    attention_gain,
    feed_gain,
    query_scale,
    cont_lengths,
):
    row_total = inputs.shape[0] * lax.axis_size("tensor")
    local_width = query_weight.shape[2]
    pair_side = lax.axis_index("dp") % 2
    own_segment = segment_ids(cont_lengths[0], row_total)
    own_place = pair_side * row_total + jnp.arange(row_total, dtype=jnp.int32)
    far_place = (1 - pair_side) * row_total + jnp.arange(PROMPT_DEV, dtype=jnp.int32)
    key_segment = jnp.concatenate([jnp.zeros((PROMPT_DEV,), jnp.int32), own_segment])
    key_place = jnp.concatenate([far_place, own_place])
    earlier = key_place[None, :] <= own_place[:, None]
    query_cont = own_segment[:, None] != 0
    allowed = (key_segment[None, :] == 0) & (query_cont | earlier) | (
        key_segment[None, :] == own_segment[:, None]
    ) & query_cont & earlier
    forward_head = partial(head_forward, allowed)
    backward_head = partial(head_backward, allowed)
    stored = []
    current = inputs
    for layer_index in range(LAYERS):
        gathered = (
            lax.all_gather(query_weight[layer_index], "dp", axis=0, tiled=True),
            lax.all_gather(key_weight[layer_index], "dp", axis=0, tiled=True),
            lax.all_gather(value_weight[layer_index], "dp", axis=0, tiled=True),
            lax.all_gather(output_weight[layer_index], "dp", axis=1, tiled=True),
            lax.all_gather(up_weight[layer_index], "dp", axis=0, tiled=True),
            lax.all_gather(down_weight[layer_index], "dp", axis=1, tiled=True),
        )
        joint_weight = jnp.concatenate([gathered[0], gathered[1], gathered[2]], axis=1)
        out_weight = gathered[3]
        inverse_attn = inverse_root(current)
        normed_all = gather_rows(lowered(current * inverse_attn * attention_gain[layer_index]))
        joint = matmul(normed_all, joint_weight)
        query_raw = joint[:, :local_width]
        gain_q = softplus(query_scale[layer_index]) * LOG_TWO_E / math.sqrt(HD)
        query_low = lowered(query_raw.reshape(row_total, local_width // HD, HD) * gain_q).reshape(
            row_total, local_width
        )
        key_low = lowered(joint[:, local_width : 2 * local_width])
        value_low = lowered(joint[:, 2 * local_width :])
        far_keys, far_values = from_partner((key_low[:PROMPT_DEV], value_low[:PROMPT_DEV]), "dp", 0)
        key_all = jnp.concatenate([far_keys, key_low], axis=0)
        value_all = jnp.concatenate([far_values, value_low], axis=0)
        head_outs, log_totals = lax.map(
            forward_head, (split_heads(query_low), split_heads(key_all), split_heads(value_all))
        )
        mixed = lowered(merge_heads(head_outs))
        middle = current + reduce_rows(mixed, out_weight)
        inverse_feed = inverse_root(middle)
        feed_local = lowered(middle * inverse_feed * feed_gain[layer_index])
        upper_weight, lower_weight = (
            lax.all_gather(gathered[4], "tensor", axis=1, tiled=True),
            lax.all_gather(gathered[5], "tensor", axis=0, tiled=True),
        )
        feed_rows = feed_local
        upper = matmul(feed_rows, upper_weight)
        hidden = lowered(upper * jax.nn.sigmoid(upper))
        branch_out = matmul(hidden, lower_weight)
        stored.append(
            (
                current,
                inverse_attn,
                normed_all,
                joint_weight,
                out_weight,
                query_raw,
                gain_q,
                query_low,
                key_all,
                value_all,
                log_totals,
                mixed,
                middle,
                inverse_feed,
                feed_rows,
                upper_weight,
                lower_weight,
                upper,
                hidden,
            )
        )
        current = middle + branch_out
    layer_grads = [None] * LAYERS
    attention_grads = [None] * LAYERS
    feed_grads = [None] * LAYERS
    scale_grads = [None] * LAYERS
    grad = cotangent
    for layer_index in reversed(range(LAYERS)):
        (
            source,
            inverse_attn,
            normed_all,
            joint_weight,
            out_weight,
            query_raw,
            gain_q,
            query_low,
            key_all,
            value_all,
            log_totals,
            mixed,
            middle,
            inverse_feed,
            feed_rows,
            upper_weight,
            lower_weight,
            upper,
            hidden,
        ) = stored[layer_index]
        grad_low = lowered(grad)
        down_grad = inner_rows(hidden, grad_low)
        hidden_grad = lowered(inner_columns(grad_low, lower_weight))
        sigmoid_upper = jax.nn.sigmoid(upper)
        upper_grad = lowered(
            hidden_grad.astype(jnp.float32)
            * (sigmoid_upper * (1.0 + upper * (1.0 - sigmoid_upper)))
        )
        up_grad = inner_rows(feed_rows, upper_grad)
        feed_grad = inner_columns(upper_grad, upper_weight)
        up_grad, down_grad = (
            lax.psum_scatter(
                up_grad.astype(jnp.bfloat16), "tensor", scatter_dimension=1, tiled=True
            ).astype(jnp.float32),
            lax.psum_scatter(
                down_grad.astype(jnp.bfloat16), "tensor", scatter_dimension=0, tiled=True
            ).astype(jnp.float32),
        )
        feed_gain_grad, middle_part = norm_backward(
            middle, inverse_feed, feed_gain[layer_index], feed_grad
        )
        grad_middle = grad + middle_part
        middle_rows = gather_grads(lowered(grad_middle))
        out_grad = inner_rows(mixed, middle_rows)
        mixed_grad = lowered(inner_columns(middle_rows, out_weight))
        query_grads, key_grads, value_grads = lax.map(
            backward_head,
            (
                split_heads(query_low),
                split_heads(key_all),
                split_heads(value_all),
                log_totals,
                split_heads(mixed_grad),
            ),
        )
        query_grad_rows = merge_heads(query_grads)
        key_grad_rows = merge_heads(key_grads)
        value_grad_rows = merge_heads(value_grads)
        back_keys, back_values = (
            from_partner(key_grad_rows[:PROMPT_DEV].astype(jnp.bfloat16), "dp", 0).astype(
                jnp.float32
            ),
            from_partner(value_grad_rows[:PROMPT_DEV].astype(jnp.bfloat16), "dp", 0).astype(
                jnp.float32
            ),
        )
        own_keys = key_grad_rows[PROMPT_DEV:]
        own_values = value_grad_rows[PROMPT_DEV:]
        own_keys = jnp.concatenate(
            [own_keys[:PROMPT_DEV] + back_keys, own_keys[PROMPT_DEV:]], axis=0
        )
        own_values = jnp.concatenate(
            [own_values[:PROMPT_DEV] + back_values, own_values[PROMPT_DEV:]], axis=0
        )
        query_heads = query_grad_rows.reshape(row_total, local_width // HD, HD)
        raw_heads = query_raw.reshape(row_total, local_width // HD, HD)
        scale_raw = jnp.sum(query_heads * raw_heads, axis=(0, 1))
        scale_grads[layer_index] = (
            scale_raw * jax.nn.sigmoid(query_scale[layer_index]) * LOG_TWO_E / math.sqrt(HD)
        )
        joint_grad = jnp.concatenate(
            [
                lowered(query_heads * gain_q).reshape(row_total, local_width),
                lowered(own_keys),
                lowered(own_values),
            ],
            axis=1,
        )
        joint_weight_grad = inner_rows(normed_all, joint_grad)
        normed_grad = reduce_back(joint_grad, joint_weight)
        attention_gain_grad, input_part = norm_backward(
            source, inverse_attn, attention_gain[layer_index], normed_grad
        )
        grad = grad_middle + input_part
        attention_grads[layer_index] = attention_gain_grad
        feed_grads[layer_index] = feed_gain_grad
        layer_grads[layer_index] = (
            joint_weight_grad[:, :local_width],
            joint_weight_grad[:, local_width : 2 * local_width],
            joint_weight_grad[:, 2 * local_width :],
            out_grad,
            up_grad,
            down_grad,
        )
    stacked = [
        jnp.stack([layer_grads[depth_index][member] for depth_index in range(LAYERS)])
        for member in range(6)
    ]
    summed = (
        lax.psum_scatter(
            stacked[0].astype(jnp.bfloat16), "dp", scatter_dimension=1, tiled=True
        ).astype(jnp.float32),
        lax.psum_scatter(
            stacked[1].astype(jnp.bfloat16), "dp", scatter_dimension=1, tiled=True
        ).astype(jnp.float32),
        lax.psum_scatter(
            stacked[2].astype(jnp.bfloat16), "dp", scatter_dimension=1, tiled=True
        ).astype(jnp.float32),
        lax.psum_scatter(
            stacked[3].astype(jnp.bfloat16), "dp", scatter_dimension=2, tiled=True
        ).astype(jnp.float32),
        lax.psum_scatter(
            stacked[4].astype(jnp.bfloat16), "dp", scatter_dimension=1, tiled=True
        ).astype(jnp.float32),
        lax.psum_scatter(
            stacked[5].astype(jnp.bfloat16), "dp", scatter_dimension=2, tiled=True
        ).astype(jnp.float32),
    )
    attention_total, feed_total, scale_total = lax.psum(
        (jnp.stack(attention_grads), jnp.stack(feed_grads), jnp.stack(scale_grads)),
        ("dp", "tensor"),
    )
    return (
        current,
        grad,
        summed[0],
        summed[1],
        summed[2],
        summed[3],
        summed[4],
        summed[5],
        attention_total,
        feed_total,
        scale_total,
    )


def solution(mesh):
    in_specs = (
        P(("dp", "tensor"), None),
        P(("dp", "tensor"), None),
        P(None, "dp", "tensor"),
        P(None, "dp", "tensor"),
        P(None, "dp", "tensor"),
        P(None, "tensor", "dp"),
        P(None, "dp", "tensor"),
        P(None, "tensor", "dp"),
        P(),
        P(),
        P(),
        P("dp", None),
    )
    out_specs = (
        P(("dp", "tensor"), None),
        P(("dp", "tensor"), None),
        P(None, "dp", "tensor"),
        P(None, "dp", "tensor"),
        P(None, "dp", "tensor"),
        P(None, "tensor", "dp"),
        P(None, "dp", "tensor"),
        P(None, "tensor", "dp"),
        P(),
        P(),
        P(),
    )
    return jax.shard_map(body, mesh=mesh, in_specs=in_specs, out_specs=out_specs, check_vma=False)
```

profile of v0, /device:TPU:0, one launch (start us, length us, event | category | flops | bytes accessed | tf_op | source)
XLA Modules:
  0.0 1912.1 jit_solution(1393445013591614731)
XLA Ops:
  26.3 62.6 %all-gather.49.cloned.1.call-done = bf16[1,1280,640]{2,1,0:T(8,128)(2,1)} async-done(((bf16[1,80,640]{2,1,0:T(8,128)(2,1)}), bf16[1,1280,640]{2,1,0:T(8,128)(2,1)}) %all-gather.49.cloned.1.call-update) | async-done | bytes 1638416 | tf_op jit(solution)/shard_map/all_gather | solution.py:174
  88.9 60.3 %all-gather.47.cloned.1.call-done = bf16[1,1280,640]{2,1,0:T(8,128)(2,1)} async-done(((bf16[1,80,640]{2,1,0:T(8,128)(2,1)}), bf16[1,1280,640]{2,1,0:T(8,128)(2,1)}) %all-gather.47.cloned.1.call-update) | async-done | bytes 1638416 | tf_op jit(solution)/shard_map/all_gather | solution.py:173
  149.2 60.1 %all-gather.45.cloned.1.call-done = bf16[1,1280,640]{2,1,0:T(8,128)(2,1)} async-done(((bf16[1,80,640]{2,1,0:T(8,128)(2,1)}), bf16[1,1280,640]{2,1,0:T(8,128)(2,1)}) %all-gather.45.cloned.1.call-update) | async-done | bytes 1638416 | tf_op jit(solution)/shard_map/all_gather | solution.py:172
  209.3 12.0 fusion.211
  245.1 11.9 collective-permute-done.1
  277.5 68.6 %while.56 = (s32[]{:T(128)}, bf16[8,1024,80]{1,2,0:T(8,128)(2,1)}, f32[8,1024]{1,0:T(8,128)S(1)}, bf16[8,1024,80]{2,1,0:T(8,128)(2,1)}, bf16[8,1536,80]{2,1,0:T(...) while((s32[]{:T(128)}, bf16[8,1024,80]{1,2,0:T(8,128)(2,1)}, ...), condition=%wide.region_6.7_spmd.clone, body=%wide.region_3.6_spmd.clone.sunk | while | flops 525335552 | bytes 20316816 | solution.py:194
  352.5 37.7 %all-gather.57.cloned.1.call-done = bf16[1,640,1280]{1,2,0:T(8,128)(2,1)} async-done(((bf16[1,640,80]{1,2,0:T(8,128)(2,1)}), bf16[1,640,1280]{1,2,0:T(8,128)(2,1)}) %all-gather.57.cloned.1.call-update) | async-done | bytes 1638416 | tf_op jit(solution)/shard_map/all_gather | solution.py:177
  392.7 9.4 reduce-scatter.17.cloned.1.call-done
  405.3 12.0 all-gather.55.cloned.1.call-done
  417.3 6.2 fusion.118
  423.5 8.7 all-gather.59.cloned.1.call-done
  432.2 5.8 multiply_reduce_fusion.5
  440.7 54.4 %all-gather.65.cloned.1.call-done = bf16[1,1280,640]{2,1,0:T(8,128)(2,1)} async-done(((bf16[1,80,640]{2,1,0:T(8,128)(2,1)}), bf16[1,1280,640]{2,1,0:T(8,128)(2,1)}) %all-gather.65.cloned.1.call-update) | async-done | bytes 1638416 | tf_op jit(solution)/shard_map/all_gather | solution.py:174
  495.2 60.5 %all-gather.63.cloned.1.call-done = bf16[1,1280,640]{2,1,0:T(8,128)(2,1)} async-done(((bf16[1,80,640]{2,1,0:T(8,128)(2,1)}), bf16[1,1280,640]{2,1,0:T(8,128)(2,1)}) %all-gather.63.cloned.1.call-update) | async-done | bytes 1638416 | tf_op jit(solution)/shard_map/all_gather | solution.py:173
  555.6 60.6 %all-gather.61.cloned.1.call-done = bf16[1,1280,640]{2,1,0:T(8,128)(2,1)} async-done(((bf16[1,80,640]{2,1,0:T(8,128)(2,1)}), bf16[1,1280,640]{2,1,0:T(8,128)(2,1)}) %all-gather.61.cloned.1.call-update) | async-done | bytes 1638416 | tf_op jit(solution)/shard_map/all_gather | solution.py:172
  616.3 11.7 all-gather.39.cloned.1.call-done
  628.0 12.0 fusion.212
  688.5 68.6 %while.57 = (s32[]{:T(128)}, bf16[8,1024,80]{1,2,0:T(8,128)(2,1)}, f32[8,1024]{1,0:T(8,128)S(1)}, bf16[8,1024,80]{2,1,0:T(8,128)(2,1)}, bf16[8,1536,80]{2,1,0:T(...) while((s32[]{:T(128)}, bf16[8,1024,80]{1,2,0:T(8,128)(2,1)}, ...), condition=%wide.region_13.14_spmd.clone, body=%wide.region_10.13_spmd.clone.sunk | while | flops 525335552 | bytes 20316816 | solution.py:194
  757.1 5.6 convolution_convert_fusion.8
  763.6 48.7 %all-gather.73.cloned.1.call-done = bf16[1,640,1280]{1,2,0:T(8,128)(2,1)} async-done(((bf16[1,640,80]{1,2,0:T(8,128)(2,1)}), bf16[1,640,1280]{1,2,0:T(8,128)(2,1)}) %all-gather.73.cloned.1.call-update) | async-done | bytes 1638416 | tf_op jit(solution)/shard_map/all_gather | solution.py:177
  812.5 11.0 reduce-scatter.19.cloned.1.call-done
  826.7 11.9 all-gather.71.cloned.1.call-done
  838.7 6.1 fusion.111
  844.7 8.8 all-gather.75.cloned.1.call-done
  853.5 5.8 fusion.142
  865.1 12.4 all-gather.41.cloned.1.call-done
  892.9 125.4 %while.58 = (s32[]{:T(128)}, f32[8,1024,80]{1,2,0:T(8,128)}, f32[8,1536,80]{1,2,0:T(8,128)}, f32[8,1536,80]{1,2,0:T(8,128)}, bf16[8,1024,80]{2,1,0:T(8,128)(2,1)...) while((s32[]{:T(128)}, f32[8,1024,80]{1,2,0:T(8,128)}, ...), condition=%wide.region_19.20_spmd.clone, body=%wide.region_17.19_spmd.clone.sunk | while | flops 1286601728 | bytes 41336480 | solution.py:285
  1028.6 11.6 collective-permute-done.5
  1040.4 13.2 collective-permute-done.4
  1054.7 7.1 convolution_convert_fusion.11
  1062.3 11.0 reduce-scatter.21.cloned.1.call-done
  1095.1 5.7 convolution_convert_fusion.5
  1107.7 5.7 copy.111
  1120.4 5.9 copy.109
  1140.3 123.2 %while.59 = (s32[]{:T(128)}, f32[8,1024,80]{1,2,0:T(8,128)}, f32[8,1536,80]{1,2,0:T(8,128)}, f32[8,1536,80]{1,2,0:T(8,128)}, bf16[8,1024,80]{2,1,0:T(8,128)(2,1)...) while((s32[]{:T(128)}, f32[8,1024,80]{1,2,0:T(8,128)}, ...), condition=%wide.region_25.26_spmd.clone, body=%wide.region_23.25_spmd.clone.sunk | while | flops 1286601728 | bytes 41336480 | solution.py:285
  1273.2 12.1 collective-permute-done.7
  1285.5 13.2 collective-permute-done.6
  1299.8 7.1 convolution_convert_fusion.10
  1308.2 8.1 convolution_convert_fusion.2
  1319.6 18.6 convolution_convert_fusion.3
  1355.4 7.2 copy.105
  1364.9 7.3 copy.106
  1382.0 7.4 convolution_add_fusion
  1391.7 43.5 %all-reduce.3 = (f32[2,1280]{1,0:T(2,128)}, f32[2,1280]{1,0:T(2,128)}, f32[2,80]{1,0:T(2,128)}) all-reduce(f32[2,1280]{1,0:T(2,128)S(1)} %pad_maximum_fusion.16, f32[2,1280]{1,0:T(2,128)S(1)} %pad_maximum_fusion.17, f32[2,80]{1,0:T(2,128)S(1)} %pad_maximum_fusion.18), channel_id=1, replica_groups=mesh['dp'=16,'tensor'=2] {'dp','tensor'}, use_global_device_ids=true, to_apply=%region_40.41 | all-reduce | flops 5280 | bytes 42240 | tf_op jit(solution)/shard_map/psum | solution.py:368
  1441.2 71.1 %reduce-scatter.27.cloned.1.call-done = bf16[2,80,640]{2,1,0:T(8,128)(2,1)} async-done(((bf16[2,1280,640]{2,1,0:T(8,128)(2,1)}), bf16[2,80,640]{2,1,0:T(8,128)(2,1)}) %reduce-scatter.27.cloned.1.call-update) | async-done | bytes 204816 | tf_op jit(solution)/shard_map/reduce_scatter | solution.py:352
  1514.0 82.4 %reduce-scatter.29.cloned.1.call-done = bf16[2,80,640]{2,1,0:T(8,128)(2,1)} async-done(((bf16[2,1280,640]{2,1,0:T(8,128)(2,1)}), bf16[2,80,640]{2,1,0:T(8,128)(2,1)}) %reduce-scatter.29.cloned.1.call-update) | async-done | bytes 204816 | tf_op jit(solution)/shard_map/reduce_scatter | solution.py:355
  1598.1 219.4 %all-reduce.7.cloned.1.call-done = (bf16[2,640,1280]{1,0,2:T(2,128)(2,1)}, bf16[2,640,1280]{1,0,2:T(2,128)(2,1)}) async-done(((bf16[2,640,1280]{1,0,2:T(2,128)(2,1)}, bf16[2,640,1280]{1,0,2:T(2,128)(2,1)}), (bf16[2,640,1280]{1,0,2:T(2,128)(2,1)}, bf16[2,640,1280]{1,0,2:T(2,128)(2,1)})) %all-reduce.7.cloned.1.call-update) | async-done | bytes 6553616
  1821.2 82.1 %reduce-scatter.31.cloned.1.call-done = bf16[2,80,640]{2,1,0:T(8,128)(2,1)} async-done(((bf16[2,1280,640]{2,1,0:T(8,128)(2,1)}), bf16[2,80,640]{2,1,0:T(8,128)(2,1)}) %reduce-scatter.31.cloned.1.call-update) | async-done | bytes 204816 | tf_op jit(solution)/shard_map/reduce_scatter | solution.py:361
  (579 shorter events, 658.2 us)
Async XLA Ops:
  7.2 19.1 %all-gather.37.cloned.1.call-start = ((), (), s32[]{:S(2)}) async-start(), calls=%async_computation.12 | async-start | bytes 3932160 | tf_op jit(solution)/shard_map/all_gather | solution.py:78
  8.1 429.9 %copy-start.42 = (f32[1280]{0:T(1024)}, f32[1280]{0:T(1024)S(1)}, u32[]{:S(2)}) copy-start(f32[1280]{0:T(1024)S(1)} %get-tuple-element.615) | copy-start | bytes 15364
  12.1 76.8 %all-gather.49.cloned.1.call-start = ((), (), s32[]{:S(2)}) async-start(), calls=%async_computation.28 | async-start | bytes 1740800 | tf_op jit(solution)/shard_map/all_gather | solution.py:174
  12.9 136.3 %all-gather.47.cloned.1.call-start = ((), (), s32[]{:S(2)}) async-start(), calls=%async_computation.27 | async-start | bytes 1740800 | tf_op jit(solution)/shard_map/all_gather | solution.py:173
  13.7 195.6 %all-gather.45.cloned.1.call-start = ((), (), s32[]{:S(2)}) async-start(), calls=%async_computation.26 | async-start | bytes 1740800 | tf_op jit(solution)/shard_map/all_gather | solution.py:172
  14.4 331.7 %all-gather.51.cloned.1.call-start = ((), (), s32[]{:S(2)}) async-start(), calls=%async_computation.29 | async-start | bytes 1740800 | tf_op jit(solution)/shard_map/all_gather | solution.py:175
  15.2 336.6 %all-gather.53.cloned.1.call-start = ((), (), s32[]{:S(2)}) async-start(), calls=%async_computation.30 | async-start | bytes 1740800 | tf_op jit(solution)/shard_map/all_gather | solution.py:176
  16.9 373.3 %all-gather.57.cloned.1.call-start = ((), (), s32[]{:S(2)}) async-start(), calls=%async_computation.32 | async-start | bytes 1740800 | tf_op jit(solution)/shard_map/all_gather | solution.py:177
  18.7 383.5 %reduce-scatter.17.cloned.1.call-start = ((), (), s32[]{:S(2)}) async-start(), calls=%async_computation.13 | async-start | bytes 3932160 | tf_op jit(solution)/shard_map/reduce_scatter | solution.py:90
  20.5 215.0 %copy-start.61 = (f32[80]{0:T(128)}, f32[80]{0:T(128)S(1)}, u32[]{:S(2)}) copy-start(f32[80]{0:T(128)S(1)} %get-tuple-element.789) | copy-start | bytes 964
  224.2 20.9 %collective-permute-start = (bf16[512,640]{1,0:T(8,128)(2,1)}, bf16[512,640]{1,0:T(8,128)(2,1)}, u32[]{:S(2)}, u32[]{:S(2)}) collective-permute-start(bf16[512,640]{1,0:T(8,128)(2,1)} %get-tuple-element.757), channel_id=1, source_target_pairs={{0,2},{2,0},{4,6},{6,4},{8,10},{10,8},{12,14},{14,12},{16,18},{18,... | collective-permute-start | bytes 1966088 | tf_op jit(solution)/shard_map/ppermute | solution.py:20
  225.6 31.3 %collective-permute-start.1 = (bf16[512,640]{1,0:T(8,128)(2,1)S(1)}, bf16[512,640]{1,0:T(8,128)(2,1)}, u32[]{:S(2)}, u32[]{:S(2)}) collective-permute-start(bf16[512,640]{1,0:T(8,128)(2,1)S(1)} %get-tuple-element.756), channel_id=1, source_target_pairs={{0,2},{2,0},{4,6},{6,4},{8,10},{10,8},{12,14},{14,12},{16,18},{18,... | collective-permute-start | bytes 1966088 | tf_op jit(solution)/shard_map/ppermute | solution.py:20
  351.7 40.9 %copy-start.54 = (f32[2,1280]{1,0:T(2,128)S(1)}, f32[2,1280]{1,0:T(2,128)}, u32[]{:S(2)}) copy-start(f32[2,1280]{1,0:T(2,128)} %param.29) | copy-start | bytes 30724
  351.8 65.5 %all-gather.55.cloned.1.call-start = ((), (), s32[]{:S(2)}) async-start(), calls=%async_computation.31 | async-start | bytes 4915200 | tf_op jit(solution)/shard_map/all_gather | solution.py:202
  352.5 79.7 %all-gather.59.cloned.1.call-start = ((), (), s32[]{:S(2)}) async-start(), calls=%async_computation.33 | async-start | bytes 4915200 | tf_op jit(solution)/shard_map/all_gather | solution.py:203
  390.2 104.9 %all-gather.65.cloned.1.call-start = ((), (), s32[]{:S(2)}) async-start(), calls=%async_computation.36 | async-start | bytes 1740800 | tf_op jit(solution)/shard_map/all_gather | solution.py:174
  391.0 164.6 %all-gather.63.cloned.1.call-start = ((), (), s32[]{:S(2)}) async-start(), calls=%async_computation.35 | async-start | bytes 1740800 | tf_op jit(solution)/shard_map/all_gather | solution.py:173
  391.6 224.7 %all-gather.61.cloned.1.call-start = ((), (), s32[]{:S(2)}) async-start(), calls=%async_computation.34 | async-start | bytes 1740800 | tf_op jit(solution)/shard_map/all_gather | solution.py:172
  392.3 235.7 %all-gather.39.cloned.1.call-start = ((), (), s32[]{:S(2)}) async-start(), calls=%async_computation.14 | async-start | bytes 3932160 | tf_op jit(solution)/shard_map/all_gather | solution.py:78
  392.7 469.4 %copy-start.51 = (f32[1280]{0:T(1024)}, f32[1280]{0:T(1024)S(1)}, u32[]{:S(2)}) copy-start(f32[1280]{0:T(1024)S(1)} %get-tuple-element.613) | copy-start | bytes 15364
  439.5 317.6 %all-gather.67.cloned.1.call-start = ((), (), s32[]{:S(2)}) async-start(), calls=%async_computation.37 | async-start | bytes 1740800 | tf_op jit(solution)/shard_map/all_gather | solution.py:175
  440.1 322.7 %all-gather.69.cloned.1.call-start = ((), (), s32[]{:S(2)}) async-start(), calls=%async_computation.38 | async-start | bytes 1740800 | tf_op jit(solution)/shard_map/all_gather | solution.py:176
  440.7 371.6 %all-gather.73.cloned.1.call-start = ((), (), s32[]{:S(2)}) async-start(), calls=%async_computation.40 | async-start | bytes 1740800 | tf_op jit(solution)/shard_map/all_gather | solution.py:177
  642.9 19.8 %collective-permute-start.2 = (bf16[512,640]{1,0:T(8,128)(2,1)}, bf16[512,640]{1,0:T(8,128)(2,1)}, u32[]{:S(2)}, u32[]{:S(2)}) collective-permute-start(bf16[512,640]{1,0:T(8,128)(2,1)} %get-tuple-element.753), channel_id=1, source_target_pairs={{0,2},{2,0},{4,6},{6,4},{8,10},{10,8},{12,14},{14,12},{16,18},{18,... | collective-permute-start | bytes 1966088 | tf_op jit(solution)/shard_map/ppermute | solution.py:20
  644.6 179.0 %reduce-scatter.19.cloned.1.call-start = ((), (), s32[]{:S(2)}) async-start(), calls=%async_computation.15 | async-start | bytes 3932160 | tf_op jit(solution)/shard_map/reduce_scatter | solution.py:90
  651.8 25.2 %collective-permute-start.3 = (bf16[512,640]{1,0:T(8,128)(2,1)S(1)}, bf16[512,640]{1,0:T(8,128)(2,1)}, u32[]{:S(2)}, u32[]{:S(2)}) collective-permute-start(bf16[512,640]{1,0:T(8,128)(2,1)S(1)} %get-tuple-element.752), channel_id=1, source_target_pairs={{0,2},{2,0},{4,6},{6,4},{8,10},{10,8},{12,14},{14,12},{16,18},{18,... | collective-permute-start | bytes 1966088 | tf_op jit(solution)/shard_map/ppermute | solution.py:20
  762.8 75.9 %all-gather.71.cloned.1.call-start = ((), (), s32[]{:S(2)}) async-start(), calls=%async_computation.39 | async-start | bytes 4915200 | tf_op jit(solution)/shard_map/all_gather | solution.py:202
  763.5 90.0 %all-gather.75.cloned.1.call-start = ((), (), s32[]{:S(2)}) async-start(), calls=%async_computation.41 | async-start | bytes 4915200 | tf_op jit(solution)/shard_map/all_gather | solution.py:203
  812.3 65.2 %all-gather.41.cloned.1.call-start = ((), (), s32[]{:S(2)}) async-start(), calls=%async_computation.16 | async-start | bytes 3932160 | tf_op jit(solution)/shard_map/all_gather | solution.py:82
  826.7 35.4 %copy-start.57 = (f32[512]{0:T(512)}, f32[512]{0:T(512)S(1)}, u32[]{:S(2)}) copy-start(f32[512]{0:T(512)S(1)} %add_rsqrt_fusion) | copy-start | bytes 6148
  864.8 208.5 %reduce-scatter.21.cloned.1.call-start = ((), (), s32[]{:S(2)}) async-start(), calls=%async_computation.17 | async-start | bytes 3932160 | tf_op jit(solution)/shard_map/reduce_scatter | solution.py:105
  1020.8 33.0 %copy-start.24 = (bf16[512,8,80]{0,2,1:T(8,128)(2,1)}, bf16[512,8,80]{0,2,1:T(8,128)(2,1)S(1)}, u32[]{:S(2)}) copy-start(bf16[512,8,80]{0,2,1:T(8,128)(2,1)S(1)} %get-tuple-element.773) | copy-start | bytes 1966084
  1022.5 17.6 collective-permute-start.5
  1024.9 28.7 %collective-permute-start.4 = (bf16[512,640]{0,1:T(8,128)(2,1)S(1)}, bf16[512,640]{0,1:T(8,128)(2,1)S(1)}, u32[]{:S(2)}, u32[]{:S(2)}) collective-permute-start(bf16[512,640]{0,1:T(8,128)(2,1)S(1)} %bitcast.417), channel_id=1, source_target_pairs={{0,2},{2,0},{4,6},{6,4},{8,10},{10,8},{12,14},{14,12},{16,18},{18,... | collective-permute-start | bytes 1966088 | tf_op jit(solution)/shard_map/ppermute | solution.py:20
  1061.8 64.6 %all-gather.43.cloned.1.call-start = ((), (), s32[]{:S(2)}) async-start(), calls=%async_computation.18 | async-start | bytes 3932160 | tf_op jit(solution)/shard_map/all_gather | solution.py:82
  1087.9 274.7 %reduce-scatter.35.cloned.1.call-start = ((), (), s32[]{:S(2)}) async-start(), calls=%async_computation.25 | async-start | bytes 4915200 | tf_op jit(solution)/shard_map/reduce_scatter | solution.py:274
  1093.4 269.2 %reduce-scatter.33.cloned.1.call-start = ((), (), s32[]{:S(2)}) async-start(), calls=%async_computation.24 | async-start | bytes 4915200 | tf_op jit(solution)/shard_map/reduce_scatter | solution.py:274
  1100.9 271.3 %reduce-scatter.39.cloned.1.call-start = ((), (), s32[]{:S(2)}) async-start(), calls=%async_computation.43 | async-start | bytes 4915200
  1113.4 261.7 %reduce-scatter.37.cloned.1.call-start = ((), (), s32[]{:S(2)}) async-start(), calls=%async_computation.42 | async-start | bytes 4915200
  1126.3 263.2 %reduce-scatter.23.cloned.1.call-start = ((), (), s32[]{:S(2)}) async-start(), calls=%async_computation.19 | async-start | bytes 3932160 | tf_op jit(solution)/shard_map/reduce_scatter | solution.py:105
  1267.7 31.3 %copy-start.28 = (bf16[512,8,80]{0,2,1:T(8,128)(2,1)}, bf16[512,8,80]{0,2,1:T(8,128)(2,1)S(1)}, u32[]{:S(2)}) copy-start(bf16[512,8,80]{0,2,1:T(8,128)(2,1)S(1)} %get-tuple-element.769) | copy-start | bytes 1966084
  1267.7 17.6 collective-permute-start.7
  1270.1 28.6 %collective-permute-start.6 = (bf16[512,640]{0,1:T(8,128)(2,1)S(1)}, bf16[512,640]{0,1:T(8,128)(2,1)S(1)}, u32[]{:S(2)}, u32[]{:S(2)}) collective-permute-start(bf16[512,640]{0,1:T(8,128)(2,1)S(1)} %bitcast.418), channel_id=1, source_target_pairs={{0,2},{2,0},{4,6},{6,4},{8,10},{10,8},{12,14},{14,12},{16,18},{18,... | collective-permute-start | bytes 1966088 | tf_op jit(solution)/shard_map/ppermute | solution.py:20
  1306.9 132.6 %reduce-scatter.25.cloned.1.call-start = ((), (), s32[]{:S(2)}) async-start(), calls=%async_computation.20 | async-start | bytes 3481600 | tf_op jit(solution)/shard_map/reduce_scatter | solution.py:349
  1341.9 170.4 %reduce-scatter.27.cloned.1.call-start = ((), (), s32[]{:S(2)}) async-start(), calls=%async_computation.21 | async-start | bytes 3481600 | tf_op jit(solution)/shard_map/reduce_scatter | solution.py:352
  1345.9 250.5 %reduce-scatter.29.cloned.1.call-start = ((), (), s32[]{:S(2)}) async-start(), calls=%async_computation.22 | async-start | bytes 3481600 | tf_op jit(solution)/shard_map/reduce_scatter | solution.py:355
  1348.1 469.5 %all-reduce.7.cloned.1.call-start = ((), (), s32[]{:S(2)}) async-start(), calls=%async_computation.44 | async-start | bytes 13107200
  1372.1 531.2 %reduce-scatter.31.cloned.1.call-start = ((), (), s32[]{:S(2)}) async-start(), calls=%async_computation.23 | async-start | bytes 3481600 | tf_op jit(solution)/shard_map/reduce_scatter | solution.py:361
  (78 other events, 544.8 us)
Sparse Core Ops, SparseCore 0:
  12.2 14.0 all-gather.36
  29.6 59.2 all-gather.48
  92.2 56.9 all-gather.46
  152.3 56.9 all-gather.44
  211.8 59.1 all-gather.50
  273.5 57.0 all-gather.52
  333.3 56.8 all-gather.56
  393.0 9.0 reduce-scatter.16
  403.7 13.4 all-gather.54
  418.7 13.4 all-gather.58
  435.8 59.2 all-gather.64
  498.6 56.9 all-gather.62
  559.3 56.9 all-gather.60
  617.7 10.2 all-gather.38
  630.9 61.4 all-gather.66
  695.3 57.0 all-gather.68
  755.2 57.0 all-gather.72
  814.5 9.0 reduce-scatter.18
  825.1 13.4 all-gather.70
  840.0 13.4 all-gather.74
  864.9 12.5 all-gather.40
  1061.9 11.3 reduce-scatter.20
  1088.1 12.5 all-gather.42
  1102.9 12.2 reduce-scatter.34
  1117.4 12.2 reduce-scatter.32
  1131.8 12.1 reduce-scatter.38
  1146.2 12.2 reduce-scatter.36
  1307.0 11.3 reduce-scatter.22
  1342.0 86.2 reduce-scatter.24
  1430.5 81.8 reduce-scatter.26
  1514.6 81.7 reduce-scatter.28
  1602.8 214.7 all-reduce.6
  1819.7 83.6 reduce-scatter.30
where the time goes:
time: 1920 us; the launch traced here: 1910 us
  waiting for transfers between devices  1070 us (56%)
  matrix products  499 us (26%)
  local copies, waits for them, and re-layouts  163 us (8%)
  other arithmetic  102 us (5%)
  blocking collectives  43.5 us (2%)
    unnamed x36, waiting for transfers between devices  224 us
    dot_general x56, matrix products, inner_columns(): lax.dot_general(former, latter, (((1,), (1,)), ((), ())), preferred_eleme...  211 us
    dot_general x40, matrix products, matmul(): return jnp.dot(former, latter, preferred_element_type=jnp.float32)  164 us
    dot_general x40, matrix products, inner_rows(): lax.dot_general(former, latter, (((0,), (0,)), ((), ())), preferred_eleme...  125 us
    all_gather x2, waiting for transfers between devices, body(): lax.all_gather(key_weight[layer_index], 'dp', axis=0, tiled=True)  121 us
    all_gather x2, waiting for transfers between devices, body(): lax.all_gather(query_weight[layer_index], 'dp', axis=0, tiled=True)  121 us
    all_gather x2, waiting for transfers between devices, body(): lax.all_gather(value_weight[layer_index], 'dp', axis=0, tiled=True)  117 us
    all_gather x2, waiting for transfers between devices, body(): lax.all_gather(down_weight[layer_index], 'dp', axis=1, tiled=True)  86.4 us
  transfers between devices with their start and end apart: 41, of which 30 were waited for; matrix products, arithmetic and copies ran while one was open for 29% of the time, Pallas kernels for 0%

commit v1 on v0

--- a/solution.py
+++ b/solution.py
@@ -74,42 +74,110 @@
     return jnp.where(offsets < 0, 0, 1 + passed)
 
 
+def pair_swap(values, axis, bit):
+    size = lax.axis_size(axis)
+    return lax.ppermute(values, axis, [(i, i ^ bit) for i in range(size)])
+
+
+def gather_orders(size):
+    if size == 16:
+        return ((8, 4, 2, 1), (8, 4, 1, 2), (1, 2, 8, 4), (8, 4, 1, 2), (1, 8, 4, 2), (2, 8, 4, 1))
+    bits = tuple(1 << k for k in reversed(range(size.bit_length() - 1)))
+    return (bits,) * 6
+
+
+def my_bit(axis, bit):
+    return (lax.axis_index(axis) & bit) != 0
+
+
+def place_of(bit, done):
+    return sum(1 for other in done if other > bit)
+
+
+def doubled_gather(shard, order):
+    values, done = shard, []
+    for bit in order:
+        other = pair_swap(values, "dp", bit)
+        upper = my_bit("dp", bit)
+        at = place_of(bit, done)
+        values = jnp.stack(
+            [jnp.where(upper, other, values), jnp.where(upper, values, other)], axis=at
+        )
+        done.append(bit)
+    return values.reshape((-1, shard.shape[1]))
+
+
+def halved_scatter(values, order):
+    size = lax.axis_size("dp")
+    width = values.shape[1]
+    left = sorted(order, reverse=True)
+    values = values.reshape((2,) * len(order) + (values.shape[0] // size, width))
+    for bit in reversed(order):
+        at = left.index(bit)
+        left.remove(bit)
+        upper = my_bit("dp", bit).astype(jnp.int32)
+        keep = lax.dynamic_index_in_dim(values, upper, at, keepdims=False)
+        send = lax.dynamic_index_in_dim(values, 1 - upper, at, keepdims=False)
+        got = pair_swap(lowered(send), "dp", bit)
+        values = keep.astype(jnp.float32) + got.astype(jnp.float32)
+        if left:
+            values = lowered(values)
+    return values
+
+
+def own_rows(values, axis="tensor"):
+    count = values.shape[0] // lax.axis_size(axis)
+    return lax.dynamic_slice_in_dim(values, lax.axis_index(axis) * count, count, 0)
+
+
 def gather_rows(local_rows):
-    return lax.all_gather(local_rows, "tensor", axis=0, tiled=True)
-
-
-def gather_grads(local_rows):
-    return lax.all_gather(local_rows, "tensor", axis=0, tiled=True)
+    if lax.axis_size("tensor") != 2:
+        return lax.all_gather(local_rows, "tensor", axis=0, tiled=True)
+    other = pair_swap(local_rows, "tensor", 1)
+    upper = my_bit("tensor", 1)
+    return jnp.concatenate(
+        [jnp.where(upper, other, local_rows), jnp.where(upper, local_rows, other)], axis=0
+    )
+
+
+gather_grads = gather_rows
+
+
+def scatter_rows(values, weight, product):
+    if lax.axis_size("tensor") != 2:
+        return lax.psum_scatter(
+            lowered(product(values, weight)), "tensor", scatter_dimension=0, tiled=True
+        ).astype(jnp.float32)
+    count = values.shape[0] // 2
+    place = lax.axis_index("tensor")
+    theirs = lax.dynamic_slice_in_dim(values, (1 - place) * count, count, 0)
+    got = pair_swap(lowered(product(theirs, weight)), "tensor", 1)
+    mine = lax.dynamic_slice_in_dim(values, place * count, count, 0)
+    return product(mine, weight) + got.astype(jnp.float32)
 
 
 def reduce_rows(values, weight):
-
-    def partial_term(offset, amount):
-        return matmul(values, weight)
-
-    return lax.psum_scatter(
-        partial_term(
-            jnp.int32(0), values.shape[0] // lax.axis_size("tensor") * lax.axis_size("tensor")
-        ).astype(jnp.bfloat16),
-        "tensor",
-        scatter_dimension=0,
-        tiled=True,
-    ).astype(jnp.float32)
+    return scatter_rows(values, weight, inner_columns)
 
 
 def reduce_back(values, weight):
-
-    def partial_term(offset, amount):
-        return inner_columns(values, weight)
-
-    return lax.psum_scatter(
-        partial_term(
-            jnp.int32(0), values.shape[0] // lax.axis_size("tensor") * lax.axis_size("tensor")
-        ).astype(jnp.bfloat16),
-        "tensor",
-        scatter_dimension=0,
-        tiled=True,
-    ).astype(jnp.float32)
+    return scatter_rows(values, weight, inner_columns)
+
+
+def feed_gather(values):
+    if lax.axis_size("tensor") != 2:
+        return lax.all_gather(values, "tensor", axis=1, tiled=True)
+    return jnp.concatenate([values, pair_swap(values, "tensor", 1)], axis=1)
+
+
+def feed_scatter(values):
+    if lax.axis_size("tensor") != 2:
+        return lax.psum_scatter(
+            lowered(values), "tensor", scatter_dimension=1, tiled=True
+        ).astype(jnp.float32)
+    count = values.shape[1] // 2
+    got = pair_swap(lowered(values[:, count:]), "tensor", 1)
+    return values[:, :count] + got.astype(jnp.float32)
 
 
 def head_forward(allowed, operands):
@@ -165,17 +233,19 @@
     ) & query_cont & earlier
     forward_head = partial(head_forward, allowed)
     backward_head = partial(head_backward, allowed)
+    orders = gather_orders(lax.axis_size("dp"))
     stored = []
     current = inputs
     for layer_index in range(LAYERS):
-        gathered = (
-            lax.all_gather(query_weight[layer_index], "dp", axis=0, tiled=True),
-            lax.all_gather(key_weight[layer_index], "dp", axis=0, tiled=True),
-            lax.all_gather(value_weight[layer_index], "dp", axis=0, tiled=True),
-            lax.all_gather(output_weight[layer_index], "dp", axis=1, tiled=True),
-            lax.all_gather(up_weight[layer_index], "dp", axis=0, tiled=True),
-            lax.all_gather(down_weight[layer_index], "dp", axis=1, tiled=True),
-        )
+        shards = (
+            query_weight[layer_index],
+            key_weight[layer_index],
+            value_weight[layer_index],
+            output_weight[layer_index].T,
+            up_weight[layer_index],
+            down_weight[layer_index].T,
+        )
+        gathered = [doubled_gather(*member) for member in zip(shards, orders)]
         joint_weight = jnp.concatenate([gathered[0], gathered[1], gathered[2]], axis=1)
         out_weight = gathered[3]
         inverse_attn = inverse_root(current)
@@ -198,14 +268,11 @@
         middle = current + reduce_rows(mixed, out_weight)
         inverse_feed = inverse_root(middle)
         feed_local = lowered(middle * inverse_feed * feed_gain[layer_index])
-        upper_weight, lower_weight = (
-            lax.all_gather(gathered[4], "tensor", axis=1, tiled=True),
-            lax.all_gather(gathered[5], "tensor", axis=0, tiled=True),
-        )
+        upper_weight, lower_weight = feed_gather(gathered[4]), feed_gather(gathered[5])
         feed_rows = feed_local
         upper = matmul(feed_rows, upper_weight)
         hidden = lowered(upper * jax.nn.sigmoid(upper))
-        branch_out = matmul(hidden, lower_weight)
+        branch_out = inner_columns(hidden, lower_weight)
         stored.append(
             (
                 current,
@@ -258,8 +325,8 @@
             hidden,
         ) = stored[layer_index]
         grad_low = lowered(grad)
-        down_grad = inner_rows(hidden, grad_low)
-        hidden_grad = lowered(inner_columns(grad_low, lower_weight))
+        down_grad = inner_rows(grad_low, hidden)
+        hidden_grad = lowered(matmul(grad_low, lower_weight))
         sigmoid_upper = jax.nn.sigmoid(upper)
         upper_grad = lowered(
             hidden_grad.astype(jnp.float32)
@@ -267,21 +334,14 @@
         )
         up_grad = inner_rows(feed_rows, upper_grad)
         feed_grad = inner_columns(upper_grad, upper_weight)
-        up_grad, down_grad = (
-            lax.psum_scatter(
-                up_grad.astype(jnp.bfloat16), "tensor", scatter_dimension=1, tiled=True
-            ).astype(jnp.float32),
-            lax.psum_scatter(
-                down_grad.astype(jnp.bfloat16), "tensor", scatter_dimension=0, tiled=True
-            ).astype(jnp.float32),
-        )
+        up_grad, down_grad = feed_scatter(up_grad), feed_scatter(down_grad)
         feed_gain_grad, middle_part = norm_backward(
             middle, inverse_feed, feed_gain[layer_index], feed_grad
         )
         grad_middle = grad + middle_part
         middle_rows = gather_grads(lowered(grad_middle))
-        out_grad = inner_rows(mixed, middle_rows)
-        mixed_grad = lowered(inner_columns(middle_rows, out_weight))
+        out_grad = inner_rows(middle_rows, mixed)
+        mixed_grad = lowered(matmul(middle_rows, out_weight))
         query_grads, key_grads, value_grads = lax.map(
             backward_head,
             (
@@ -333,7 +393,7 @@
         grad = grad_middle + input_part
         attention_grads[layer_index] = attention_gain_grad
         feed_grads[layer_index] = feed_gain_grad
-        layer_grads[layer_index] = (
+        members = (
             joint_weight_grad[:, :local_width],
             joint_weight_grad[:, local_width : 2 * local_width],
             joint_weight_grad[:, 2 * local_width :],
@@ -341,30 +401,15 @@
             up_grad,
             down_grad,
         )
-    stacked = [
+        reduced = [
+            halved_scatter(lowered(member), order) for member, order in zip(members, orders)
+        ]
+        reduced[3], reduced[5] = reduced[3].T, reduced[5].T
+        layer_grads[layer_index] = reduced
+    summed = [
         jnp.stack([layer_grads[depth_index][member] for depth_index in range(LAYERS)])
         for member in range(6)
     ]
-    summed = (
-        lax.psum_scatter(
-            stacked[0].astype(jnp.bfloat16), "dp", scatter_dimension=1, tiled=True
-        ).astype(jnp.float32),
-        lax.psum_scatter(
-            stacked[1].astype(jnp.bfloat16), "dp", scatter_dimension=1, tiled=True
-        ).astype(jnp.float32),
-        lax.psum_scatter(
-            stacked[2].astype(jnp.bfloat16), "dp", scatter_dimension=1, tiled=True
-        ).astype(jnp.float32),
-        lax.psum_scatter(
-            stacked[3].astype(jnp.bfloat16), "dp", scatter_dimension=2, tiled=True
-        ).astype(jnp.float32),
-        lax.psum_scatter(
-            stacked[4].astype(jnp.bfloat16), "dp", scatter_dimension=1, tiled=True
-        ).astype(jnp.float32),
-        lax.psum_scatter(
-            stacked[5].astype(jnp.bfloat16), "dp", scatter_dimension=2, tiled=True
-        ).astype(jnp.float32),
-    )
     attention_total, feed_total, scale_total = lax.psum(
         (jnp.stack(attention_grads), jnp.stack(feed_grads), jnp.stack(scale_grads)),
         ("dp", "tensor"),

time: 1920 us -> 1240 us (0.65)
  waiting for transfers between devices: 1070 us -> 317 us
  starting transfers between devices: 12.5 us -> 120 us
  other arithmetic: 102 us -> 153 us
  matrix products: 499 us -> 451 us
  local copies, waits for them, and re-layouts: 163 us -> 136 us
    all_gather x20 -> x0, waiting for transfers between devices: 516 us -> none  [the longest x2 121 us: body(): lax.all_gather(key_weight[layer_index], 'dp', axis=0, tiled=True)]
    ppermute x0 -> x112, waiting for transfers between devices: none -> 288 us  [pair_swap(): return lax.ppermute(values, axis, [(i, i ^ bit) for i in range(size)])]
    reduce_scatter x10 -> x0, waiting for transfers between devices: 267 us -> none  [the longest x1 82.4 us: body(): lax.psum_scatter(stacked[2].astype(jnp.bfloat16), 'dp', scatter_dimension...]
    unnamed x36 -> x0, waiting for transfers between devices: 224 us -> none
    ppermute x0 -> x112, starting transfers between devices: none -> 113 us  [pair_swap(): return lax.ppermute(values, axis, [(i, i ^ bit) for i in range(size)])]
    ppermute x8, waiting for transfers between devices: 66.7 us -> 29 us  [from_partner(): lax.ppermute(shard, axis, [(i, i ^ 1 << distance) for i in range(lax.axis...]
    concatenate x0 -> x2, other arithmetic: none -> 35 us  [body(): jnp.concatenate([lowered(query_heads * gain_q).reshape(row_total, local_w...]
    unnamed x184 -> x297, local copies, waits for them, and re-layouts: 71.4 us -> 37.5 us
  transfers between devices with their start and end apart: 41 -> 120, of which waited for: 30 -> 42; matrix products, arithmetic and copies ran while one was open for 29% -> 58% of each run, Pallas kernels for 0% -> 0%
where the time goes in v1:
time: 1240 us; the launch traced here: 1220 us
  matrix products  451 us (36%)
  waiting for transfers between devices  317 us (26%)
  other arithmetic  153 us (12%)
  local copies, waits for them, and re-layouts  136 us (11%)
  starting transfers between devices  120 us (10%)
  blocking collectives  38.4 us (3%)
    ppermute x112, waiting for transfers between devices, pair_swap(): return lax.ppermute(values, axis, [(i, i ^ bit) for i in range(size)])  288 us
    dot_general x60, matrix products, inner_columns(): lax.dot_general(former, latter, (((1,), (1,)), ((), ())), preferred_eleme...  223 us
    dot_general x40, matrix products, matmul(): return jnp.dot(former, latter, preferred_element_type=jnp.float32)  137 us
    ppermute x112, starting transfers between devices, pair_swap(): return lax.ppermute(values, axis, [(i, i ^ bit) for i in range(size)])  113 us
    dot_general x40, matrix products, inner_rows(): lax.dot_general(former, latter, (((0,), (0,)), ((), ())), preferred_eleme...  91.2 us
    psum x1, blocking collectives, body(): lax.psum((jnp.stack(attention_grads), jnp.stack(feed_grads), jnp.stack(sc...  38.4 us
    unnamed x297, local copies, waits for them, and re-layouts  37.5 us
    convert_element_type x60, other arithmetic, lowered(): return values.astype(jnp.bfloat16)  35.4 us
  transfers between devices with their start and end apart: 120, of which 42 were waited for; matrix products, arithmetic and copies ran while one was open for 58% of the time, Pallas kernels for 0%

profile of v1, /device:TPU:0, one launch (start us, length us, event | category | flops | bytes accessed | tf_op | source)
XLA Modules:
  0.0 1222.3 jit_solution(13738881878316074597)
XLA Ops:
  48.1 10.2 collective-permute-done.6
  80.9 14.9 %collective-permute-done.56 = bf16[2,80,640]{2,1,0:T(8,128)(2,1)S(1)} collective-permute-done((bf16[2,80,640]{2,1,0:T(8,128)(2,1)S(1)}, bf16[2,80,640]{2,1,0:T(8,128)(2,1)S(1)}, u32[]{:S(2)}, u32[]{:S(2)}) %collective-permute-start.56) | collective-permute-done | bytes 204832 | tf_op jit(solution)/shard_map/ppermute | solution.py:79
  109.8 13.7 %collective-permute-done.27 = bf16[2,2,80,640]{3,2,1,0:T(8,128)(2,1)S(1)} collective-permute-done((bf16[2,2,80,640]{3,2,1,0:T(8,128)(2,1)S(1)}, bf16[2,2,80,640]{3,2,1,0:T(8,128)(2,1)S(1)}, u32[]{:S(2)}, u32[]{:S(2)}) %collective-permute-start.27) | collective-permute-done | bytes 409632 | tf_op jit(solution)/shard_map/ppermute | solution.py:79
  134.4 6.3 collective-permute-done.33
  156.5 6.5 collective-permute-done.12
  165.0 10.8 collective-permute-done.8
  179.6 7.7 fusion.253
  230.1 68.8 %while.56 = (s32[]{:T(128)}, bf16[8,1024,80]{1,2,0:T(8,128)(2,1)}, f32[8,1024]{1,0:T(8,128)S(1)}, bf16[8,1024,80]{2,1,0:T(8,128)(2,1)}, bf16[8,1536,80]{2,1,0:T(...) while((s32[]{:T(128)}, bf16[8,1024,80]{1,2,0:T(8,128)(2,1)}, ...), condition=%wide.region_6.7_spmd.clone, body=%wide.region_3.6_spmd.clone.sunk | while | flops 525335552 | bytes 20316816 | solution.py:264
  320.3 8.6 collective-permute-done.38
  336.0 9.1 fusion.254
  388.7 68.8 %while.57 = (s32[]{:T(128)}, bf16[8,1024,80]{1,2,0:T(8,128)(2,1)}, f32[8,1024]{1,0:T(8,128)S(1)}, bf16[8,1024,80]{2,1,0:T(8,128)(2,1)}, bf16[8,1536,80]{2,1,0:T(...) while((s32[]{:T(128)}, bf16[8,1024,80]{1,2,0:T(8,128)(2,1)}, ...), condition=%wide.region_12.13_spmd.clone, body=%wide.region_9.12_spmd.clone.sunk | while | flops 525335552 | bytes 20316816 | solution.py:264
  481.4 6.5 multiply_reduce_fusion
  497.5 5.7 convolution_add_fusion
  515.5 117.5 %while.58 = (s32[]{:T(128)}, f32[8,1024,80]{1,2,0:T(8,128)}, f32[8,1536,80]{1,2,0:T(8,128)}, f32[8,1536,80]{1,2,0:T(8,128)}, bf16[8,1024,80]{2,1,0:T(8,128)(2,1)...) while((s32[]{:T(128)}, f32[8,1024,80]{1,2,0:T(8,128)}, ...), condition=%wide.region_17.18_spmd.clone, body=%wide.region_15.17_spmd.clone.sunk | while | flops 1286601728 | bytes 41336480 | solution.py:345
  517.7 5.0 fusion.321
  532.4 5.0 fusion.321
  547.0 5.0 fusion.321
  561.6 5.0 fusion.321
  576.2 5.0 fusion.321
  590.8 5.0 fusion.321
  605.3 5.0 fusion.321
  619.9 5.0 fusion.321
  655.1 13.8 %collective-permute-done.61 = bf16[512,640]{0,1:T(8,128)(2,1)S(1)} collective-permute-done((bf16[512,640]{0,1:T(8,128)(2,1)S(1)}, bf16[512,640]{0,1:T(8,128)(2,1)S(1)}, u32[]{:S(2)}, u32[]{:S(2)}) %collective-permute-start.61) | collective-permute-done | bytes 655392 | tf_op jit(solution)/shard_map/ppermute | solution.py:20
  669.1 17.4 %maximum_maximum_fusion = bf16[1024,1920]{0,1:T(8,128)(2,1)S(1)} fusion(bf16[512,640]{0,1:T(8,128)(2,1)S(1)} %bitcast.958, bf16[512,640]{0,1:T(8,128)(2,1)S(1)} %fusion.157, bf16[512,640]{0,1:T(8,128)(2,1)S(1)} %bitcast.962, bf16[512,640]{0,1:T(8,128)(2,1)S(1)} %fusion.158, bf16[1024,640]{0,1:T(8,128)(2,1)S(1)} %bitcast.947), kind=kLoop, calls=%fused_computation.127 | loop fusion | flops 19660800 | bytes 7864320 | tf_op jit(solution)/shard_map/concatenate | solution.py:380
  686.4 7.4 convolution_convert_fusion.2
  693.8 5.4 convolution_convert_fusion.11
  708.2 21.2 %collective-permute-done.97 = bf16[2,2,80,640]{3,2,0,1:T(8,128)(2,1)S(1)} collective-permute-done((bf16[2,2,80,640]{3,2,0,1:T(8,128)(2,1)S(1)}, bf16[2,2,80,640]{3,2,0,1:T(8,128)(2,1)S(1)}, u32[]{:S(2)}, u32[]{:S(2)}) %collective-permute-start.97) | collective-permute-done | bytes 409632 | tf_op jit(solution)/shard_map/ppermute | solution.py:79
  731.2 5.1 collective-permute-done.98
  743.4 13.1 %collective-permute-done.99 = bf16[80,640]{1,0:T(8,128)(2,1)S(1)} collective-permute-done((bf16[80,640]{1,0:T(8,128)(2,1)S(1)}, bf16[80,640]{1,0:T(8,128)(2,1)S(1)}, u32[]{:S(2)}, u32[]{:S(2)}) %collective-permute-start.99) | collective-permute-done | bytes 102432 | tf_op jit(solution)/shard_map/ppermute | solution.py:79
  762.2 24.1 %collective-permute-done.108 = bf16[2,80,640]{2,1,0:T(8,128)(2,1)S(1)} collective-permute-done((bf16[2,80,640]{2,1,0:T(8,128)(2,1)S(1)}, bf16[2,80,640]{2,1,0:T(8,128)(2,1)S(1)}, u32[]{:S(2)}, u32[]{:S(2)}) %collective-permute-start.108) | collective-permute-done | bytes 204832 | tf_op jit(solution)/shard_map/ppermute | solution.py:79
  786.4 10.0 collective-permute-done.118
  836.8 6.9 collective-permute-done.75
  861.5 123.3 %while.59 = (s32[]{:T(128)}, f32[8,1024,80]{1,2,0:T(8,128)}, f32[8,1536,80]{1,2,0:T(8,128)}, f32[8,1536,80]{1,2,0:T(8,128)}, bf16[8,1024,80]{2,1,0:T(8,128)(2,1)...) while((s32[]{:T(128)}, f32[8,1024,80]{1,2,0:T(8,128)}, ...), condition=%wide.region_22.23_spmd.clone, body=%wide.region_20.22_spmd.clone.sunk | while | flops 1286601728 | bytes 41336480 | solution.py:345
  864.4 5.0 fusion.334
  879.8 5.0 fusion.334
  925.9 5.0 fusion.334
  971.9 5.0 fusion.334
  1006.9 13.8 %collective-permute-done.65 = bf16[512,640]{0,1:T(8,128)(2,1)S(1)} collective-permute-done((bf16[512,640]{0,1:T(8,128)(2,1)S(1)}, bf16[512,640]{0,1:T(8,128)(2,1)S(1)}, u32[]{:S(2)}, u32[]{:S(2)}) %collective-permute-start.65) | collective-permute-done | bytes 655392 | tf_op jit(solution)/shard_map/ppermute | solution.py:20
  1020.9 17.6 %maximum_maximum_fusion.1 = bf16[1024,1920]{0,1:T(8,128)(2,1)S(1)} fusion(bf16[512,640]{0,1:T(8,128)(2,1)S(1)} %bitcast.956, bf16[512,640]{0,1:T(8,128)(2,1)S(1)} %fusion.155, bf16[512,640]{0,1:T(8,128)(2,1)S(1)} %bitcast.960, bf16[512,640]{0,1:T(8,128)(2,1)S(1)} %fusion.156, bf16[1024,640]{0,1:T(8,128)(2,1)S(1)} %bitcast.945), kind=kLoop, calls=%fused_computation.128 | loop fusion | flops 19660800 | bytes 7864320 | tf_op jit(solution)/shard_map/concatenate | solution.py:380
  1038.5 7.4 convolution_convert_fusion.3
  1045.9 5.4 convolution_convert_fusion.10
  1058.7 22.8 %collective-permute-done.93 = bf16[2,2,80,640]{3,2,0,1:T(8,128)(2,1)S(1)} collective-permute-done((bf16[2,2,80,640]{3,2,0,1:T(8,128)(2,1)S(1)}, bf16[2,2,80,640]{3,2,0,1:T(8,128)(2,1)S(1)}, u32[]{:S(2)}, u32[]{:S(2)}) %collective-permute-start.93) | collective-permute-done | bytes 409632 | tf_op jit(solution)/shard_map/ppermute | solution.py:79
  1081.8 6.6 collective-permute-done.94
  1093.1 14.6 %collective-permute-done.95 = bf16[80,640]{1,0:T(8,128)(2,1)S(1)} collective-permute-done((bf16[80,640]{1,0:T(8,128)(2,1)S(1)}, bf16[80,640]{1,0:T(8,128)(2,1)S(1)}, u32[]{:S(2)}, u32[]{:S(2)}) %collective-permute-start.95) | collective-permute-done | bytes 102432 | tf_op jit(solution)/shard_map/ppermute | solution.py:79
  1113.8 24.4 %collective-permute-done.103 = bf16[2,80,640]{2,1,0:T(8,128)(2,1)S(1)} collective-permute-done((bf16[2,80,640]{2,1,0:T(8,128)(2,1)S(1)}, bf16[2,80,640]{2,1,0:T(8,128)(2,1)S(1)}, u32[]{:S(2)}, u32[]{:S(2)}) %collective-permute-start.103) | collective-permute-done | bytes 204832 | tf_op jit(solution)/shard_map/ppermute | solution.py:79
  1138.2 10.0 collective-permute-done.113
  1169.9 38.4 %all-reduce.1 = (f32[2,1280]{1,0:T(2,128)}, f32[2,1280]{1,0:T(2,128)}, f32[2,80]{1,0:T(2,128)}) all-reduce(f32[2,1280]{1,0:T(2,128)S(1)} %pad_maximum_fusion.88, f32[2,1280]{1,0:T(2,128)S(1)} %copy-done.112, f32[2,80]{1,0:T(2,128)S(1)} %pad_maximum_fusion.90), channel_id=1, replica_groups=mesh['dp'=16,'tensor'=2] {'dp','tensor'}, use_global_device_ids=true, to_apply=%region_26.27 | all-reduce | flops 5280 | bytes 42240 | tf_op jit(solution)/shard_map/psum | solution.py:413
  1213.9 5.4 collective-permute-done.71
  (1033 shorter events, 765.2 us)
Async XLA Ops:
  28.5 126.1 %collective-permute-start = (bf16[512,1280]{1,0:T(8,128)(2,1)}, bf16[512,1280]{1,0:T(8,128)(2,1)S(1)}, u32[]{:S(2)}, u32[]{:S(2)}) collective-permute-start(bf16[512,1280]{1,0:T(8,128)(2,1)} %multiply_convert_fusion.7), channel_id=1, source_target_pairs={{0,1},{1,0},{2,3},{3,2},{4,5},{5,4},{6,7},{7,6},{8,9},{9,8},{10,11... | collective-permute-start | bytes 3932168 | tf_op jit(solution)/shard_map/ppermute | solution.py:79
  70.3 25.5 %collective-permute-start.56 = (bf16[2,80,640]{2,1,0:T(8,128)(2,1)S(1)}, bf16[2,80,640]{2,1,0:T(8,128)(2,1)S(1)}, u32[]{:S(2)}, u32[]{:S(2)}) collective-permute-start(bf16[2,80,640]{2,1,0:T(8,128)(2,1)S(1)} %pad_maximum_fusion.87), channel_id=1, source_target_pairs={{0,16},{2,18},{4,20},{6,22},{8,24},{10,26},{12,28},{14,30},{16,0},... | collective-permute-start | bytes 614408 | tf_op jit(solution)/shard_map/ppermute | solution.py:79
  74.0 26.2 %collective-permute-start.51 = (bf16[2,80,640]{2,1,0:T(8,128)(2,1)S(1)}, bf16[2,80,640]{2,1,0:T(8,128)(2,1)S(1)}, u32[]{:S(2)}, u32[]{:S(2)}) collective-permute-start(bf16[2,80,640]{2,1,0:T(8,128)(2,1)S(1)} %pad_maximum_fusion.86), channel_id=1, source_target_pairs={{0,16},{2,18},{4,20},{6,22},{8,24},{10,26},{12,28},{14,30},{16,0},... | collective-permute-start | bytes 614408 | tf_op jit(solution)/shard_map/ppermute | solution.py:79
  80.3 25.8 %collective-permute-start.11 = (bf16[2,2,80,640]{3,2,1,0:T(8,128)(2,1)S(1)}, bf16[2,2,80,640]{3,2,1,0:T(8,128)(2,1)S(1)}, u32[]{:S(2)}, u32[]{:S(2)}) collective-permute-start(bf16[2,2,80,640]{3,2,1,0:T(8,128)(2,1)S(1)} %pad_maximum_fusion.60), channel_id=1, source_target_pairs={{0,16},{2,18},{4,20},{6,22},{8,24},{10,26},{12,28},{14,30},{16,0},... | collective-permute-start | bytes 1228808 | tf_op jit(solution)/shard_map/ppermute | solution.py:79
  134.2 62.8 %collective-permute-start.18 = (bf16[2,2,2,80,640]{4,3,0,1,2:T(8,128)(2,1)}, bf16[2,2,2,80,640]{4,3,0,1,2:T(8,128)(2,1)}, u32[]{:S(2)}, u32[]{:S(2)}) collective-permute-start(bf16[2,2,2,80,640]{4,3,0,1,2:T(8,128)(2,1)} %pad_maximum_fusion.49), channel_id=1, source_target_pairs={{0,4},{2,6},{4,0},{6,2},{8,12},{10,14},{12,8},{14,10},{16,20},{18,... | collective-permute-start | bytes 2457608 | tf_op jit(solution)/shard_map/ppermute | solution.py:79
  145.9 29.9 %collective-permute-start.8 = (bf16[2,2,2,80,640]{4,3,0,1,2:T(8,128)(2,1)S(1)}, bf16[2,2,2,80,640]{4,3,0,1,2:T(8,128)(2,1)S(1)}, u32[]{:S(2)}, u32[]{:S(2)}) collective-permute-start(bf16[2,2,2,80,640]{4,3,0,1,2:T(8,128)(2,1)S(1)} %pad_maximum_fusion.47), channel_id=1, source_target_pairs={{0,4},{2,6},{4,0},{6,2},{8,12},{10,14},{12,8},{14,10},{16,20},{18,... | collective-permute-start | bytes 2457608 | tf_op jit(solution)/shard_map/ppermute | solution.py:79
  151.8 26.7 %collective-permute-start.4 = (bf16[2,2,2,80,640]{4,3,2,1,0:T(8,128)(2,1)S(1)}, bf16[2,2,2,80,640]{4,3,2,1,0:T(8,128)(2,1)S(1)}, u32[]{:S(2)}, u32[]{:S(2)}) collective-permute-start(bf16[2,2,2,80,640]{4,3,2,1,0:T(8,128)(2,1)S(1)} %pad_maximum_fusion.46), channel_id=1, source_target_pairs={{0,2},{2,0},{4,6},{6,4},{8,10},{10,8},{12,14},{14,12},{16,18},{18,... | collective-permute-start | bytes 2457608 | tf_op jit(solution)/shard_map/ppermute | solution.py:79
  154.6 149.6 %collective-permute-start.28 = (bf16[2,2,2,80,640]{4,3,2,0,1:T(8,128)(2,1)}, bf16[2,2,2,80,640]{4,3,2,0,1:T(8,128)(2,1)}, u32[]{:S(2)}, u32[]{:S(2)}) collective-permute-start(bf16[2,2,2,80,640]{4,3,2,0,1:T(8,128)(2,1)} %pad_maximum_fusion.51), channel_id=1, source_target_pairs={{0,2},{2,0},{4,6},{6,4},{8,10},{10,8},{12,14},{14,12},{16,18},{18,... | collective-permute-start | bytes 2457608 | tf_op jit(solution)/shard_map/ppermute | solution.py:79
  163.0 138.9 %collective-permute-start.23 = (bf16[2,2,2,80,640]{4,3,2,0,1:T(8,128)(2,1)}, bf16[2,2,2,80,640]{4,3,2,0,1:T(8,128)(2,1)}, u32[]{:S(2)}, u32[]{:S(2)}) collective-permute-start(bf16[2,2,2,80,640]{4,3,2,0,1:T(8,128)(2,1)} %pad_maximum_fusion.50), channel_id=1, source_target_pairs={{0,4},{2,6},{4,0},{6,2},{8,12},{10,14},{12,8},{14,10},{16,20},{18,... | collective-permute-start | bytes 2457608 | tf_op jit(solution)/shard_map/ppermute | solution.py:79
  175.8 157.4 %collective-permute-start.48 = (bf16[2,2,2,80,640]{4,3,0,1,2:T(8,128)(2,1)}, bf16[2,2,2,80,640]{4,3,0,1,2:T(8,128)(2,1)}, u32[]{:S(2)}, u32[]{:S(2)}) collective-permute-start(bf16[2,2,2,80,640]{4,3,0,1,2:T(8,128)(2,1)} %pad_maximum_fusion.55), channel_id=1, source_target_pairs={{0,4},{2,6},{4,0},{6,2},{8,12},{10,14},{12,8},{14,10},{16,20},{18,... | collective-permute-start | bytes 2457608 | tf_op jit(solution)/shard_map/ppermute | solution.py:79
  207.7 101.0 %collective-permute-start.42 = (bf16[2,2,2,80,640]{4,3,2,1,0:T(8,128)(2,1)}, bf16[2,2,2,80,640]{4,3,2,1,0:T(8,128)(2,1)}, u32[]{:S(2)}, u32[]{:S(2)}) collective-permute-start(bf16[2,2,2,80,640]{4,3,2,1,0:T(8,128)(2,1)} %pad_maximum_fusion.54), channel_id=1, source_target_pairs={{0,8},{2,10},{4,12},{6,14},{8,0},{10,2},{12,4},{14,6},{16,24},{18,... | collective-permute-start | bytes 2457608 | tf_op jit(solution)/shard_map/ppermute | solution.py:79
  313.3 151.5 %collective-permute-start.58 = (bf16[2,2,2,80,640]{4,3,2,0,1:T(8,128)(2,1)}, bf16[2,2,2,80,640]{4,3,2,0,1:T(8,128)(2,1)}, u32[]{:S(2)}, u32[]{:S(2)}) collective-permute-start(bf16[2,2,2,80,640]{4,3,2,0,1:T(8,128)(2,1)} %pad_maximum_fusion.57), channel_id=1, source_target_pairs={{0,2},{2,0},{4,6},{6,4},{8,10},{10,8},{12,14},{14,12},{16,18},{18,... | collective-permute-start | bytes 2457608 | tf_op jit(solution)/shard_map/ppermute | solution.py:79
  328.9 132.6 %collective-permute-start.53 = (bf16[2,2,2,80,640]{4,3,0,1,2:T(8,128)(2,1)}, bf16[2,2,2,80,640]{4,3,0,1,2:T(8,128)(2,1)}, u32[]{:S(2)}, u32[]{:S(2)}) collective-permute-start(bf16[2,2,2,80,640]{4,3,0,1,2:T(8,128)(2,1)} %pad_maximum_fusion.56), channel_id=1, source_target_pairs={{0,4},{2,6},{4,0},{6,2},{8,12},{10,14},{12,8},{14,10},{16,20},{18,... | collective-permute-start | bytes 2457608 | tf_op jit(solution)/shard_map/ppermute | solution.py:79
  491.9 153.9 %collective-permute-start.105 = (bf16[1280,640]{1,0:T(8,128)(2,1)}, bf16[1280,640]{1,0:T(8,128)(2,1)}, u32[]{:S(2)}, u32[]{:S(2)}) collective-permute-start(bf16[1280,640]{1,0:T(8,128)(2,1)} %slice.422), channel_id=1, source_target_pairs={{0,1},{1,0},{2,3},{3,2},{4,5},{5,4},{6,7},{7,6},{8,9},{9,8},{10,11... | collective-permute-start | bytes 4915208 | tf_op jit(solution)/shard_map/ppermute | solution.py:79
  495.8 154.2 %collective-permute-start.115 = (bf16[1280,640]{1,0:T(8,128)(2,1)}, bf16[1280,640]{1,0:T(8,128)(2,1)}, u32[]{:S(2)}, u32[]{:S(2)}) collective-permute-start(bf16[1280,640]{1,0:T(8,128)(2,1)} %slice.420), channel_id=1, source_target_pairs={{0,1},{1,0},{2,3},{3,2},{4,5},{5,4},{6,7},{7,6},{8,9},{9,8},{10,11... | collective-permute-start | bytes 4915208 | tf_op jit(solution)/shard_map/ppermute | solution.py:79
  638.5 30.4 %collective-permute-start.61 = (bf16[512,640]{0,1:T(8,128)(2,1)S(1)}, bf16[512,640]{0,1:T(8,128)(2,1)S(1)}, u32[]{:S(2)}, u32[]{:S(2)}) collective-permute-start(bf16[512,640]{0,1:T(8,128)(2,1)S(1)} %bitcast.999), channel_id=1, source_target_pairs={{0,2},{2,0},{4,6},{6,4},{8,10},{10,8},{12,14},{14,12},{16,18},{18,... | collective-permute-start | bytes 1966088 | tf_op jit(solution)/shard_map/ppermute | solution.py:20
  643.7 57.4 %collective-permute-start.96 = (bf16[2,2,2,80,640]{4,3,0,1,2:T(8,128)(2,1)}, bf16[2,2,2,80,640]{4,3,0,1,2:T(8,128)(2,1)S(1)}, u32[]{:S(2)}, u32[]{:S(2)}) collective-permute-start(bf16[2,2,2,80,640]{4,3,0,1,2:T(8,128)(2,1)} %bitcast.828), channel_id=1, source_target_pairs={{0,4},{2,6},{4,0},{6,2},{8,12},{10,14},{12,8},{14,10},{16,20},{18,... | collective-permute-start | bytes 2457608 | tf_op jit(solution)/shard_map/ppermute | solution.py:79
  648.9 53.2 %collective-permute-start.106 = (bf16[2,2,2,80,640]{4,3,2,0,1:T(8,128)(2,1)}, bf16[2,2,2,80,640]{4,3,2,0,1:T(8,128)(2,1)}, u32[]{:S(2)}, u32[]{:S(2)}) collective-permute-start(bf16[2,2,2,80,640]{4,3,2,0,1:T(8,128)(2,1)} %bitcast.826), channel_id=1, source_target_pairs={{0,4},{2,6},{4,0},{6,2},{8,12},{10,14},{12,8},{14,10},{16,20},{18,... | collective-permute-start | bytes 2457608 | tf_op jit(solution)/shard_map/ppermute | solution.py:79
  652.9 52.1 %collective-permute-start.116 = (bf16[2,2,2,80,640]{4,3,2,0,1:T(8,128)(2,1)}, bf16[2,2,2,80,640]{4,3,2,0,1:T(8,128)(2,1)}, u32[]{:S(2)}, u32[]{:S(2)}) collective-permute-start(bf16[2,2,2,80,640]{4,3,2,0,1:T(8,128)(2,1)} %bitcast.824), channel_id=1, source_target_pairs={{0,2},{2,0},{4,6},{6,4},{8,10},{10,8},{12,14},{14,12},{16,18},{18,... | collective-permute-start | bytes 2457608 | tf_op jit(solution)/shard_map/ppermute | solution.py:79
  699.2 110.9 %collective-permute-start.63 = (bf16[512,1280]{1,0:T(8,128)(2,1)S(1)}, bf16[512,1280]{1,0:T(8,128)(2,1)}, u32[]{:S(2)}, u32[]{:S(2)}) collective-permute-start(bf16[512,1280]{1,0:T(8,128)(2,1)S(1)} %convolution_convert_fusion.11), channel_id=1, source_target_pairs={{0,1},{1,0},{2,3},{3,2},{4,5},{5,4},{6,7},{7,6},{8,9},{9,8},{10,11... | collective-permute-start | bytes 3932168 | tf_op jit(solution)/shard_map/ppermute | solution.py:79
  700.0 38.0 %collective-permute-start.72 = (bf16[2,2,2,80,640]{4,3,0,1,2:T(8,128)(2,1)S(1)}, bf16[2,2,2,80,640]{4,3,0,1,2:T(8,128)(2,1)S(1)}, u32[]{:S(2)}, u32[]{:S(2)}) collective-permute-start(bf16[2,2,2,80,640]{4,3,0,1,2:T(8,128)(2,1)S(1)} %bitcast.994), channel_id=1, source_target_pairs={{0,2},{2,0},{4,6},{6,4},{8,10},{10,8},{12,14},{14,12},{16,18},{18,... | collective-permute-start | bytes 2457608 | tf_op jit(solution)/shard_map/ppermute | solution.py:79
  701.1 40.7 %collective-permute-start.80 = (bf16[2,2,2,80,640]{4,3,0,1,2:T(8,128)(2,1)S(1)}, bf16[2,2,2,80,640]{4,3,0,1,2:T(8,128)(2,1)S(1)}, u32[]{:S(2)}, u32[]{:S(2)}) collective-permute-start(bf16[2,2,2,80,640]{4,3,0,1,2:T(8,128)(2,1)S(1)} %bitcast.992), channel_id=1, source_target_pairs={{0,4},{2,6},{4,0},{6,2},{8,12},{10,14},{12,8},{14,10},{16,20},{18,... | collective-permute-start | bytes 2457608 | tf_op jit(solution)/shard_map/ppermute | solution.py:79
  702.1 27.3 %collective-permute-start.97 = (bf16[2,2,80,640]{3,2,0,1:T(8,128)(2,1)S(1)}, bf16[2,2,80,640]{3,2,0,1:T(8,128)(2,1)S(1)}, u32[]{:S(2)}, u32[]{:S(2)}) collective-permute-start(bf16[2,2,80,640]{3,2,0,1:T(8,128)(2,1)S(1)} %dynamic-slice_bitcast_fusion.6), channel_id=1, source_target_pairs={{0,2},{2,0},{4,6},{6,4},{8,10},{10,8},{12,14},{14,12},{16,18},{18,... | collective-permute-start | bytes 1228808 | tf_op jit(solution)/shard_map/ppermute | solution.py:79
  705.0 33.8 %collective-permute-start.88 = (bf16[2,2,2,80,640]{4,3,2,1,0:T(8,128)(2,1)S(1)}, bf16[2,2,2,80,640]{4,3,2,1,0:T(8,128)(2,1)S(1)}, u32[]{:S(2)}, u32[]{:S(2)}) collective-permute-start(bf16[2,2,2,80,640]{4,3,2,1,0:T(8,128)(2,1)S(1)} %dynamic-slice_bitcast_fusion), channel_id=1, source_target_pairs={{0,8},{2,10},{4,12},{6,14},{8,0},{10,2},{12,4},{14,6},{16,24},{18,... | collective-permute-start | bytes 2457608 | tf_op jit(solution)/shard_map/ppermute | solution.py:79
  741.8 64.6 %collective-permute-start.73 = (bf16[2,2,80,640]{3,2,0,1:T(8,128)(2,1)S(1)}, bf16[2,2,80,640]{3,2,0,1:T(8,128)(2,1)S(1)}, u32[]{:S(2)}, u32[]{:S(2)}) collective-permute-start(bf16[2,2,80,640]{3,2,0,1:T(8,128)(2,1)S(1)} %dynamic-slice_bitcast_fusion.12), channel_id=1, source_target_pairs={{0,4},{2,6},{4,0},{6,2},{8,12},{10,14},{12,8},{14,10},{16,20},{18,... | collective-permute-start | bytes 1228808 | tf_op jit(solution)/shard_map/ppermute | solution.py:79
  756.5 50.1 %collective-permute-start.81 = (bf16[2,2,80,640]{3,2,0,1:T(8,128)(2,1)S(1)}, bf16[2,2,80,640]{3,2,0,1:T(8,128)(2,1)S(1)}, u32[]{:S(2)}, u32[]{:S(2)}) collective-permute-start(bf16[2,2,80,640]{3,2,0,1:T(8,128)(2,1)S(1)} %dynamic-slice_bitcast_fusion.10), channel_id=1, source_target_pairs={{0,2},{2,0},{4,6},{6,4},{8,10},{10,8},{12,14},{14,12},{16,18},{18,... | collective-permute-start | bytes 1228808 | tf_op jit(solution)/shard_map/ppermute | solution.py:79
  758.0 50.9 %collective-permute-start.89 = (bf16[2,2,80,640]{3,2,1,0:T(8,128)(2,1)S(1)}, bf16[2,2,80,640]{3,2,1,0:T(8,128)(2,1)S(1)}, u32[]{:S(2)}, u32[]{:S(2)}) collective-permute-start(bf16[2,2,80,640]{3,2,1,0:T(8,128)(2,1)S(1)} %dynamic-slice_bitcast_fusion.8), channel_id=1, source_target_pairs={{0,16},{2,18},{4,20},{6,22},{8,24},{10,26},{12,28},{14,30},{16,0},... | collective-permute-start | bytes 1228808 | tf_op jit(solution)/shard_map/ppermute | solution.py:79
  806.6 26.9 %collective-permute-start.74 = (bf16[2,80,640]{2,1,0:T(8,128)(2,1)S(1)}, bf16[2,80,640]{2,1,0:T(8,128)(2,1)S(1)}, u32[]{:S(2)}, u32[]{:S(2)}) collective-permute-start(bf16[2,80,640]{2,1,0:T(8,128)(2,1)S(1)} %dynamic-slice_bitcast_fusion.24), channel_id=1, source_target_pairs={{0,8},{2,10},{4,12},{6,14},{8,0},{10,2},{12,4},{14,6},{16,24},{18,... | collective-permute-start | bytes 614408 | tf_op jit(solution)/shard_map/ppermute | solution.py:79
  806.8 26.8 %collective-permute-start.82 = (bf16[2,80,640]{2,1,0:T(8,128)(2,1)S(1)}, bf16[2,80,640]{2,1,0:T(8,128)(2,1)S(1)}, u32[]{:S(2)}, u32[]{:S(2)}) collective-permute-start(bf16[2,80,640]{2,1,0:T(8,128)(2,1)S(1)} %dynamic-slice_bitcast_fusion.22), channel_id=1, source_target_pairs={{0,8},{2,10},{4,12},{6,14},{8,0},{10,2},{12,4},{14,6},{16,24},{18,... | collective-permute-start | bytes 614408 | tf_op jit(solution)/shard_map/ppermute | solution.py:79
  809.0 25.1 %collective-permute-start.90 = (bf16[2,80,640]{2,1,0:T(8,128)(2,1)S(1)}, bf16[2,80,640]{2,1,0:T(8,128)(2,1)S(1)}, u32[]{:S(2)}, u32[]{:S(2)}) collective-permute-start(bf16[2,80,640]{2,1,0:T(8,128)(2,1)S(1)} %dynamic-slice_bitcast_fusion.20), channel_id=1, source_target_pairs={{0,4},{2,6},{4,0},{6,2},{8,12},{10,14},{12,8},{14,10},{16,20},{18,... | collective-permute-start | bytes 614408 | tf_op jit(solution)/shard_map/ppermute | solution.py:79
  830.4 167.2 %collective-permute-start.100 = (bf16[1280,640]{1,0:T(8,128)(2,1)}, bf16[1280,640]{1,0:T(8,128)(2,1)}, u32[]{:S(2)}, u32[]{:S(2)}) collective-permute-start(bf16[1280,640]{1,0:T(8,128)(2,1)} %slice.423), channel_id=1, source_target_pairs={{0,1},{1,0},{2,3},{3,2},{4,5},{5,4},{6,7},{7,6},{8,9},{9,8},{10,11... | collective-permute-start | bytes 4915208 | tf_op jit(solution)/shard_map/ppermute | solution.py:79
  833.5 168.6 %collective-permute-start.110 = (bf16[1280,640]{1,0:T(8,128)(2,1)}, bf16[1280,640]{1,0:T(8,128)(2,1)}, u32[]{:S(2)}, u32[]{:S(2)}) collective-permute-start(bf16[1280,640]{1,0:T(8,128)(2,1)} %slice.421), channel_id=1, source_target_pairs={{0,1},{1,0},{2,3},{3,2},{4,5},{5,4},{6,7},{7,6},{8,9},{9,8},{10,11... | collective-permute-start | bytes 4915208 | tf_op jit(solution)/shard_map/ppermute | solution.py:79
  990.7 30.0 %collective-permute-start.65 = (bf16[512,640]{0,1:T(8,128)(2,1)S(1)}, bf16[512,640]{0,1:T(8,128)(2,1)S(1)}, u32[]{:S(2)}, u32[]{:S(2)}) collective-permute-start(bf16[512,640]{0,1:T(8,128)(2,1)S(1)} %bitcast.997), channel_id=1, source_target_pairs={{0,2},{2,0},{4,6},{6,4},{8,10},{10,8},{12,14},{14,12},{16,18},{18,... | collective-permute-start | bytes 1966088 | tf_op jit(solution)/shard_map/ppermute | solution.py:20
  995.9 57.6 %collective-permute-start.92 = (bf16[2,2,2,80,640]{4,3,0,1,2:T(8,128)(2,1)}, bf16[2,2,2,80,640]{4,3,0,1,2:T(8,128)(2,1)S(1)}, u32[]{:S(2)}, u32[]{:S(2)}) collective-permute-start(bf16[2,2,2,80,640]{4,3,0,1,2:T(8,128)(2,1)} %bitcast.829), channel_id=1, source_target_pairs={{0,4},{2,6},{4,0},{6,2},{8,12},{10,14},{12,8},{14,10},{16,20},{18,... | collective-permute-start | bytes 2457608 | tf_op jit(solution)/shard_map/ppermute | solution.py:79
  1001.0 53.8 %collective-permute-start.101 = (bf16[2,2,2,80,640]{4,3,2,0,1:T(8,128)(2,1)}, bf16[2,2,2,80,640]{4,3,2,0,1:T(8,128)(2,1)}, u32[]{:S(2)}, u32[]{:S(2)}) collective-permute-start(bf16[2,2,2,80,640]{4,3,2,0,1:T(8,128)(2,1)} %bitcast.827), channel_id=1, source_target_pairs={{0,4},{2,6},{4,0},{6,2},{8,12},{10,14},{12,8},{14,10},{16,20},{18,... | collective-permute-start | bytes 2457608 | tf_op jit(solution)/shard_map/ppermute | solution.py:79
  1005.0 52.2 %collective-permute-start.111 = (bf16[2,2,2,80,640]{4,3,2,0,1:T(8,128)(2,1)}, bf16[2,2,2,80,640]{4,3,2,0,1:T(8,128)(2,1)}, u32[]{:S(2)}, u32[]{:S(2)}) collective-permute-start(bf16[2,2,2,80,640]{4,3,2,0,1:T(8,128)(2,1)} %bitcast.825), channel_id=1, source_target_pairs={{0,2},{2,0},{4,6},{6,4},{8,10},{10,8},{12,14},{14,12},{16,18},{18,... | collective-permute-start | bytes 2457608 | tf_op jit(solution)/shard_map/ppermute | solution.py:79
  1051.3 111.7 %collective-permute-start.67 = (bf16[512,1280]{1,0:T(8,128)(2,1)S(1)}, bf16[512,1280]{1,0:T(8,128)(2,1)}, u32[]{:S(2)}, u32[]{:S(2)}) collective-permute-start(bf16[512,1280]{1,0:T(8,128)(2,1)S(1)} %convolution_convert_fusion.10), channel_id=1, source_target_pairs={{0,1},{1,0},{2,3},{3,2},{4,5},{5,4},{6,7},{7,6},{8,9},{9,8},{10,11... | collective-permute-start | bytes 3932168 | tf_op jit(solution)/shard_map/ppermute | solution.py:79
  1052.0 36.8 %collective-permute-start.68 = (bf16[2,2,2,80,640]{4,3,0,1,2:T(8,128)(2,1)S(1)}, bf16[2,2,2,80,640]{4,3,0,1,2:T(8,128)(2,1)S(1)}, u32[]{:S(2)}, u32[]{:S(2)}) collective-permute-start(bf16[2,2,2,80,640]{4,3,0,1,2:T(8,128)(2,1)S(1)} %bitcast.995), channel_id=1, source_target_pairs={{0,2},{2,0},{4,6},{6,4},{8,10},{10,8},{12,14},{14,12},{16,18},{18,... | collective-permute-start | bytes 2457608 | tf_op jit(solution)/shard_map/ppermute | solution.py:79
  1053.6 37.3 %collective-permute-start.76 = (bf16[2,2,2,80,640]{4,3,0,1,2:T(8,128)(2,1)S(1)}, bf16[2,2,2,80,640]{4,3,0,1,2:T(8,128)(2,1)S(1)}, u32[]{:S(2)}, u32[]{:S(2)}) collective-permute-start(bf16[2,2,2,80,640]{4,3,0,1,2:T(8,128)(2,1)S(1)} %bitcast.993), channel_id=1, source_target_pairs={{0,4},{2,6},{4,0},{6,2},{8,12},{10,14},{12,8},{14,10},{16,20},{18,... | collective-permute-start | bytes 2457608 | tf_op jit(solution)/shard_map/ppermute | solution.py:79
  1054.8 26.7 %collective-permute-start.93 = (bf16[2,2,80,640]{3,2,0,1:T(8,128)(2,1)S(1)}, bf16[2,2,80,640]{3,2,0,1:T(8,128)(2,1)S(1)}, u32[]{:S(2)}, u32[]{:S(2)}) collective-permute-start(bf16[2,2,80,640]{3,2,0,1:T(8,128)(2,1)S(1)} %dynamic-slice_bitcast_fusion.7), channel_id=1, source_target_pairs={{0,2},{2,0},{4,6},{6,4},{8,10},{10,8},{12,14},{14,12},{16,18},{18,... | collective-permute-start | bytes 1228808 | tf_op jit(solution)/shard_map/ppermute | solution.py:79
  1057.2 34.7 %collective-permute-start.84 = (bf16[2,2,2,80,640]{4,3,2,1,0:T(8,128)(2,1)S(1)}, bf16[2,2,2,80,640]{4,3,2,1,0:T(8,128)(2,1)S(1)}, u32[]{:S(2)}, u32[]{:S(2)}) collective-permute-start(bf16[2,2,2,80,640]{4,3,2,1,0:T(8,128)(2,1)S(1)} %dynamic-slice_bitcast_fusion.1), channel_id=1, source_target_pairs={{0,8},{2,10},{4,12},{6,14},{8,0},{10,2},{12,4},{14,6},{16,24},{18,... | collective-permute-start | bytes 2457608 | tf_op jit(solution)/shard_map/ppermute | solution.py:79
  1088.8 24.7 %collective-permute-start.112 = (bf16[2,2,80,640]{3,2,1,0:T(8,128)(2,1)S(1)}, bf16[2,2,80,640]{3,2,1,0:T(8,128)(2,1)S(1)}, u32[]{:S(2)}, u32[]{:S(2)}) collective-permute-start(bf16[2,2,80,640]{3,2,1,0:T(8,128)(2,1)S(1)} %dynamic-slice_bitcast_fusion.3), channel_id=1, source_target_pairs={{0,8},{2,10},{4,12},{6,14},{8,0},{10,2},{12,4},{14,6},{16,24},{18,... | collective-permute-start | bytes 1228808 | tf_op jit(solution)/shard_map/ppermute | solution.py:79
  1091.9 67.5 %collective-permute-start.69 = (bf16[2,2,80,640]{3,2,0,1:T(8,128)(2,1)S(1)}, bf16[2,2,80,640]{3,2,0,1:T(8,128)(2,1)S(1)}, u32[]{:S(2)}, u32[]{:S(2)}) collective-permute-start(bf16[2,2,80,640]{3,2,0,1:T(8,128)(2,1)S(1)} %dynamic-slice_bitcast_fusion.13), channel_id=1, source_target_pairs={{0,4},{2,6},{4,0},{6,2},{8,12},{10,14},{12,8},{14,10},{16,20},{18,... | collective-permute-start | bytes 1228808 | tf_op jit(solution)/shard_map/ppermute | solution.py:79
  1107.7 51.9 %collective-permute-start.77 = (bf16[2,2,80,640]{3,2,0,1:T(8,128)(2,1)S(1)}, bf16[2,2,80,640]{3,2,0,1:T(8,128)(2,1)S(1)}, u32[]{:S(2)}, u32[]{:S(2)}) collective-permute-start(bf16[2,2,80,640]{3,2,0,1:T(8,128)(2,1)S(1)} %dynamic-slice_bitcast_fusion.11), channel_id=1, source_target_pairs={{0,2},{2,0},{4,6},{6,4},{8,10},{10,8},{12,14},{14,12},{16,18},{18,... | collective-permute-start | bytes 1228808 | tf_op jit(solution)/shard_map/ppermute | solution.py:79
  1109.9 52.0 %collective-permute-start.85 = (bf16[2,2,80,640]{3,2,1,0:T(8,128)(2,1)S(1)}, bf16[2,2,80,640]{3,2,1,0:T(8,128)(2,1)S(1)}, u32[]{:S(2)}, u32[]{:S(2)}) collective-permute-start(bf16[2,2,80,640]{3,2,1,0:T(8,128)(2,1)S(1)} %dynamic-slice_bitcast_fusion.9), channel_id=1, source_target_pairs={{0,16},{2,18},{4,20},{6,22},{8,24},{10,26},{12,28},{14,30},{16,0},... | collective-permute-start | bytes 1228808 | tf_op jit(solution)/shard_map/ppermute | solution.py:79
  1159.5 48.7 %collective-permute-start.70 = (bf16[2,80,640]{2,1,0:T(8,128)(2,1)S(1)}, bf16[2,80,640]{2,1,0:T(8,128)(2,1)S(1)}, u32[]{:S(2)}, u32[]{:S(2)}) collective-permute-start(bf16[2,80,640]{2,1,0:T(8,128)(2,1)S(1)} %dynamic-slice_bitcast_fusion.25), channel_id=1, source_target_pairs={{0,8},{2,10},{4,12},{6,14},{8,0},{10,2},{12,4},{14,6},{16,24},{18,... | collective-permute-start | bytes 614408 | tf_op jit(solution)/shard_map/ppermute | solution.py:79
  1159.8 50.9 %collective-permute-start.78 = (bf16[2,80,640]{2,1,0:T(8,128)(2,1)S(1)}, bf16[2,80,640]{2,1,0:T(8,128)(2,1)S(1)}, u32[]{:S(2)}, u32[]{:S(2)}) collective-permute-start(bf16[2,80,640]{2,1,0:T(8,128)(2,1)S(1)} %dynamic-slice_bitcast_fusion.23), channel_id=1, source_target_pairs={{0,8},{2,10},{4,12},{6,14},{8,0},{10,2},{12,4},{14,6},{16,24},{18,... | collective-permute-start | bytes 614408 | tf_op jit(solution)/shard_map/ppermute | solution.py:79
  1162.0 49.5 %collective-permute-start.86 = (bf16[2,80,640]{2,1,0:T(8,128)(2,1)S(1)}, bf16[2,80,640]{2,1,0:T(8,128)(2,1)S(1)}, u32[]{:S(2)}, u32[]{:S(2)}) collective-permute-start(bf16[2,80,640]{2,1,0:T(8,128)(2,1)S(1)} %dynamic-slice_bitcast_fusion.21), channel_id=1, source_target_pairs={{0,4},{2,6},{4,0},{6,2},{8,12},{10,14},{12,8},{14,10},{16,20},{18,... | collective-permute-start | bytes 614408 | tf_op jit(solution)/shard_map/ppermute | solution.py:79
  (217 other events, 3041.5 us)

commit v2 on v1

v2 whole, which is shorter than its diff:
```python
from functools import partial
import math

import jax
import jax.numpy as jnp
from jax import lax
from jax.experimental import pallas as pl
from jax.experimental.pallas import tpu as pltpu
from jax.sharding import PartitionSpec as P

HD = 80
LAYERS = 2
PROMPT_DEV = 512
TILE = 256

EPSILON = 1e-06
LOG_TWO_E = 1.4426950408889634
LN_TWO = 0.6931471805599453
NEGATIVE = -1e30


def lowered(values):
    return values.astype(jnp.bfloat16)


def dot_nn(former, latter):
    return jnp.dot(former, latter, preferred_element_type=jnp.float32)


def dot_tn(former, latter):
    return lax.dot_general(
        former, latter, (((0,), (0,)), ((), ())), preferred_element_type=jnp.float32
    )


def dot_nt(former, latter):
    return lax.dot_general(
        former, latter, (((1,), (1,)), ((), ())), preferred_element_type=jnp.float32
    )


def inverse_root(source):
    return lax.rsqrt(jnp.mean(source * source, axis=0, keepdims=True) + EPSILON)


def softplus(values):
    return jnp.log1p(jnp.exp(values))


def norm_backward(source, inverse, gain, incoming):
    unit = source * inverse
    gain_grad = jnp.sum(incoming * unit, axis=1)
    scaled = incoming * gain
    return (
        gain_grad,
        inverse * (scaled - unit * jnp.mean(scaled * unit, axis=0, keepdims=True)),
    )


def pair_swap(values, axis, bit):
    size = lax.axis_size(axis)
    return lax.ppermute(values, axis, [(i, i ^ bit) for i in range(size)])


def my_bit(axis, bit):
    return (lax.axis_index(axis) & bit) != 0


def exchange_orders(size):
    if size == 16:
        return (8, 4, 2, 1), (8, 4, 1, 2), (1, 8, 4, 2), (2, 8, 4, 1)
    bits = tuple(1 << k for k in reversed(range(size.bit_length() - 1)))
    return (bits,) * 4


def doubled_gather(shards, order):
    values, done = shards, []
    for bit in order:
        other = pair_swap(values, "dp", bit)
        upper = my_bit("dp", bit)
        at = 1 + sum(1 for earlier in done if earlier > bit)
        values = jnp.stack(
            [jnp.where(upper, other, values), jnp.where(upper, values, other)], axis=at
        )
        done.append(bit)
    return values.reshape((shards.shape[0], -1, shards.shape[2]))


def halved_scatter(values, order):
    members, rows, width = values.shape
    left = sorted(order, reverse=True)
    values = values.reshape((members,) + (2,) * len(order) + (rows >> len(order), width))
    for bit in reversed(order):
        at = 1 + left.index(bit)
        left.remove(bit)
        upper = my_bit("dp", bit).astype(jnp.int32)
        keep = lax.dynamic_index_in_dim(values, upper, at, keepdims=False)
        send = lax.dynamic_index_in_dim(values, 1 - upper, at, keepdims=False)
        got = pair_swap(send, "dp", bit)
        values = keep.astype(jnp.float32) + got.astype(jnp.float32)
        if left:
            values = lowered(values)
    return values


def gather_tokens(local):
    if lax.axis_size("tensor") != 2:
        return lax.all_gather(local, "tensor", axis=1, tiled=True)
    other = pair_swap(local, "tensor", 1)
    upper = my_bit("tensor", 1)
    return jnp.concatenate([jnp.where(upper, other, local), jnp.where(upper, local, other)], axis=1)


def scatter_tokens(product, *values):
    if lax.axis_size("tensor") != 2:
        return lax.psum_scatter(
            lowered(product(*values)), "tensor", scatter_dimension=1, tiled=True
        ).astype(jnp.float32)
    count = values[0].shape[1] // 2
    place = lax.axis_index("tensor")
    theirs = [lax.dynamic_slice_in_dim(v, (1 - place) * count, count, 1) for v in values]
    got = pair_swap(lowered(product(*theirs)), "tensor", 1)
    mine = [lax.dynamic_slice_in_dim(v, place * count, count, 1) for v in values]
    return product(*mine) + got.astype(jnp.float32)


def feed_gather(values):
    if lax.axis_size("tensor") != 2:
        return lax.all_gather(values, "tensor", axis=1, tiled=True)
    return jnp.concatenate([values, pair_swap(values, "tensor", 1)], axis=1)


def feed_scatter(values):
    if lax.axis_size("tensor") != 2:
        return lax.psum_scatter(lowered(values), "tensor", scatter_dimension=1, tiled=True)
    count = values.shape[1] // 2
    got = pair_swap(lowered(values[:, count:]), "tensor", 1)
    return lowered(values[:, :count] + got.astype(jnp.float32))


def key_parts(tile):
    first = tile * TILE
    if first < PROMPT_DEV:
        return ([(0, first, "free")] if first else []) + [(first, TILE, "earlier")]
    return [(0, PROMPT_DEV, "free"), (PROMPT_DEV, first - PROMPT_DEV + TILE, "segment")]


def masked(scores, kind, first_key, first_query, start):
    if kind == "free":
        return scores
    key = lax.broadcasted_iota(jnp.int32, scores.shape, 0) + first_key
    query = lax.broadcasted_iota(jnp.int32, scores.shape, 1) + first_query
    allowed = key <= query
    if kind == "segment":
        allowed = allowed & (key >= start)
    return jnp.where(allowed, scores, NEGATIVE)


def forward_kernel(side_ref, start_ref, q_ref, kf_ref, ko_ref, vf_ref, vo_ref, out_ref, lse_ref):
    far_k = kf_ref[...].T
    own_k = ko_ref[...].T

    def work(tile, far):
        first = tile * TILE
        at = slice(first, first + TILE)
        query = q_ref[:, at]
        start = start_ref[:, at]
        parts = [(dot_nn(far_k, query), vf_ref[...])] if far else []
        for key, count, kind in key_parts(tile):
            scores = dot_nn(own_k[key : key + count], query)
            parts.append((masked(scores, kind, key, first, start), vo_ref[:, key : key + count]))
        highest = jnp.max(parts[0][0], axis=0, keepdims=True)
        for scores, _ in parts[1:]:
            highest = jnp.maximum(highest, jnp.max(scores, axis=0, keepdims=True))
        total, mixed = 0.0, 0.0
        for scores, value in parts:
            weights = jnp.exp2(scores - highest)
            total = total + jnp.sum(weights, axis=0, keepdims=True)
            mixed = mixed + dot_nn(value, lowered(weights))
        out_ref[:, at] = lowered(mixed / total)
        lse_ref[:, at] = highest + jnp.log2(total)

    tiles = range(q_ref.shape[1] // TILE)

    @pl.when(side_ref[0] == 0)
    def _():
        for tile in tiles:
            work(tile, tile * TILE >= PROMPT_DEV)

    @pl.when(side_ref[0] != 0)
    def _():
        for tile in tiles:
            work(tile, True)


def backward_kernel(
    side_ref,
    start_ref,
    q_ref,
    kf_ref,
    ko_ref,
    vf_ref,
    vo_ref,
    out_ref,
    grad_ref,
    lse_ref,
    dq_ref,
    dkf_ref,
    dko_ref,
    dvf_ref,
    dvo_ref,
    kf_total,
    ko_total,
    vf_total,
    vo_total,
):
    far = (kf_ref[...].T, vf_ref[...].T, kf_ref, kf_total, vf_total)
    own = (ko_ref[...].T, vo_ref[...].T, ko_ref, ko_total, vo_total)
    deltas = jnp.sum(
        out_ref[...].astype(jnp.float32) * grad_ref[...].astype(jnp.float32), axis=0, keepdims=True
    )

    def work(tile, with_far, seen):
        first = tile * TILE
        at = slice(first, first + TILE)
        query, grad = q_ref[:, at], grad_ref[:, at]
        start, lse, delta = start_ref[:, at], lse_ref[:, at], deltas[:, at]
        parts = [(far, 0, PROMPT_DEV, "free")] if with_far else []
        parts += [(own,) + part for part in key_parts(tile)]
        dq = 0.0
        for source, key, count, kind in parts:
            keys, values, keys_t, k_total, v_total = source
            scores = masked(dot_nn(keys[key : key + count], query), kind, key, first, start)
            shares = jnp.exp2(scores - lse)
            d_shares = dot_nn(values[key : key + count], grad)
            d_scores = lowered(shares * (d_shares - delta))
            dv = dot_nt(grad, lowered(shares))
            dk = dot_nt(query, d_scores)
            dq = dq + dot_nn(keys_t[:, key : key + count], d_scores)
            for offset in range(0, count, TILE):
                there = slice(key + offset, key + offset + TILE)
                here = slice(offset, offset + TILE)
                mark = (source is own, key + offset)
                if mark in seen:
                    k_total[:, there] += dk[:, here]
                    v_total[:, there] += dv[:, here]
                else:
                    seen.add(mark)
                    k_total[:, there] = dk[:, here]
                    v_total[:, there] = dv[:, here]
        dq_ref[:, at] = dq

    tiles = range(q_ref.shape[1] // TILE)

    @pl.when(side_ref[0] == 0)
    def _():
        seen = set()
        for tile in tiles:
            work(tile, tile * TILE >= PROMPT_DEV, seen)

    @pl.when(side_ref[0] != 0)
    def _():
        seen = set()
        for tile in tiles:
            work(tile, True, seen)

    dkf_ref[...] = lowered(kf_total[...] * LN_TWO)
    dko_ref[...] = lowered(ko_total[...] * LN_TWO)
    dvf_ref[...] = lowered(vf_total[...])
    dvo_ref[...] = lowered(vo_total[...])


def head_block(count):
    return pl.BlockSpec((HD, count), lambda head: (head, 0))


def attention_specs(tokens):
    return [
        pl.BlockSpec(memory_space=pltpu.SMEM),
        pl.BlockSpec((1, tokens), lambda head: (0, 0)),
        head_block(tokens),
        head_block(PROMPT_DEV),
        head_block(tokens),
        head_block(PROMPT_DEV),
        head_block(tokens),
    ]


def attention(side, start, queries, far_keys, own_keys, far_values, own_values):
    width, tokens = queries.shape
    heads = width // HD
    pairs = heads * tokens * (tokens + PROMPT_DEV)
    return pl.pallas_call(
        forward_kernel,
        grid=(heads,),
        in_specs=attention_specs(tokens),
        out_specs=[
            head_block(tokens),
            pl.BlockSpec((None, 1, tokens), lambda head: (head, 0, 0)),
        ],
        out_shape=[
            jax.ShapeDtypeStruct(queries.shape, jnp.bfloat16),
            jax.ShapeDtypeStruct((heads, 1, tokens), jnp.float32),
        ],
        compiler_params=pltpu.CompilerParams(vmem_limit_bytes=32 << 20),
        cost_estimate=pl.CostEstimate(
            flops=16 * HD * pairs, bytes_accessed=8 * width * tokens, transcendentals=pairs
        ),
        name="attention",
    )(side, start, queries, far_keys, own_keys, far_values, own_values)


def attention_back(
    side, start, queries, far_keys, own_keys, far_values, own_values, mixed, grads, lse
):
    width, tokens = queries.shape
    heads = width // HD
    pairs = heads * tokens * (tokens + PROMPT_DEV)
    far, own = (width, PROMPT_DEV), (width, tokens)
    return pl.pallas_call(
        backward_kernel,
        grid=(heads,),
        in_specs=attention_specs(tokens)
        + [
            head_block(tokens),
            head_block(tokens),
            pl.BlockSpec((None, 1, tokens), lambda head: (head, 0, 0)),
        ],
        out_specs=[head_block(count) for count in (tokens, PROMPT_DEV, tokens, PROMPT_DEV, tokens)],
        out_shape=[jax.ShapeDtypeStruct(own, jnp.float32)]
        + [jax.ShapeDtypeStruct(shape, jnp.bfloat16) for shape in (far, own, far, own)],
        scratch_shapes=[
            pltpu.VMEM((HD, count), jnp.float32)
            for count in (PROMPT_DEV, tokens, PROMPT_DEV, tokens)
        ],
        compiler_params=pltpu.CompilerParams(vmem_limit_bytes=32 << 20),
        cost_estimate=pl.CostEstimate(
            flops=32 * HD * pairs, bytes_accessed=20 * width * tokens, transcendentals=pairs
        ),
        name="attention_back",
    )(side, start, queries, far_keys, own_keys, far_values, own_values, mixed, grads, lse)


def segment_starts(lengths_row, tokens):
    place = jnp.arange(tokens, dtype=jnp.int32) - PROMPT_DEV
    bounds = jnp.cumsum(lengths_row)
    passed = jnp.where(place[:, None] >= bounds[None, :], bounds[None, :], 0)
    return (PROMPT_DEV + jnp.max(passed, axis=1))[None, :]


def body(
    inputs,
    cotangent,
    query_weight,
    key_weight,
    value_weight,
    output_weight,
    up_weight,
    down_weight,
    attention_gain,
    feed_gain,
    query_scale,
    cont_lengths,
):
    tokens = inputs.shape[0] * lax.axis_size("tensor")
    heads = query_weight.shape[2] // HD
    order_a, order_b, order_c, order_d = exchange_orders(lax.axis_size("dp"))
    side = (lax.axis_index("dp") % 2).astype(jnp.int32)[None]
    start = segment_starts(cont_lengths[0], tokens)

    def gathered(order, *members):
        return doubled_gather(jnp.stack(members), order)

    weights = []
    for layer in range(LAYERS):
        out_shard, down_shard = output_weight[layer].T, down_weight[layer].T
        if layer == 0:
            (wk,) = gathered(order_a, key_weight[layer])
            (wv,) = gathered(order_c, value_weight[layer])
            (wq,) = gathered(order_d, query_weight[layer])
            (wo,) = gathered(order_b, out_shard)
            (wu,) = gathered(order_c, up_weight[layer])
            (wd,) = gathered(order_d, down_shard)
        else:
            wk, wv = gathered(order_c, key_weight[layer], value_weight[layer])
            wq, wo = gathered(order_d, query_weight[layer], out_shard)
            wu, wd = gathered(order_b, up_weight[layer], down_shard)
        weights.append((wq, wk, wv, wo, wu, wd))

    gains, stored = [], []
    current = inputs.T
    for layer in range(LAYERS):
        wq, wk, wv, wo, wu, wd = weights[layer]
        attn_gain, ff_gain = attention_gain[layer][:, None], feed_gain[layer][:, None]
        inverse_attn = inverse_root(current)
        normed = gather_tokens(lowered(current * inverse_attn * attn_gain))
        keys = lowered(dot_tn(wk, normed))
        far_keys = pair_swap(keys[:, :PROMPT_DEV], "dp", 1)
        values = lowered(dot_tn(wv, normed))
        far_values = pair_swap(values[:, :PROMPT_DEV], "dp", 1)
        gain_q = softplus(query_scale[layer]) * LOG_TWO_E / math.sqrt(HD)
        gain_rows = jnp.tile(gain_q, heads)[:, None]
        queries = lowered(dot_tn(wq, normed) * (gain_rows * LOG_TWO_E))
        seen = (side, start, queries, far_keys, keys, far_values, values)
        mixed, lse = attention(*seen)
        middle = current + scatter_tokens(lambda rows: dot_nn(wo, rows), mixed)
        inverse_feed = inverse_root(middle)
        feed = lowered(middle * inverse_feed * ff_gain)
        wu, wd = feed_gather(wu), feed_gather(wd)
        upper = dot_tn(wu, feed)
        hidden = lowered(upper * jax.nn.sigmoid(upper))
        stored.append(
            (
                (current, inverse_attn, attn_gain, normed),
                (gain_q, gain_rows, seen, mixed, lse),
                (middle, inverse_feed, ff_gain, feed, upper, hidden),
                (wq, wk, wv, wo, wu, wd),
            )
        )
        current = middle + dot_nn(wd, hidden)

    layer_grads = [None] * LAYERS
    small_grads = [None] * LAYERS
    grad = cotangent.T
    for layer in reversed(range(LAYERS)):
        (
            (source, inverse_attn, attn_gain, normed),
            (gain_q, gain_rows, seen, mixed, lse),
            (middle, inverse_feed, ff_gain, feed, upper, hidden),
            (wq, wk, wv, wo, wu, wd),
        ) = stored[layer]
        grad_low = lowered(grad)
        down_grad = feed_scatter(dot_nt(grad_low, hidden))
        d_hidden = lowered(dot_tn(wd, grad_low)).astype(jnp.float32)
        sigmoid = jax.nn.sigmoid(upper)
        d_upper = lowered(d_hidden * (sigmoid * (1.0 + upper * (1.0 - sigmoid))))
        up_grad = feed_scatter(dot_nt(feed, d_upper))
        feed_gain_grad, part = norm_backward(middle, inverse_feed, ff_gain, dot_nn(wu, d_upper))
        grad_middle = grad + part
        middle_low = gather_tokens(lowered(grad_middle))
        d_mixed = lowered(dot_tn(wo, middle_low))
        out_grad = lowered(dot_nt(middle_low, mixed))
        dq, far_dk, own_dk, far_dv, own_dv = attention_back(*seen, mixed, d_mixed, lse)
        back_keys = pair_swap(far_dk, "dp", 1).astype(jnp.float32)
        back_values = pair_swap(far_dv, "dp", 1).astype(jnp.float32)
        pad = ((0, 0), (0, tokens - PROMPT_DEV))
        d_keys = lowered(own_dk.astype(jnp.float32) + jnp.pad(back_keys, pad))
        d_values = lowered(own_dv.astype(jnp.float32) + jnp.pad(back_values, pad))
        scale_raw = jnp.sum((dq * seen[2].astype(jnp.float32)).reshape(heads, HD, tokens), (0, 2))
        scale_raw = scale_raw / (gain_q * LOG_TWO_E)
        scale_grad = scale_raw * jax.nn.sigmoid(query_scale[layer]) * LOG_TWO_E / math.sqrt(HD)
        d_raw = lowered(dq * gain_rows)
        d_normed = scatter_tokens(
            lambda dq, dk, dv: dot_nn(wq, dq) + dot_nn(wk, dk) + dot_nn(wv, dv),
            d_raw,
            d_keys,
            d_values,
        )
        query_grad = lowered(dot_nt(normed, d_raw))
        key_grad = lowered(dot_nt(normed, d_keys))
        value_grad = lowered(dot_nt(normed, d_values))
        attn_gain_grad, part = norm_backward(source, inverse_attn, attn_gain, d_normed)
        grad = grad_middle + part
        small_grads[layer] = (attn_gain_grad, feed_gain_grad, scale_grad)

        def scattered(order, *members):
            return halved_scatter(jnp.stack(members), order)

        if layer == 0:
            (up_grad,) = scattered(order_c, up_grad)
            (down_grad,) = scattered(order_d, down_grad)
            (out_grad,) = scattered(order_b, out_grad)
            (query_grad,) = scattered(order_d, query_grad)
            (key_grad,) = scattered(order_a, key_grad)
            (value_grad,) = scattered(order_c, value_grad)
        else:
            up_grad, down_grad = scattered(order_b, up_grad, down_grad)
            query_grad, out_grad = scattered(order_d, query_grad, out_grad)
            key_grad, value_grad = scattered(order_c, key_grad, value_grad)
        layer_grads[layer] = (query_grad, key_grad, value_grad, out_grad.T, up_grad, down_grad.T)

    summed = [jnp.stack(members) for members in zip(*layer_grads)]
    small = lax.psum(tuple(jnp.stack(members) for members in zip(*small_grads)), ("dp", "tensor"))
    return (current.T, grad.T, *summed, *small)


def solution(mesh):
    in_specs = (
        P(("dp", "tensor"), None),
        P(("dp", "tensor"), None),
        P(None, "dp", "tensor"),
        P(None, "dp", "tensor"),
        P(None, "dp", "tensor"),
        P(None, "tensor", "dp"),
        P(None, "dp", "tensor"),
        P(None, "tensor", "dp"),
        P(),
        P(),
        P(),
        P("dp", None),
    )
    out_specs = (
        P(("dp", "tensor"), None),
        P(("dp", "tensor"), None),
        P(None, "dp", "tensor"),
        P(None, "dp", "tensor"),
        P(None, "dp", "tensor"),
        P(None, "tensor", "dp"),
        P(None, "dp", "tensor"),
        P(None, "tensor", "dp"),
        P(),
        P(),
        P(),
    )
    return jax.shard_map(body, mesh=mesh, in_specs=in_specs, out_specs=out_specs, check_vma=False)
```

time: 1240 us -> 844 us (0.68)
  matrix products: 451 us -> 108 us
  other arithmetic: 153 us -> 56.5 us
  Pallas kernels: 0 us -> 86.6 us
  local copies, waits for them, and re-layouts: 136 us -> 58.5 us
  waiting for transfers between devices: 317 us -> 364 us
    dot_general x140 -> x44, matrix products: 451 us -> 108 us  [the longest x20 43.7 us: dot_nn(): return jnp.dot(former, latter, preferred_element_type=jnp.float32)]
    pallas_call x0 -> x4, Pallas kernels: none -> 86.6 us  [the longest x2 54.3 us: attention_back(): pl.pallas_call(backward_kernel, grid=(heads,), in_specs=attention_specs(t...]
    ppermute x112 -> x96, waiting for transfers between devices: 288 us -> 364 us  [pair_swap(): return lax.ppermute(values, axis, [(i, i ^ bit) for i in range(size)])]
    concatenate x7 -> x0, other arithmetic: 45.9 us -> none  [the longest x2 35 us: body(): jnp.concatenate([lowered(query_heads * gain_q).reshape(row_total, local_w...]
    ppermute x8 -> x0, waiting for transfers between devices: 29 us -> none  [from_partner(): lax.ppermute(shard, axis, [(i, i ^ 1 << distance) for i in range(lax.axis...]
    slice x20 -> x10, local copies, waits for them, and re-layouts: 27.5 us -> 5.56 us  [the longest x1 1.55 us: body(): wu, = gathered(order_c, up_weight[layer])]
    reduce_sum x20 -> x5, other arithmetic: 17.9 us -> 1.31 us  [the longest x4 1.06 us: body(): jnp.sum((dq * seen[2].astype(jnp.float32)).reshape(heads, HD, tokens), (0...]
    concatenate x5 -> x0, local copies, waits for them, and re-layouts: 15.9 us -> none  [the longest x2 7.96 us: body(): key_all = jnp.concatenate([far_keys, key_low], axis=0)]
  transfers between devices with their start and end apart: 120 -> 96, of which waited for: 42 -> 37; matrix products, arithmetic and copies ran while one was open for 58% -> 23% of each run, Pallas kernels for 0% -> 10%
where the time goes in v2:
time: 844 us; the launch traced here: 834 us
  waiting for transfers between devices  364 us (43%)
  starting transfers between devices  118 us (14%)
  matrix products  108 us (13%)
  Pallas kernels  86.6 us (10%)
  local copies, waits for them, and re-layouts  58.5 us (7%)
  other arithmetic  56.5 us (7%)
  blocking collectives  38.3 us (5%)
    ppermute x96, waiting for transfers between devices, pair_swap(): return lax.ppermute(values, axis, [(i, i ^ bit) for i in range(size)])  364 us
    ppermute x96, starting transfers between devices, pair_swap(): return lax.ppermute(values, axis, [(i, i ^ bit) for i in range(size)])  118 us
    pallas_call x2, Pallas kernels, attention_back(): pl.pallas_call(backward_kernel, grid=(heads,), in_specs=attention_specs(t...  54.3 us
    dot_general x20, matrix products, dot_nn(): return jnp.dot(former, latter, preferred_element_type=jnp.float32)  43.7 us
    psum x1, blocking collectives, body(): lax.psum(tuple((jnp.stack(members) for members in zip(*small_grads))), ('...  38.3 us
    pallas_call x2, Pallas kernels, attention(): pl.pallas_call(forward_kernel, grid=(heads,), in_specs=attention_specs(to...  32.4 us
    dot_general x12, matrix products, dot_nt(): lax.dot_general(former, latter, (((1,), (1,)), ((), ())), preferred_eleme...  32.2 us
    dot_general x12, matrix products, dot_tn(): lax.dot_general(former, latter, (((0,), (0,)), ((), ())), preferred_eleme...  31.7 us
  transfers between devices with their start and end apart: 96, of which 37 were waited for; matrix products, arithmetic and copies ran while one was open for 23% of the time, Pallas kernels for 10%

profile of v2, /device:TPU:0, one launch (start us, length us, event | category | flops | bytes accessed | tf_op | source)
XLA Modules:
  0.0 834.0 jit_solution(8077437409196672946)
XLA Ops:
  2.2 4.0 collective-permute-start
  35.8 8.0 collective-permute-done.10
  43.8 3.9 collective-permute-start.21
  49.3 8.0 collective-permute-done.5
  61.9 8.7 %collective-permute-done.21 = bf16[1,2,80,640]{3,2,1,0:T(8,128)(2,1)S(1)} collective-permute-done((bf16[1,2,80,640]{3,2,1,0:T(8,128)(2,1)S(1)}, bf16[1,2,80,640]{3,2,1,0:T(8,128)(2,1)S(1)}, u32[]{:S(2)}, u32[]{:S(2)}) %collective-permute-start.21) | collective-permute-done | bytes 204832 | tf_op jit(solution)/shard_map/ppermute | solution.py:62
  78.7 10.3 %collective-permute-done.6 = bf16[1,2,2,80,640]{4,3,2,1,0:T(8,128)(2,1)S(1)} collective-permute-done((bf16[1,2,2,80,640]{4,3,2,1,0:T(8,128)(2,1)S(1)}, bf16[1,2,2,80,640]{4,3,2,1,0:T(8,128)(2,1)S(1)}, u32[]{:S(2)}, u32[]{:S(2)}) %collective-permute-start.6) | collective-permute-done | bytes 409632 | tf_op jit(solution)/shard_map/ppermute | solution.py:62
  92.0 14.6 %collective-permute-done.16 = bf16[1,2,2,80,640]{4,3,2,1,0:T(8,128)(2,1)S(1)} collective-permute-done((bf16[1,2,2,80,640]{4,3,2,1,0:T(8,128)(2,1)S(1)}, bf16[1,2,2,80,640]{4,3,2,1,0:T(8,128)(2,1)S(1)}, u32[]{:S(2)}, u32[]{:S(2)}) %collective-permute-start.16) | collective-permute-done | bytes 409632 | tf_op jit(solution)/shard_map/ppermute | solution.py:62
  107.1 8.4 %collective-permute-done.27 = bf16[1,2,2,80,640]{4,3,2,1,0:T(8,128)(2,1)S(1)} collective-permute-done((bf16[1,2,2,80,640]{4,3,2,1,0:T(8,128)(2,1)S(1)}, bf16[1,2,2,80,640]{4,3,2,1,0:T(8,128)(2,1)S(1)}, u32[]{:S(2)}, u32[]{:S(2)}) %collective-permute-start.27) | collective-permute-done | bytes 409632 | tf_op jit(solution)/shard_map/ppermute | solution.py:62
  115.6 11.4 %collective-permute-done.22 = bf16[1,2,2,80,640]{4,3,1,2,0:T(8,128)(2,1)S(1)} collective-permute-done((bf16[1,2,2,80,640]{4,3,1,2,0:T(8,128)(2,1)S(1)}, bf16[1,2,2,80,640]{4,3,1,2,0:T(8,128)(2,1)S(1)}, u32[]{:S(2)}, u32[]{:S(2)}) %collective-permute-start.22) | collective-permute-done | bytes 409632 | tf_op jit(solution)/shard_map/ppermute | solution.py:62
  138.4 26.6 %collective-permute-done.12 = bf16[1,2,2,2,80,640]{5,4,1,2,3,0:T(8,128)(2,1)S(1)} collective-permute-done((bf16[1,2,2,2,80,640]{5,4,1,2,3,0:T(8,128)(2,1)S(1)}, bf16[1,2,2,2,80,640]{5,4,1,2,3,0:T(8,128)(2,1)S(1)}, u32[]{:S(2)}, u32[]{:S(2)}) %collective-permute-start.12) | collective-permute-done | bytes 819232 | tf_op jit(solution)/shard_map/ppermute | solution.py:62
  179.6 20.7 %collective-permute-done.13.kf_ref = bf16[640,512]{1,0:T(8,128)(2,1)S(1)} collective-permute-done((bf16[640,512]{1,0:T(8,128)(2,1)S(1)}, bf16[640,512]{1,0:T(8,128)(2,1)S(1)}, u32[]{:S(2)}, u32[]{:S(2)}) %collective-permute-start.13) | collective-permute-done | bytes 655392 | tf_op jit(solution)/shard_map/ppermute | solution.py:62
  200.9 11.0 %collective-permute-done.18.vf_ref = bf16[640,512]{1,0:T(8,128)(2,1)S(1)} collective-permute-done((bf16[640,512]{1,0:T(8,128)(2,1)S(1)}, bf16[640,512]{1,0:T(8,128)(2,1)S(1)}, u32[]{:S(2)}, u32[]{:S(2)}) %collective-permute-start.18) | collective-permute-done | bytes 655392 | tf_op jit(solution)/shard_map/ppermute | solution.py:62
  212.0 16.2 %attention.2 = (bf16[640,1024]{1,0:T(8,128)(2,1)S(1)}, f32[8,1,1024]{2,1,0:T(1,128)S(1)}) custom-call(s32[1]{0:T(128)} %bitcast.18.side_ref, s32[1,1024]{1,0:T(1,128)S(1)} %bitcast.555, bf16[640,1024]{1,0:T(8,128)(2,1)S(1)} %multiply_convert_fusion.8.q_ref, bf16[640,512]{1,0:T(8,128)(2,1)S(1)} %collective-permute-done.13.kf_ref, ...), custom_call_target="tpu_custom_call" | custom-call | flops 16106127360 | bytes 5242880 | tf_op jit(solution)/shard_map/attention/pallas_call | solution.py:293
  231.0 5.2 collective-permute-start.33
  245.1 30.2 %collective-permute-done.38 = bf16[2,2,2,2,80,640]{5,4,3,0,1,2:T(8,128)(2,1)S(1)} collective-permute-done((bf16[2,2,2,2,80,640]{5,4,3,0,1,2:T(8,128)(2,1)S(1)}, bf16[2,2,2,2,80,640]{5,4,3,0,1,2:T(8,128)(2,1)S(1)}, u32[]{:S(2)}, u32[]{:S(2)}) %collective-permute-start.38) | collective-permute-done | bytes 1638432 | tf_op jit(solution)/shard_map/ppermute | solution.py:62
  286.0 11.1 %collective-permute-done.39.kf_ref = bf16[640,512]{1,0:T(8,128)(2,1)S(1)} collective-permute-done((bf16[640,512]{1,0:T(8,128)(2,1)S(1)}, bf16[640,512]{1,0:T(8,128)(2,1)S(1)}, u32[]{:S(2)}, u32[]{:S(2)}) %collective-permute-start.39) | collective-permute-done | bytes 655392 | tf_op jit(solution)/shard_map/ppermute | solution.py:62
  297.1 11.6 %collective-permute-done.40.vf_ref = bf16[640,512]{1,0:T(8,128)(2,1)S(1)} collective-permute-done((bf16[640,512]{1,0:T(8,128)(2,1)S(1)}, bf16[640,512]{1,0:T(8,128)(2,1)S(1)}, u32[]{:S(2)}, u32[]{:S(2)}) %collective-permute-start.40) | collective-permute-done | bytes 655392 | tf_op jit(solution)/shard_map/ppermute | solution.py:62
  308.8 16.2 %attention.3 = (bf16[640,1024]{1,0:T(8,128)(2,1)S(1)}, f32[8,1,1024]{2,1,0:T(1,128)S(1)}) custom-call(s32[1]{0:T(128)} %bitcast.18.side_ref, s32[1,1024]{1,0:T(1,128)S(1)} %bitcast.556, bf16[640,1024]{1,0:T(8,128)(2,1)S(1)} %multiply_convert_fusion.4.q_ref, bf16[640,512]{1,0:T(8,128)(2,1)S(1)} %collective-permute-done.39.kf_ref, ...), custom_call_target="tpu_custom_call" | custom-call | flops 16106127360 | bytes 5242880 | tf_op jit(solution)/shard_map/attention/pallas_call | solution.py:293
  331.1 3.4 copy.155
  334.5 4.0 multiply_reduce_fusion.10
  338.6 4.9 fusion.20
  343.5 5.4 fusion.16
  348.9 4.4 multiply_reduce_fusion.2
  356.5 5.5 fusion.9
  362.0 3.6 copy.181
  365.6 6.9 fusion.116
  372.5 3.4 slice.190
  388.4 27.1 %attention_back.2 = (f32[640,1024]{1,0:T(8,128)S(1)}, bf16[640,512]{1,0:T(8,128)(2,1)}, bf16[640,1024]{1,0:T(8,128)(2,1)S(1)}, bf16[640,512]{1,0:T(8,128)(2,1)}, bf16[640,1024]{1,0:T(8,128)(2,1)S(1)}) custom-call(s32[1]{0:T(128)} %bitcast.18.side_ref, s32[1,1024]{1,0:T(1,128)S(1)} %bitcast.557, bf16[640,1024]{1,0:T(8,128)(2,1)S(1)} %multiply_convert_fusion.4.q_ref, ...), custom_call_target="tpu_custom_call" | custom-call | flops 32212254720 | bytes 13107200 | tf_op jit(solution)/shard_map/attention_back/pallas_call | solution.py:320
  415.6 11.3 %collective-permute-start.49 = (bf16[640,512]{1,0:T(8,128)(2,1)}, bf16[640,512]{1,0:T(8,128)(2,1)}, u32[]{:S(2)}, u32[]{:S(2)}) collective-permute-start(bf16[640,512]{1,0:T(8,128)(2,1)} %get-tuple-element.30), channel_id=1, source_target_pairs={{0,2},{2,0},{4,6},{6,4},{8,10},{10,8},{12,14},{14,12},{16,18},{18,... | collective-permute-start | bytes 1966088 | tf_op jit(solution)/shard_map/ppermute | solution.py:62
  449.5 7.3 collective-permute-done.50
  467.1 24.7 %collective-permute-done.60 = bf16[2,2,2,2,80,640]{5,4,0,3,1,2:T(8,128)(2,1)} collective-permute-done((bf16[2,2,2,2,80,640]{5,4,0,3,1,2:T(8,128)(2,1)}, bf16[2,2,2,2,80,640]{5,4,0,3,1,2:T(8,128)(2,1)}, u32[]{:S(2)}, u32[]{:S(2)}) %collective-permute-start.60) | collective-permute-done | bytes 1638432 | tf_op jit(solution)/shard_map/ppermute | solution.py:62
  498.5 4.1 fusion.17
  519.2 5.5 collective-permute-start.62
  525.1 18.2 %collective-permute-done.62 = bf16[2,2,80,640]{3,2,0,1:T(8,128)(2,1)S(1)} collective-permute-done((bf16[2,2,80,640]{3,2,0,1:T(8,128)(2,1)S(1)}, bf16[2,2,80,640]{3,2,0,1:T(8,128)(2,1)S(1)}, u32[]{:S(2)}, u32[]{:S(2)}) %collective-permute-start.62) | collective-permute-done | bytes 409632 | tf_op jit(solution)/shard_map/ppermute | solution.py:62
  544.3 6.3 collective-permute-done.63
  553.1 11.3 %collective-permute-done.69 = bf16[2,2,2,80,640]{4,3,0,2,1:T(8,128)(2,1)S(1)} collective-permute-done((bf16[2,2,2,80,640]{4,3,0,2,1:T(8,128)(2,1)S(1)}, bf16[2,2,2,80,640]{4,3,0,2,1:T(8,128)(2,1)S(1)}, u32[]{:S(2)}, u32[]{:S(2)}) %collective-permute-start.69) | collective-permute-done | bytes 819232 | tf_op jit(solution)/shard_map/ppermute | solution.py:62
  566.7 10.7 %collective-permute-done.89 = bf16[2,2,80,640]{3,2,0,1:T(8,128)(2,1)S(1)} collective-permute-done((bf16[2,2,80,640]{3,2,0,1:T(8,128)(2,1)S(1)}, bf16[2,2,80,640]{3,2,0,1:T(8,128)(2,1)S(1)}, u32[]{:S(2)}, u32[]{:S(2)}) %collective-permute-start.89) | collective-permute-done | bytes 409632 | tf_op jit(solution)/shard_map/ppermute | solution.py:62
  583.1 27.1 %attention_back.3 = (f32[640,1024]{1,0:T(8,128)S(1)}, bf16[640,512]{1,0:T(8,128)(2,1)}, bf16[640,1024]{1,0:T(8,128)(2,1)S(1)}, bf16[640,512]{1,0:T(8,128)(2,1)S(1)}, bf16[640,1024]{1,0:T(8,128)(2,1)S(1)}) custom-call(s32[1]{0:T(128)} %bitcast.18.side_ref, s32[1,1024]{1,0:T(1,128)S(1)} %bitcast.558, bf16[640,1024]{1,0:T(8,128)(2,1)S(1)} %copy-done.1, ...), custom_call_target="tpu_custom_call" | custom-call | flops 32212254720 | bytes 13107200 | tf_op jit(solution)/shard_map/attention_back/pallas_call | solution.py:320
  617.0 3.5 convolution_convert_fusion.7
  620.5 5.6 collective-permute-start.53
  642.2 34.2 %collective-permute-done.71 = bf16[2,80,640]{2,1,0:T(8,128)(2,1)S(1)} collective-permute-done((bf16[2,80,640]{2,1,0:T(8,128)(2,1)S(1)}, bf16[2,80,640]{2,1,0:T(8,128)(2,1)S(1)}, u32[]{:S(2)}, u32[]{:S(2)}) %collective-permute-start.71) | collective-permute-done | bytes 204832 | tf_op jit(solution)/shard_map/ppermute | solution.py:62
  700.8 4.2 collective-permute-done.57
  706.8 15.6 %collective-permute-done.77 = bf16[1,2,2,80,640]{4,3,1,2,0:T(8,128)(2,1)S(1)} collective-permute-done((bf16[1,2,2,80,640]{4,3,1,2,0:T(8,128)(2,1)S(1)}, bf16[1,2,2,80,640]{4,3,1,2,0:T(8,128)(2,1)S(1)}, u32[]{:S(2)}, u32[]{:S(2)}) %collective-permute-start.77) | collective-permute-done | bytes 409632 | tf_op jit(solution)/shard_map/ppermute | solution.py:62
  724.7 8.1 collective-permute-done.58
  732.9 5.7 collective-permute-done.78
  755.9 7.6 collective-permute-done.83
  763.7 4.7 collective-permute-done.94
  784.8 38.3 %all-reduce.4 = (f32[2,1280]{1,0:T(2,128)}, f32[2,1280]{1,0:T(2,128)}, f32[2,80]{1,0:T(2,128)}) all-reduce(f32[2,1280]{1,0:T(2,128)S(1)} %pad_maximum_fusion.69, f32[2,1280]{1,0:T(2,128)S(1)} %pad_maximum_fusion.70, f32[2,80]{1,0:T(2,128)S(1)} %pad_maximum_fusion.71), channel_id=1, replica_groups=mesh['dp'=16,'tensor'=2] {'dp','tensor'}, use_global_device_ids=true, to_apply=%region_12.13 | all-reduce | flops 5280 | bytes 42240 | tf_op jit(solution)/shard_map/psum | solution.py:483
  (697 shorter events, 281.0 us)
Async XLA Ops:
  16.3 119.5 %collective-permute-start.8 = (bf16[1280,512]{1,0:T(8,128)(2,1)}, bf16[1280,512]{1,0:T(8,128)(2,1)}, u32[]{:S(2)}, u32[]{:S(2)}) collective-permute-start(bf16[1280,512]{1,0:T(8,128)(2,1)} %multiply_convert_fusion.9), channel_id=1, source_target_pairs={{0,1},{1,0},{2,3},{3,2},{4,5},{5,4},{6,7},{7,6},{8,9},{9,8},{10,11... | collective-permute-start | bytes 3932168 | tf_op jit(solution)/shard_map/ppermute | solution.py:62
  30.0 27.3 %collective-permute-start.5 = (bf16[1,2,80,640]{3,2,1,0:T(8,128)(2,1)S(1)}, bf16[1,2,80,640]{3,2,1,0:T(8,128)(2,1)S(1)}, u32[]{:S(2)}, u32[]{:S(2)}) collective-permute-start(bf16[1,2,80,640]{3,2,1,0:T(8,128)(2,1)S(1)} %pad_maximum_fusion.61), channel_id=1, source_target_pairs={{0,16},{2,18},{4,20},{6,22},{8,24},{10,26},{12,28},{14,30},{16,0},... | collective-permute-start | bytes 614408 | tf_op jit(solution)/shard_map/ppermute | solution.py:62
  34.3 27.4 %collective-permute-start.26 = (bf16[1,2,80,640]{3,2,1,0:T(8,128)(2,1)S(1)}, bf16[1,2,80,640]{3,2,1,0:T(8,128)(2,1)S(1)}, u32[]{:S(2)}, u32[]{:S(2)}) collective-permute-start(bf16[1,2,80,640]{3,2,1,0:T(8,128)(2,1)S(1)} %pad_maximum_fusion.65), channel_id=1, source_target_pairs={{0,16},{2,18},{4,20},{6,22},{8,24},{10,26},{12,28},{14,30},{16,0},... | collective-permute-start | bytes 614408 | tf_op jit(solution)/shard_map/ppermute | solution.py:62
  74.0 32.6 %collective-permute-start.16 = (bf16[1,2,2,80,640]{4,3,2,1,0:T(8,128)(2,1)S(1)}, bf16[1,2,2,80,640]{4,3,2,1,0:T(8,128)(2,1)S(1)}, u32[]{:S(2)}, u32[]{:S(2)}) collective-permute-start(bf16[1,2,2,80,640]{4,3,2,1,0:T(8,128)(2,1)S(1)} %pad_maximum_fusion.48), channel_id=1, source_target_pairs={{0,8},{2,10},{4,12},{6,14},{8,0},{10,2},{12,4},{14,6},{16,24},{18,... | collective-permute-start | bytes 1228808 | tf_op jit(solution)/shard_map/ppermute | solution.py:62
  78.6 36.9 %collective-permute-start.27 = (bf16[1,2,2,80,640]{4,3,2,1,0:T(8,128)(2,1)S(1)}, bf16[1,2,2,80,640]{4,3,2,1,0:T(8,128)(2,1)S(1)}, u32[]{:S(2)}, u32[]{:S(2)}) collective-permute-start(bf16[1,2,2,80,640]{4,3,2,1,0:T(8,128)(2,1)S(1)} %pad_maximum_fusion.50), channel_id=1, source_target_pairs={{0,8},{2,10},{4,12},{6,14},{8,0},{10,2},{12,4},{14,6},{16,24},{18,... | collective-permute-start | bytes 1228808 | tf_op jit(solution)/shard_map/ppermute | solution.py:62
  89.0 37.9 %collective-permute-start.22 = (bf16[1,2,2,80,640]{4,3,1,2,0:T(8,128)(2,1)S(1)}, bf16[1,2,2,80,640]{4,3,1,2,0:T(8,128)(2,1)S(1)}, u32[]{:S(2)}, u32[]{:S(2)}) collective-permute-start(bf16[1,2,2,80,640]{4,3,1,2,0:T(8,128)(2,1)S(1)} %pad_maximum_fusion.49), channel_id=1, source_target_pairs={{0,8},{2,10},{4,12},{6,14},{8,0},{10,2},{12,4},{14,6},{16,24},{18,... | collective-permute-start | bytes 1228808 | tf_op jit(solution)/shard_map/ppermute | solution.py:62
  89.1 39.8 %collective-permute-start.31 = (bf16[2,2,80,640]{3,2,1,0:T(8,128)(2,1)S(1)}, bf16[2,2,80,640]{3,2,1,0:T(8,128)(2,1)S(1)}, u32[]{:S(2)}, u32[]{:S(2)}) collective-permute-start(bf16[2,2,80,640]{3,2,1,0:T(8,128)(2,1)S(1)} %pad_maximum_fusion.51), channel_id=1, source_target_pairs={{0,16},{2,18},{4,20},{6,22},{8,24},{10,26},{12,28},{14,30},{16,0},... | collective-permute-start | bytes 1228808 | tf_op jit(solution)/shard_map/ppermute | solution.py:62
  127.0 46.3 %collective-permute-start.3 = (bf16[1,2,2,2,80,640]{5,4,3,2,1,0:T(8,128)(2,1)S(1)}, bf16[1,2,2,2,80,640]{5,4,3,2,1,0:T(8,128)(2,1)S(1)}, u32[]{:S(2)}, u32[]{:S(2)}) collective-permute-start(bf16[1,2,2,2,80,640]{5,4,3,2,1,0:T(8,128)(2,1)S(1)} %pad_maximum_fusion.36), channel_id=1, source_target_pairs={{0,4},{2,6},{4,0},{6,2},{8,12},{10,14},{12,8},{14,10},{16,20},{18,... | collective-permute-start | bytes 2457608 | tf_op jit(solution)/shard_map/ppermute | solution.py:62
  129.0 42.4 %collective-permute-start.7 = (bf16[1,2,2,2,80,640]{5,4,3,1,2,0:T(8,128)(2,1)S(1)}, bf16[1,2,2,2,80,640]{5,4,3,1,2,0:T(8,128)(2,1)S(1)}, u32[]{:S(2)}, u32[]{:S(2)}) collective-permute-start(bf16[1,2,2,2,80,640]{5,4,3,1,2,0:T(8,128)(2,1)S(1)} %pad_maximum_fusion.37), channel_id=1, source_target_pairs={{0,2},{2,0},{4,6},{6,4},{8,10},{10,8},{12,14},{14,12},{16,18},{18,... | collective-permute-start | bytes 2457608 | tf_op jit(solution)/shard_map/ppermute | solution.py:62
  130.0 35.0 %collective-permute-start.12 = (bf16[1,2,2,2,80,640]{5,4,1,2,3,0:T(8,128)(2,1)S(1)}, bf16[1,2,2,2,80,640]{5,4,1,2,3,0:T(8,128)(2,1)S(1)}, u32[]{:S(2)}, u32[]{:S(2)}) collective-permute-start(bf16[1,2,2,2,80,640]{5,4,1,2,3,0:T(8,128)(2,1)S(1)} %pad_maximum_fusion.38), channel_id=1, source_target_pairs={{0,2},{2,0},{4,6},{6,4},{8,10},{10,8},{12,14},{14,12},{16,18},{18,... | collective-permute-start | bytes 2457608 | tf_op jit(solution)/shard_map/ppermute | solution.py:62
  134.1 32.1 %collective-permute-start.17 = (bf16[1,2,2,2,80,640]{5,4,3,1,2,0:T(8,128)(2,1)S(1)}, bf16[1,2,2,2,80,640]{5,4,3,1,2,0:T(8,128)(2,1)S(1)}, u32[]{:S(2)}, u32[]{:S(2)}) collective-permute-start(bf16[1,2,2,2,80,640]{5,4,3,1,2,0:T(8,128)(2,1)S(1)} %pad_maximum_fusion.39), channel_id=1, source_target_pairs={{0,4},{2,6},{4,0},{6,2},{8,12},{10,14},{12,8},{14,10},{16,20},{18,... | collective-permute-start | bytes 2457608 | tf_op jit(solution)/shard_map/ppermute | solution.py:62
  135.9 39.0 %collective-permute-start.28 = (bf16[1,2,2,2,80,640]{5,4,3,1,2,0:T(8,128)(2,1)S(1)}, bf16[1,2,2,2,80,640]{5,4,3,1,2,0:T(8,128)(2,1)S(1)}, u32[]{:S(2)}, u32[]{:S(2)}) collective-permute-start(bf16[1,2,2,2,80,640]{5,4,3,1,2,0:T(8,128)(2,1)S(1)} %pad_maximum_fusion.41), channel_id=1, source_target_pairs={{0,4},{2,6},{4,0},{6,2},{8,12},{10,14},{12,8},{14,10},{16,20},{18,... | collective-permute-start | bytes 2457608 | tf_op jit(solution)/shard_map/ppermute | solution.py:62
  165.0 64.4 %collective-permute-start.23 = (bf16[1,2,2,2,80,640]{5,4,1,2,3,0:T(8,128)(2,1)S(1)}, bf16[1,2,2,2,80,640]{5,4,1,2,3,0:T(8,128)(2,1)S(1)}, u32[]{:S(2)}, u32[]{:S(2)}) collective-permute-start(bf16[1,2,2,2,80,640]{5,4,1,2,3,0:T(8,128)(2,1)S(1)} %pad_maximum_fusion.40), channel_id=1, source_target_pairs={{0,2},{2,0},{4,6},{6,4},{8,10},{10,8},{12,14},{14,12},{16,18},{18,... | collective-permute-start | bytes 2457608 | tf_op jit(solution)/shard_map/ppermute | solution.py:62
  166.3 64.2 %collective-permute-start.32 = (bf16[2,2,2,80,640]{4,3,2,1,0:T(8,128)(2,1)S(1)}, bf16[2,2,2,80,640]{4,3,2,1,0:T(8,128)(2,1)S(1)}, u32[]{:S(2)}, u32[]{:S(2)}) collective-permute-start(bf16[2,2,2,80,640]{4,3,2,1,0:T(8,128)(2,1)S(1)} %pad_maximum_fusion.42), channel_id=1, source_target_pairs={{0,8},{2,10},{4,12},{6,14},{8,0},{10,2},{12,4},{14,6},{16,24},{18,... | collective-permute-start | bytes 2457608 | tf_op jit(solution)/shard_map/ppermute | solution.py:62
  171.3 59.6 %collective-permute-start.37 = (bf16[2,2,2,80,640]{4,3,2,0,1:T(8,128)(2,1)S(1)}, bf16[2,2,2,80,640]{4,3,2,0,1:T(8,128)(2,1)S(1)}, u32[]{:S(2)}, u32[]{:S(2)}) collective-permute-start(bf16[2,2,2,80,640]{4,3,2,0,1:T(8,128)(2,1)S(1)} %pad_maximum_fusion.43), channel_id=1, source_target_pairs={{0,8},{2,10},{4,12},{6,14},{8,0},{10,2},{12,4},{14,6},{16,24},{18,... | collective-permute-start | bytes 2457608 | tf_op jit(solution)/shard_map/ppermute | solution.py:62
  173.3 26.9 %collective-permute-start.13 = (bf16[640,512]{1,0:T(8,128)(2,1)S(1)}, bf16[640,512]{1,0:T(8,128)(2,1)S(1)}, u32[]{:S(2)}, u32[]{:S(2)}) collective-permute-start(bf16[640,512]{1,0:T(8,128)(2,1)S(1)} %slice.132), channel_id=1, source_target_pairs={{0,2},{2,0},{4,6},{6,4},{8,10},{10,8},{12,14},{14,12},{16,18},{18,... | collective-permute-start | bytes 1966088 | tf_op jit(solution)/shard_map/ppermute | solution.py:62
  174.8 37.1 %collective-permute-start.18 = (bf16[640,512]{1,0:T(8,128)(2,1)S(1)}, bf16[640,512]{1,0:T(8,128)(2,1)S(1)}, u32[]{:S(2)}, u32[]{:S(2)}) collective-permute-start(bf16[640,512]{1,0:T(8,128)(2,1)S(1)} %slice.133), channel_id=1, source_target_pairs={{0,2},{2,0},{4,6},{6,4},{8,10},{10,8},{12,14},{14,12},{16,18},{18,... | collective-permute-start | bytes 1966088 | tf_op jit(solution)/shard_map/ppermute | solution.py:62
  200.2 42.9 %collective-permute-start.44 = (bf16[2,2,2,80,640]{4,3,0,1,2:T(8,128)(2,1)S(1)}, bf16[2,2,2,80,640]{4,3,0,1,2:T(8,128)(2,1)S(1)}, u32[]{:S(2)}, u32[]{:S(2)}) collective-permute-start(bf16[2,2,2,80,640]{4,3,0,1,2:T(8,128)(2,1)S(1)} %pad_maximum_fusion.44), channel_id=1, source_target_pairs={{0,2},{2,0},{4,6},{6,4},{8,10},{10,8},{12,14},{14,12},{16,18},{18,... | collective-permute-start | bytes 2457608 | tf_op jit(solution)/shard_map/ppermute | solution.py:62
  231.0 45.3 %collective-permute-start.33 = (bf16[2,2,2,2,80,640]{5,4,3,2,1,0:T(8,128)(2,1)S(1)}, bf16[2,2,2,2,80,640]{5,4,3,2,1,0:T(8,128)(2,1)S(1)}, u32[]{:S(2)}, u32[]{:S(2)}) collective-permute-start(bf16[2,2,2,2,80,640]{5,4,3,2,1,0:T(8,128)(2,1)S(1)} %pad_maximum_fusion.29), channel_id=1, source_target_pairs={{0,2},{2,0},{4,6},{6,4},{8,10},{10,8},{12,14},{14,12},{16,18},{18,... | collective-permute-start | bytes 4915208 | tf_op jit(solution)/shard_map/ppermute | solution.py:62
  236.6 38.7 %collective-permute-start.38 = (bf16[2,2,2,2,80,640]{5,4,3,0,1,2:T(8,128)(2,1)S(1)}, bf16[2,2,2,2,80,640]{5,4,3,0,1,2:T(8,128)(2,1)S(1)}, u32[]{:S(2)}, u32[]{:S(2)}) collective-permute-start(bf16[2,2,2,2,80,640]{5,4,3,0,1,2:T(8,128)(2,1)S(1)} %pad_maximum_fusion.30), channel_id=1, source_target_pairs={{0,4},{2,6},{4,0},{6,2},{8,12},{10,14},{12,8},{14,10},{16,20},{18,... | collective-permute-start | bytes 4915208 | tf_op jit(solution)/shard_map/ppermute | solution.py:62
  243.1 33.7 %collective-permute-start.34 = (bf16[1280,512]{1,0:T(8,128)(2,1)S(1)}, bf16[1280,512]{1,0:T(8,128)(2,1)S(1)}, u32[]{:S(2)}, u32[]{:S(2)}) collective-permute-start(bf16[1280,512]{1,0:T(8,128)(2,1)S(1)} %multiply_convert_fusion.5), channel_id=1, source_target_pairs={{0,1},{1,0},{2,3},{3,2},{4,5},{5,4},{6,7},{7,6},{8,9},{9,8},{10,11... | collective-permute-start | bytes 3932168 | tf_op jit(solution)/shard_map/ppermute | solution.py:62
  243.5 83.7 %collective-permute-start.45 = (bf16[2,2,2,2,80,640]{5,4,3,0,1,2:T(8,128)(2,1)S(1)}, bf16[2,2,2,2,80,640]{5,4,3,0,1,2:T(8,128)(2,1)S(1)}, u32[]{:S(2)}, u32[]{:S(2)}) collective-permute-start(bf16[2,2,2,2,80,640]{5,4,3,0,1,2:T(8,128)(2,1)S(1)} %pad_maximum_fusion.31), channel_id=1, source_target_pairs={{0,4},{2,6},{4,0},{6,2},{8,12},{10,14},{12,8},{14,10},{16,20},{18,... | collective-permute-start | bytes 4915208 | tf_op jit(solution)/shard_map/ppermute | solution.py:62
  375.9 64.4 %collective-permute-start.85 = (bf16[1280,640]{1,0:T(8,128)(2,1)}, bf16[1280,640]{1,0:T(8,128)(2,1)}, u32[]{:S(2)}, u32[]{:S(2)}) collective-permute-start(bf16[1280,640]{1,0:T(8,128)(2,1)} %slice.190), channel_id=1, source_target_pairs={{0,1},{1,0},{2,3},{3,2},{4,5},{5,4},{6,7},{7,6},{8,9},{9,8},{10,11... | collective-permute-start | bytes 4915208 | tf_op jit(solution)/shard_map/ppermute | solution.py:62
  379.5 63.6 %collective-permute-start.86 = (bf16[1280,640]{1,0:T(8,128)(2,1)}, bf16[1280,640]{1,0:T(8,128)(2,1)}, u32[]{:S(2)}, u32[]{:S(2)}) collective-permute-start(bf16[1280,640]{1,0:T(8,128)(2,1)} %slice.189), channel_id=1, source_target_pairs={{0,1},{1,0},{2,3},{3,2},{4,5},{5,4},{6,7},{7,6},{8,9},{9,8},{10,11... | collective-permute-start | bytes 4915208 | tf_op jit(solution)/shard_map/ppermute | solution.py:62
  415.6 30.4 %collective-permute-start.49 = (bf16[640,512]{1,0:T(8,128)(2,1)}, bf16[640,512]{1,0:T(8,128)(2,1)}, u32[]{:S(2)}, u32[]{:S(2)}) collective-permute-start(bf16[640,512]{1,0:T(8,128)(2,1)} %get-tuple-element.30), channel_id=1, source_target_pairs={{0,2},{2,0},{4,6},{6,4},{8,10},{10,8},{12,14},{14,12},{16,18},{18,... | collective-permute-start | bytes 1966088 | tf_op jit(solution)/shard_map/ppermute | solution.py:62
  426.9 29.8 %collective-permute-start.50 = (bf16[640,512]{1,0:T(8,128)(2,1)}, bf16[640,512]{1,0:T(8,128)(2,1)S(1)}, u32[]{:S(2)}, u32[]{:S(2)}) collective-permute-start(bf16[640,512]{1,0:T(8,128)(2,1)} %get-tuple-element.32), channel_id=1, source_target_pairs={{0,2},{2,0},{4,6},{6,4},{8,10},{10,8},{12,14},{14,12},{16,18},{18,... | collective-permute-start | bytes 1966088 | tf_op jit(solution)/shard_map/ppermute | solution.py:62
  434.3 57.5 %collective-permute-start.60 = (bf16[2,2,2,2,80,640]{5,4,0,3,1,2:T(8,128)(2,1)}, bf16[2,2,2,2,80,640]{5,4,0,3,1,2:T(8,128)(2,1)}, u32[]{:S(2)}, u32[]{:S(2)}) collective-permute-start(bf16[2,2,2,2,80,640]{5,4,0,3,1,2:T(8,128)(2,1)} %bitcast.548), channel_id=1, source_target_pairs={{0,2},{2,0},{4,6},{6,4},{8,10},{10,8},{12,14},{14,12},{16,18},{18,... | collective-permute-start | bytes 4915208 | tf_op jit(solution)/shard_map/ppermute | solution.py:62
  445.4 61.7 %collective-permute-start.87 = (bf16[2,2,2,2,80,640]{5,4,0,1,2,3:T(8,128)(2,1)S(1)}, bf16[2,2,2,2,80,640]{5,4,0,1,2,3:T(8,128)(2,1)S(1)}, u32[]{:S(2)}, u32[]{:S(2)}) collective-permute-start(bf16[2,2,2,2,80,640]{5,4,0,1,2,3:T(8,128)(2,1)S(1)} %bitcast.600), channel_id=1, source_target_pairs={{0,4},{2,6},{4,0},{6,2},{8,12},{10,14},{12,8},{14,10},{16,20},{18,... | collective-permute-start | bytes 4915208 | tf_op jit(solution)/shard_map/ppermute | solution.py:62
  459.4 34.6 %collective-permute-start.51 = (bf16[1280,512]{1,0:T(8,128)(2,1)S(1)}, bf16[1280,512]{1,0:T(8,128)(2,1)S(1)}, u32[]{:S(2)}, u32[]{:S(2)}) collective-permute-start(bf16[1280,512]{1,0:T(8,128)(2,1)S(1)} %fusion.10), channel_id=1, source_target_pairs={{0,1},{1,0},{2,3},{3,2},{4,5},{5,4},{6,7},{7,6},{8,9},{9,8},{10,11... | collective-permute-start | bytes 3932168 | tf_op jit(solution)/shard_map/ppermute | solution.py:62
  465.4 53.8 %collective-permute-start.68 = (bf16[2,2,2,2,80,640]{5,4,0,3,1,2:T(8,128)(2,1)S(1)}, bf16[2,2,2,2,80,640]{5,4,0,3,1,2:T(8,128)(2,1)S(1)}, u32[]{:S(2)}, u32[]{:S(2)}) collective-permute-start(bf16[2,2,2,2,80,640]{5,4,0,3,1,2:T(8,128)(2,1)S(1)} %bitcast.599), channel_id=1, source_target_pairs={{0,4},{2,6},{4,0},{6,2},{8,12},{10,14},{12,8},{14,10},{16,20},{18,... | collective-permute-start | bytes 4915208 | tf_op jit(solution)/shard_map/ppermute | solution.py:62
  507.1 71.8 %collective-permute-start.52 = (bf16[1280,512]{1,0:T(8,128)(2,1)S(1)}, bf16[1280,512]{1,0:T(8,128)(2,1)S(1)}, u32[]{:S(2)}, u32[]{:S(2)}) collective-permute-start(bf16[1280,512]{1,0:T(8,128)(2,1)S(1)} %get-tuple-element.87), channel_id=1, source_target_pairs={{0,1},{1,0},{2,3},{3,2},{4,5},{5,4},{6,7},{7,6},{8,9},{9,8},{10,11... | collective-permute-start | bytes 3932168 | tf_op jit(solution)/shard_map/ppermute | solution.py:62
  507.6 35.9 %collective-permute-start.88 = (bf16[2,2,2,80,640]{4,3,0,1,2:T(8,128)(2,1)S(1)}, bf16[2,2,2,80,640]{4,3,0,1,2:T(8,128)(2,1)S(1)}, u32[]{:S(2)}, u32[]{:S(2)}) collective-permute-start(bf16[2,2,2,80,640]{4,3,0,1,2:T(8,128)(2,1)S(1)} %dynamic-slice_bitcast_fusion), channel_id=1, source_target_pairs={{0,2},{2,0},{4,6},{6,4},{8,10},{10,8},{12,14},{14,12},{16,18},{18,... | collective-permute-start | bytes 2457608 | tf_op jit(solution)/shard_map/ppermute | solution.py:62
  512.7 123.6 %collective-permute-start.80 = (bf16[1280,640]{1,0:T(8,128)(2,1)}, bf16[1280,640]{1,0:T(8,128)(2,1)}, u32[]{:S(2)}, u32[]{:S(2)}) collective-permute-start(bf16[1280,640]{1,0:T(8,128)(2,1)} %slice.191), channel_id=1, source_target_pairs={{0,1},{1,0},{2,3},{3,2},{4,5},{5,4},{6,7},{7,6},{8,9},{9,8},{10,11... | collective-permute-start | bytes 4915208 | tf_op jit(solution)/shard_map/ppermute | solution.py:62
  518.6 120.0 %collective-permute-start.91 = (bf16[1280,640]{1,0:T(8,128)(2,1)}, bf16[1280,640]{1,0:T(8,128)(2,1)}, u32[]{:S(2)}, u32[]{:S(2)}) collective-permute-start(bf16[1280,640]{1,0:T(8,128)(2,1)} %slice.188), channel_id=1, source_target_pairs={{0,1},{1,0},{2,3},{3,2},{4,5},{5,4},{6,7},{7,6},{8,9},{9,8},{10,11... | collective-permute-start | bytes 4915208 | tf_op jit(solution)/shard_map/ppermute | solution.py:62
  565.5 68.7 %collective-permute-start.70 = (bf16[2,2,80,640]{3,2,0,1:T(8,128)(2,1)}, bf16[2,2,80,640]{3,2,0,1:T(8,128)(2,1)}, u32[]{:S(2)}, u32[]{:S(2)}) collective-permute-start(bf16[2,2,80,640]{3,2,0,1:T(8,128)(2,1)} %dynamic-slice_bitcast_fusion.8), channel_id=1, source_target_pairs={{0,16},{2,18},{4,20},{6,22},{8,24},{10,26},{12,28},{14,30},{16,0},... | collective-permute-start | bytes 1228808 | tf_op jit(solution)/shard_map/ppermute | solution.py:62
  578.4 53.6 %collective-permute-start.90 = (bf16[2,80,640]{2,1,0:T(8,128)(2,1)}, bf16[2,80,640]{2,1,0:T(8,128)(2,1)}, u32[]{:S(2)}, u32[]{:S(2)}) collective-permute-start(bf16[2,80,640]{2,1,0:T(8,128)(2,1)} %dynamic-slice_bitcast_fusion.13), channel_id=1, source_target_pairs={{0,16},{2,18},{4,20},{6,22},{8,24},{10,26},{12,28},{14,30},{16,0},... | collective-permute-start | bytes 614408 | tf_op jit(solution)/shard_map/ppermute | solution.py:62
  620.5 57.2 %collective-permute-start.53 = (bf16[640,512]{1,0:T(8,128)(2,1)}, bf16[640,512]{1,0:T(8,128)(2,1)}, u32[]{:S(2)}, u32[]{:S(2)}) collective-permute-start(bf16[640,512]{1,0:T(8,128)(2,1)} %get-tuple-element.36), channel_id=1, source_target_pairs={{0,2},{2,0},{4,6},{6,4},{8,10},{10,8},{12,14},{14,12},{16,18},{18,... | collective-permute-start | bytes 1966088 | tf_op jit(solution)/shard_map/ppermute | solution.py:62
  631.9 53.1 %collective-permute-start.54 = (bf16[640,512]{1,0:T(8,128)(2,1)S(1)}, bf16[640,512]{1,0:T(8,128)(2,1)S(1)}, u32[]{:S(2)}, u32[]{:S(2)}) collective-permute-start(bf16[640,512]{1,0:T(8,128)(2,1)S(1)} %get-tuple-element.38), channel_id=1, source_target_pairs={{0,2},{2,0},{4,6},{6,4},{8,10},{10,8},{12,14},{14,12},{16,18},{18,... | collective-permute-start | bytes 1966088 | tf_op jit(solution)/shard_map/ppermute | solution.py:62
  634.2 57.0 %collective-permute-start.56 = (bf16[1,2,2,2,80,640]{5,4,3,1,2,0:T(8,128)(2,1)S(1)}, bf16[1,2,2,2,80,640]{5,4,3,1,2,0:T(8,128)(2,1)S(1)}, u32[]{:S(2)}, u32[]{:S(2)}) collective-permute-start(bf16[1,2,2,2,80,640]{5,4,3,1,2,0:T(8,128)(2,1)S(1)} %bitcast.610), channel_id=1, source_target_pairs={{0,2},{2,0},{4,6},{6,4},{8,10},{10,8},{12,14},{14,12},{16,18},{18,... | collective-permute-start | bytes 2457608 | tf_op jit(solution)/shard_map/ppermute | solution.py:62
  636.3 55.8 %collective-permute-start.76 = (bf16[1,2,2,2,80,640]{5,4,1,2,3,0:T(8,128)(2,1)S(1)}, bf16[1,2,2,2,80,640]{5,4,1,2,3,0:T(8,128)(2,1)S(1)}, u32[]{:S(2)}, u32[]{:S(2)}) collective-permute-start(bf16[1,2,2,2,80,640]{5,4,1,2,3,0:T(8,128)(2,1)S(1)} %bitcast.609), channel_id=1, source_target_pairs={{0,4},{2,6},{4,0},{6,2},{8,12},{10,14},{12,8},{14,10},{16,20},{18,... | collective-permute-start | bytes 2457608 | tf_op jit(solution)/shard_map/ppermute | solution.py:62
  638.6 37.7 %collective-permute-start.71 = (bf16[2,80,640]{2,1,0:T(8,128)(2,1)S(1)}, bf16[2,80,640]{2,1,0:T(8,128)(2,1)S(1)}, u32[]{:S(2)}, u32[]{:S(2)}) collective-permute-start(bf16[2,80,640]{2,1,0:T(8,128)(2,1)S(1)} %dynamic-slice_bitcast_fusion.17), channel_id=1, source_target_pairs={{0,2},{2,0},{4,6},{6,4},{8,10},{10,8},{12,14},{14,12},{16,18},{18,... | collective-permute-start | bytes 614408 | tf_op jit(solution)/shard_map/ppermute | solution.py:62
  689.1 90.9 %collective-permute-start.55 = (bf16[1280,512]{1,0:T(8,128)(2,1)S(1)}, bf16[1280,512]{1,0:T(8,128)(2,1)S(1)}, u32[]{:S(2)}, u32[]{:S(2)}) collective-permute-start(bf16[1280,512]{1,0:T(8,128)(2,1)S(1)} %fusion.11), channel_id=1, source_target_pairs={{0,1},{1,0},{2,3},{3,2},{4,5},{5,4},{6,7},{7,6},{8,9},{9,8},{10,11... | collective-permute-start | bytes 3932168 | tf_op jit(solution)/shard_map/ppermute | solution.py:62
  691.3 47.7 %collective-permute-start.64 = (bf16[1,2,2,2,80,640]{5,4,1,2,3,0:T(8,128)(2,1)S(1)}, bf16[1,2,2,2,80,640]{5,4,1,2,3,0:T(8,128)(2,1)S(1)}, u32[]{:S(2)}, u32[]{:S(2)}) collective-permute-start(bf16[1,2,2,2,80,640]{5,4,1,2,3,0:T(8,128)(2,1)S(1)} %bitcast.613), channel_id=1, source_target_pairs={{0,2},{2,0},{4,6},{6,4},{8,10},{10,8},{12,14},{14,12},{16,18},{18,... | collective-permute-start | bytes 2457608 | tf_op jit(solution)/shard_map/ppermute | solution.py:62
  692.1 48.8 %collective-permute-start.72 = (bf16[1,2,2,2,80,640]{5,4,3,1,2,0:T(8,128)(2,1)S(1)}, bf16[1,2,2,2,80,640]{5,4,3,1,2,0:T(8,128)(2,1)S(1)}, u32[]{:S(2)}, u32[]{:S(2)}) collective-permute-start(bf16[1,2,2,2,80,640]{5,4,3,1,2,0:T(8,128)(2,1)S(1)} %bitcast.611), channel_id=1, source_target_pairs={{0,4},{2,6},{4,0},{6,2},{8,12},{10,14},{12,8},{14,10},{16,20},{18,... | collective-permute-start | bytes 2457608 | tf_op jit(solution)/shard_map/ppermute | solution.py:62
  704.9 46.0 %collective-permute-start.82 = (bf16[1,2,2,80,640]{4,3,2,1,0:T(8,128)(2,1)S(1)}, bf16[1,2,2,80,640]{4,3,2,1,0:T(8,128)(2,1)S(1)}, u32[]{:S(2)}, u32[]{:S(2)}) collective-permute-start(bf16[1,2,2,80,640]{4,3,2,1,0:T(8,128)(2,1)S(1)} %dynamic-slice_bitcast_fusion.5), channel_id=1, source_target_pairs={{0,8},{2,10},{4,12},{6,14},{8,0},{10,2},{12,4},{14,6},{16,24},{18,... | collective-permute-start | bytes 1228808 | tf_op jit(solution)/shard_map/ppermute | solution.py:62
  744.5 29.6 %collective-permute-start.65 = (bf16[1,2,2,80,640]{4,3,1,2,0:T(8,128)(2,1)S(1)}, bf16[1,2,2,80,640]{4,3,1,2,0:T(8,128)(2,1)S(1)}, u32[]{:S(2)}, u32[]{:S(2)}) collective-permute-start(bf16[1,2,2,80,640]{4,3,1,2,0:T(8,128)(2,1)S(1)} %dynamic-slice_bitcast_fusion.9), channel_id=1, source_target_pairs={{0,4},{2,6},{4,0},{6,2},{8,12},{10,14},{12,8},{14,10},{16,20},{18,... | collective-permute-start | bytes 1228808 | tf_op jit(solution)/shard_map/ppermute | solution.py:62
  774.9 48.2 %collective-permute-start.66 = (bf16[1,2,80,640]{3,2,1,0:T(8,128)(2,1)}, bf16[1,2,80,640]{3,2,1,0:T(8,128)(2,1)}, u32[]{:S(2)}, u32[]{:S(2)}) collective-permute-start(bf16[1,2,80,640]{3,2,1,0:T(8,128)(2,1)} %dynamic-slice_bitcast_fusion.18), channel_id=1, source_target_pairs={{0,8},{2,10},{4,12},{6,14},{8,0},{10,2},{12,4},{14,6},{16,24},{18,... | collective-permute-start | bytes 614408 | tf_op jit(solution)/shard_map/ppermute | solution.py:62
  776.6 49.8 %collective-permute-start.74 = (bf16[1,2,80,640]{3,2,1,0:T(8,128)(2,1)}, bf16[1,2,80,640]{3,2,1,0:T(8,128)(2,1)}, u32[]{:S(2)}, u32[]{:S(2)}) collective-permute-start(bf16[1,2,80,640]{3,2,1,0:T(8,128)(2,1)} %dynamic-slice_bitcast_fusion.16), channel_id=1, source_target_pairs={{0,16},{2,18},{4,20},{6,22},{8,24},{10,26},{12,28},{14,30},{16,0},... | collective-permute-start | bytes 614408 | tf_op jit(solution)/shard_map/ppermute | solution.py:62
  (176 other events, 2837.6 us)

commit v3 on v2

v3 whole, which is shorter than its diff:
```python
from functools import partial
import math

import jax
import jax.numpy as jnp
from jax import lax
from jax.experimental import pallas as pl
from jax.experimental.pallas import tpu as pltpu
from jax.sharding import PartitionSpec as P

HD = 80
LAYERS = 2
PROMPT_DEV = 512
TILE = 256

EPSILON = 1e-06
LOG_TWO_E = 1.4426950408889634
LN_TWO = 0.6931471805599453
NEGATIVE = -1e30


def lowered(values):
    return values.astype(jnp.bfloat16)


def dot_nn(former, latter):
    return jnp.dot(former, latter, preferred_element_type=jnp.float32)


def dot_tn(former, latter):
    return lax.dot_general(
        former, latter, (((0,), (0,)), ((), ())), preferred_element_type=jnp.float32
    )


def dot_nt(former, latter):
    return lax.dot_general(
        former, latter, (((1,), (1,)), ((), ())), preferred_element_type=jnp.float32
    )


def inverse_root(source):
    return lax.rsqrt(jnp.mean(source * source, axis=0, keepdims=True) + EPSILON)


def softplus(values):
    return jnp.log1p(jnp.exp(values))


def norm_backward(source, inverse, gain, incoming):
    unit = source * inverse
    gain_grad = jnp.sum(incoming * unit, axis=1)
    scaled = incoming * gain
    return (
        gain_grad,
        inverse * (scaled - unit * jnp.mean(scaled * unit, axis=0, keepdims=True)),
    )


def pair_swap(values, axis, bit):
    size = lax.axis_size(axis)
    return lax.ppermute(values, axis, [(i, i ^ bit) for i in range(size)])


def my_bit(axis, bit):
    return (lax.axis_index(axis) & bit) != 0


def exchange_orders(size):
    if size == 16:
        return (8, 4, 2, 1), (8, 4, 1, 2), (1, 2, 8, 4)
    bits = tuple(1 << k for k in reversed(range(size.bit_length() - 1)))
    return (bits,) * 3


def zero_after(values):
    corner = values[(0,) * values.ndim]
    return jnp.minimum((corner.astype(jnp.float32) > 3e38).astype(jnp.int32), 0)


def doubled_gather(shard, order):
    values, done, marks = shard, [], []
    for bit in order:
        other = pair_swap(values, "dp", bit)
        marks.append(other)
        upper = my_bit("dp", bit)
        at = sum(1 for earlier in done if earlier > bit)
        values = jnp.stack(
            [jnp.where(upper, other, values), jnp.where(upper, values, other)], axis=at
        )
        done.append(bit)
    return values.reshape((-1, shard.shape[1])), zero_after(marks[-2])


def halved_scatter(values, order):
    rows, width = values.shape
    left = sorted(order, reverse=True)
    values = values.reshape((2,) * len(order) + (rows >> len(order), width))
    for bit in reversed(order):
        at = left.index(bit)
        left.remove(bit)
        upper = my_bit("dp", bit).astype(jnp.int32)
        keep = lax.dynamic_index_in_dim(values, upper, at, keepdims=False)
        send = lax.dynamic_index_in_dim(values, 1 - upper, at, keepdims=False)
        got = pair_swap(send, "dp", bit)
        values = keep.astype(jnp.float32) + got.astype(jnp.float32)
        if left:
            values = lowered(values)
    return values


def total_sum(values):
    for axis in ("tensor", "dp"):
        bit = 1
        while bit < lax.axis_size(axis):
            values = values + pair_swap(values, axis, bit)
            bit *= 2
    return values


def gather_tokens(local):
    if lax.axis_size("tensor") != 2:
        return lax.all_gather(local, "tensor", axis=1, tiled=True)
    other = pair_swap(local, "tensor", 1)
    upper = my_bit("tensor", 1)
    return jnp.concatenate([jnp.where(upper, other, local), jnp.where(upper, local, other)], axis=1)


def far_tokens(normed):
    part = PROMPT_DEV // lax.axis_size("tensor")
    place = lax.axis_index("tensor") * part
    return gather_tokens(pair_swap(lax.dynamic_slice_in_dim(normed, place, part, 1), "dp", 1))


def scatter_tokens(product, *values):
    if lax.axis_size("tensor") != 2:
        return lax.psum_scatter(
            lowered(product(*values)), "tensor", scatter_dimension=1, tiled=True
        ).astype(jnp.float32)
    count = values[0].shape[1] // 2
    place = lax.axis_index("tensor")
    theirs = [lax.dynamic_slice_in_dim(v, (1 - place) * count, count, 1) for v in values]
    got = pair_swap(lowered(product(*theirs)), "tensor", 1)
    mine = [lax.dynamic_slice_in_dim(v, place * count, count, 1) for v in values]
    return product(*mine) + got.astype(jnp.float32)


def feed_gather(values):
    if lax.axis_size("tensor") != 2:
        return lax.all_gather(values, "tensor", axis=1, tiled=True)
    return jnp.concatenate([values, pair_swap(values, "tensor", 1)], axis=1)


def feed_scatter(values):
    if lax.axis_size("tensor") != 2:
        return lax.psum_scatter(lowered(values), "tensor", scatter_dimension=1, tiled=True)
    count = values.shape[1] // 2
    got = pair_swap(lowered(values[:, count:]), "tensor", 1)
    return lowered(values[:, :count] + got.astype(jnp.float32))


def key_parts(tile):
    first = tile * TILE
    if first < PROMPT_DEV:
        return ([(0, first, "free")] if first else []) + [(first, TILE, "earlier")]
    return [(0, PROMPT_DEV, "free"), (PROMPT_DEV, first - PROMPT_DEV + TILE, "segment")]


def masked(scores, kind, first_key, first_query, start):
    if kind == "free":
        return scores
    key = lax.broadcasted_iota(jnp.int32, scores.shape, 0) + first_key
    query = lax.broadcasted_iota(jnp.int32, scores.shape, 1) + first_query
    allowed = key <= query
    if kind == "segment":
        allowed = allowed & (key >= start)
    return jnp.where(allowed, scores, NEGATIVE)


def spans(reference):
    tokens = reference.shape[1]
    return [(tile, slice(tile * TILE, tile * TILE + TILE)) for tile in range(tokens // TILE)]


def by_side(side_ref, reference, meets, skips):
    prompt = [at for tile, at in spans(reference) if tile * TILE < PROMPT_DEV]

    @pl.when(side_ref[0] == 0)
    def _():
        for at in prompt:
            skips(at)

    @pl.when(side_ref[0] != 0)
    def _():
        for at in prompt:
            meets(at)

    for tile, at in spans(reference):
        if at not in prompt:
            meets(at)


def own_forward(start_ref, q_ref, k_ref, v_ref, sum_ref, top_ref, total_ref):
    keys = k_ref[...].T
    for tile, at in spans(q_ref):
        query, start = q_ref[:, at], start_ref[:, at]
        parts = []
        for key, count, kind in key_parts(tile):
            scores = dot_nn(keys[key : key + count], query)
            scores = masked(scores, kind, key, tile * TILE, start)
            parts.append((scores, v_ref[:, key : key + count]))
        highest = jnp.max(parts[0][0], axis=0, keepdims=True)
        for scores, _ in parts[1:]:
            highest = jnp.maximum(highest, jnp.max(scores, axis=0, keepdims=True))
        total, mixed = 0.0, 0.0
        for scores, value in parts:
            weights = jnp.exp2(scores - highest)
            total = total + jnp.sum(weights, axis=0, keepdims=True)
            mixed = mixed + dot_nn(value, lowered(weights))
        sum_ref[:, at] = mixed
        top_ref[:, at] = highest
        total_ref[:, at] = total


def far_forward(
    side_ref, q_ref, k_ref, v_ref, sum_ref, top_ref, total_ref, out_ref, lse_ref
):
    keys = k_ref[...].T

    def meets(at):
        scores = dot_nn(keys, q_ref[:, at])
        highest = jnp.maximum(top_ref[:, at], jnp.max(scores, axis=0, keepdims=True))
        weights = jnp.exp2(scores - highest)
        scale = jnp.exp2(top_ref[:, at] - highest)
        total = total_ref[:, at] * scale + jnp.sum(weights, axis=0, keepdims=True)
        mixed = sum_ref[:, at] * scale + dot_nn(v_ref[...], lowered(weights))
        out_ref[:, at] = lowered(mixed / total)
        lse_ref[:, at] = highest + jnp.log2(total)

    def skips(at):
        out_ref[:, at] = lowered(sum_ref[:, at] / total_ref[:, at])
        lse_ref[:, at] = top_ref[:, at] + jnp.log2(total_ref[:, at])

    by_side(side_ref, q_ref, meets, skips)


def score_grads(scores, lse, d_shares, delta):
    shares = jnp.exp2(scores - lse)
    return lowered(shares), lowered(shares * (d_shares - delta))


def far_backward(
    side_ref, q_ref, k_ref, v_ref, out_ref, grad_ref, lse_ref, dq_ref, delta_ref, dk_ref, dv_ref
):
    keys, values = k_ref[...].T, v_ref[...].T
    delta_ref[...] = jnp.sum(
        out_ref[...].astype(jnp.float32) * grad_ref[...].astype(jnp.float32), axis=0, keepdims=True
    )

    def terms(at):
        query, grad = q_ref[:, at], grad_ref[:, at]
        shares, d_scores = score_grads(
            dot_nn(keys, query), lse_ref[:, at], dot_nn(values, grad), delta_ref[:, at]
        )
        dq_ref[:, at] = dot_nn(k_ref[...], d_scores)
        return dot_nt(query, d_scores), dot_nt(grad, shares)

    def close(tiles):
        dk, dv = 0.0, 0.0
        for at in tiles:
            k_term, v_term = terms(at)
            dk, dv = dk + k_term, dv + v_term
        dk_ref[...] = lowered(dk * LN_TWO)
        dv_ref[...] = lowered(dv)

    tiles = [at for _, at in spans(q_ref)]
    conts = [at for tile, at in spans(q_ref) if tile * TILE >= PROMPT_DEV]

    @pl.when(side_ref[0] == 0)
    def _():
        for at in tiles:
            if at not in conts:
                dq_ref[:, at] = jnp.zeros_like(dq_ref[:, at])
        close(conts)

    @pl.when(side_ref[0] != 0)
    def _():
        close(tiles)


def own_backward(
    start_ref,
    gain_ref,
    q_ref,
    k_ref,
    v_ref,
    grad_ref,
    lse_ref,
    delta_ref,
    far_dq_ref,
    dq_ref,
    dk_ref,
    dv_ref,
    scale_ref,
    k_total,
    v_total,
):
    keys, values = k_ref[...].T, v_ref[...].T
    seen = set()
    scale = 0.0
    for tile, at in spans(q_ref):
        query, grad = q_ref[:, at], grad_ref[:, at]
        dq = far_dq_ref[:, at]
        for key, count, kind in key_parts(tile):
            scores = dot_nn(keys[key : key + count], query)
            scores = masked(scores, kind, key, tile * TILE, start_ref[:, at])
            shares, d_scores = score_grads(
                scores, lse_ref[:, at], dot_nn(values[key : key + count], grad), delta_ref[:, at]
            )
            dv = dot_nt(grad, shares)
            dk = dot_nt(query, d_scores)
            dq = dq + dot_nn(k_ref[:, key : key + count], d_scores)
            for offset in range(0, count, TILE):
                there = slice(key + offset, key + offset + TILE)
                here = slice(offset, offset + TILE)
                if key + offset in seen:
                    k_total[:, there] += dk[:, here]
                    v_total[:, there] += dv[:, here]
                else:
                    seen.add(key + offset)
                    k_total[:, there] = dk[:, here]
                    v_total[:, there] = dv[:, here]
        dq_ref[:, at] = lowered(dq * gain_ref[...])
        scale = scale + jnp.sum(dq * query.astype(jnp.float32), axis=1, keepdims=True)
    dk_ref[...] = lowered(k_total[...] * LN_TWO)
    dv_ref[...] = lowered(v_total[...])
    scale_ref[...] = scale


SCALAR = pl.BlockSpec(memory_space=pltpu.SMEM)


def rows_block(count):
    return pl.BlockSpec((HD, count), lambda head: (head, 0))


def flat_block(count):
    return pl.BlockSpec((None, 1, count), lambda head: (head, 0, 0))


def same_block(*shape):
    return pl.BlockSpec(shape, lambda head: (0, 0))


def per_head(kernel, name, heads, area, products, ins, outs, scratch=()):
    flops = 2 * 256 * area * heads * products
    moved = sum(array.size * array.dtype.itemsize for _, array in ins)
    return pl.pallas_call(
        kernel,
        grid=(heads,),
        in_specs=[spec for spec, _ in ins],
        out_specs=[spec for spec, _, _ in outs],
        out_shape=[jax.ShapeDtypeStruct(shape, kind) for _, shape, kind in outs],
        scratch_shapes=list(scratch),
        compiler_params=pltpu.CompilerParams(vmem_limit_bytes=32 << 20),
        cost_estimate=pl.CostEstimate(
            flops=flops, bytes_accessed=moved, transcendentals=area * heads
        ),
        name=name,
    )(*[array for _, array in ins])


def attention_own(start, queries, keys, values):
    width, tokens = queries.shape
    heads = width // HD
    all_rows, flat = rows_block(tokens), flat_block(tokens)
    return per_head(
        own_forward,
        "attention_own",
        heads,
        tokens * tokens * 5 // 8,
        3,
        [
            (same_block(1, tokens), start),
            (all_rows, queries),
            (all_rows, keys),
            (all_rows, values),
        ],
        [
            (all_rows, (width, tokens), jnp.float32),
            (flat, (heads, 1, tokens), jnp.float32),
            (flat, (heads, 1, tokens), jnp.float32),
        ],
    )


def attention_far(side, queries, keys, values, partial_sum, top, total):
    width, tokens = queries.shape
    heads = width // HD
    all_rows, flat, far_rows = rows_block(tokens), flat_block(tokens), rows_block(PROMPT_DEV)
    return per_head(
        far_forward,
        "attention_far",
        heads,
        tokens * PROMPT_DEV,
        3,
        [
            (SCALAR, side),
            (all_rows, queries),
            (far_rows, keys),
            (far_rows, values),
            (all_rows, partial_sum),
            (flat, top),
            (flat, total),
        ],
        [
            (all_rows, (width, tokens), jnp.bfloat16),
            (flat, (heads, 1, tokens), jnp.float32),
        ],
    )


def attention_far_back(side, queries, keys, values, mixed, grads, lse):
    width, tokens = queries.shape
    heads = width // HD
    all_rows, flat, far_rows = rows_block(tokens), flat_block(tokens), rows_block(PROMPT_DEV)
    return per_head(
        far_backward,
        "attention_far_back",
        heads,
        tokens * PROMPT_DEV,
        6,
        [
            (SCALAR, side),
            (all_rows, queries),
            (far_rows, keys),
            (far_rows, values),
            (all_rows, mixed),
            (all_rows, grads),
            (flat, lse),
        ],
        [
            (all_rows, (width, tokens), jnp.float32),
            (flat, (heads, 1, tokens), jnp.float32),
            (far_rows, (width, PROMPT_DEV), jnp.bfloat16),
            (far_rows, (width, PROMPT_DEV), jnp.bfloat16),
        ],
    )


def attention_own_back(start, gain, queries, keys, values, grads, lse, delta, far_dq):
    width, tokens = queries.shape
    heads = width // HD
    all_rows, flat = rows_block(tokens), flat_block(tokens)
    return per_head(
        own_backward,
        "attention_own_back",
        heads,
        tokens * tokens * 5 // 8,
        6,
        [
            (same_block(1, tokens), start),
            (same_block(HD, 1), gain),
            (all_rows, queries),
            (all_rows, keys),
            (all_rows, values),
            (all_rows, grads),
            (flat, lse),
            (flat, delta),
            (all_rows, far_dq),
        ],
        [
            (all_rows, (width, tokens), jnp.bfloat16),
            (all_rows, (width, tokens), jnp.bfloat16),
            (all_rows, (width, tokens), jnp.bfloat16),
            (pl.BlockSpec((HD, 1), lambda head: (head, 0)), (width, 1), jnp.float32),
        ],
        [pltpu.VMEM((HD, tokens), jnp.float32)] * 2,
    )


def segment_starts(lengths_row, tokens):
    place = jnp.arange(tokens, dtype=jnp.int32) - PROMPT_DEV
    bounds = jnp.cumsum(lengths_row)
    passed = jnp.where(place[:, None] >= bounds[None, :], bounds[None, :], 0)
    return (PROMPT_DEV + jnp.max(passed, axis=1))[None, :]


def body(
    inputs,
    cotangent,
    query_weight,
    key_weight,
    value_weight,
    output_weight,
    up_weight,
    down_weight,
    attention_gain,
    feed_gain,
    query_scale,
    cont_lengths,
):
    tokens = inputs.shape[0] * lax.axis_size("tensor")
    heads = query_weight.shape[2] // HD
    orders = exchange_orders(lax.axis_size("dp"))
    side = (lax.axis_index("dp") % 2).astype(jnp.int32)[None]
    start = segment_starts(cont_lengths[0], tokens)

    weights = []
    waits = [jnp.int32(0)] * 3
    for layer in range(LAYERS):
        members = (
            (key_weight, False),
            (value_weight, False),
            (query_weight, False),
            (output_weight, True),
            (up_weight, False),
            (down_weight, True),
        )
        full = []
        for place, (member, flip) in enumerate(members):
            lane = place % 3
            shard = lax.dynamic_index_in_dim(member, layer + waits[lane], 0, keepdims=False)
            whole, waits[lane] = doubled_gather(shard.T if flip else shard, orders[lane])
            full.append(whole)
        weights.append(full)

    stored = []
    current = inputs.T
    for layer in range(LAYERS):
        wk, wv, wq, wo, wu, wd = weights[layer]
        attn_gain, ff_gain = attention_gain[layer][:, None], feed_gain[layer][:, None]
        inverse_attn = inverse_root(current)
        normed = gather_tokens(lowered(current * inverse_attn * attn_gain))
        far_normed = far_tokens(normed)
        keys = lowered(dot_tn(wk, normed))
        values = lowered(dot_tn(wv, normed))
        gain_q = softplus(query_scale[layer]) * LOG_TWO_E / math.sqrt(HD)
        gain_rows = jnp.tile(gain_q, heads)[:, None]
        queries = lowered(dot_tn(wq, normed) * (gain_rows * LOG_TWO_E))
        partial_sum = attention_own(start, queries, keys, values)
        far_keys = lowered(dot_tn(wk, far_normed))
        far_values = lowered(dot_tn(wv, far_normed))
        mixed, lse = attention_far(side, queries, far_keys, far_values, *partial_sum)
        middle = current + scatter_tokens(lambda rows: dot_nn(wo, rows), mixed)
        inverse_feed = inverse_root(middle)
        feed = lowered(middle * inverse_feed * ff_gain)
        wu, wd = feed_gather(wu), feed_gather(wd)
        upper = dot_tn(wu, feed)
        hidden = lowered(upper * jax.nn.sigmoid(upper))
        stored.append(
            (
                (current, inverse_attn, attn_gain, normed),
                (gain_q, queries, keys, values, far_keys, far_values, mixed, lse),
                (middle, inverse_feed, ff_gain, feed, upper, hidden),
                (wk, wv, wq, wo, wu, wd),
            )
        )
        current = middle + dot_nn(wd, hidden)

    layer_grads = [None] * LAYERS
    small_grads = [None] * LAYERS
    grad = cotangent.T
    for layer in reversed(range(LAYERS)):
        (
            (source, inverse_attn, attn_gain, normed),
            (gain_q, queries, keys, values, far_keys, far_values, mixed, lse),
            (middle, inverse_feed, ff_gain, feed, upper, hidden),
            (wk, wv, wq, wo, wu, wd),
        ) = stored[layer]
        grad_low = lowered(grad)
        down_grad = feed_scatter(dot_nt(grad_low, hidden))
        d_hidden = lowered(dot_tn(wd, grad_low)).astype(jnp.float32)
        sigmoid = jax.nn.sigmoid(upper)
        d_upper = lowered(d_hidden * (sigmoid * (1.0 + upper * (1.0 - sigmoid))))
        up_grad = feed_scatter(dot_nt(feed, d_upper))
        feed_gain_grad, part = norm_backward(middle, inverse_feed, ff_gain, dot_nn(wu, d_upper))
        grad_middle = grad + part
        middle_low = gather_tokens(lowered(grad_middle))
        d_mixed = lowered(dot_tn(wo, middle_low))
        far_dq, delta, far_dk, far_dv = attention_far_back(
            side, queries, far_keys, far_values, mixed, d_mixed, lse
        )
        back_keys = pair_swap(far_dk, "dp", 1).astype(jnp.float32)
        back_values = pair_swap(far_dv, "dp", 1).astype(jnp.float32)
        out_grad = lowered(dot_nt(middle_low, mixed))
        d_raw, own_dk, own_dv, scale_rows = attention_own_back(
            start, gain_q[:, None], queries, keys, values, d_mixed, lse, delta, far_dq
        )
        pad = ((0, 0), (0, tokens - PROMPT_DEV))
        d_keys = lowered(own_dk.astype(jnp.float32) + jnp.pad(back_keys, pad))
        d_values = lowered(own_dv.astype(jnp.float32) + jnp.pad(back_values, pad))
        scale_raw = jnp.sum(scale_rows.reshape(heads, HD), 0) / (gain_q * LOG_TWO_E)
        scale_grad = scale_raw * jax.nn.sigmoid(query_scale[layer]) * LOG_TWO_E / math.sqrt(HD)
        d_normed = scatter_tokens(
            lambda dq, dk, dv: dot_nn(wq, dq) + dot_nn(wk, dk) + dot_nn(wv, dv),
            d_raw,
            d_keys,
            d_values,
        )
        query_grad = lowered(dot_nt(normed, d_raw))
        key_grad = lowered(dot_nt(normed, d_keys))
        value_grad = lowered(dot_nt(normed, d_values))
        attn_gain_grad, part = norm_backward(source, inverse_attn, attn_gain, d_normed)
        grad = grad_middle + part
        small_grads[layer] = jnp.concatenate([attn_gain_grad, feed_gain_grad, scale_grad])
        down_grad, up_grad, out_grad, query_grad, key_grad, value_grad = [
            halved_scatter(member, orders[place % 3])
            for place, member in enumerate(
                (down_grad, up_grad, out_grad, query_grad, key_grad, value_grad)
            )
        ]
        layer_grads[layer] = (query_grad, key_grad, value_grad, out_grad.T, up_grad, down_grad.T)

    summed = [jnp.stack(members) for members in zip(*layer_grads)]
    small = total_sum(jnp.stack(small_grads))
    width = current.shape[0]
    return (
        current.T,
        grad.T,
        *summed,
        small[:, :width],
        small[:, width : 2 * width],
        small[:, 2 * width :],
    )


def solution(mesh):
    in_specs = (
        P(("dp", "tensor"), None),
        P(("dp", "tensor"), None),
        P(None, "dp", "tensor"),
        P(None, "dp", "tensor"),
        P(None, "dp", "tensor"),
        P(None, "tensor", "dp"),
        P(None, "dp", "tensor"),
        P(None, "tensor", "dp"),
        P(),
        P(),
        P(),
        P("dp", None),
    )
    out_specs = (
        P(("dp", "tensor"), None),
        P(("dp", "tensor"), None),
        P(None, "dp", "tensor"),
        P(None, "dp", "tensor"),
        P(None, "dp", "tensor"),
        P(None, "tensor", "dp"),
        P(None, "dp", "tensor"),
        P(None, "tensor", "dp"),
        P(),
        P(),
        P(),
    )
    return jax.shard_map(body, mesh=mesh, in_specs=in_specs, out_specs=out_specs, check_vma=False)
```

time: 844 us -> 880 us (1.043)
  blocking collectives: 38.3 us -> 0 us
  starting transfers between devices: 118 us -> 155 us
  waiting for transfers between devices: 364 us -> 329 us
  other arithmetic: 56.5 us -> 82.1 us
  local copies, waits for them, and re-layouts: 58.5 us -> 81.4 us
  Pallas kernels: 86.6 us -> 99.4 us
    psum x1 -> x0, blocking collectives: 38.3 us -> none  [body(): lax.psum(tuple((jnp.stack(members) for members in zip(*small_grads))), ('...]
    ppermute x96 -> x125, starting transfers between devices: 118 us -> 155 us  [pair_swap(): return lax.ppermute(values, axis, [(i, i ^ bit) for i in range(size)])]
    ppermute x96 -> x125, waiting for transfers between devices: 364 us -> 329 us  [pair_swap(): return lax.ppermute(values, axis, [(i, i ^ bit) for i in range(size)])]
    another operation x71 -> x96, other arithmetic: 12.1 us -> 31.7 us  [doubled_gather(): jnp.stack([jnp.where(upper, other, values), jnp.where(upper, values, othe...]
    pallas_call x4 -> x8, Pallas kernels: 86.6 us -> 99.4 us  [per_head(): pl.pallas_call(kernel, grid=(heads,), in_specs=[spec for spec, _ in ins],...]
    unnamed x263 -> x384, local copies, waits for them, and re-layouts: 30.5 us -> 41.6 us
    dot_general x12 -> x16, matrix products: 31.7 us -> 35 us  [dot_tn(): lax.dot_general(former, latter, (((0,), (0,)), ((), ())), preferred_eleme...]
    convert_element_type x39 -> x48, other arithmetic: 26.8 us -> 29.8 us  [lowered(): return values.astype(jnp.bfloat16)]
  transfers between devices with their start and end apart: 96 -> 125, of which waited for: 37 -> 51; matrix products, arithmetic and copies ran while one was open for 23% -> 26% of each run, Pallas kernels for 10% -> 11%
where the time goes in v3:
time: 880 us; the launch traced here: 869 us
  waiting for transfers between devices  329 us (37%)
  starting transfers between devices  155 us (18%)
  matrix products  111 us (13%)
  Pallas kernels  99.4 us (11%)
  other arithmetic  82.1 us (9%)
  local copies, waits for them, and re-layouts  81.4 us (9%)
  between operations  10.9 us (1%)
    ppermute x125, waiting for transfers between devices, pair_swap(): return lax.ppermute(values, axis, [(i, i ^ bit) for i in range(size)])  329 us
    ppermute x125, starting transfers between devices, pair_swap(): return lax.ppermute(values, axis, [(i, i ^ bit) for i in range(size)])  155 us
    pallas_call x8, Pallas kernels, per_head(): pl.pallas_call(kernel, grid=(heads,), in_specs=[spec for spec, _ in ins],...  99.4 us
    dot_general x20, matrix products, dot_nn(): return jnp.dot(former, latter, preferred_element_type=jnp.float32)  42.9 us
    unnamed x384, local copies, waits for them, and re-layouts  41.6 us
    dot_general x16, matrix products, dot_tn(): lax.dot_general(former, latter, (((0,), (0,)), ((), ())), preferred_eleme...  35 us
    dot_general x12, matrix products, dot_nt(): lax.dot_general(former, latter, (((1,), (1,)), ((), ())), preferred_eleme...  33 us
    another operation x96, other arithmetic, doubled_gather(): jnp.stack([jnp.where(upper, other, values), jnp.where(upper, values, othe...  31.7 us
  transfers between devices with their start and end apart: 125, of which 51 were waited for; matrix products, arithmetic and copies ran while one was open for 26% of the time, Pallas kernels for 11%

profile of v3, /device:TPU:0, one launch (start us, length us, event | category | flops | bytes accessed | tf_op | source)
XLA Modules:
  0.0 868.8 jit_solution(2817464561322493994)
XLA Ops:
  48.8 10.1 %collective-permute-done.9 = bf16[2,2,80,640]{3,2,1,0:T(8,128)(2,1)} collective-permute-done((bf16[2,2,80,640]{3,2,1,0:T(8,128)(2,1)}, bf16[2,2,80,640]{3,2,1,0:T(8,128)(2,1)}, u32[]{:S(2)}, u32[]{:S(2)}) %collective-permute-start.9) | collective-permute-done | bytes 409632 | tf_op jit(solution)/shard_map/ppermute | solution.py:62
  80.3 5.2 collective-permute-done.26
  88.5 5.0 collective-permute-done.21
  150.0 13.4 %attention_own.2 = (f32[640,1024]{1,0:T(8,128)S(1)}, f32[8,1,1024]{2,1,0:T(1,128)S(1)}, f32[8,1,1024]{2,1,0:T(1,128)S(1)}) custom-call(s32[1,1024]{1,0:T(1,128)S(1)} %bitcast.729, bf16[640,1024]{1,0:T(8,128)(2,1)S(1)} %multiply_convert_fusion.6.q_ref, bf16[640,1024]{1,0:T(8,128)(2,1)S(1)} %convolution_convert_fusion.15.k_ref, ...), custom_call_target="tpu_custom_call" | custom-call | flops 8053063680 | bytes 3936256 | tf_op jit(solution)/shard_map/attention_own/pallas_call | solution.py:358
  166.9 6.5 collective-permute-start.23
  205.5 7.6 collective-permute-done.51
  222.1 8.1 attention_far.2
  231.5 7.8 collective-permute-start.57
  239.7 5.5 collective-permute-done.57
  264.2 7.1 collective-permute-done.36
  281.1 8.9 %collective-permute-done.43 = bf16[1280,256]{1,0:T(8,128)(2,1)S(1)} collective-permute-done((bf16[1280,256]{1,0:T(8,128)(2,1)S(1)}, bf16[1280,256]{1,0:T(8,128)(2,1)S(1)}, u32[]{:S(2)}, u32[]{:S(2)}) %collective-permute-start.43) | collective-permute-done | bytes 655392 | tf_op jit(solution)/shard_map/ppermute | solution.py:62
  290.0 13.4 %attention_own.3 = (f32[640,1024]{1,0:T(8,128)S(1)}, f32[8,1,1024]{2,1,0:T(1,128)S(1)}, f32[8,1,1024]{2,1,0:T(1,128)S(1)}) custom-call(s32[1,1024]{1,0:T(1,128)S(1)} %bitcast.730, bf16[640,1024]{1,0:T(8,128)(2,1)S(1)} %multiply_convert_fusion.2.q_ref, bf16[640,1024]{1,0:T(8,128)(2,1)S(1)} %convolution_convert_fusion.13.k_ref, ...), custom_call_target="tpu_custom_call" | custom-call | flops 8053063680 | bytes 3936256 | tf_op jit(solution)/shard_map/attention_own/pallas_call | solution.py:358
  305.7 7.7 attention_far.3
  327.8 4.9 fusion.15
  332.7 5.4 fusion.11
  338.1 5.0 multiply_reduce_fusion
  345.7 5.5 fusion.4
  354.9 4.6 convolution_bitcast_fusion
  377.4 9.5 %attention_far_back.2 = (f32[640,1024]{1,0:T(8,128)S(1)}, f32[8,1,1024]{2,1,0:T(1,128)S(1)}, bf16[640,512]{1,0:T(8,128)(2,1)S(1)}, bf16[640,512]{1,0:T(8,128)(2,1)S(1)}) custom-call(s32[1]{0:T(128)} %bitcast.22.side_ref, bf16[640,1024]{1,0:T(8,128)(2,1)S(1)} %copy-done.25, bf16[640,512]{1,0:T(8,128)(2,1)S(1)} %convolution_convert_fusion.17.k_ref, ...), custom_call_target="tpu_custom_call" | custom-call | flops 12884901888 | bytes 5275652 | tf_op jit(solution)/shard_map/attention_far_back/pallas_call | solution.py:358
  388.6 19.0 %attention_own_back.2 = (bf16[640,1024]{1,0:T(8,128)(2,1)S(1)}, bf16[640,1024]{1,0:T(8,128)(2,1)S(1)}, bf16[640,1024]{1,0:T(8,128)(2,1)S(1)}, f32[640,1]{1,0:T(8,128)S(1)}) custom-call(s32[1,1024]{1,0:T(1,128)S(1)} %bitcast.731, f32[80,1]{1,0:T(8,128)S(1)} %copy.193.gain_ref, bf16[640,1024]{1,0:T(8,128)(2,1)S(1)} %copy-done.25, ...), custom_call_target="tpu_custom_call" | custom-call | flops 16106127360 | bytes 7934272 | tf_op jit(solution)/shard_map/attention_own_back/pallas_call | solution.py:358
  408.9 15.4 %collective-permute-start.61 = (bf16[640,512]{1,0:T(8,128)(2,1)}, bf16[640,512]{1,0:T(8,128)(2,1)}, u32[]{:S(2)}, u32[]{:S(2)}) collective-permute-start(bf16[640,512]{1,0:T(8,128)(2,1)} %copy-done.4), channel_id=1, source_target_pairs={{0,2},{2,0},{4,6},{6,4},{8,10},{10,8},{12,14},{14,12},{16,18},{18,... | collective-permute-start | bytes 1966088 | tf_op jit(solution)/shard_map/ppermute | solution.py:62
  438.5 14.9 %collective-permute-done.62 = bf16[640,512]{1,0:T(8,128)(2,1)} collective-permute-done((bf16[640,512]{1,0:T(8,128)(2,1)}, bf16[640,512]{1,0:T(8,128)(2,1)}, u32[]{:S(2)}, u32[]{:S(2)}) %collective-permute-start.62) | collective-permute-done | bytes 655392 | tf_op jit(solution)/shard_map/ppermute | solution.py:62
  467.3 17.6 %collective-permute-done.97 = bf16[2,2,80,640]{3,2,1,0:T(8,128)(2,1)S(1)} collective-permute-done((bf16[2,2,80,640]{3,2,1,0:T(8,128)(2,1)S(1)}, bf16[2,2,80,640]{3,2,1,0:T(8,128)(2,1)S(1)}, u32[]{:S(2)}, u32[]{:S(2)}) %collective-permute-start.97) | collective-permute-done | bytes 409632 | tf_op jit(solution)/shard_map/ppermute | solution.py:62
  497.4 13.9 %collective-permute-done.89 = bf16[2,2,80,640]{3,2,1,0:T(8,128)(2,1)S(1)} collective-permute-done((bf16[2,2,80,640]{3,2,1,0:T(8,128)(2,1)S(1)}, bf16[2,2,80,640]{3,2,1,0:T(8,128)(2,1)S(1)}, u32[]{:S(2)}, u32[]{:S(2)}) %collective-permute-start.89) | collective-permute-done | bytes 409632 | tf_op jit(solution)/shard_map/ppermute | solution.py:62
  543.1 9.4 %attention_far_back.3 = (f32[640,1024]{1,0:T(8,128)S(1)}, f32[8,1,1024]{2,1,0:T(1,128)S(1)}, bf16[640,512]{1,0:T(8,128)(2,1)S(1)}, bf16[640,512]{1,0:T(8,128)(2,1)S(1)}) custom-call(s32[1]{0:T(128)} %bitcast.22.side_ref, bf16[640,1024]{1,0:T(8,128)(2,1)S(1)} %copy-done.23, bf16[640,512]{1,0:T(8,128)(2,1)S(1)} %copy-done.13, bf16[640,512]{1,0:T(8,128)(2,1)S(1)} %copy-done.11, ...), custom_call_target="tpu_custom_call" | custom-call | flops 12884901888 | bytes 5275652 | tf_op jit(solution)/shard_map/attention_far_back/pallas_call | solution.py:358
  554.2 19.0 %attention_own_back.3 = (bf16[640,1024]{1,0:T(8,128)(2,1)S(1)}, bf16[640,1024]{1,0:T(8,128)(2,1)S(1)}, bf16[640,1024]{1,0:T(8,128)(2,1)S(1)}, f32[640,1]{1,0:T(8,128)S(1)}) custom-call(s32[1,1024]{1,0:T(1,128)S(1)} %bitcast.732, f32[80,1]{1,0:T(8,128)S(1)} %copy.198.gain_ref, bf16[640,1024]{1,0:T(8,128)(2,1)S(1)} %copy-done.23, ...), custom_call_target="tpu_custom_call" | custom-call | flops 16106127360 | bytes 7934272 | tf_op jit(solution)/shard_map/attention_own_back/pallas_call | solution.py:358
  574.6 8.5 collective-permute-start.65
  600.3 12.5 %collective-permute-done.66 = bf16[640,512]{1,0:T(8,128)(2,1)S(1)} collective-permute-done((bf16[640,512]{1,0:T(8,128)(2,1)}, bf16[640,512]{1,0:T(8,128)(2,1)S(1)}, u32[]{:S(2)}, u32[]{:S(2)}) %collective-permute-start.66) | collective-permute-done | bytes 655392 | tf_op jit(solution)/shard_map/ppermute | solution.py:62
  631.6 16.3 %collective-permute-done.72 = bf16[2,2,2,80,640]{4,3,0,1,2:T(8,128)(2,1)S(1)} collective-permute-done((bf16[2,2,2,80,640]{4,3,0,1,2:T(8,128)(2,1)S(1)}, bf16[2,2,2,80,640]{4,3,0,1,2:T(8,128)(2,1)S(1)}, u32[]{:S(2)}, u32[]{:S(2)}) %collective-permute-start.72) | collective-permute-done | bytes 819232 | tf_op jit(solution)/shard_map/ppermute | solution.py:62
  649.1 16.4 %collective-permute-done.111 = bf16[2,2,2,80,640]{4,3,0,1,2:T(8,128)(2,1)S(1)} collective-permute-done((bf16[2,2,2,80,640]{4,3,0,1,2:T(8,128)(2,1)S(1)}, bf16[2,2,2,80,640]{4,3,0,1,2:T(8,128)(2,1)S(1)}, u32[]{:S(2)}, u32[]{:S(2)}) %collective-permute-start.111) | collective-permute-done | bytes 819232 | tf_op jit(solution)/shard_map/ppermute | solution.py:62
  666.8 15.9 %collective-permute-done.116 = bf16[2,2,2,80,640]{4,3,0,1,2:T(8,128)(2,1)S(1)} collective-permute-done((bf16[2,2,2,80,640]{4,3,0,1,2:T(8,128)(2,1)S(1)}, bf16[2,2,2,80,640]{4,3,0,1,2:T(8,128)(2,1)S(1)}, u32[]{:S(2)}, u32[]{:S(2)}) %collective-permute-start.116) | collective-permute-done | bytes 819232 | tf_op jit(solution)/shard_map/ppermute | solution.py:62
  685.6 18.5 %collective-permute-done.93 = bf16[2,2,80,640]{3,2,1,0:T(8,128)(2,1)S(1)} collective-permute-done((bf16[2,2,80,640]{3,2,1,0:T(8,128)(2,1)S(1)}, bf16[2,2,80,640]{3,2,1,0:T(8,128)(2,1)S(1)}, u32[]{:S(2)}, u32[]{:S(2)}) %collective-permute-start.93) | collective-permute-done | bytes 409632 | tf_op jit(solution)/shard_map/ppermute | solution.py:62
  705.4 7.2 collective-permute-done.69
  712.7 7.4 collective-permute-done.73
  726.2 6.3 collective-permute-done.70
  732.9 5.4 collective-permute-done.74
  743.4 6.4 collective-permute-done.95
  749.9 6.3 collective-permute-done.71
  756.2 10.9 %collective-permute-done.75 = bf16[80,640]{1,0:T(8,128)(2,1)S(1)} collective-permute-done((bf16[80,640]{1,0:T(8,128)(2,1)S(1)}, bf16[80,640]{1,0:T(8,128)(2,1)S(1)}, u32[]{:S(2)}, u32[]{:S(2)}) %collective-permute-start.75) | collective-permute-done | bytes 102432 | tf_op jit(solution)/shard_map/ppermute | solution.py:62
  775.2 10.0 %collective-permute-done.113 = bf16[2,80,640]{2,1,0:T(8,128)(2,1)S(1)} collective-permute-done((bf16[2,80,640]{2,1,0:T(8,128)(2,1)S(1)}, bf16[2,80,640]{2,1,0:T(8,128)(2,1)S(1)}, u32[]{:S(2)}, u32[]{:S(2)}) %collective-permute-start.113) | collective-permute-done | bytes 204832 | tf_op jit(solution)/shard_map/ppermute | solution.py:62
  785.3 6.6 collective-permute-done.118
  792.3 5.6 collective-permute-done.103
  798.5 5.4 collective-permute-done.108
  805.3 7.2 collective-permute-done.114
  812.5 6.1 collective-permute-done.119
  818.7 5.6 collective-permute-done.104
  825.1 4.9 collective-permute-done.109
  861.8 4.7 collective-permute-done.79
  (948 shorter events, 413.5 us)
Async XLA Ops:
  16.6 77.5 %collective-permute-start.11 = (bf16[1280,512]{1,0:T(8,128)(2,1)}, bf16[1280,512]{1,0:T(8,128)(2,1)}, u32[]{:S(2)}, u32[]{:S(2)}) collective-permute-start(bf16[1280,512]{1,0:T(8,128)(2,1)} %multiply_convert_fusion.7), channel_id=1, source_target_pairs={{0,1},{1,0},{2,3},{3,2},{4,5},{5,4},{6,7},{7,6},{8,9},{9,8},{10,11... | collective-permute-start | bytes 3932168 | tf_op jit(solution)/shard_map/ppermute | solution.py:62
  70.6 49.5 %collective-permute-start.18 = (bf16[2,2,2,80,640]{4,3,0,1,2:T(8,128)(2,1)}, bf16[2,2,2,80,640]{4,3,0,1,2:T(8,128)(2,1)}, u32[]{:S(2)}, u32[]{:S(2)}) collective-permute-start(bf16[2,2,2,80,640]{4,3,0,1,2:T(8,128)(2,1)} %pad_maximum_fusion.45), channel_id=1, source_target_pairs={{0,4},{2,6},{4,0},{6,2},{8,12},{10,14},{12,8},{14,10},{16,20},{18,... | collective-permute-start | bytes 2457608 | tf_op jit(solution)/shard_map/ppermute | solution.py:62
  75.5 50.9 %collective-permute-start.12 = (bf16[2,2,2,80,640]{4,3,0,1,2:T(8,128)(2,1)}, bf16[2,2,2,80,640]{4,3,0,1,2:T(8,128)(2,1)}, u32[]{:S(2)}, u32[]{:S(2)}) collective-permute-start(bf16[2,2,2,80,640]{4,3,0,1,2:T(8,128)(2,1)} %pad_maximum_fusion.44), channel_id=1, source_target_pairs={{0,2},{2,0},{4,6},{6,4},{8,10},{10,8},{12,14},{14,12},{16,18},{18,... | collective-permute-start | bytes 2457608 | tf_op jit(solution)/shard_map/ppermute | solution.py:62
  102.4 31.7 %collective-permute-start.10 = (bf16[2,2,2,80,640]{4,3,2,1,0:T(8,128)(2,1)}, bf16[2,2,2,80,640]{4,3,2,1,0:T(8,128)(2,1)}, u32[]{:S(2)}, u32[]{:S(2)}) collective-permute-start(bf16[2,2,2,80,640]{4,3,2,1,0:T(8,128)(2,1)} %pad_maximum_fusion.43), channel_id=1, source_target_pairs={{0,8},{2,10},{4,12},{6,14},{8,0},{10,2},{12,4},{14,6},{16,24},{18,... | collective-permute-start | bytes 2457608 | tf_op jit(solution)/shard_map/ppermute | solution.py:62
  106.2 60.7 %collective-permute-start.13 = (bf16[1280,256]{1,0:T(8,128)(2,1)}, bf16[1280,256]{1,0:T(8,128)(2,1)}, u32[]{:S(2)}, u32[]{:S(2)}) collective-permute-start(bf16[1280,256]{1,0:T(8,128)(2,1)} %fusion.47), channel_id=1, source_target_pairs={{0,2},{2,0},{4,6},{6,4},{8,10},{10,8},{12,14},{14,12},{16,18},{18,... | collective-permute-start | bytes 1966088 | tf_op jit(solution)/shard_map/ppermute | solution.py:62
  126.4 59.1 %collective-permute-start.28 = (bf16[2,2,2,80,640]{4,3,0,1,2:T(8,128)(2,1)}, bf16[2,2,2,80,640]{4,3,0,1,2:T(8,128)(2,1)}, u32[]{:S(2)}, u32[]{:S(2)}) collective-permute-start(bf16[2,2,2,80,640]{4,3,0,1,2:T(8,128)(2,1)} %pad_maximum_fusion.47), channel_id=1, source_target_pairs={{0,4},{2,6},{4,0},{6,2},{8,12},{10,14},{12,8},{14,10},{16,20},{18,... | collective-permute-start | bytes 2457608 | tf_op jit(solution)/shard_map/ppermute | solution.py:62
  148.0 28.9 %collective-permute-start.32 = (bf16[2,2,80,640]{3,2,0,1:T(8,128)(2,1)}, bf16[2,2,80,640]{3,2,0,1:T(8,128)(2,1)}, u32[]{:S(2)}, u32[]{:S(2)}) collective-permute-start(bf16[2,2,80,640]{3,2,0,1:T(8,128)(2,1)} %pad_maximum_fusion.60), channel_id=1, source_target_pairs={{0,4},{2,6},{4,0},{6,2},{8,12},{10,14},{12,8},{14,10},{16,20},{18,... | collective-permute-start | bytes 1228808 | tf_op jit(solution)/shard_map/ppermute | solution.py:62
  148.3 25.1 %collective-permute-start.39 = (bf16[2,2,80,640]{3,2,1,0:T(8,128)(2,1)S(1)}, bf16[2,2,80,640]{3,2,1,0:T(8,128)(2,1)S(1)}, u32[]{:S(2)}, u32[]{:S(2)}) collective-permute-start(bf16[2,2,80,640]{3,2,1,0:T(8,128)(2,1)S(1)} %pad_maximum_fusion.62), channel_id=1, source_target_pairs={{0,16},{2,18},{4,20},{6,22},{8,24},{10,26},{12,28},{14,30},{16,0},... | collective-permute-start | bytes 1228808 | tf_op jit(solution)/shard_map/ppermute | solution.py:62
  165.0 29.8 %collective-permute-start.6 = (bf16[2,2,2,80,640]{4,3,2,1,0:T(8,128)(2,1)}, bf16[2,2,2,80,640]{4,3,2,1,0:T(8,128)(2,1)}, u32[]{:S(2)}, u32[]{:S(2)}) collective-permute-start(bf16[2,2,2,80,640]{4,3,2,1,0:T(8,128)(2,1)} %pad_maximum_fusion.42), channel_id=1, source_target_pairs={{0,2},{2,0},{4,6},{6,4},{8,10},{10,8},{12,14},{14,12},{16,18},{18,... | collective-permute-start | bytes 2457608 | tf_op jit(solution)/shard_map/ppermute | solution.py:62
  166.9 23.0 %collective-permute-start.23 = (bf16[2,2,2,80,640]{4,3,2,1,0:T(8,128)(2,1)}, bf16[2,2,2,80,640]{4,3,2,1,0:T(8,128)(2,1)}, u32[]{:S(2)}, u32[]{:S(2)}) collective-permute-start(bf16[2,2,2,80,640]{4,3,2,1,0:T(8,128)(2,1)} %pad_maximum_fusion.46), channel_id=1, source_target_pairs={{0,8},{2,10},{4,12},{6,14},{8,0},{10,2},{12,4},{14,6},{16,24},{18,... | collective-permute-start | bytes 2457608 | tf_op jit(solution)/shard_map/ppermute | solution.py:62
  173.4 41.3 %collective-permute-start.14 = (bf16[1280,256]{1,0:T(8,128)(2,1)}, bf16[1280,256]{1,0:T(8,128)(2,1)}, u32[]{:S(2)}, u32[]{:S(2)}) collective-permute-start(bf16[1280,256]{1,0:T(8,128)(2,1)} %collective-permute-done.13), channel_id=1, source_target_pairs={{0,1},{1,0},{2,3},{3,2},{4,5},{5,4},{6,7},{7,6},{8,9},{9,8},{10,11... | collective-permute-start | bytes 1966088 | tf_op jit(solution)/shard_map/ppermute | solution.py:62
  189.9 55.9 %collective-permute-start.48 = (bf16[2,2,2,80,640]{4,3,1,0,2:T(8,128)(2,1)S(1)}, bf16[2,2,2,80,640]{4,3,1,0,2:T(8,128)(2,1)S(1)}, u32[]{:S(2)}, u32[]{:S(2)}) collective-permute-start(bf16[2,2,2,80,640]{4,3,1,0,2:T(8,128)(2,1)S(1)} %pad_maximum_fusion.51), channel_id=1, source_target_pairs={{0,4},{2,6},{4,0},{6,2},{8,12},{10,14},{12,8},{14,10},{16,20},{18,... | collective-permute-start | bytes 2457608 | tf_op jit(solution)/shard_map/ppermute | solution.py:62
  192.9 66.3 %collective-permute-start.42 = (bf16[2,2,2,80,640]{4,3,0,1,2:T(8,128)(2,1)S(1)}, bf16[2,2,2,80,640]{4,3,0,1,2:T(8,128)(2,1)S(1)}, u32[]{:S(2)}, u32[]{:S(2)}) collective-permute-start(bf16[2,2,2,80,640]{4,3,0,1,2:T(8,128)(2,1)S(1)} %pad_maximum_fusion.50), channel_id=1, source_target_pairs={{0,2},{2,0},{4,6},{6,4},{8,10},{10,8},{12,14},{14,12},{16,18},{18,... | collective-permute-start | bytes 2457608 | tf_op jit(solution)/shard_map/ppermute | solution.py:62
  205.3 44.9 %collective-permute-start.29 = (bf16[1280,640]{1,0:T(8,128)(2,1)S(1)}, bf16[1280,640]{1,0:T(8,128)(2,1)S(1)}, u32[]{:S(2)}, u32[]{:S(2)}) collective-permute-start(bf16[1280,640]{1,0:T(8,128)(2,1)S(1)} %bitcast.770), channel_id=1, source_target_pairs={{0,1},{1,0},{2,3},{3,2},{4,5},{5,4},{6,7},{7,6},{8,9},{9,8},{10,11... | collective-permute-start | bytes 4915208 | tf_op jit(solution)/shard_map/ppermute | solution.py:62
  214.7 24.6 %collective-permute-start.52 = (bf16[2,2,80,640]{3,2,1,0:T(8,128)(2,1)S(1)}, bf16[2,2,80,640]{3,2,1,0:T(8,128)(2,1)S(1)}, u32[]{:S(2)}, u32[]{:S(2)}) collective-permute-start(bf16[2,2,80,640]{3,2,1,0:T(8,128)(2,1)S(1)} %pad_maximum_fusion.64), channel_id=1, source_target_pairs={{0,16},{2,18},{4,20},{6,22},{8,24},{10,26},{12,28},{14,30},{16,0},... | collective-permute-start | bytes 1228808 | tf_op jit(solution)/shard_map/ppermute | solution.py:62
  246.6 69.5 %collective-permute-start.58 = (bf16[2,2,2,80,640]{4,3,1,0,2:T(8,128)(2,1)S(1)}, bf16[2,2,2,80,640]{4,3,1,0,2:T(8,128)(2,1)S(1)}, u32[]{:S(2)}, u32[]{:S(2)}) collective-permute-start(bf16[2,2,2,80,640]{4,3,1,0,2:T(8,128)(2,1)S(1)} %pad_maximum_fusion.53), channel_id=1, source_target_pairs={{0,4},{2,6},{4,0},{6,2},{8,12},{10,14},{12,8},{14,10},{16,20},{18,... | collective-permute-start | bytes 2457608 | tf_op jit(solution)/shard_map/ppermute | solution.py:62
  254.3 63.5 %collective-permute-start.53 = (bf16[2,2,2,80,640]{4,3,2,1,0:T(8,128)(2,1)S(1)}, bf16[2,2,2,80,640]{4,3,2,1,0:T(8,128)(2,1)S(1)}, u32[]{:S(2)}, u32[]{:S(2)}) collective-permute-start(bf16[2,2,2,80,640]{4,3,2,1,0:T(8,128)(2,1)S(1)} %pad_maximum_fusion.52), channel_id=1, source_target_pairs={{0,8},{2,10},{4,12},{6,14},{8,0},{10,2},{12,4},{14,6},{16,24},{18,... | collective-permute-start | bytes 2457608 | tf_op jit(solution)/shard_map/ppermute | solution.py:62
  363.1 69.4 %collective-permute-start.115 = (bf16[1280,640]{1,0:T(8,128)(2,1)}, bf16[1280,640]{1,0:T(8,128)(2,1)}, u32[]{:S(2)}, u32[]{:S(2)}) collective-permute-start(bf16[1280,640]{1,0:T(8,128)(2,1)} %slice.169), channel_id=1, source_target_pairs={{0,1},{1,0},{2,3},{3,2},{4,5},{5,4},{6,7},{7,6},{8,9},{9,8},{10,11... | collective-permute-start | bytes 4915208 | tf_op jit(solution)/shard_map/ppermute | solution.py:62
  367.0 68.5 %collective-permute-start.105 = (bf16[1280,640]{1,0:T(8,128)(2,1)}, bf16[1280,640]{1,0:T(8,128)(2,1)}, u32[]{:S(2)}, u32[]{:S(2)}) collective-permute-start(bf16[1280,640]{1,0:T(8,128)(2,1)} %slice.171), channel_id=1, source_target_pairs={{0,1},{1,0},{2,3},{3,2},{4,5},{5,4},{6,7},{7,6},{8,9},{9,8},{10,11... | collective-permute-start | bytes 4915208 | tf_op jit(solution)/shard_map/ppermute | solution.py:62
  375.7 85.9 %collective-permute-start.96 = (bf16[2,2,2,80,640]{4,3,2,1,0:T(8,128)(2,1)}, bf16[2,2,2,80,640]{4,3,2,1,0:T(8,128)(2,1)}, u32[]{:S(2)}, u32[]{:S(2)}) collective-permute-start(bf16[2,2,2,80,640]{4,3,2,1,0:T(8,128)(2,1)} %dynamic-slice_bitcast_fusion), channel_id=1, source_target_pairs={{0,8},{2,10},{4,12},{6,14},{8,0},{10,2},{12,4},{14,6},{16,24},{18,... | collective-permute-start | bytes 2457608 | tf_op jit(solution)/shard_map/ppermute | solution.py:62
  408.9 49.8 %collective-permute-start.61 = (bf16[640,512]{1,0:T(8,128)(2,1)}, bf16[640,512]{1,0:T(8,128)(2,1)}, u32[]{:S(2)}, u32[]{:S(2)}) collective-permute-start(bf16[640,512]{1,0:T(8,128)(2,1)} %copy-done.4), channel_id=1, source_target_pairs={{0,2},{2,0},{4,6},{6,4},{8,10},{10,8},{12,14},{14,12},{16,18},{18,... | collective-permute-start | bytes 1966088 | tf_op jit(solution)/shard_map/ppermute | solution.py:62
  424.3 29.2 %collective-permute-start.62 = (bf16[640,512]{1,0:T(8,128)(2,1)}, bf16[640,512]{1,0:T(8,128)(2,1)}, u32[]{:S(2)}, u32[]{:S(2)}) collective-permute-start(bf16[640,512]{1,0:T(8,128)(2,1)} %copy-done.5), channel_id=1, source_target_pairs={{0,2},{2,0},{4,6},{6,4},{8,10},{10,8},{12,14},{14,12},{16,18},{18,... | collective-permute-start | bytes 1966088 | tf_op jit(solution)/shard_map/ppermute | solution.py:62
  457.1 35.2 %collective-permute-start.88 = (bf16[2,2,2,80,640]{4,3,2,1,0:T(8,128)(2,1)S(1)}, bf16[2,2,2,80,640]{4,3,2,1,0:T(8,128)(2,1)S(1)}, u32[]{:S(2)}, u32[]{:S(2)}) collective-permute-start(bf16[2,2,2,80,640]{4,3,2,1,0:T(8,128)(2,1)S(1)} %dynamic-slice_bitcast_fusion.2), channel_id=1, source_target_pairs={{0,8},{2,10},{4,12},{6,14},{8,0},{10,2},{12,4},{14,6},{16,24},{18,... | collective-permute-start | bytes 2457608 | tf_op jit(solution)/shard_map/ppermute | solution.py:62
  463.2 21.7 %collective-permute-start.97 = (bf16[2,2,80,640]{3,2,1,0:T(8,128)(2,1)S(1)}, bf16[2,2,80,640]{3,2,1,0:T(8,128)(2,1)S(1)}, u32[]{:S(2)}, u32[]{:S(2)}) collective-permute-start(bf16[2,2,80,640]{3,2,1,0:T(8,128)(2,1)S(1)} %dynamic-slice_bitcast_fusion.8), channel_id=1, source_target_pairs={{0,16},{2,18},{4,20},{6,22},{8,24},{10,26},{12,28},{14,30},{16,0},... | collective-permute-start | bytes 1228808 | tf_op jit(solution)/shard_map/ppermute | solution.py:62
  486.9 25.6 %collective-permute-start.63 = (bf16[1280,512]{1,0:T(8,128)(2,1)S(1)}, bf16[1280,512]{1,0:T(8,128)(2,1)S(1)}, u32[]{:S(2)}, u32[]{:S(2)}) collective-permute-start(bf16[1280,512]{1,0:T(8,128)(2,1)S(1)} %fusion.5), channel_id=1, source_target_pairs={{0,1},{1,0},{2,3},{3,2},{4,5},{5,4},{6,7},{7,6},{8,9},{9,8},{10,11... | collective-permute-start | bytes 3932168 | tf_op jit(solution)/shard_map/ppermute | solution.py:62
  532.2 60.0 %collective-permute-start.110 = (bf16[1280,640]{1,0:T(8,128)(2,1)}, bf16[1280,640]{1,0:T(8,128)(2,1)}, u32[]{:S(2)}, u32[]{:S(2)}) collective-permute-start(bf16[1280,640]{1,0:T(8,128)(2,1)} %slice.170), channel_id=1, source_target_pairs={{0,1},{1,0},{2,3},{3,2},{4,5},{5,4},{6,7},{7,6},{8,9},{9,8},{10,11... | collective-permute-start | bytes 4915208 | tf_op jit(solution)/shard_map/ppermute | solution.py:62
  534.4 62.3 %collective-permute-start.100 = (bf16[1280,640]{1,0:T(8,128)(2,1)}, bf16[1280,640]{1,0:T(8,128)(2,1)}, u32[]{:S(2)}, u32[]{:S(2)}) collective-permute-start(bf16[1280,640]{1,0:T(8,128)(2,1)} %slice.172), channel_id=1, source_target_pairs={{0,1},{1,0},{2,3},{3,2},{4,5},{5,4},{6,7},{7,6},{8,9},{9,8},{10,11... | collective-permute-start | bytes 4915208 | tf_op jit(solution)/shard_map/ppermute | solution.py:62
  541.9 84.4 %collective-permute-start.92 = (bf16[2,2,2,80,640]{4,3,2,1,0:T(8,128)(2,1)}, bf16[2,2,2,80,640]{4,3,2,1,0:T(8,128)(2,1)}, u32[]{:S(2)}, u32[]{:S(2)}) collective-permute-start(bf16[2,2,2,80,640]{4,3,2,1,0:T(8,128)(2,1)} %dynamic-slice_bitcast_fusion.1), channel_id=1, source_target_pairs={{0,8},{2,10},{4,12},{6,14},{8,0},{10,2},{12,4},{14,6},{16,24},{18,... | collective-permute-start | bytes 2457608 | tf_op jit(solution)/shard_map/ppermute | solution.py:62
  574.6 44.2 %collective-permute-start.65 = (bf16[640,512]{1,0:T(8,128)(2,1)}, bf16[640,512]{1,0:T(8,128)(2,1)S(1)}, u32[]{:S(2)}, u32[]{:S(2)}) collective-permute-start(bf16[640,512]{1,0:T(8,128)(2,1)} %copy-done.2), channel_id=1, source_target_pairs={{0,2},{2,0},{4,6},{6,4},{8,10},{10,8},{12,14},{14,12},{16,18},{18,... | collective-permute-start | bytes 1966088 | tf_op jit(solution)/shard_map/ppermute | solution.py:62
  583.1 29.8 %collective-permute-start.66 = (bf16[640,512]{1,0:T(8,128)(2,1)}, bf16[640,512]{1,0:T(8,128)(2,1)S(1)}, u32[]{:S(2)}, u32[]{:S(2)}) collective-permute-start(bf16[640,512]{1,0:T(8,128)(2,1)} %copy-done.3), channel_id=1, source_target_pairs={{0,2},{2,0},{4,6},{6,4},{8,10},{10,8},{12,14},{14,12},{16,18},{18,... | collective-permute-start | bytes 1966088 | tf_op jit(solution)/shard_map/ppermute | solution.py:62
  592.2 38.2 %collective-permute-start.68 = (bf16[2,2,2,80,640]{4,3,0,1,2:T(8,128)(2,1)S(1)}, bf16[2,2,2,80,640]{4,3,0,1,2:T(8,128)(2,1)S(1)}, u32[]{:S(2)}, u32[]{:S(2)}) collective-permute-start(bf16[2,2,2,80,640]{4,3,0,1,2:T(8,128)(2,1)S(1)} %bitcast.797), channel_id=1, source_target_pairs={{0,2},{2,0},{4,6},{6,4},{8,10},{10,8},{12,14},{14,12},{16,18},{18,... | collective-permute-start | bytes 2457608 | tf_op jit(solution)/shard_map/ppermute | solution.py:62
  596.7 51.3 %collective-permute-start.72 = (bf16[2,2,2,80,640]{4,3,0,1,2:T(8,128)(2,1)S(1)}, bf16[2,2,2,80,640]{4,3,0,1,2:T(8,128)(2,1)S(1)}, u32[]{:S(2)}, u32[]{:S(2)}) collective-permute-start(bf16[2,2,2,80,640]{4,3,0,1,2:T(8,128)(2,1)S(1)} %bitcast.794), channel_id=1, source_target_pairs={{0,2},{2,0},{4,6},{6,4},{8,10},{10,8},{12,14},{14,12},{16,18},{18,... | collective-permute-start | bytes 2457608 | tf_op jit(solution)/shard_map/ppermute | solution.py:62
  612.8 52.7 %collective-permute-start.111 = (bf16[2,2,2,80,640]{4,3,0,1,2:T(8,128)(2,1)S(1)}, bf16[2,2,2,80,640]{4,3,0,1,2:T(8,128)(2,1)S(1)}, u32[]{:S(2)}, u32[]{:S(2)}) collective-permute-start(bf16[2,2,2,80,640]{4,3,0,1,2:T(8,128)(2,1)S(1)} %bitcast.798), channel_id=1, source_target_pairs={{0,2},{2,0},{4,6},{6,4},{8,10},{10,8},{12,14},{14,12},{16,18},{18,... | collective-permute-start | bytes 2457608 | tf_op jit(solution)/shard_map/ppermute | solution.py:62
  618.9 63.8 %collective-permute-start.116 = (bf16[2,2,2,80,640]{4,3,0,1,2:T(8,128)(2,1)S(1)}, bf16[2,2,2,80,640]{4,3,0,1,2:T(8,128)(2,1)S(1)}, u32[]{:S(2)}, u32[]{:S(2)}) collective-permute-start(bf16[2,2,2,80,640]{4,3,0,1,2:T(8,128)(2,1)S(1)} %bitcast.795), channel_id=1, source_target_pairs={{0,2},{2,0},{4,6},{6,4},{8,10},{10,8},{12,14},{14,12},{16,18},{18,... | collective-permute-start | bytes 2457608 | tf_op jit(solution)/shard_map/ppermute | solution.py:62
  626.3 57.6 %collective-permute-start.101 = (bf16[2,2,2,80,640]{4,3,0,1,2:T(8,128)(2,1)S(1)}, bf16[2,2,2,80,640]{4,3,0,1,2:T(8,128)(2,1)S(1)}, u32[]{:S(2)}, u32[]{:S(2)}) collective-permute-start(bf16[2,2,2,80,640]{4,3,0,1,2:T(8,128)(2,1)S(1)} %bitcast.796), channel_id=1, source_target_pairs={{0,4},{2,6},{4,0},{6,2},{8,12},{10,14},{12,8},{14,10},{16,20},{18,... | collective-permute-start | bytes 2457608 | tf_op jit(solution)/shard_map/ppermute | solution.py:62
  630.4 53.9 %collective-permute-start.106 = (bf16[2,2,2,80,640]{4,3,0,1,2:T(8,128)(2,1)S(1)}, bf16[2,2,2,80,640]{4,3,0,1,2:T(8,128)(2,1)S(1)}, u32[]{:S(2)}, u32[]{:S(2)}) collective-permute-start(bf16[2,2,2,80,640]{4,3,0,1,2:T(8,128)(2,1)S(1)} %bitcast.793), channel_id=1, source_target_pairs={{0,4},{2,6},{4,0},{6,2},{8,12},{10,14},{12,8},{14,10},{16,20},{18,... | collective-permute-start | bytes 2457608 | tf_op jit(solution)/shard_map/ppermute | solution.py:62
  647.9 91.4 %collective-permute-start.84 = (bf16[2,2,2,80,640]{4,3,2,1,0:T(8,128)(2,1)S(1)}, bf16[2,2,2,80,640]{4,3,2,1,0:T(8,128)(2,1)S(1)}, u32[]{:S(2)}, u32[]{:S(2)}) collective-permute-start(bf16[2,2,2,80,640]{4,3,2,1,0:T(8,128)(2,1)S(1)} %dynamic-slice_bitcast_fusion.3), channel_id=1, source_target_pairs={{0,8},{2,10},{4,12},{6,14},{8,0},{10,2},{12,4},{14,6},{16,24},{18,... | collective-permute-start | bytes 2457608 | tf_op jit(solution)/shard_map/ppermute | solution.py:62
  665.5 75.2 %collective-permute-start.76 = (bf16[2,2,2,80,640]{4,3,0,1,2:T(8,128)(2,1)S(1)}, bf16[2,2,2,80,640]{4,3,0,1,2:T(8,128)(2,1)S(1)}, u32[]{:S(2)}, u32[]{:S(2)}) collective-permute-start(bf16[2,2,2,80,640]{4,3,0,1,2:T(8,128)(2,1)S(1)} %bitcast.792), channel_id=1, source_target_pairs={{0,4},{2,6},{4,0},{6,2},{8,12},{10,14},{12,8},{14,10},{16,20},{18,... | collective-permute-start | bytes 2457608 | tf_op jit(solution)/shard_map/ppermute | solution.py:62
  682.7 60.1 %collective-permute-start.80 = (bf16[2,2,2,80,640]{4,3,0,1,2:T(8,128)(2,1)S(1)}, bf16[2,2,2,80,640]{4,3,0,1,2:T(8,128)(2,1)S(1)}, u32[]{:S(2)}, u32[]{:S(2)}) collective-permute-start(bf16[2,2,2,80,640]{4,3,0,1,2:T(8,128)(2,1)S(1)} %bitcast.791), channel_id=1, source_target_pairs={{0,4},{2,6},{4,0},{6,2},{8,12},{10,14},{12,8},{14,10},{16,20},{18,... | collective-permute-start | bytes 2457608 | tf_op jit(solution)/shard_map/ppermute | solution.py:62
  684.3 28.3 %collective-permute-start.69 = (bf16[2,2,80,640]{3,2,0,1:T(8,128)(2,1)S(1)}, bf16[2,2,80,640]{3,2,0,1:T(8,128)(2,1)S(1)}, u32[]{:S(2)}, u32[]{:S(2)}) collective-permute-start(bf16[2,2,80,640]{3,2,0,1:T(8,128)(2,1)S(1)} %dynamic-slice_bitcast_fusion.15), channel_id=1, source_target_pairs={{0,4},{2,6},{4,0},{6,2},{8,12},{10,14},{12,8},{14,10},{16,20},{18,... | collective-permute-start | bytes 1228808 | tf_op jit(solution)/shard_map/ppermute | solution.py:62
  712.6 120.1 %collective-permute-start.67 = (bf16[1280,512]{1,0:T(8,128)(2,1)S(1)}, bf16[1280,512]{1,0:T(8,128)(2,1)S(1)}, u32[]{:S(2)}, u32[]{:S(2)}) collective-permute-start(bf16[1280,512]{1,0:T(8,128)(2,1)S(1)} %fusion.6), channel_id=1, source_target_pairs={{0,1},{1,0},{2,3},{3,2},{4,5},{5,4},{6,7},{7,6},{8,9},{9,8},{10,11... | collective-permute-start | bytes 3932168 | tf_op jit(solution)/shard_map/ppermute | solution.py:62
  738.3 32.1 %collective-permute-start.112 = (bf16[2,2,80,640]{3,2,0,1:T(8,128)(2,1)S(1)}, bf16[2,2,80,640]{3,2,0,1:T(8,128)(2,1)S(1)}, u32[]{:S(2)}, u32[]{:S(2)}) collective-permute-start(bf16[2,2,80,640]{3,2,0,1:T(8,128)(2,1)S(1)} %dynamic-slice_bitcast_fusion.5), channel_id=1, source_target_pairs={{0,4},{2,6},{4,0},{6,2},{8,12},{10,14},{12,8},{14,10},{16,20},{18,... | collective-permute-start | bytes 1228808 | tf_op jit(solution)/shard_map/ppermute | solution.py:62
  739.3 31.2 %collective-permute-start.117 = (bf16[2,2,80,640]{3,2,0,1:T(8,128)(2,1)S(1)}, bf16[2,2,80,640]{3,2,0,1:T(8,128)(2,1)S(1)}, u32[]{:S(2)}, u32[]{:S(2)}) collective-permute-start(bf16[2,2,80,640]{3,2,0,1:T(8,128)(2,1)S(1)} %dynamic-slice_bitcast_fusion.4), channel_id=1, source_target_pairs={{0,4},{2,6},{4,0},{6,2},{8,12},{10,14},{12,8},{14,10},{16,20},{18,... | collective-permute-start | bytes 1228808 | tf_op jit(solution)/shard_map/ppermute | solution.py:62
  740.7 30.4 %collective-permute-start.102 = (bf16[2,2,80,640]{3,2,0,1:T(8,128)(2,1)S(1)}, bf16[2,2,80,640]{3,2,0,1:T(8,128)(2,1)S(1)}, u32[]{:S(2)}, u32[]{:S(2)}) collective-permute-start(bf16[2,2,80,640]{3,2,0,1:T(8,128)(2,1)S(1)} %dynamic-slice_bitcast_fusion.7), channel_id=1, source_target_pairs={{0,2},{2,0},{4,6},{6,4},{8,10},{10,8},{12,14},{14,12},{16,18},{18,... | collective-permute-start | bytes 1228808 | tf_op jit(solution)/shard_map/ppermute | solution.py:62
  770.4 60.4 %collective-permute-start.85 = (bf16[2,2,80,640]{3,2,1,0:T(8,128)(2,1)S(1)}, bf16[2,2,80,640]{3,2,1,0:T(8,128)(2,1)S(1)}, u32[]{:S(2)}, u32[]{:S(2)}) collective-permute-start(bf16[2,2,80,640]{3,2,1,0:T(8,128)(2,1)S(1)} %dynamic-slice_bitcast_fusion.11), channel_id=1, source_target_pairs={{0,16},{2,18},{4,20},{6,22},{8,24},{10,26},{12,28},{14,30},{16,0},... | collective-permute-start | bytes 1228808 | tf_op jit(solution)/shard_map/ppermute | solution.py:62
  770.5 62.1 %collective-permute-start.77 = (bf16[2,2,80,640]{3,2,0,1:T(8,128)(2,1)S(1)}, bf16[2,2,80,640]{3,2,0,1:T(8,128)(2,1)S(1)}, u32[]{:S(2)}, u32[]{:S(2)}) collective-permute-start(bf16[2,2,80,640]{3,2,0,1:T(8,128)(2,1)S(1)} %dynamic-slice_bitcast_fusion.13), channel_id=1, source_target_pairs={{0,2},{2,0},{4,6},{6,4},{8,10},{10,8},{12,14},{14,12},{16,18},{18,... | collective-permute-start | bytes 1228808 | tf_op jit(solution)/shard_map/ppermute | solution.py:62
  771.1 65.1 %collective-permute-start.81 = (bf16[2,2,80,640]{3,2,0,1:T(8,128)(2,1)S(1)}, bf16[2,2,80,640]{3,2,0,1:T(8,128)(2,1)S(1)}, u32[]{:S(2)}, u32[]{:S(2)}) collective-permute-start(bf16[2,2,80,640]{3,2,0,1:T(8,128)(2,1)S(1)} %dynamic-slice_bitcast_fusion.12), channel_id=1, source_target_pairs={{0,2},{2,0},{4,6},{6,4},{8,10},{10,8},{12,14},{14,12},{16,18},{18,... | collective-permute-start | bytes 1228808 | tf_op jit(solution)/shard_map/ppermute | solution.py:62
  831.6 23.1 %collective-permute-start.86 = (bf16[2,80,640]{2,1,0:T(8,128)(2,1)}, bf16[2,80,640]{2,1,0:T(8,128)(2,1)}, u32[]{:S(2)}, u32[]{:S(2)}) collective-permute-start(bf16[2,80,640]{2,1,0:T(8,128)(2,1)} %dynamic-slice_bitcast_fusion.23), channel_id=1, source_target_pairs={{0,4},{2,6},{4,0},{6,2},{8,12},{10,14},{12,8},{14,10},{16,20},{18,... | collective-permute-start | bytes 614408 | tf_op jit(solution)/shard_map/ppermute | solution.py:62
  (267 other events, 2388.5 us)

commit v4 on v3

--- a/solution.py
+++ b/solution.py
@@ -62,51 +62,235 @@
     return lax.ppermute(values, axis, [(i, i ^ bit) for i in range(size)])
 
 
-def my_bit(axis, bit):
-    return (lax.axis_index(axis) & bit) != 0
-
-
 def exchange_orders(size):
     if size == 16:
-        return (8, 4, 2, 1), (8, 4, 1, 2), (1, 2, 8, 4)
+        return (8, 4), ((2, 1), (1, 2))
     bits = tuple(1 << k for k in reversed(range(size.bit_length() - 1)))
-    return (bits,) * 3
-
-
-def zero_after(values):
-    corner = values[(0,) * values.ndim]
-    return jnp.minimum((corner.astype(jnp.float32) > 3e38).astype(jnp.int32), 0)
-
-
-def doubled_gather(shard, order):
-    values, done, marks = shard, [], []
-    for bit in order:
-        other = pair_swap(values, "dp", bit)
-        marks.append(other)
-        upper = my_bit("dp", bit)
-        at = sum(1 for earlier in done if earlier > bit)
-        values = jnp.stack(
-            [jnp.where(upper, other, values), jnp.where(upper, values, other)], axis=at
+    first, rest = bits[:1], bits[1:]
+    half = len(rest) // 2
+    return first, (rest, rest[half:] + rest[:half])
+
+
+WHOLE = pl.BlockSpec(memory_space=pltpu.VMEM)
+SCALAR = pl.BlockSpec(memory_space=pltpu.SMEM)
+UNREAD = pl.BlockSpec(memory_space=pl.ANY)
+
+
+def dp_bits(bits):
+    place = lax.axis_index("dp")
+    return jnp.stack([((place & bit) != 0).astype(jnp.int32) for bit in bits])
+
+
+def quick_call(kernel, name, arrays, after, out_shape):
+    out = pl.pallas_call(
+        kernel,
+        in_specs=[SCALAR] + [WHOLE] * (len(arrays) - 1) + [UNREAD] * len(after),
+        out_specs=[WHOLE] * len(out_shape),
+        out_shape=out_shape,
+        compiler_params=pltpu.CompilerParams(vmem_limit_bytes=48 << 20),
+        cost_estimate=pl.CostEstimate(flops=1, bytes_accessed=1, transcendentals=0),
+        name=name,
+    )(*arrays, *after)
+    return list(out)
+
+
+class Gather:
+    def __init__(self, pairs, orders):
+        self.first, self.rest = orders
+        self.queue = [jnp.stack(pair)[:, None] for pair in pairs]
+        self.early, self.early_at = None, 0
+        self.late, self.late_at = None, 0
+        self.ready = []
+
+    def tick(self, *after):
+        if self.early is None and self.queue:
+            self.early, self.early_at = self.queue.pop(0), 0
+        if self.late is None and self.early is not None and self.early_at == len(self.first):
+            self.late, self.late_at = self.early, 0
+            self.early, self.early_at = (self.queue.pop(0), 0) if self.queue else (None, 0)
+        jobs = []
+        early = self.early is not None and self.early_at < len(self.first)
+        if early:
+            jobs.append((self.early, self.first[: self.early_at + 1]))
+        if self.late is not None:
+            for values, order in zip(self.late, self.rest):
+                jobs.append((values, self.first + order[: self.late_at + 1]))
+        if not jobs:
+            return []
+        got = [pair_swap(values, "dp", done[-1]) for values, done in jobs]
+        plans, shapes = [], []
+        for values, done in jobs:
+            members, blocks, rows, width = values.shape
+            before = 1 << sum(1 for bit in done[:-1] if bit > done[-1])
+            parts = members if members > 1 and len(done) == len(self.first) else 1
+            plans.append((members, before, blocks // before, parts, len(shapes)))
+            shapes += [(members // parts, 2 * blocks, rows, width)] * parts
+        count = len(jobs)
+
+        def join(bit_ref, *refs):
+            outs = refs[len(refs) - len(shapes) :]
+            for job, (members, before, blocks, parts, at) in enumerate(plans):
+                bit = bit_ref[job]
+                for member in range(members):
+                    out, row = (outs[at + member], 0) if parts > 1 else (outs[at], member)
+                    for step in range(before):
+                        here = pl.ds(step * blocks, blocks)
+                        place = 2 * step * blocks
+                        ours, theirs = place + bit * blocks, place + (1 - bit) * blocks
+                        out[row, pl.ds(ours, blocks)] = refs[job][member, here]
+                        out[row, pl.ds(theirs, blocks)] = refs[count + job][member, here]
+
+        outs = quick_call(
+            join,
+            "join_halves",
+            [dp_bits([done[-1] for _, done in jobs]), *[values for values, _ in jobs], *got],
+            after,
+            [jax.ShapeDtypeStruct(shape, jnp.bfloat16) for shape in shapes],
         )
-        done.append(bit)
-    return values.reshape((-1, shard.shape[1])), zero_after(marks[-2])
-
-
-def halved_scatter(values, order):
-    rows, width = values.shape
-    left = sorted(order, reverse=True)
-    values = values.reshape((2,) * len(order) + (rows >> len(order), width))
-    for bit in reversed(order):
-        at = left.index(bit)
-        left.remove(bit)
-        upper = my_bit("dp", bit).astype(jnp.int32)
-        keep = lax.dynamic_index_in_dim(values, upper, at, keepdims=False)
-        send = lax.dynamic_index_in_dim(values, 1 - upper, at, keepdims=False)
-        got = pair_swap(send, "dp", bit)
-        values = keep.astype(jnp.float32) + got.astype(jnp.float32)
-        if left:
-            values = lowered(values)
-    return values
+        if early:
+            self.early_at += 1
+            done = self.early_at == len(self.first)
+            self.early = outs[:2] if done else outs[0]
+        if self.late is not None:
+            self.late, self.late_at = outs[-2:], self.late_at + 1
+            if self.late_at == len(self.rest[0]):
+                width = self.late[0].shape[-1]
+                self.ready.append([values.reshape((-1, width)) for values in self.late])
+                self.late = None
+        return outs
+
+    def take(self):
+        while not self.ready:
+            self.tick()
+        return self.ready.pop(0)
+
+
+class Scatter:
+    def __init__(self, orders):
+        self.first, self.rest = orders
+        self.bits = sorted(self.first + self.rest[0], reverse=True)
+        self.queue, self.late, self.early, self.done = [], None, None, []
+
+    def push(self, *pair):
+        rows = pair[0].shape[0] >> len(self.bits)
+        shape = (1, 1 << len(self.bits), rows, pair[0].shape[1])
+        self.queue.append([values.reshape(shape) for values in pair])
+
+    def run(self, jobs, after):
+        plans, ins, shapes, bits = [], [], [], []
+        for held, got, left, bit, joined in jobs:
+            blocks, rows, width = held[0].shape[1:]
+            members = sum(values.shape[0] for values in held)
+            at = left.index(bit) if bit else 0
+            behind = blocks // 2 >> at if bit else blocks
+            plans.append((len(held), len(ins), bool(got), 1 << at, behind, bit, joined, len(shapes)))
+            ins += held + (got or [])
+            bits.append(bit or 1)
+            if bit:
+                groups = 1 if joined else members
+                shapes += [((members // groups, blocks // 2, rows, width), jnp.bfloat16)] * (
+                    2 * groups
+                )
+            else:
+                shapes += [((rows, width), jnp.float32)] * members
+        inputs = len(ins)
+
+        def add(bit_ref, *refs):
+            sources, outs = refs[:inputs], refs[len(refs) - len(shapes) :]
+            for job, (arrays, at, come, before, behind, bit, joined, out_at) in enumerate(plans):
+                mine = bit_ref[job]
+                member = 0
+                for array in range(arrays):
+                    held = sources[at + array]
+                    for row in range(held.shape[0]):
+
+                        def total(start):
+                            values = held[row, pl.ds(start, behind)]
+                            if come:
+                                other = sources[at + arrays + array][row, pl.ds(start, behind)]
+                                values = values.astype(jnp.float32) + other.astype(jnp.float32)
+                            return values
+
+                        if bit is None:
+                            outs[out_at + member][...] = total(0)[0]
+                        else:
+                            keep, send, place = (
+                                (outs[out_at], outs[out_at + 1], member)
+                                if joined
+                                else (outs[out_at + 2 * member], outs[out_at + 2 * member + 1], 0)
+                            )
+                            for step in range(before):
+                                start = 2 * step * behind
+                                there = pl.ds(step * behind, behind)
+                                keep[place, there] = lowered(total(start + mine * behind))
+                                send[place, there] = lowered(total(start + (1 - mine) * behind))
+                        member += 1
+
+        return quick_call(
+            add,
+            "add_halves",
+            [dp_bits(bits), *ins],
+            after,
+            [jax.ShapeDtypeStruct(shape, kind) for shape, kind in shapes],
+        )
+
+    def enter(self):
+        if self.late is not None or not self.queue:
+            return []
+        pair = self.queue.pop(0)
+        jobs = [
+            ([values], None, self.bits, order[-1], False) for values, order in zip(pair, self.rest)
+        ]
+        outs = self.run(jobs, ())
+        self.late = (outs[0::2], outs[1::2], 1)
+        return outs
+
+    def tick(self, *after):
+        self.enter()
+        jobs, steps = [], len(self.rest[0])
+        if self.early is not None:
+            keep, send, at = self.early
+            bits = self.first[: len(self.first) - at + 1]
+            left = sorted(bits[:-1], reverse=True)
+            got = [pair_swap(send, "dp", bits[-1])]
+            jobs.append(([keep], got, left, bits[-2] if left else None, True))
+        if self.late is not None:
+            keeps, sends, at = self.late
+            got = [
+                pair_swap(send, "dp", order[steps - at]) for send, order in zip(sends, self.rest)
+            ]
+            for keep, come, order in zip(keeps, got, self.rest):
+                left = sorted(self.first + order[: steps - at], reverse=True)
+                if at < steps:
+                    jobs.append(([keep], [come], left, order[steps - at - 1], False))
+            if at == steps:
+                jobs.append((keeps, got, left, self.first[-1], True))
+        if not jobs:
+            return []
+        outs = self.run(jobs, after)
+        rest = outs
+        if self.early is not None:
+            if at_end(self.early[2], self.first):
+                self.done.append(rest[:2])
+                self.early = None
+            else:
+                self.early = (rest[0], rest[1], self.early[2] + 1)
+            rest = rest[2:]
+        if self.late is not None:
+            if self.late[2] == steps:
+                self.early, self.late = (rest[0], rest[1], 1), None
+            else:
+                self.late = (rest[0::2], rest[1::2], self.late[2] + 1)
+        return outs
+
+    def finish(self):
+        while self.queue or self.late or self.early:
+            self.tick()
+        return self.done
+
+
+def at_end(step, bits):
+    return step == len(bits)
 
 
 def total_sum(values):
@@ -122,7 +306,7 @@
     if lax.axis_size("tensor") != 2:
         return lax.all_gather(local, "tensor", axis=1, tiled=True)
     other = pair_swap(local, "tensor", 1)
-    upper = my_bit("tensor", 1)
+    upper = lax.axis_index("tensor") != 0
     return jnp.concatenate([jnp.where(upper, other, local), jnp.where(upper, local, other)], axis=1)
 
 
@@ -145,18 +329,17 @@
     return product(*mine) + got.astype(jnp.float32)
 
 
-def feed_gather(values):
+def feed_parts(values):
     if lax.axis_size("tensor") != 2:
-        return lax.all_gather(values, "tensor", axis=1, tiled=True)
-    return jnp.concatenate([values, pair_swap(values, "tensor", 1)], axis=1)
-
-
-def feed_scatter(values):
+        return [lax.all_gather(values, "tensor", axis=1, tiled=True)]
+    return [values, pair_swap(values, "tensor", 1)]
+
+
+def feed_total(parts):
     if lax.axis_size("tensor") != 2:
-        return lax.psum_scatter(lowered(values), "tensor", scatter_dimension=1, tiled=True)
-    count = values.shape[1] // 2
-    got = pair_swap(lowered(values[:, count:]), "tensor", 1)
-    return lowered(values[:, :count] + got.astype(jnp.float32))
+        return lax.psum_scatter(lowered(parts[0]), "tensor", scatter_dimension=1, tiled=True)
+    got = pair_swap(lowered(parts[1]), "tensor", 1)
+    return lowered(parts[0] + got.astype(jnp.float32))
 
 
 def key_parts(tile):
@@ -250,7 +433,7 @@
 
 
 def far_backward(
-    side_ref, q_ref, k_ref, v_ref, out_ref, grad_ref, lse_ref, dq_ref, delta_ref, dk_ref, dv_ref
+    side_ref, q_ref, k_ref, v_ref, out_ref, grad_ref, lse_ref, dq_ref, delta_ref, dkv_ref
 ):
     keys, values = k_ref[...].T, v_ref[...].T
     delta_ref[...] = jnp.sum(
@@ -270,8 +453,8 @@
         for at in tiles:
             k_term, v_term = terms(at)
             dk, dv = dk + k_term, dv + v_term
-        dk_ref[...] = lowered(dk * LN_TWO)
-        dv_ref[...] = lowered(dv)
+        dkv_ref[0] = lowered(dk * LN_TWO)
+        dkv_ref[1] = lowered(dv)
 
     tiles = [at for _, at in spans(q_ref)]
     conts = [at for tile, at in spans(q_ref) if tile * TILE >= PROMPT_DEV]
@@ -337,9 +520,6 @@
     scale_ref[...] = scale
 
 
-SCALAR = pl.BlockSpec(memory_space=pltpu.SMEM)
-
-
 def rows_block(count):
     return pl.BlockSpec((HD, count), lambda head: (head, 0))
 
@@ -352,13 +532,18 @@
     return pl.BlockSpec(shape, lambda head: (0, 0))
 
 
-def per_head(kernel, name, heads, area, products, ins, outs, scratch=()):
+def per_head(kernel, name, heads, area, products, ins, outs, after=(), scratch=()):
     flops = 2 * 256 * area * heads * products
     moved = sum(array.size * array.dtype.itemsize for _, array in ins)
+    count = len(ins)
+
+    def work(*refs):
+        kernel(*refs[:count], *refs[count + len(after) :])
+
     return pl.pallas_call(
-        kernel,
+        work,
         grid=(heads,),
-        in_specs=[spec for spec, _ in ins],
+        in_specs=[spec for spec, _ in ins] + [UNREAD] * len(after),
         out_specs=[spec for spec, _, _ in outs],
         out_shape=[jax.ShapeDtypeStruct(shape, kind) for _, shape, kind in outs],
         scratch_shapes=list(scratch),
@@ -367,10 +552,10 @@
             flops=flops, bytes_accessed=moved, transcendentals=area * heads
         ),
         name=name,
-    )(*[array for _, array in ins])
-
-
-def attention_own(start, queries, keys, values):
+    )(*[array for _, array in ins], *after)
+
+
+def attention_own(start, queries, keys, values, after):
     width, tokens = queries.shape
     heads = width // HD
     all_rows, flat = rows_block(tokens), flat_block(tokens)
@@ -391,10 +576,11 @@
             (flat, (heads, 1, tokens), jnp.float32),
             (flat, (heads, 1, tokens), jnp.float32),
         ],
-    )
-
-
-def attention_far(side, queries, keys, values, partial_sum, top, total):
+        after,
+    )
+
+
+def attention_far(side, queries, keys, values, partial_sum, top, total, after):
     width, tokens = queries.shape
     heads = width // HD
     all_rows, flat, far_rows = rows_block(tokens), flat_block(tokens), rows_block(PROMPT_DEV)
@@ -417,10 +603,11 @@
             (all_rows, (width, tokens), jnp.bfloat16),
             (flat, (heads, 1, tokens), jnp.float32),
         ],
-    )
-
-
-def attention_far_back(side, queries, keys, values, mixed, grads, lse):
+        after,
+    )
+
+
+def attention_far_back(side, queries, keys, values, mixed, grads, lse, after):
     width, tokens = queries.shape
     heads = width // HD
     all_rows, flat, far_rows = rows_block(tokens), flat_block(tokens), rows_block(PROMPT_DEV)
@@ -442,13 +629,17 @@
         [
             (all_rows, (width, tokens), jnp.float32),
             (flat, (heads, 1, tokens), jnp.float32),
-            (far_rows, (width, PROMPT_DEV), jnp.bfloat16),
-            (far_rows, (width, PROMPT_DEV), jnp.bfloat16),
+            (
+                pl.BlockSpec((2, HD, PROMPT_DEV), lambda head: (0, head, 0)),
+                (2, width, PROMPT_DEV),
+                jnp.bfloat16,
+            ),
         ],
-    )
-
-
-def attention_own_back(start, gain, queries, keys, values, grads, lse, delta, far_dq):
+        after,
+    )
+
+
+def attention_own_back(start, gain, queries, keys, values, grads, lse, delta, far_dq, after):
     width, tokens = queries.shape
     heads = width // HD
     all_rows, flat = rows_block(tokens), flat_block(tokens)
@@ -475,6 +666,7 @@
             (all_rows, (width, tokens), jnp.bfloat16),
             (pl.BlockSpec((HD, 1), lambda head: (head, 0)), (width, 1), jnp.float32),
         ],
+        after,
         [pltpu.VMEM((HD, tokens), jnp.float32)] * 2,
     )
 
@@ -506,90 +698,107 @@
     side = (lax.axis_index("dp") % 2).astype(jnp.int32)[None]
     start = segment_starts(cont_lengths[0], tokens)
 
-    weights = []
-    waits = [jnp.int32(0)] * 3
+    pairs = []
     for layer in range(LAYERS):
-        members = (
-            (key_weight, False),
-            (value_weight, False),
-            (query_weight, False),
-            (output_weight, True),
-            (up_weight, False),
-            (down_weight, True),
-        )
-        full = []
-        for place, (member, flip) in enumerate(members):
-            lane = place % 3
-            shard = lax.dynamic_index_in_dim(member, layer + waits[lane], 0, keepdims=False)
-            whole, waits[lane] = doubled_gather(shard.T if flip else shard, orders[lane])
-            full.append(whole)
-        weights.append(full)
-
+        pairs.append((key_weight[layer], value_weight[layer]))
+        pairs.append((query_weight[layer], output_weight[layer].T))
+        pairs.append((up_weight[layer], down_weight[layer].T))
+
+    gather = Gather(pairs, orders)
     stored = []
     current = inputs.T
     for layer in range(LAYERS):
-        wk, wv, wq, wo, wu, wd = weights[layer]
-        attn_gain, ff_gain = attention_gain[layer][:, None], feed_gain[layer][:, None]
+        attn_gain = attention_gain[layer][:, None]
+        ff_gain = feed_gain[layer][:, None]
         inverse_attn = inverse_root(current)
         normed = gather_tokens(lowered(current * inverse_attn * attn_gain))
         far_normed = far_tokens(normed)
+        wk, wv = gather.take()
         keys = lowered(dot_tn(wk, normed))
         values = lowered(dot_tn(wv, normed))
+        gather.tick(keys, values)
+        far_keys = lowered(dot_tn(wk, far_normed))
+        far_values = lowered(dot_tn(wv, far_normed))
+        gather.tick(far_keys, far_values)
+        wq, wo = gather.take()
         gain_q = softplus(query_scale[layer]) * LOG_TWO_E / math.sqrt(HD)
         gain_rows = jnp.tile(gain_q, heads)[:, None]
         queries = lowered(dot_tn(wq, normed) * (gain_rows * LOG_TWO_E))
-        partial_sum = attention_own(start, queries, keys, values)
-        far_keys = lowered(dot_tn(wk, far_normed))
-        far_values = lowered(dot_tn(wv, far_normed))
-        mixed, lse = attention_far(side, queries, far_keys, far_values, *partial_sum)
+        own_sum, top, total = attention_own(start, queries, keys, values, ())
+        ready = gather.tick(top)
+        mixed, lse = attention_far(side, queries, far_keys, far_values, own_sum, top, total, ready)
         middle = current + scatter_tokens(lambda rows: dot_nn(wo, rows), mixed)
+        gather.tick(middle)
+        wu, wd = gather.take()
         inverse_feed = inverse_root(middle)
         feed = lowered(middle * inverse_feed * ff_gain)
-        wu, wd = feed_gather(wu), feed_gather(wd)
-        upper = dot_tn(wu, feed)
-        hidden = lowered(upper * jax.nn.sigmoid(upper))
+        ups, downs = feed_parts(wu), feed_parts(wd)
+        uppers = [dot_tn(w, feed) for w in ups]
+        gather.tick(*uppers)
+        hiddens = [lowered(upper * jax.nn.sigmoid(upper)) for upper in uppers]
         stored.append(
             (
                 (current, inverse_attn, attn_gain, normed),
                 (gain_q, queries, keys, values, far_keys, far_values, mixed, lse),
-                (middle, inverse_feed, ff_gain, feed, upper, hidden),
-                (wk, wv, wq, wo, wu, wd),
+                (middle, inverse_feed, ff_gain, feed, uppers, hiddens),
+                (wk, wv, wq, wo, ups, downs),
             )
         )
-        current = middle + dot_nn(wd, hidden)
-
-    layer_grads = [None] * LAYERS
+        current = middle + sum(dot_nn(w, hidden) for w, hidden in zip(downs, hiddens))
+        gather.tick(current)
+
+    sums = Scatter(orders)
     small_grads = [None] * LAYERS
     grad = cotangent.T
     for layer in reversed(range(LAYERS)):
         (
             (source, inverse_attn, attn_gain, normed),
             (gain_q, queries, keys, values, far_keys, far_values, mixed, lse),
-            (middle, inverse_feed, ff_gain, feed, upper, hidden),
-            (wk, wv, wq, wo, wu, wd),
+            (middle, inverse_feed, ff_gain, feed, uppers, hiddens),
+            (wk, wv, wq, wo, ups, downs),
         ) = stored[layer]
         grad_low = lowered(grad)
-        down_grad = feed_scatter(dot_nt(grad_low, hidden))
-        d_hidden = lowered(dot_tn(wd, grad_low)).astype(jnp.float32)
-        sigmoid = jax.nn.sigmoid(upper)
-        d_upper = lowered(d_hidden * (sigmoid * (1.0 + upper * (1.0 - sigmoid))))
-        up_grad = feed_scatter(dot_nt(feed, d_upper))
-        feed_gain_grad, part = norm_backward(middle, inverse_feed, ff_gain, dot_nn(wu, d_upper))
+        d_uppers = []
+        for w, upper in zip(downs, uppers):
+            d_hidden = lowered(dot_tn(w, grad_low)).astype(jnp.float32)
+            sigmoid = jax.nn.sigmoid(upper)
+            d_uppers.append(lowered(d_hidden * (sigmoid * (1.0 + upper * (1.0 - sigmoid)))))
+        d_feed = sum(dot_nn(w, d_upper) for w, d_upper in zip(ups, d_uppers))
+        feed_gain_grad, part = norm_backward(middle, inverse_feed, ff_gain, d_feed)
         grad_middle = grad + part
+        sums.tick(grad_middle)
+        down_grad = feed_total([dot_nt(grad_low, hidden) for hidden in hiddens])
+        up_grad = feed_total([dot_nt(feed, d_upper) for d_upper in d_uppers])
+        sums.tick(down_grad, up_grad)
+        sums.push(down_grad, up_grad)
         middle_low = gather_tokens(lowered(grad_middle))
         d_mixed = lowered(dot_tn(wo, middle_low))
-        far_dq, delta, far_dk, far_dv = attention_far_back(
-            side, queries, far_keys, far_values, mixed, d_mixed, lse
+        out_grad = lowered(dot_nt(middle_low, mixed))
+        ready = sums.enter()
+        far_dq, delta, far_dkv = attention_far_back(
+            side, queries, far_keys, far_values, mixed, d_mixed, lse, ready
         )
-        back_keys = pair_swap(far_dk, "dp", 1).astype(jnp.float32)
-        back_values = pair_swap(far_dv, "dp", 1).astype(jnp.float32)
-        out_grad = lowered(dot_nt(middle_low, mixed))
+        back = pair_swap(far_dkv, "dp", 1).astype(jnp.float32)
+        ready = sums.tick(delta, out_grad)
         d_raw, own_dk, own_dv, scale_rows = attention_own_back(
-            start, gain_q[:, None], queries, keys, values, d_mixed, lse, delta, far_dq
+            start,
+            gain_q[:, None],
+            queries,
+            keys,
+            values,
+            d_mixed,
+            lse,
+            delta,
+            far_dq,
+            ready,
         )
+        sums.tick(scale_rows)
+        query_grad = lowered(dot_nt(normed, d_raw))
+        sums.push(out_grad, query_grad)
+        sums.enter()
         pad = ((0, 0), (0, tokens - PROMPT_DEV))
-        d_keys = lowered(own_dk.astype(jnp.float32) + jnp.pad(back_keys, pad))
-        d_values = lowered(own_dv.astype(jnp.float32) + jnp.pad(back_values, pad))
+        d_keys = lowered(own_dk.astype(jnp.float32) + jnp.pad(back[0], pad))
+        d_values = lowered(own_dv.astype(jnp.float32) + jnp.pad(back[1], pad))
         scale_raw = jnp.sum(scale_rows.reshape(heads, HD), 0) / (gain_q * LOG_TWO_E)
         scale_grad = scale_raw * jax.nn.sigmoid(query_scale[layer]) * LOG_TWO_E / math.sqrt(HD)
         d_normed = scatter_tokens(
@@ -598,19 +807,22 @@
             d_keys,
             d_values,
         )
-        query_grad = lowered(dot_nt(normed, d_raw))
+        sums.tick(d_normed)
         key_grad = lowered(dot_nt(normed, d_keys))
         value_grad = lowered(dot_nt(normed, d_values))
+        sums.push(key_grad, value_grad)
         attn_gain_grad, part = norm_backward(source, inverse_attn, attn_gain, d_normed)
         grad = grad_middle + part
+        sums.tick(grad)
         small_grads[layer] = jnp.concatenate([attn_gain_grad, feed_gain_grad, scale_grad])
-        down_grad, up_grad, out_grad, query_grad, key_grad, value_grad = [
-            halved_scatter(member, orders[place % 3])
-            for place, member in enumerate(
-                (down_grad, up_grad, out_grad, query_grad, key_grad, value_grad)
-            )
-        ]
-        layer_grads[layer] = (query_grad, key_grad, value_grad, out_grad.T, up_grad, down_grad.T)
+    done = sums.finish()
+    layer_grads = []
+    for layer in range(LAYERS):
+        at = 3 * (LAYERS - 1 - layer)
+        (down_grad, up_grad), (out_grad, query_grad), (key_grad, value_grad) = done[at : at + 3]
+        layer_grads.append(
+            (query_grad, key_grad, value_grad, out_grad.T, up_grad, down_grad.T)
+        )
 
     summed = [jnp.stack(members) for members in zip(*layer_grads)]
     small = total_sum(jnp.stack(small_grads))

time: 880 us -> 723 us (0.82)
  waiting for transfers between devices: 329 us -> 189 us
  Pallas kernels: 99.4 us -> 152 us
  other arithmetic: 82.1 us -> 34.5 us
  matrix products: 111 us -> 148 us
  starting transfers between devices: 155 us -> 126 us
  local copies, waits for them, and re-layouts: 81.4 us -> 59.1 us
    ppermute x125 -> x99, waiting for transfers between devices: 329 us -> 189 us  [pair_swap(): return lax.ppermute(values, axis, [(i, i ^ bit) for i in range(size)])]
    pallas_call x8 -> x42, Pallas kernels: 99.4 us -> 152 us  [the longest x8 99.7 us: per_head(): pl.pallas_call(work, grid=(heads,), in_specs=[spec for spec, _ in ins] +...]
    another operation x97 -> x6, other arithmetic: 33.1 us -> 0.56 us  [the longest x5 0.38 us: dp_bits(): return jnp.stack([(place & bit != 0).astype(jnp.int32) for bit in bits])]
    ppermute x125 -> x99, starting transfers between devices: 155 us -> 126 us  [pair_swap(): return lax.ppermute(values, axis, [(i, i ^ bit) for i in range(size)])]
    dot_general x12 -> x16, matrix products: 33 us -> 52 us  [dot_nt(): lax.dot_general(former, latter, (((1,), (1,)), ((), ())), preferred_eleme...]
    convert_element_type x48 -> x12, other arithmetic: 29.8 us -> 10.9 us  [lowered(): return values.astype(jnp.bfloat16)]
    dot_general x20 -> x24, matrix products: 42.9 us -> 57.8 us  [dot_nn(): return jnp.dot(former, latter, preferred_element_type=jnp.float32)]
    slice x15 -> x5, local copies, waits for them, and re-layouts: 15.6 us -> 3.41 us  [the longest x1 1.6 us: body(): pairs.append((up_weight[layer], down_weight[layer].T))]
  transfers between devices with their start and end apart: 125 -> 99, of which waited for: 51 -> 37; matrix products, arithmetic and copies ran while one was open for 26% -> 25% of each run, Pallas kernels for 11% -> 17%
where the time goes in v4:
time: 723 us; the launch traced here: 712 us
  waiting for transfers between devices  189 us (26%)
  Pallas kernels  152 us (21%)
  matrix products  148 us (20%)
  starting transfers between devices  126 us (17%)
  local copies, waits for them, and re-layouts  59.1 us (8%)
  other arithmetic  34.5 us (5%)
    ppermute x99, waiting for transfers between devices, pair_swap(): return lax.ppermute(values, axis, [(i, i ^ bit) for i in range(size)])  189 us
    ppermute x99, starting transfers between devices, pair_swap(): return lax.ppermute(values, axis, [(i, i ^ bit) for i in range(size)])  126 us
    pallas_call x8, Pallas kernels, per_head(): pl.pallas_call(work, grid=(heads,), in_specs=[spec for spec, _ in ins] +...  99.7 us
    dot_general x24, matrix products, dot_nn(): return jnp.dot(former, latter, preferred_element_type=jnp.float32)  57.8 us
    dot_general x16, matrix products, dot_nt(): lax.dot_general(former, latter, (((1,), (1,)), ((), ())), preferred_eleme...  52 us
    pallas_call x34, Pallas kernels, quick_call(): pl.pallas_call(kernel, in_specs=[SCALAR] + [WHOLE] * (len(arrays) - 1) +...  51.9 us
    unnamed x370, local copies, waits for them, and re-layouts  48.4 us
    dot_general x20, matrix products, dot_tn(): lax.dot_general(former, latter, (((0,), (0,)), ((), ())), preferred_eleme...  38.7 us
  transfers between devices with their start and end apart: 99, of which 37 were waited for; matrix products, arithmetic and copies ran while one was open for 25% of the time, Pallas kernels for 17%

profile of v4, /device:TPU:0, one launch (start us, length us, event | category | flops | bytes accessed | tf_op | source)
XLA Modules:
  0.0 712.1 jit_solution(12090553754047963617)
XLA Ops:
  1.8 4.1 collective-permute-start
  11.2 4.2 collective-permute-done.refs_1_
  15.5 5.2 collective-permute-start.1
  23.9 9.0 %collective-permute-done.1.refs_1_ = bf16[2,2,80,640]{3,2,1,0:T(8,128)(2,1)S(1)} collective-permute-done((bf16[2,2,80,640]{3,2,1,0:T(8,128)(2,1)S(1)}, bf16[2,2,80,640]{3,2,1,0:T(8,128)(2,1)S(1)}, u32[]{:S(2)}, u32[]{:S(2)}) %collective-permute-start.1) | collective-permute-done | bytes 409632 | tf_op jit(solution)/shard_map/ppermute | solution.py:62
  38.7 5.8 collective-permute-done.3.refs_4_
  52.4 9.4 %collective-permute-done.5.refs_3_ = bf16[2,2,80,640]{3,2,1,0:T(8,128)(2,1)S(1)} collective-permute-done((bf16[2,2,80,640]{3,2,1,0:T(8,128)(2,1)S(1)}, bf16[2,2,80,640]{3,2,1,0:T(8,128)(2,1)S(1)}, u32[]{:S(2)}, u32[]{:S(2)}) %collective-permute-start.5) | collective-permute-done | bytes 409632 | tf_op jit(solution)/shard_map/ppermute | solution.py:62
  72.2 9.5 %collective-permute-done.15 = bf16[1280,256]{1,0:T(8,128)(2,1)S(1)} collective-permute-done((bf16[1280,256]{1,0:T(8,128)(2,1)S(1)}, bf16[1280,256]{1,0:T(8,128)(2,1)S(1)}, u32[]{:S(2)}, u32[]{:S(2)}) %collective-permute-start.15) | collective-permute-done | bytes 655392 | tf_op jit(solution)/shard_map/ppermute | solution.py:62
  94.0 6.9 collective-permute-done.12.refs_3_
  100.9 8.9 %collective-permute-done.13.refs_4_ = bf16[1,8,80,640]{3,2,1,0:T(8,128)(2,1)S(1)} collective-permute-done((bf16[1,8,80,640]{3,2,1,0:T(8,128)(2,1)S(1)}, bf16[1,8,80,640]{3,2,1,0:T(8,128)(2,1)S(1)}, u32[]{:S(2)}, u32[]{:S(2)}) %collective-permute-start.13) | collective-permute-done | bytes 819232 | tf_op jit(solution)/shard_map/ppermute | solution.py:62
  119.4 13.6 %attention_own.2 = (f32[640,1024]{1,0:T(8,128)S(1)}, f32[8,1,1024]{2,1,0:T(1,128)S(1)}, f32[8,1,1024]{2,1,0:T(1,128)S(1)}) custom-call(s32[1,1024]{1,0:T(1,128)S(1)} %bitcast.243, bf16[640,1024]{1,0:T(8,128)(2,1)S(1)} %multiply_convert_fusion.4.refs_1_.refs_2_, bf16[640,1024]{1,0:T(8,128)(2,1)S(1)} %convolution_convert_fusion.17.refs_6_.refs_2_.refs_3_, ...), custom_call_target="tpu_custom_call" | custom-call | flops 8053063680 | bytes 3936256 | tf_op jit(solution)/shard_map/attention_own/pallas_call | solution.py:543
  133.8 7.7 %attention_far.2 = (bf16[640,1024]{1,0:T(8,128)(2,1)S(1)}, f32[8,1,1024]{2,1,0:T(1,128)S(1)}) custom-call(s32[1]{0:T(128)} %bitcast.17.refs_0_, bf16[640,1024]{1,0:T(8,128)(2,1)S(1)} %multiply_convert_fusion.4.refs_1_.refs_2_, bf16[640,512]{1,0:T(8,128)(2,1)S(1)} %convolution_convert_fusion.25.refs_6_.refs_2_, ...), custom_call_target="tpu_custom_call" | custom-call | flops 6442450944 | bytes 5308420 | tf_op jit(solution)/shard_map/attention_far/pallas_call | solution.py:543
  143.8 8.4 %collective-permute-start.22 = (bf16[1,8,80,640]{3,2,1,0:T(8,128)(2,1)S(1)}, bf16[1,8,80,640]{3,2,1,0:T(8,128)(2,1)S(1)}, u32[]{:S(2)}, u32[]{:S(2)}) collective-permute-start(bf16[1,8,80,640]{3,2,1,0:T(8,128)(2,1)S(1)} %get-tuple-element.180.refs_8_.refs_1_), channel_id=1, source_target_pairs={{0,2},{2,0},{4,6},{6,4},{8,10},{10,8},{12,14},{14,12},{16,18},{18,... | collective-permute-start | bytes 2457608 | tf_op jit(solution)/shard_map/ppermute | solution.py:62
  155.4 5.7 multiply_reduce_fusion.10
  161.1 4.2 collective-permute-done.21.refs_3_
  165.3 5.9 collective-permute-done.22.refs_4_
  186.7 3.7 collective-permute-start.26
  190.4 9.4 %collective-permute-done.26.refs_3_ = bf16[2,1,80,640]{3,2,1,0:T(8,128)(2,1)S(1)} collective-permute-done((bf16[2,1,80,640]{3,2,1,0:T(8,128)(2,1)S(1)}, bf16[2,1,80,640]{3,2,1,0:T(8,128)(2,1)S(1)}, u32[]{:S(2)}, u32[]{:S(2)}) %collective-permute-start.26) | collective-permute-done | bytes 204832 | tf_op jit(solution)/shard_map/ppermute | solution.py:62
  210.9 11.9 %collective-permute-done.29.refs_3_ = bf16[2,2,80,640]{3,2,1,0:T(8,128)(2,1)} collective-permute-done((bf16[2,2,80,640]{3,2,1,0:T(8,128)(2,1)}, bf16[2,2,80,640]{3,2,1,0:T(8,128)(2,1)}, u32[]{:S(2)}, u32[]{:S(2)}) %collective-permute-start.29) | collective-permute-done | bytes 409632 | tf_op jit(solution)/shard_map/ppermute | solution.py:62
  229.0 7.6 %collective-permute-done.39 = bf16[1280,256]{1,0:T(8,128)(2,1)} collective-permute-done((bf16[1280,256]{1,0:T(8,128)(2,1)}, bf16[1280,256]{1,0:T(8,128)(2,1)}, u32[]{:S(2)}, u32[]{:S(2)}) %collective-permute-start.39) | collective-permute-done | bytes 655392 | tf_op jit(solution)/shard_map/ppermute | solution.py:62
  251.0 5.3 collective-permute-done.36.refs_3_
  256.3 8.9 %collective-permute-done.37.refs_4_ = bf16[1,8,80,640]{3,2,1,0:T(8,128)(2,1)S(1)} collective-permute-done((bf16[1,8,80,640]{3,2,1,0:T(8,128)(2,1)S(1)}, bf16[1,8,80,640]{3,2,1,0:T(8,128)(2,1)S(1)}, u32[]{:S(2)}, u32[]{:S(2)}) %collective-permute-start.37) | collective-permute-done | bytes 819232 | tf_op jit(solution)/shard_map/ppermute | solution.py:62
  275.1 13.5 %attention_own.3 = (f32[640,1024]{1,0:T(8,128)S(1)}, f32[8,1,1024]{2,1,0:T(1,128)S(1)}, f32[8,1,1024]{2,1,0:T(1,128)S(1)}) custom-call(s32[1,1024]{1,0:T(1,128)S(1)} %bitcast.244, bf16[640,1024]{1,0:T(8,128)(2,1)S(1)} %multiply_convert_fusion.1.refs_1_.refs_2_, bf16[640,1024]{1,0:T(8,128)(2,1)S(1)} %convolution_convert_fusion.15.refs_6_.refs_2_.refs_3_, ...), custom_call_target="tpu_custom_call" | custom-call | flops 8053063680 | bytes 3936256 | tf_op jit(solution)/shard_map/attention_own/pallas_call | solution.py:543
  289.3 7.7 %attention_far.3 = (bf16[640,1024]{1,0:T(8,128)(2,1)S(1)}, f32[8,1,1024]{2,1,0:T(1,128)S(1)}) custom-call(s32[1]{0:T(128)} %bitcast.17.refs_0_, bf16[640,1024]{1,0:T(8,128)(2,1)S(1)} %multiply_convert_fusion.1.refs_1_.refs_2_, bf16[640,512]{1,0:T(8,128)(2,1)S(1)} %convolution_convert_fusion.23.refs_6_.refs_2_, ...), custom_call_target="tpu_custom_call" | custom-call | flops 6442450944 | bytes 5308420 | tf_op jit(solution)/shard_map/attention_far/pallas_call | solution.py:543
  303.0 8.4 %collective-permute-start.44 = (bf16[1,8,80,640]{3,2,1,0:T(8,128)(2,1)S(1)}, bf16[1,8,80,640]{3,2,1,0:T(8,128)(2,1)S(1)}, u32[]{:S(2)}, u32[]{:S(2)}) collective-permute-start(bf16[1,8,80,640]{3,2,1,0:T(8,128)(2,1)S(1)} %get-tuple-element.204.refs_7_.refs_0_), channel_id=1, source_target_pairs={{0,2},{2,0},{4,6},{6,4},{8,10},{10,8},{12,14},{14,12},{16,18},{18,... | collective-permute-start | bytes 2457608 | tf_op jit(solution)/shard_map/ppermute | solution.py:62
  314.9 5.1 multiply_reduce_fusion.8
  320.0 10.4 %collective-permute-done.44.refs_2_ = bf16[1,8,80,640]{3,2,1,0:T(8,128)(2,1)S(1)} collective-permute-done((bf16[1,8,80,640]{3,2,1,0:T(8,128)(2,1)S(1)}, bf16[1,8,80,640]{3,2,1,0:T(8,128)(2,1)S(1)}, u32[]{:S(2)}, u32[]{:S(2)}) %collective-permute-start.44) | collective-permute-done | bytes 819232 | tf_op jit(solution)/shard_map/ppermute | solution.py:62
  356.9 3.7 convolution_convert_fusion.7.refs_5_
  368.9 4.6 add_convert_fusion.2
  377.3 9.6 %attention_far_back.2 = (f32[640,1024]{1,0:T(8,128)S(1)}, f32[8,1,1024]{2,1,0:T(1,128)S(1)}, bf16[2,640,512]{2,1,0:T(8,128)(2,1)S(1)}) custom-call(s32[1]{0:T(128)} %bitcast.17.refs_0_, bf16[640,1024]{1,0:T(8,128)(2,1)S(1)} %copy-done.69, bf16[640,512]{1,0:T(8,128)(2,1)S(1)} %copy-done.20, bf16[640,512]{1,0:T(8,128)(2,1)S(1)} %copy-done.22, ...), custom_call_target="tpu_custom_call" | custom-call | flops 12884901888 | bytes 5275652 | tf_op jit(solution)/shard_map/attention_far_back/pallas_call | solution.py:543
  388.4 8.8 %collective-permute-start.53 = (bf16[2,640,512]{2,1,0:T(8,128)(2,1)S(1)}, bf16[2,640,512]{2,1,0:T(8,128)(2,1)S(1)}, u32[]{:S(2)}, u32[]{:S(2)}) collective-permute-start(bf16[2,640,512]{2,1,0:T(8,128)(2,1)S(1)} %get-tuple-element.222), channel_id=1, source_target_pairs={{0,2},{2,0},{4,6},{6,4},{8,10},{10,8},{12,14},{14,12},{16,18},{18,... | collective-permute-start | bytes 3932168 | tf_op jit(solution)/shard_map/ppermute | solution.py:62
  401.0 19.0 %attention_own_back.2 = (bf16[640,1024]{1,0:T(8,128)(2,1)S(1)}, bf16[640,1024]{1,0:T(8,128)(2,1)S(1)}, bf16[640,1024]{1,0:T(8,128)(2,1)S(1)}, f32[640,1]{1,0:T(8,128)S(1)}) custom-call(s32[1,1024]{1,0:T(1,128)S(1)} %bitcast.245, f32[80,1]{1,0:T(8,128)S(1)} %copy.65.refs_1_, bf16[640,1024]{1,0:T(8,128)(2,1)S(1)} %copy-done.69, ...), custom_call_target="tpu_custom_call" | custom-call | flops 16106127360 | bytes 7934272 | tf_op jit(solution)/shard_map/attention_own_back/pallas_call | solution.py:543
  420.0 5.9 collective-permute-done.53
  437.2 5.2 convolution_convert_fusion.6
  501.1 8.3 %collective-permute-done.67.refs_3_ = bf16[1,8,80,640]{3,2,1,0:T(8,128)(2,1)} collective-permute-done((bf16[1,8,80,640]{3,2,1,0:T(8,128)(2,1)}, bf16[1,8,80,640]{3,2,1,0:T(8,128)(2,1)}, u32[]{:S(2)}, u32[]{:S(2)}) %collective-permute-start.67) | collective-permute-done | bytes 819232 | tf_op jit(solution)/shard_map/ppermute | solution.py:62
  525.3 3.9 add_convert_fusion.refs_7_
  536.7 9.6 %attention_far_back.3 = (f32[640,1024]{1,0:T(8,128)S(1)}, f32[8,1,1024]{2,1,0:T(1,128)S(1)}, bf16[2,640,512]{2,1,0:T(8,128)(2,1)S(1)}) custom-call(s32[1]{0:T(128)} %bitcast.17.refs_0_, bf16[640,1024]{1,0:T(8,128)(2,1)S(1)} %copy-done.66, bf16[640,512]{1,0:T(8,128)(2,1)S(1)} %copy-done.16, bf16[640,512]{1,0:T(8,128)(2,1)S(1)} %copy-done.18, ...), custom_call_target="tpu_custom_call" | custom-call | flops 12884901888 | bytes 5275652 | tf_op jit(solution)/shard_map/attention_far_back/pallas_call | solution.py:543
  547.8 8.9 %collective-permute-start.75 = (bf16[2,640,512]{2,1,0:T(8,128)(2,1)S(1)}, bf16[2,640,512]{2,1,0:T(8,128)(2,1)}, u32[]{:S(2)}, u32[]{:S(2)}) collective-permute-start(bf16[2,640,512]{2,1,0:T(8,128)(2,1)S(1)} %get-tuple-element.266), channel_id=1, source_target_pairs={{0,2},{2,0},{4,6},{6,4},{8,10},{10,8},{12,14},{14,12},{16,18},{18,... | collective-permute-start | bytes 3932168 | tf_op jit(solution)/shard_map/ppermute | solution.py:62
  563.5 19.1 %attention_own_back.3 = (bf16[640,1024]{1,0:T(8,128)(2,1)S(1)}, bf16[640,1024]{1,0:T(8,128)(2,1)S(1)}, bf16[640,1024]{1,0:T(8,128)(2,1)S(1)}, f32[640,1]{1,0:T(8,128)S(1)}) custom-call(s32[1,1024]{1,0:T(1,128)S(1)} %bitcast.246, f32[80,1]{1,0:T(8,128)S(1)} %copy.71.refs_1_, bf16[640,1024]{1,0:T(8,128)(2,1)S(1)} %copy-done.67, ...), custom_call_target="tpu_custom_call" | custom-call | flops 16106127360 | bytes 7934272 | tf_op jit(solution)/shard_map/attention_own_back/pallas_call | solution.py:543
  582.6 3.9 collective-permute-done.75
  616.8 4.8 multiply_reduce_fusion.3
  624.4 3.7 convolution_convert_fusion
  638.1 3.9 multiply_add_fusion.refs_6_
  642.0 5.1 collective-permute-done.83.refs_1_
  647.2 14.3 %collective-permute-done.84.refs_4_ = bf16[1,4,80,640]{3,2,1,0:T(8,128)(2,1)S(1)} collective-permute-done((bf16[1,4,80,640]{3,2,1,0:T(8,128)(2,1)S(1)}, bf16[1,4,80,640]{3,2,1,0:T(8,128)(2,1)S(1)}, u32[]{:S(2)}, u32[]{:S(2)}) %collective-permute-start.84) | collective-permute-done | bytes 409632 | tf_op jit(solution)/shard_map/ppermute | solution.py:62
  668.4 5.3 collective-permute-done.86.refs_1_
  679.3 4.8 fusion.10
  695.9 5.1 collective-permute-done.92.refs_1_
  703.4 6.7 collective-permute-done.93.refs_1_
  (711 shorter events, 344.4 us)
Async XLA Ops:
  9.8 38.7 %collective-permute-start.11 = (bf16[1280,512]{1,0:T(8,128)(2,1)}, bf16[1280,512]{1,0:T(8,128)(2,1)}, u32[]{:S(2)}, u32[]{:S(2)}) collective-permute-start(bf16[1280,512]{1,0:T(8,128)(2,1)} %multiply_convert_fusion.5), channel_id=1, source_target_pairs={{0,1},{1,0},{2,3},{3,2},{4,5},{5,4},{6,7},{7,6},{8,9},{9,8},{10,11... | collective-permute-start | bytes 3932168 | tf_op jit(solution)/shard_map/ppermute | solution.py:62
  11.1 27.6 %collective-permute-start.2 = (bf16[2,1,80,640]{3,2,1,0:T(8,128)(2,1)S(1)}, bf16[2,1,80,640]{3,2,1,0:T(8,128)(2,1)S(1)}, u32[]{:S(2)}, u32[]{:S(2)}) collective-permute-start(bf16[2,1,80,640]{3,2,1,0:T(8,128)(2,1)S(1)} %maximum_bitcast_fusion.1.refs_0_), channel_id=1, source_target_pairs={{0,16},{2,18},{4,20},{6,22},{8,24},{10,26},{12,28},{14,30},{16,0},... | collective-permute-start | bytes 614408 | tf_op jit(solution)/shard_map/ppermute | solution.py:62
  36.1 52.1 %collective-permute-start.8 = (bf16[2,1,80,640]{3,2,1,0:T(8,128)(2,1)S(1)}, bf16[2,1,80,640]{3,2,1,0:T(8,128)(2,1)S(1)}, u32[]{:S(2)}, u32[]{:S(2)}) collective-permute-start(bf16[2,1,80,640]{3,2,1,0:T(8,128)(2,1)S(1)} %maximum_bitcast_fusion.refs_0_), channel_id=1, source_target_pairs={{0,16},{2,18},{4,20},{6,22},{8,24},{10,26},{12,28},{14,30},{16,0},... | collective-permute-start | bytes 614408 | tf_op jit(solution)/shard_map/ppermute | solution.py:62
  46.4 21.2 %collective-permute-start.6 = (bf16[1,8,80,640]{3,2,1,0:T(8,128)(2,1)S(1)}, bf16[1,8,80,640]{3,2,1,0:T(8,128)(2,1)S(1)}, u32[]{:S(2)}, u32[]{:S(2)}) collective-permute-start(bf16[1,8,80,640]{3,2,1,0:T(8,128)(2,1)S(1)} %get-tuple-element.163.refs_1_), channel_id=1, source_target_pairs={{0,2},{2,0},{4,6},{6,4},{8,10},{10,8},{12,14},{14,12},{16,18},{18,... | collective-permute-start | bytes 2457608 | tf_op jit(solution)/shard_map/ppermute | solution.py:62
  48.0 19.7 %collective-permute-start.7 = (bf16[1,8,80,640]{3,2,1,0:T(8,128)(2,1)S(1)}, bf16[1,8,80,640]{3,2,1,0:T(8,128)(2,1)S(1)}, u32[]{:S(2)}, u32[]{:S(2)}) collective-permute-start(bf16[1,8,80,640]{3,2,1,0:T(8,128)(2,1)S(1)} %get-tuple-element.164.refs_2_), channel_id=1, source_target_pairs={{0,4},{2,6},{4,0},{6,2},{8,12},{10,14},{12,8},{14,10},{16,20},{18,... | collective-permute-start | bytes 2457608 | tf_op jit(solution)/shard_map/ppermute | solution.py:62
  51.5 30.2 %collective-permute-start.15 = (bf16[1280,256]{1,0:T(8,128)(2,1)S(1)}, bf16[1280,256]{1,0:T(8,128)(2,1)S(1)}, u32[]{:S(2)}, u32[]{:S(2)}) collective-permute-start(bf16[1280,256]{1,0:T(8,128)(2,1)S(1)} %fusion.32), channel_id=1, source_target_pairs={{0,2},{2,0},{4,6},{6,4},{8,10},{10,8},{12,14},{14,12},{16,18},{18,... | collective-permute-start | bytes 1966088 | tf_op jit(solution)/shard_map/ppermute | solution.py:62
  61.8 71.2 %collective-permute-start.17 = (bf16[2,1,80,640]{3,2,1,0:T(8,128)(2,1)S(1)}, bf16[2,1,80,640]{3,2,1,0:T(8,128)(2,1)S(1)}, u32[]{:S(2)}, u32[]{:S(2)}) collective-permute-start(bf16[2,1,80,640]{3,2,1,0:T(8,128)(2,1)S(1)} %maximum_bitcast_fusion.3.refs_0_), channel_id=1, source_target_pairs={{0,16},{2,18},{4,20},{6,22},{8,24},{10,26},{12,28},{14,30},{16,0},... | collective-permute-start | bytes 614408 | tf_op jit(solution)/shard_map/ppermute | solution.py:62
  89.2 20.5 %collective-permute-start.13 = (bf16[1,8,80,640]{3,2,1,0:T(8,128)(2,1)S(1)}, bf16[1,8,80,640]{3,2,1,0:T(8,128)(2,1)S(1)}, u32[]{:S(2)}, u32[]{:S(2)}) collective-permute-start(bf16[1,8,80,640]{3,2,1,0:T(8,128)(2,1)S(1)} %get-tuple-element.170.refs_1_), channel_id=1, source_target_pairs={{0,2},{2,0},{4,6},{6,4},{8,10},{10,8},{12,14},{14,12},{16,18},{18,... | collective-permute-start | bytes 2457608 | tf_op jit(solution)/shard_map/ppermute | solution.py:62
  90.7 20.2 %collective-permute-start.14 = (bf16[1,8,80,640]{3,2,1,0:T(8,128)(2,1)S(1)}, bf16[1,8,80,640]{3,2,1,0:T(8,128)(2,1)S(1)}, u32[]{:S(2)}, u32[]{:S(2)}) collective-permute-start(bf16[1,8,80,640]{3,2,1,0:T(8,128)(2,1)S(1)} %get-tuple-element.171.refs_2_), channel_id=1, source_target_pairs={{0,4},{2,6},{4,0},{6,2},{8,12},{10,14},{12,8},{14,10},{16,20},{18,... | collective-permute-start | bytes 2457608 | tf_op jit(solution)/shard_map/ppermute | solution.py:62
  143.8 27.3 %collective-permute-start.22 = (bf16[1,8,80,640]{3,2,1,0:T(8,128)(2,1)S(1)}, bf16[1,8,80,640]{3,2,1,0:T(8,128)(2,1)S(1)}, u32[]{:S(2)}, u32[]{:S(2)}) collective-permute-start(bf16[1,8,80,640]{3,2,1,0:T(8,128)(2,1)S(1)} %get-tuple-element.180.refs_8_.refs_1_), channel_id=1, source_target_pairs={{0,2},{2,0},{4,6},{6,4},{8,10},{10,8},{12,14},{14,12},{16,18},{18,... | collective-permute-start | bytes 2457608 | tf_op jit(solution)/shard_map/ppermute | solution.py:62
  152.2 20.4 %collective-permute-start.23 = (bf16[1,8,80,640]{3,2,1,0:T(8,128)(2,1)S(1)}, bf16[1,8,80,640]{3,2,1,0:T(8,128)(2,1)S(1)}, u32[]{:S(2)}, u32[]{:S(2)}) collective-permute-start(bf16[1,8,80,640]{3,2,1,0:T(8,128)(2,1)S(1)} %get-tuple-element.181.refs_9_.refs_2_), channel_id=1, source_target_pairs={{0,4},{2,6},{4,0},{6,2},{8,12},{10,14},{12,8},{14,10},{16,20},{18,... | collective-permute-start | bytes 2457608 | tf_op jit(solution)/shard_map/ppermute | solution.py:62
  184.6 18.9 %collective-permute-start.35 = (bf16[1280,512]{1,0:T(8,128)(2,1)S(1)}, bf16[1280,512]{1,0:T(8,128)(2,1)}, u32[]{:S(2)}, u32[]{:S(2)}) collective-permute-start(bf16[1280,512]{1,0:T(8,128)(2,1)S(1)} %multiply_convert_fusion.2), channel_id=1, source_target_pairs={{0,1},{1,0},{2,3},{3,2},{4,5},{5,4},{6,7},{7,6},{8,9},{9,8},{10,11... | collective-permute-start | bytes 3932168 | tf_op jit(solution)/shard_map/ppermute | solution.py:62
  201.3 21.5 %collective-permute-start.30 = (bf16[1,8,80,640]{3,2,1,0:T(8,128)(2,1)S(1)}, bf16[1,8,80,640]{3,2,1,0:T(8,128)(2,1)S(1)}, u32[]{:S(2)}, u32[]{:S(2)}) collective-permute-start(bf16[1,8,80,640]{3,2,1,0:T(8,128)(2,1)S(1)} %get-tuple-element.188.refs_1_), channel_id=1, source_target_pairs={{0,2},{2,0},{4,6},{6,4},{8,10},{10,8},{12,14},{14,12},{16,18},{18,... | collective-permute-start | bytes 2457608 | tf_op jit(solution)/shard_map/ppermute | solution.py:62
  203.0 19.8 %collective-permute-start.31 = (bf16[1,8,80,640]{3,2,1,0:T(8,128)(2,1)S(1)}, bf16[1,8,80,640]{3,2,1,0:T(8,128)(2,1)S(1)}, u32[]{:S(2)}, u32[]{:S(2)}) collective-permute-start(bf16[1,8,80,640]{3,2,1,0:T(8,128)(2,1)S(1)} %get-tuple-element.189.refs_2_), channel_id=1, source_target_pairs={{0,4},{2,6},{4,0},{6,2},{8,12},{10,14},{12,8},{14,10},{16,20},{18,... | collective-permute-start | bytes 2457608 | tf_op jit(solution)/shard_map/ppermute | solution.py:62
  207.2 29.4 %collective-permute-start.39 = (bf16[1280,256]{1,0:T(8,128)(2,1)}, bf16[1280,256]{1,0:T(8,128)(2,1)}, u32[]{:S(2)}, u32[]{:S(2)}) collective-permute-start(bf16[1280,256]{1,0:T(8,128)(2,1)} %fusion.31), channel_id=1, source_target_pairs={{0,2},{2,0},{4,6},{6,4},{8,10},{10,8},{12,14},{14,12},{16,18},{18,... | collective-permute-start | bytes 1966088 | tf_op jit(solution)/shard_map/ppermute | solution.py:62
  207.7 35.6 %collective-permute-start.32 = (bf16[2,1,80,640]{3,2,1,0:T(8,128)(2,1)S(1)}, bf16[2,1,80,640]{3,2,1,0:T(8,128)(2,1)}, u32[]{:S(2)}, u32[]{:S(2)}) collective-permute-start(bf16[2,1,80,640]{3,2,1,0:T(8,128)(2,1)S(1)} %maximum_bitcast_fusion.4.refs_0_), channel_id=1, source_target_pairs={{0,16},{2,18},{4,20},{6,22},{8,24},{10,26},{12,28},{14,30},{16,0},... | collective-permute-start | bytes 614408 | tf_op jit(solution)/shard_map/ppermute | solution.py:62
  245.4 19.8 %collective-permute-start.37 = (bf16[1,8,80,640]{3,2,1,0:T(8,128)(2,1)S(1)}, bf16[1,8,80,640]{3,2,1,0:T(8,128)(2,1)S(1)}, u32[]{:S(2)}, u32[]{:S(2)}) collective-permute-start(bf16[1,8,80,640]{3,2,1,0:T(8,128)(2,1)S(1)} %get-tuple-element.195.refs_1_), channel_id=1, source_target_pairs={{0,2},{2,0},{4,6},{6,4},{8,10},{10,8},{12,14},{14,12},{16,18},{18,... | collective-permute-start | bytes 2457608 | tf_op jit(solution)/shard_map/ppermute | solution.py:62
  247.2 19.4 %collective-permute-start.38 = (bf16[1,8,80,640]{3,2,1,0:T(8,128)(2,1)S(1)}, bf16[1,8,80,640]{3,2,1,0:T(8,128)(2,1)S(1)}, u32[]{:S(2)}, u32[]{:S(2)}) collective-permute-start(bf16[1,8,80,640]{3,2,1,0:T(8,128)(2,1)S(1)} %get-tuple-element.196.refs_2_), channel_id=1, source_target_pairs={{0,4},{2,6},{4,0},{6,2},{8,12},{10,14},{12,8},{14,10},{16,20},{18,... | collective-permute-start | bytes 2457608 | tf_op jit(solution)/shard_map/ppermute | solution.py:62
  303.0 27.3 %collective-permute-start.44 = (bf16[1,8,80,640]{3,2,1,0:T(8,128)(2,1)S(1)}, bf16[1,8,80,640]{3,2,1,0:T(8,128)(2,1)S(1)}, u32[]{:S(2)}, u32[]{:S(2)}) collective-permute-start(bf16[1,8,80,640]{3,2,1,0:T(8,128)(2,1)S(1)} %get-tuple-element.204.refs_7_.refs_0_), channel_id=1, source_target_pairs={{0,2},{2,0},{4,6},{6,4},{8,10},{10,8},{12,14},{14,12},{16,18},{18,... | collective-permute-start | bytes 2457608 | tf_op jit(solution)/shard_map/ppermute | solution.py:62
  311.4 20.4 %collective-permute-start.45 = (bf16[1,8,80,640]{3,2,1,0:T(8,128)(2,1)S(1)}, bf16[1,8,80,640]{3,2,1,0:T(8,128)(2,1)S(1)}, u32[]{:S(2)}, u32[]{:S(2)}) collective-permute-start(bf16[1,8,80,640]{3,2,1,0:T(8,128)(2,1)S(1)} %get-tuple-element.205.refs_8_.refs_1_), channel_id=1, source_target_pairs={{0,4},{2,6},{4,0},{6,2},{8,12},{10,14},{12,8},{14,10},{16,20},{18,... | collective-permute-start | bytes 2457608 | tf_op jit(solution)/shard_map/ppermute | solution.py:62
  375.4 21.8 %collective-permute-start.51 = (bf16[1,8,80,640]{3,2,1,0:T(8,128)(2,1)S(1)}, bf16[1,8,80,640]{3,2,1,0:T(8,128)(2,1)S(1)}, u32[]{:S(2)}, u32[]{:S(2)}) collective-permute-start(bf16[1,8,80,640]{3,2,1,0:T(8,128)(2,1)S(1)} %get-tuple-element.211.refs_8_), channel_id=1, source_target_pairs={{0,2},{2,0},{4,6},{6,4},{8,10},{10,8},{12,14},{14,12},{16,18},{18,... | collective-permute-start | bytes 2457608 | tf_op jit(solution)/shard_map/ppermute | solution.py:62
  375.8 21.4 %collective-permute-start.52 = (bf16[1,8,80,640]{3,2,1,0:T(8,128)(2,1)S(1)}, bf16[1,8,80,640]{3,2,1,0:T(8,128)(2,1)S(1)}, u32[]{:S(2)}, u32[]{:S(2)}) collective-permute-start(bf16[1,8,80,640]{3,2,1,0:T(8,128)(2,1)S(1)} %get-tuple-element.213.refs_10_), channel_id=1, source_target_pairs={{0,4},{2,6},{4,0},{6,2},{8,12},{10,14},{12,8},{14,10},{16,20},{18,... | collective-permute-start | bytes 2457608 | tf_op jit(solution)/shard_map/ppermute | solution.py:62
  388.4 37.5 %collective-permute-start.53 = (bf16[2,640,512]{2,1,0:T(8,128)(2,1)S(1)}, bf16[2,640,512]{2,1,0:T(8,128)(2,1)S(1)}, u32[]{:S(2)}, u32[]{:S(2)}) collective-permute-start(bf16[2,640,512]{2,1,0:T(8,128)(2,1)S(1)} %get-tuple-element.222), channel_id=1, source_target_pairs={{0,2},{2,0},{4,6},{6,4},{8,10},{10,8},{12,14},{14,12},{16,18},{18,... | collective-permute-start | bytes 3932168 | tf_op jit(solution)/shard_map/ppermute | solution.py:62
  434.8 18.3 %collective-permute-start.54 = (bf16[1280,512]{1,0:T(8,128)(2,1)}, bf16[1280,512]{1,0:T(8,128)(2,1)}, u32[]{:S(2)}, u32[]{:S(2)}) collective-permute-start(bf16[1280,512]{1,0:T(8,128)(2,1)} %fusion.12), channel_id=1, source_target_pairs={{0,1},{1,0},{2,3},{3,2},{4,5},{5,4},{6,7},{7,6},{8,9},{9,8},{10,11... | collective-permute-start | bytes 3932168 | tf_op jit(solution)/shard_map/ppermute | solution.py:62
  444.2 29.5 %collective-permute-start.61 = (bf16[1,8,80,640]{3,2,1,0:T(8,128)(2,1)S(1)}, bf16[1,8,80,640]{3,2,1,0:T(8,128)(2,1)S(1)}, u32[]{:S(2)}, u32[]{:S(2)}) collective-permute-start(bf16[1,8,80,640]{3,2,1,0:T(8,128)(2,1)S(1)} %get-tuple-element.235), channel_id=1, source_target_pairs={{0,2},{2,0},{4,6},{6,4},{8,10},{10,8},{12,14},{14,12},{16,18},{18,... | collective-permute-start | bytes 2457608 | tf_op jit(solution)/shard_map/ppermute | solution.py:62
  444.6 29.1 %collective-permute-start.62 = (bf16[1,8,80,640]{3,2,1,0:T(8,128)(2,1)S(1)}, bf16[1,8,80,640]{3,2,1,0:T(8,128)(2,1)S(1)}, u32[]{:S(2)}, u32[]{:S(2)}) collective-permute-start(bf16[1,8,80,640]{3,2,1,0:T(8,128)(2,1)S(1)} %get-tuple-element.237), channel_id=1, source_target_pairs={{0,4},{2,6},{4,0},{6,2},{8,12},{10,14},{12,8},{14,10},{16,20},{18,... | collective-permute-start | bytes 2457608 | tf_op jit(solution)/shard_map/ppermute | solution.py:62
  447.5 26.2 %collective-permute-start.60 = (bf16[2,2,80,640]{3,2,1,0:T(8,128)(2,1)S(1)}, bf16[2,2,80,640]{3,2,1,0:T(8,128)(2,1)S(1)}, u32[]{:S(2)}, u32[]{:S(2)}) collective-permute-start(bf16[2,2,80,640]{3,2,1,0:T(8,128)(2,1)S(1)} %get-tuple-element.233), channel_id=1, source_target_pairs={{0,8},{2,10},{4,12},{6,14},{8,0},{10,2},{12,4},{14,6},{16,24},{18,... | collective-permute-start | bytes 1228808 | tf_op jit(solution)/shard_map/ppermute | solution.py:62
  471.4 41.8 %collective-permute-start.55 = (bf16[1280,512]{1,0:T(8,128)(2,1)}, bf16[1280,512]{1,0:T(8,128)(2,1)}, u32[]{:S(2)}, u32[]{:S(2)}) collective-permute-start(bf16[1280,512]{1,0:T(8,128)(2,1)} %get-tuple-element.354), channel_id=1, source_target_pairs={{0,1},{1,0},{2,3},{3,2},{4,5},{5,4},{6,7},{7,6},{8,9},{9,8},{10,11... | collective-permute-start | bytes 3932168 | tf_op jit(solution)/shard_map/ppermute | solution.py:62
  489.2 20.1 %collective-permute-start.67 = (bf16[1,8,80,640]{3,2,1,0:T(8,128)(2,1)}, bf16[1,8,80,640]{3,2,1,0:T(8,128)(2,1)}, u32[]{:S(2)}, u32[]{:S(2)}) collective-permute-start(bf16[1,8,80,640]{3,2,1,0:T(8,128)(2,1)} %get-tuple-element.247), channel_id=1, source_target_pairs={{0,2},{2,0},{4,6},{6,4},{8,10},{10,8},{12,14},{14,12},{16,18},{18,... | collective-permute-start | bytes 2457608 | tf_op jit(solution)/shard_map/ppermute | solution.py:62
  489.2 20.1 %collective-permute-start.68 = (bf16[1,8,80,640]{3,2,1,0:T(8,128)(2,1)}, bf16[1,8,80,640]{3,2,1,0:T(8,128)(2,1)}, u32[]{:S(2)}, u32[]{:S(2)}) collective-permute-start(bf16[1,8,80,640]{3,2,1,0:T(8,128)(2,1)} %get-tuple-element.249), channel_id=1, source_target_pairs={{0,4},{2,6},{4,0},{6,2},{8,12},{10,14},{12,8},{14,10},{16,20},{18,... | collective-permute-start | bytes 2457608 | tf_op jit(solution)/shard_map/ppermute | solution.py:62
  498.5 23.9 %collective-permute-start.56 = (bf16[1280,640]{1,0:T(8,128)(2,1)}, bf16[1280,640]{1,0:T(8,128)(2,1)}, u32[]{:S(2)}, u32[]{:S(2)}) collective-permute-start(bf16[1280,640]{1,0:T(8,128)(2,1)} %convolution_convert_fusion.9), channel_id=1, source_target_pairs={{0,1},{1,0},{2,3},{3,2},{4,5},{5,4},{6,7},{7,6},{8,9},{9,8},{10,11... | collective-permute-start | bytes 4915208 | tf_op jit(solution)/shard_map/ppermute | solution.py:62
  531.3 25.4 %collective-permute-start.72 = (bf16[2,2,80,640]{3,2,1,0:T(8,128)(2,1)S(1)}, bf16[2,2,80,640]{3,2,1,0:T(8,128)(2,1)S(1)}, u32[]{:S(2)}, u32[]{:S(2)}) collective-permute-start(bf16[2,2,80,640]{3,2,1,0:T(8,128)(2,1)S(1)} %get-tuple-element.257), channel_id=1, source_target_pairs={{0,8},{2,10},{4,12},{6,14},{8,0},{10,2},{12,4},{14,6},{16,24},{18,... | collective-permute-start | bytes 1228808 | tf_op jit(solution)/shard_map/ppermute | solution.py:62
  535.9 20.8 %collective-permute-start.73 = (bf16[1,8,80,640]{3,2,1,0:T(8,128)(2,1)S(1)}, bf16[1,8,80,640]{3,2,1,0:T(8,128)(2,1)S(1)}, u32[]{:S(2)}, u32[]{:S(2)}) collective-permute-start(bf16[1,8,80,640]{3,2,1,0:T(8,128)(2,1)S(1)} %get-tuple-element.226.refs_8_), channel_id=1, source_target_pairs={{0,2},{2,0},{4,6},{6,4},{8,10},{10,8},{12,14},{14,12},{16,18},{18,... | collective-permute-start | bytes 2457608 | tf_op jit(solution)/shard_map/ppermute | solution.py:62
  536.2 20.5 %collective-permute-start.74 = (bf16[1,8,80,640]{3,2,1,0:T(8,128)(2,1)S(1)}, bf16[1,8,80,640]{3,2,1,0:T(8,128)(2,1)S(1)}, u32[]{:S(2)}, u32[]{:S(2)}) collective-permute-start(bf16[1,8,80,640]{3,2,1,0:T(8,128)(2,1)S(1)} %get-tuple-element.228.refs_10_), channel_id=1, source_target_pairs={{0,4},{2,6},{4,0},{6,2},{8,12},{10,14},{12,8},{14,10},{16,20},{18,... | collective-permute-start | bytes 2457608 | tf_op jit(solution)/shard_map/ppermute | solution.py:62
  547.8 38.7 %collective-permute-start.75 = (bf16[2,640,512]{2,1,0:T(8,128)(2,1)S(1)}, bf16[2,640,512]{2,1,0:T(8,128)(2,1)}, u32[]{:S(2)}, u32[]{:S(2)}) collective-permute-start(bf16[2,640,512]{2,1,0:T(8,128)(2,1)S(1)} %get-tuple-element.266), channel_id=1, source_target_pairs={{0,2},{2,0},{4,6},{6,4},{8,10},{10,8},{12,14},{14,12},{16,18},{18,... | collective-permute-start | bytes 3932168 | tf_op jit(solution)/shard_map/ppermute | solution.py:62
  558.5 47.8 %collective-permute-start.77 = (bf16[2,1,80,640]{3,2,1,0:T(8,128)(2,1)}, bf16[2,1,80,640]{3,2,1,0:T(8,128)(2,1)}, u32[]{:S(2)}, u32[]{:S(2)}) collective-permute-start(bf16[2,1,80,640]{3,2,1,0:T(8,128)(2,1)} %get-tuple-element.259.refs_10_), channel_id=1, source_target_pairs={{0,16},{2,18},{4,20},{6,22},{8,24},{10,26},{12,28},{14,30},{16,0},... | collective-permute-start | bytes 614408 | tf_op jit(solution)/shard_map/ppermute | solution.py:62
  559.9 48.1 %collective-permute-start.78 = (bf16[1,4,80,640]{3,2,1,0:T(8,128)(2,1)}, bf16[1,4,80,640]{3,2,1,0:T(8,128)(2,1)}, u32[]{:S(2)}, u32[]{:S(2)}) collective-permute-start(bf16[1,4,80,640]{3,2,1,0:T(8,128)(2,1)} %get-tuple-element.261.refs_12_), channel_id=1, source_target_pairs={{0,4},{2,6},{4,0},{6,2},{8,12},{10,14},{12,8},{14,10},{16,20},{18,... | collective-permute-start | bytes 1228808 | tf_op jit(solution)/shard_map/ppermute | solution.py:62
  560.4 47.6 %collective-permute-start.79 = (bf16[1,4,80,640]{3,2,1,0:T(8,128)(2,1)}, bf16[1,4,80,640]{3,2,1,0:T(8,128)(2,1)}, u32[]{:S(2)}, u32[]{:S(2)}) collective-permute-start(bf16[1,4,80,640]{3,2,1,0:T(8,128)(2,1)} %get-tuple-element.263.refs_14_), channel_id=1, source_target_pairs={{0,2},{2,0},{4,6},{6,4},{8,10},{10,8},{12,14},{14,12},{16,18},{18,... | collective-permute-start | bytes 1228808 | tf_op jit(solution)/shard_map/ppermute | solution.py:62
  596.8 19.1 %collective-permute-start.76 = (bf16[1280,512]{1,0:T(8,128)(2,1)}, bf16[1280,512]{1,0:T(8,128)(2,1)}, u32[]{:S(2)}, u32[]{:S(2)}) collective-permute-start(bf16[1280,512]{1,0:T(8,128)(2,1)} %fusion.11), channel_id=1, source_target_pairs={{0,1},{1,0},{2,3},{3,2},{4,5},{5,4},{6,7},{7,6},{8,9},{9,8},{10,11... | collective-permute-start | bytes 3932168 | tf_op jit(solution)/shard_map/ppermute | solution.py:62
  604.0 28.7 %collective-permute-start.81 = (bf16[1,8,80,640]{3,2,1,0:T(8,128)(2,1)}, bf16[1,8,80,640]{3,2,1,0:T(8,128)(2,1)}, u32[]{:S(2)}, u32[]{:S(2)}) collective-permute-start(bf16[1,8,80,640]{3,2,1,0:T(8,128)(2,1)} %get-tuple-element.272), channel_id=1, source_target_pairs={{0,2},{2,0},{4,6},{6,4},{8,10},{10,8},{12,14},{14,12},{16,18},{18,... | collective-permute-start | bytes 2457608 | tf_op jit(solution)/shard_map/ppermute | solution.py:62
  606.4 27.4 %collective-permute-start.82 = (bf16[1,8,80,640]{3,2,1,0:T(8,128)(2,1)}, bf16[1,8,80,640]{3,2,1,0:T(8,128)(2,1)S(1)}, u32[]{:S(2)}, u32[]{:S(2)}) collective-permute-start(bf16[1,8,80,640]{3,2,1,0:T(8,128)(2,1)} %copy-done.61), channel_id=1, source_target_pairs={{0,4},{2,6},{4,0},{6,2},{8,12},{10,14},{12,8},{14,10},{16,20},{18,... | collective-permute-start | bytes 2457608 | tf_op jit(solution)/shard_map/ppermute | solution.py:62
  611.6 22.2 %collective-permute-start.80 = (bf16[2,2,80,640]{3,2,1,0:T(8,128)(2,1)S(1)}, bf16[2,2,80,640]{3,2,1,0:T(8,128)(2,1)S(1)}, u32[]{:S(2)}, u32[]{:S(2)}) collective-permute-start(bf16[2,2,80,640]{3,2,1,0:T(8,128)(2,1)S(1)} %get-tuple-element.270), channel_id=1, source_target_pairs={{0,8},{2,10},{4,12},{6,14},{8,0},{10,2},{12,4},{14,6},{16,24},{18,... | collective-permute-start | bytes 1228808 | tf_op jit(solution)/shard_map/ppermute | solution.py:62
  629.7 38.7 %collective-permute-start.87 = (bf16[1,8,80,640]{3,2,1,0:T(8,128)(2,1)S(1)}, bf16[1,8,80,640]{3,2,1,0:T(8,128)(2,1)S(1)}, u32[]{:S(2)}, u32[]{:S(2)}) collective-permute-start(bf16[1,8,80,640]{3,2,1,0:T(8,128)(2,1)S(1)} %get-tuple-element.284), channel_id=1, source_target_pairs={{0,2},{2,0},{4,6},{6,4},{8,10},{10,8},{12,14},{14,12},{16,18},{18,... | collective-permute-start | bytes 2457608 | tf_op jit(solution)/shard_map/ppermute | solution.py:62
  632.6 35.8 %collective-permute-start.88 = (bf16[1,8,80,640]{3,2,1,0:T(8,128)(2,1)S(1)}, bf16[1,8,80,640]{3,2,1,0:T(8,128)(2,1)S(1)}, u32[]{:S(2)}, u32[]{:S(2)}) collective-permute-start(bf16[1,8,80,640]{3,2,1,0:T(8,128)(2,1)S(1)} %get-tuple-element.286), channel_id=1, source_target_pairs={{0,4},{2,6},{4,0},{6,2},{8,12},{10,14},{12,8},{14,10},{16,20},{18,... | collective-permute-start | bytes 2457608 | tf_op jit(solution)/shard_map/ppermute | solution.py:62
  637.1 24.3 %collective-permute-start.84 = (bf16[1,4,80,640]{3,2,1,0:T(8,128)(2,1)S(1)}, bf16[1,4,80,640]{3,2,1,0:T(8,128)(2,1)S(1)}, u32[]{:S(2)}, u32[]{:S(2)}) collective-permute-start(bf16[1,4,80,640]{3,2,1,0:T(8,128)(2,1)S(1)} %get-tuple-element.279), channel_id=1, source_target_pairs={{0,4},{2,6},{4,0},{6,2},{8,12},{10,14},{12,8},{14,10},{16,20},{18,... | collective-permute-start | bytes 1228808 | tf_op jit(solution)/shard_map/ppermute | solution.py:62
  638.1 23.4 %collective-permute-start.85 = (bf16[1,4,80,640]{3,2,1,0:T(8,128)(2,1)S(1)}, bf16[1,4,80,640]{3,2,1,0:T(8,128)(2,1)S(1)}, u32[]{:S(2)}, u32[]{:S(2)}) collective-permute-start(bf16[1,4,80,640]{3,2,1,0:T(8,128)(2,1)S(1)} %get-tuple-element.280), channel_id=1, source_target_pairs={{0,2},{2,0},{4,6},{6,4},{8,10},{10,8},{12,14},{14,12},{16,18},{18,... | collective-permute-start | bytes 1228808 | tf_op jit(solution)/shard_map/ppermute | solution.py:62
  647.2 19.8 %collective-permute-start.97 = (f32[2,2640]{1,0:T(2,128)S(1)}, f32[2,2640]{1,0:T(2,128)S(1)}, u32[]{:S(2)}, u32[]{:S(2)}) collective-permute-start(f32[2,2640]{1,0:T(2,128)S(1)} %add.287), channel_id=1, source_target_pairs={{0,8},{2,10},{4,12},{6,14},{8,0},{10,2},{12,4},{14,6},{16,24},{18,... | collective-permute-start | bytes 63368 | tf_op jit(solution)/shard_map/ppermute | solution.py:62
  667.0 22.4 %collective-permute-start.98 = (f32[2,2640]{1,0:T(2,128)S(1)}, f32[2,2640]{1,0:T(2,128)S(1)}, u32[]{:S(2)}, u32[]{:S(2)}) collective-permute-start(f32[2,2640]{1,0:T(2,128)S(1)} %add.288), channel_id=1, source_target_pairs={{0,16},{2,18},{4,20},{6,22},{8,24},{10,26},{12,28},{14,30},{16,0},... | collective-permute-start | bytes 63368 | tf_op jit(solution)/shard_map/ppermute | solution.py:62
  (234 other events, 1896.7 us)

commit v5 on v4

--- a/solution.py
+++ b/solution.py
@@ -39,22 +39,8 @@
     )
 
 
-def inverse_root(source):
-    return lax.rsqrt(jnp.mean(source * source, axis=0, keepdims=True) + EPSILON)
-
-
 def softplus(values):
     return jnp.log1p(jnp.exp(values))
-
-
-def norm_backward(source, inverse, gain, incoming):
-    unit = source * inverse
-    gain_grad = jnp.sum(incoming * unit, axis=1)
-    scaled = incoming * gain
-    return (
-        gain_grad,
-        inverse * (scaled - unit * jnp.mean(scaled * unit, axis=0, keepdims=True)),
-    )
 
 
 def pair_swap(values, axis, bit):
@@ -98,6 +84,7 @@
     def __init__(self, pairs, orders):
         self.first, self.rest = orders
         self.queue = [jnp.stack(pair)[:, None] for pair in pairs]
+        self.left = len(pairs)
         self.early, self.early_at = None, 0
         self.late, self.late_at = None, 0
         self.ready = []
@@ -126,13 +113,27 @@
             plans.append((members, before, blocks // before, parts, len(shapes)))
             shapes += [(members // parts, 2 * blocks, rows, width)] * parts
         count = len(jobs)
+        merged = self.late is not None and self.merges() and (
+            self.late_at + 1 == len(self.rest[0])
+        )
+        if merged:
+            at = plans[-2][-1]
+            shapes[at:] = [(2,) + shapes[at][1:]]
+        following = self.queue[:1]
 
         def join(bit_ref, *refs):
-            outs = refs[len(refs) - len(shapes) :]
+            outs = refs[len(refs) - len(shapes) - len(following) :]
+            if following:
+                outs[-1][...] = refs[2 * count][...]
             for job, (members, before, blocks, parts, at) in enumerate(plans):
                 bit = bit_ref[job]
                 for member in range(members):
-                    out, row = (outs[at + member], 0) if parts > 1 else (outs[at], member)
+                    if merged and job == count - 1:
+                        out, row = outs[at - 1], 1
+                    elif parts > 1:
+                        out, row = outs[at + member], 0
+                    else:
+                        out, row = outs[at], member
                     for step in range(before):
                         here = pl.ds(step * blocks, blocks)
                         place = 2 * step * blocks
@@ -143,21 +144,36 @@
         outs = quick_call(
             join,
             "join_halves",
-            [dp_bits([done[-1] for _, done in jobs]), *[values for values, _ in jobs], *got],
+            [
+                dp_bits([done[-1] for _, done in jobs]),
+                *[values for values, _ in jobs],
+                *got,
+                *following,
+            ],
             after,
-            [jax.ShapeDtypeStruct(shape, jnp.bfloat16) for shape in shapes],
-        )
+            [
+                jax.ShapeDtypeStruct(shape, jnp.bfloat16)
+                for shape in shapes + [values.shape for values in following]
+            ],
+        )
+        if following:
+            self.queue[0] = outs.pop()
         if early:
             self.early_at += 1
             done = self.early_at == len(self.first)
             self.early = outs[:2] if done else outs[0]
         if self.late is not None:
-            self.late, self.late_at = outs[-2:], self.late_at + 1
+            self.late, self.late_at = outs[-1:] if merged else outs[-2:], self.late_at + 1
             if self.late_at == len(self.rest[0]):
                 width = self.late[0].shape[-1]
-                self.ready.append([values.reshape((-1, width)) for values in self.late])
+                shape = (2, -1, width) if merged else (-1, width)
+                self.ready.append([values.reshape(shape) for values in self.late])
                 self.late = None
+                self.left -= 1
         return outs
+
+    def merges(self):
+        return self.left % 3 == 1
 
     def take(self):
         while not self.ready:
@@ -171,10 +187,15 @@
         self.bits = sorted(self.first + self.rest[0], reverse=True)
         self.queue, self.late, self.early, self.done = [], None, None, []
 
-    def push(self, *pair):
+    def push(self, *pair, came=(None, None)):
         rows = pair[0].shape[0] >> len(self.bits)
         shape = (1, 1 << len(self.bits), rows, pair[0].shape[1])
-        self.queue.append([values.reshape(shape) for values in pair])
+        self.queue.append(
+            [
+                ([values.reshape(shape)], None if more is None else [more.reshape(shape)], order)
+                for values, more, order in zip(pair, came, self.rest)
+            ]
+        )
 
     def run(self, jobs, after):
         plans, ins, shapes, bits = [], [], [], []
@@ -237,9 +258,8 @@
     def enter(self):
         if self.late is not None or not self.queue:
             return []
-        pair = self.queue.pop(0)
         jobs = [
-            ([values], None, self.bits, order[-1], False) for values, order in zip(pair, self.rest)
+            (held, came, self.bits, order[-1], False) for held, came, order in self.queue.pop(0)
         ]
         outs = self.run(jobs, ())
         self.late = (outs[0::2], outs[1::2], 1)
@@ -293,53 +313,88 @@
     return step == len(bits)
 
 
-def total_sum(values):
-    for axis in ("tensor", "dp"):
-        bit = 1
-        while bit < lax.axis_size(axis):
-            values = values + pair_swap(values, axis, bit)
-            bit *= 2
-    return values
-
-
 def gather_tokens(local):
     if lax.axis_size("tensor") != 2:
-        return lax.all_gather(local, "tensor", axis=1, tiled=True)
+        values = lax.all_gather(local, "tensor", axis=1, tiled=True)
+        return values, values
     other = pair_swap(local, "tensor", 1)
     upper = lax.axis_index("tensor") != 0
-    return jnp.concatenate([jnp.where(upper, other, local), jnp.where(upper, local, other)], axis=1)
-
-
-def far_tokens(normed):
+    values = [jnp.where(upper, other, local), jnp.where(upper, local, other)]
+    return jnp.concatenate(values, axis=1), other
+
+
+def far_part(normed):
     part = PROMPT_DEV // lax.axis_size("tensor")
     place = lax.axis_index("tensor") * part
-    return gather_tokens(pair_swap(lax.dynamic_slice_in_dim(normed, place, part, 1), "dp", 1))
+    return pair_swap(lax.dynamic_slice_in_dim(normed, place, part, 1), "dp", 1)
 
 
 def scatter_tokens(product, *values):
     if lax.axis_size("tensor") != 2:
-        return lax.psum_scatter(
-            lowered(product(*values)), "tensor", scatter_dimension=1, tiled=True
-        ).astype(jnp.float32)
+        return [
+            lax.psum_scatter(
+                lowered(product(*values)), "tensor", scatter_dimension=1, tiled=True
+            )
+        ]
     count = values[0].shape[1] // 2
     place = lax.axis_index("tensor")
     theirs = [lax.dynamic_slice_in_dim(v, (1 - place) * count, count, 1) for v in values]
     got = pair_swap(lowered(product(*theirs)), "tensor", 1)
     mine = [lax.dynamic_slice_in_dim(v, place * count, count, 1) for v in values]
-    return product(*mine) + got.astype(jnp.float32)
-
-
-def feed_parts(values):
+    return [lowered(product(*mine)), got]
+
+
+def feed_parts(both):
     if lax.axis_size("tensor") != 2:
-        return [lax.all_gather(values, "tensor", axis=1, tiled=True)]
-    return [values, pair_swap(values, "tensor", 1)]
+        whole = lax.all_gather(both, "tensor", axis=2, tiled=True)
+        return [whole[0]], [whole[1]]
+    other = pair_swap(both, "tensor", 1)
+    return [both[0], other[0]], [both[1], other[1]]
 
 
 def feed_total(parts):
     if lax.axis_size("tensor") != 2:
-        return lax.psum_scatter(lowered(parts[0]), "tensor", scatter_dimension=1, tiled=True)
-    got = pair_swap(lowered(parts[1]), "tensor", 1)
-    return lowered(parts[0] + got.astype(jnp.float32))
+        whole = lax.psum_scatter(lowered(parts[0]), "tensor", scatter_dimension=1, tiled=True)
+        return whole, None
+    return lowered(parts[0]), pair_swap(lowered(parts[1]), "tensor", 1)
+
+
+def tied(gain, after):
+    if not after:
+        return gain
+    corner = after[0][(0,) * after[0].ndim].astype(jnp.float32)
+    return gain + jnp.minimum((corner > 3e38).astype(jnp.int32), 0).astype(jnp.float32)
+
+
+def norm(terms, gain, after=()):
+    total = sum(term.astype(jnp.float32) for term in terms)
+    inverse = lax.rsqrt(jnp.mean(total * total, axis=0, keepdims=True) + EPSILON)
+    return total, inverse, lowered(total * inverse * tied(gain, after))
+
+
+def norm_back(source, inverse, gain, grad, terms, after=()):
+    incoming = sum(term.astype(jnp.float32) for term in terms)
+    unit = source * inverse
+    gain_grad = jnp.sum(incoming * unit, axis=1)
+    scaled = incoming * tied(gain, after)
+    total = grad + inverse * (scaled - unit * jnp.mean(scaled * unit, axis=0, keepdims=True))
+    return total, lowered(total), gain_grad
+
+
+def first_slot(_):
+    return jnp.zeros((1,), jnp.int32)
+
+
+def add_back(own_keys, own_values, back, after):
+    def kernel(_, keys_ref, values_ref, back_ref, *refs):
+        for place, (ref, out) in enumerate(zip((keys_ref, values_ref), refs[-2:])):
+            prompt = ref[:, :PROMPT_DEV].astype(jnp.float32) + back_ref[place].astype(jnp.float32)
+            out[:, :PROMPT_DEV] = lowered(prompt)
+            out[:, PROMPT_DEV:] = ref[:, PROMPT_DEV:]
+
+    out = [jax.ShapeDtypeStruct(own_keys.shape, jnp.bfloat16)] * 2
+    arrays = [first_slot(back), own_keys, own_values, back]
+    return quick_call(kernel, "add_back", arrays, after, out)
 
 
 def key_parts(tile):
@@ -365,44 +420,41 @@
     return [(tile, slice(tile * TILE, tile * TILE + TILE)) for tile in range(tokens // TILE)]
 
 
-def by_side(side_ref, reference, meets, skips):
-    prompt = [at for tile, at in spans(reference) if tile * TILE < PROMPT_DEV]
-
-    @pl.when(side_ref[0] == 0)
-    def _():
-        for at in prompt:
-            skips(at)
-
-    @pl.when(side_ref[0] != 0)
-    def _():
-        for at in prompt:
-            meets(at)
-
-    for tile, at in spans(reference):
-        if at not in prompt:
-            meets(at)
+def ahead(items, first, second):
+    items = list(items)
+    held = first(items[0])
+    for place, item in enumerate(items):
+        following = first(items[place + 1]) if place + 1 < len(items) else None
+        second(item, held)
+        held = following
 
 
 def own_forward(start_ref, q_ref, k_ref, v_ref, sum_ref, top_ref, total_ref):
     keys = k_ref[...].T
-    for tile, at in spans(q_ref):
+
+    def scores_of(item):
+        tile, at = item
         query, start = q_ref[:, at], start_ref[:, at]
-        parts = []
-        for key, count, kind in key_parts(tile):
-            scores = dot_nn(keys[key : key + count], query)
-            scores = masked(scores, kind, key, tile * TILE, start)
-            parts.append((scores, v_ref[:, key : key + count]))
-        highest = jnp.max(parts[0][0], axis=0, keepdims=True)
-        for scores, _ in parts[1:]:
+        return [
+            masked(dot_nn(keys[key : key + count], query), kind, key, tile * TILE, start)
+            for key, count, kind in key_parts(tile)
+        ]
+
+    def mix(item, parts):
+        tile, at = item
+        highest = jnp.max(parts[0], axis=0, keepdims=True)
+        for scores in parts[1:]:
             highest = jnp.maximum(highest, jnp.max(scores, axis=0, keepdims=True))
         total, mixed = 0.0, 0.0
-        for scores, value in parts:
+        for scores, (key, count, _) in zip(parts, key_parts(tile)):
             weights = jnp.exp2(scores - highest)
             total = total + jnp.sum(weights, axis=0, keepdims=True)
-            mixed = mixed + dot_nn(value, lowered(weights))
+            mixed = mixed + dot_nn(v_ref[:, key : key + count], lowered(weights))
         sum_ref[:, at] = mixed
         top_ref[:, at] = highest
         total_ref[:, at] = total
+
+    ahead(spans(q_ref), scores_of, mix)
 
 
 def far_forward(
@@ -410,8 +462,10 @@
 ):
     keys = k_ref[...].T
 
-    def meets(at):
-        scores = dot_nn(keys, q_ref[:, at])
+    def scores_of(at):
+        return dot_nn(keys, q_ref[:, at])
+
+    def mix(at, scores):
         highest = jnp.maximum(top_ref[:, at], jnp.max(scores, axis=0, keepdims=True))
         weights = jnp.exp2(scores - highest)
         scale = jnp.exp2(top_ref[:, at] - highest)
@@ -420,11 +474,20 @@
         out_ref[:, at] = lowered(mixed / total)
         lse_ref[:, at] = highest + jnp.log2(total)
 
-    def skips(at):
-        out_ref[:, at] = lowered(sum_ref[:, at] / total_ref[:, at])
-        lse_ref[:, at] = top_ref[:, at] + jnp.log2(total_ref[:, at])
-
-    by_side(side_ref, q_ref, meets, skips)
+    tiles = [at for _, at in spans(q_ref)]
+    conts = [at for tile, at in spans(q_ref) if tile * TILE >= PROMPT_DEV]
+
+    @pl.when(side_ref[0] == 0)
+    def _():
+        for at in tiles:
+            if at not in conts:
+                out_ref[:, at] = lowered(sum_ref[:, at] / total_ref[:, at])
+                lse_ref[:, at] = top_ref[:, at] + jnp.log2(total_ref[:, at])
+        ahead(conts, scores_of, mix)
+
+    @pl.when(side_ref[0] != 0)
+    def _():
+        ahead(tiles, scores_of, mix)
 
 
 def score_grads(scores, lse, d_shares, delta):
@@ -440,21 +503,22 @@
         out_ref[...].astype(jnp.float32) * grad_ref[...].astype(jnp.float32), axis=0, keepdims=True
     )
 
-    def terms(at):
-        query, grad = q_ref[:, at], grad_ref[:, at]
-        shares, d_scores = score_grads(
-            dot_nn(keys, query), lse_ref[:, at], dot_nn(values, grad), delta_ref[:, at]
-        )
-        dq_ref[:, at] = dot_nn(k_ref[...], d_scores)
-        return dot_nt(query, d_scores), dot_nt(grad, shares)
+    def begin(at):
+        return dot_nn(keys, q_ref[:, at]), dot_nn(values, grad_ref[:, at])
 
     def close(tiles):
-        dk, dv = 0.0, 0.0
-        for at in tiles:
-            k_term, v_term = terms(at)
-            dk, dv = dk + k_term, dv + v_term
-        dkv_ref[0] = lowered(dk * LN_TWO)
-        dkv_ref[1] = lowered(dv)
+        sums = [0.0, 0.0]
+
+        def terms(at, held):
+            scores, d_shares = held
+            shares, d_scores = score_grads(scores, lse_ref[:, at], d_shares, delta_ref[:, at])
+            dq_ref[:, at] = dot_nn(k_ref[...], d_scores)
+            sums[0] = sums[0] + dot_nt(q_ref[:, at], d_scores)
+            sums[1] = sums[1] + dot_nt(grad_ref[:, at], shares)
+
+        ahead(tiles, begin, terms)
+        dkv_ref[0] = lowered(sums[0] * LN_TWO)
+        dkv_ref[1] = lowered(sums[1])
 
     tiles = [at for _, at in spans(q_ref)]
     conts = [at for tile, at in spans(q_ref) if tile * TILE >= PROMPT_DEV]
@@ -489,35 +553,46 @@
     v_total,
 ):
     keys, values = k_ref[...].T, v_ref[...].T
-    seen = set()
-    scale = 0.0
+    seen, dqs, scales = set(), {}, [0.0]
+
+    def begin(item):
+        (tile, at), (key, count, kind), _ = item
+        scores = dot_nn(keys[key : key + count], q_ref[:, at])
+        scores = masked(scores, kind, key, tile * TILE, start_ref[:, at])
+        return scores, dot_nn(values[key : key + count], grad_ref[:, at])
+
+    def terms(item, held):
+        (tile, at), (key, count, _), last = item
+        scores, d_shares = held
+        query, grad = q_ref[:, at], grad_ref[:, at]
+        shares, d_scores = score_grads(scores, lse_ref[:, at], d_shares, delta_ref[:, at])
+        dv = dot_nt(grad, shares)
+        dk = dot_nt(query, d_scores)
+        dq = dqs.get(tile, far_dq_ref[:, at]) + dot_nn(k_ref[:, key : key + count], d_scores)
+        dqs[tile] = dq
+        for offset in range(0, count, TILE):
+            there = slice(key + offset, key + offset + TILE)
+            here = slice(offset, offset + TILE)
+            if key + offset in seen:
+                k_total[:, there] += dk[:, here]
+                v_total[:, there] += dv[:, here]
+            else:
+                seen.add(key + offset)
+                k_total[:, there] = dk[:, here]
+                v_total[:, there] = dv[:, here]
+        if last:
+            dq_ref[:, at] = lowered(dq * gain_ref[...])
+            product = jnp.sum(dq * query.astype(jnp.float32), axis=1, keepdims=True)
+            scales[0] = scales[0] + product
+
+    items = []
     for tile, at in spans(q_ref):
-        query, grad = q_ref[:, at], grad_ref[:, at]
-        dq = far_dq_ref[:, at]
-        for key, count, kind in key_parts(tile):
-            scores = dot_nn(keys[key : key + count], query)
-            scores = masked(scores, kind, key, tile * TILE, start_ref[:, at])
-            shares, d_scores = score_grads(
-                scores, lse_ref[:, at], dot_nn(values[key : key + count], grad), delta_ref[:, at]
-            )
-            dv = dot_nt(grad, shares)
-            dk = dot_nt(query, d_scores)
-            dq = dq + dot_nn(k_ref[:, key : key + count], d_scores)
-            for offset in range(0, count, TILE):
-                there = slice(key + offset, key + offset + TILE)
-                here = slice(offset, offset + TILE)
-                if key + offset in seen:
-                    k_total[:, there] += dk[:, here]
-                    v_total[:, there] += dv[:, here]
-                else:
-                    seen.add(key + offset)
-                    k_total[:, there] = dk[:, here]
-                    v_total[:, there] = dv[:, here]
-        dq_ref[:, at] = lowered(dq * gain_ref[...])
-        scale = scale + jnp.sum(dq * query.astype(jnp.float32), axis=1, keepdims=True)
+        parts = key_parts(tile)
+        items += [((tile, at), part, part is parts[-1]) for part in parts]
+    ahead(items, begin, terms)
     dk_ref[...] = lowered(k_total[...] * LN_TWO)
     dv_ref[...] = lowered(v_total[...])
-    scale_ref[...] = scale
+    scale_ref[...] = scales[0]
 
 
 def rows_block(count):
@@ -533,7 +608,7 @@
 
 
 def per_head(kernel, name, heads, area, products, ins, outs, after=(), scratch=()):
-    flops = 2 * 256 * area * heads * products
+    flops = 40 * area * heads * products
     moved = sum(array.size * array.dtype.itemsize for _, array in ins)
     count = len(ins)
 
@@ -589,7 +664,7 @@
         "attention_far",
         heads,
         tokens * PROMPT_DEV,
-        3,
+        2,
         [
             (SCALAR, side),
             (all_rows, queries),
@@ -616,7 +691,7 @@
         "attention_far_back",
         heads,
         tokens * PROMPT_DEV,
-        6,
+        3,
         [
             (SCALAR, side),
             (all_rows, queries),
@@ -648,7 +723,7 @@
         "attention_own_back",
         heads,
         tokens * tokens * 5 // 8,
-        6,
+        4,
         [
             (same_block(1, tokens), start),
             (same_block(HD, 1), gain),
@@ -706,35 +781,48 @@
 
     gather = Gather(pairs, orders)
     stored = []
-    current = inputs.T
+    terms = [inputs.T]
+    ready = ()
     for layer in range(LAYERS):
         attn_gain = attention_gain[layer][:, None]
         ff_gain = feed_gain[layer][:, None]
-        inverse_attn = inverse_root(current)
-        normed = gather_tokens(lowered(current * inverse_attn * attn_gain))
-        far_normed = far_tokens(normed)
-        wk, wv = gather.take()
+        current, inverse_attn, low = norm(terms, attn_gain, ready)
+        normed, came = gather_tokens(low)
+        gather.tick(came)
+        if layer == 0:
+            far = far_part(normed)
+            gather.tick(far)
+            far_normed, came = gather_tokens(far)
+            gather.tick(came)
+            wk, wv = gather.take()
+            gather.tick()
         keys = lowered(dot_tn(wk, normed))
         values = lowered(dot_tn(wv, normed))
         gather.tick(keys, values)
-        far_keys = lowered(dot_tn(wk, far_normed))
-        far_values = lowered(dot_tn(wv, far_normed))
-        gather.tick(far_keys, far_values)
         wq, wo = gather.take()
         gain_q = softplus(query_scale[layer]) * LOG_TWO_E / math.sqrt(HD)
         gain_rows = jnp.tile(gain_q, heads)[:, None]
         queries = lowered(dot_tn(wq, normed) * (gain_rows * LOG_TWO_E))
         own_sum, top, total = attention_own(start, queries, keys, values, ())
-        ready = gather.tick(top)
+        if layer:
+            far = far_part(normed)
+            ready = gather.tick(top, far)
+            far_normed, _ = gather_tokens(far)
+        far_keys = lowered(dot_tn(wk, far_normed))
+        far_values = lowered(dot_tn(wv, far_normed))
+        if not layer:
+            ready = gather.tick(top, far_keys, far_values)
         mixed, lse = attention_far(side, queries, far_keys, far_values, own_sum, top, total, ready)
-        middle = current + scatter_tokens(lambda rows: dot_nn(wo, rows), mixed)
-        gather.tick(middle)
-        wu, wd = gather.take()
-        inverse_feed = inverse_root(middle)
-        feed = lowered(middle * inverse_feed * ff_gain)
-        ups, downs = feed_parts(wu), feed_parts(wd)
+        gather.tick(lse)
+        (both,) = gather.take()
+        terms = scatter_tokens(lambda rows: dot_nn(wo, rows), mixed)
+        ups, downs = feed_parts(both)
+        ready = gather.tick(terms[-1])
+        middle, inverse_feed, feed = norm([current, *terms], ff_gain, ready)
         uppers = [dot_tn(w, feed) for w in ups]
-        gather.tick(*uppers)
+        ready = gather.tick(*uppers)
+        if layer + 1 < LAYERS:
+            following = gather.take()
         hiddens = [lowered(upper * jax.nn.sigmoid(upper)) for upper in uppers]
         stored.append(
             (
@@ -744,12 +832,15 @@
                 (wk, wv, wq, wo, ups, downs),
             )
         )
-        current = middle + sum(dot_nn(w, hidden) for w, hidden in zip(downs, hiddens))
-        gather.tick(current)
+        terms = [middle, sum(dot_nn(w, hidden) for w, hidden in zip(downs, hiddens))]
+        if layer + 1 < LAYERS:
+            wk, wv = following
+    current = terms[0] + terms[1]
 
     sums = Scatter(orders)
     small_grads = [None] * LAYERS
     grad = cotangent.T
+    grad_low = lowered(grad)
     for layer in reversed(range(LAYERS)):
         (
             (source, inverse_attn, attn_gain, normed),
@@ -757,29 +848,33 @@
             (middle, inverse_feed, ff_gain, feed, uppers, hiddens),
             (wk, wv, wq, wo, ups, downs),
         ) = stored[layer]
-        grad_low = lowered(grad)
         d_uppers = []
         for w, upper in zip(downs, uppers):
             d_hidden = lowered(dot_tn(w, grad_low)).astype(jnp.float32)
             sigmoid = jax.nn.sigmoid(upper)
             d_uppers.append(lowered(d_hidden * (sigmoid * (1.0 + upper * (1.0 - sigmoid)))))
         d_feed = sum(dot_nn(w, d_upper) for w, d_upper in zip(ups, d_uppers))
-        feed_gain_grad, part = norm_backward(middle, inverse_feed, ff_gain, d_feed)
-        grad_middle = grad + part
-        sums.tick(grad_middle)
-        down_grad = feed_total([dot_nt(grad_low, hidden) for hidden in hiddens])
-        up_grad = feed_total([dot_nt(feed, d_upper) for d_upper in d_uppers])
-        sums.tick(down_grad, up_grad)
-        sums.push(down_grad, up_grad)
-        middle_low = gather_tokens(lowered(grad_middle))
+        ready = sums.tick(d_feed)
+        grad_middle, low, feed_gain_grad = norm_back(
+            middle, inverse_feed, ff_gain, grad, [d_feed], ready
+        )
+        middle_low, came = gather_tokens(low)
+        down_grad, down_came = feed_total([dot_nt(grad_low, hidden) for hidden in hiddens])
+        up_grad, up_came = feed_total([dot_nt(feed, d_upper) for d_upper in d_uppers])
+        if down_came is None:
+            stepped = sums.tick(came, down_grad, up_grad)
+            sums.push(down_grad, up_grad)
+        else:
+            stepped = sums.tick(came, down_came, up_came)
+            sums.push(down_grad, up_grad, came=(down_came, up_came))
         d_mixed = lowered(dot_tn(wo, middle_low))
         out_grad = lowered(dot_nt(middle_low, mixed))
-        ready = sums.enter()
+        ready = [*sums.enter(), *stepped]
         far_dq, delta, far_dkv = attention_far_back(
             side, queries, far_keys, far_values, mixed, d_mixed, lse, ready
         )
-        back = pair_swap(far_dkv, "dp", 1).astype(jnp.float32)
-        ready = sums.tick(delta, out_grad)
+        back = pair_swap(far_dkv, "dp", 1)
+        ready = sums.tick(delta)
         d_raw, own_dk, own_dv, scale_rows = attention_own_back(
             start,
             gain_q[:, None],
@@ -792,29 +887,35 @@
             far_dq,
             ready,
         )
-        sums.tick(scale_rows)
+        ready = sums.tick(scale_rows)
         query_grad = lowered(dot_nt(normed, d_raw))
         sums.push(out_grad, query_grad)
         sums.enter()
-        pad = ((0, 0), (0, tokens - PROMPT_DEV))
-        d_keys = lowered(own_dk.astype(jnp.float32) + jnp.pad(back[0], pad))
-        d_values = lowered(own_dv.astype(jnp.float32) + jnp.pad(back[1], pad))
+        d_keys, d_values = add_back(own_dk, own_dv, back, ready)
         scale_raw = jnp.sum(scale_rows.reshape(heads, HD), 0) / (gain_q * LOG_TWO_E)
         scale_grad = scale_raw * jax.nn.sigmoid(query_scale[layer]) * LOG_TWO_E / math.sqrt(HD)
-        d_normed = scatter_tokens(
+        terms = scatter_tokens(
             lambda dq, dk, dv: dot_nn(wq, dq) + dot_nn(wk, dk) + dot_nn(wv, dv),
             d_raw,
             d_keys,
             d_values,
         )
-        sums.tick(d_normed)
+        ready = sums.tick(terms[-1])
+        grad, grad_low, attn_gain_grad = norm_back(
+            source, inverse_attn, attn_gain, grad_middle, terms, ready
+        )
         key_grad = lowered(dot_nt(normed, d_keys))
         value_grad = lowered(dot_nt(normed, d_values))
         sums.push(key_grad, value_grad)
-        attn_gain_grad, part = norm_backward(source, inverse_attn, attn_gain, d_normed)
-        grad = grad_middle + part
-        sums.tick(grad)
+        sums.tick(grad, key_grad, value_grad)
         small_grads[layer] = jnp.concatenate([attn_gain_grad, feed_gain_grad, scale_grad])
+    small = jnp.stack(small_grads)
+    for axis in ("tensor", "dp"):
+        bit = 1
+        while bit < lax.axis_size(axis):
+            came = pair_swap(small, axis, bit)
+            after = sums.tick(came) if axis == "dp" else ()
+            small, bit = tied(small + came, after), 2 * bit
     done = sums.finish()
     layer_grads = []
     for layer in range(LAYERS):
@@ -825,7 +926,6 @@
         )
 
     summed = [jnp.stack(members) for members in zip(*layer_grads)]
-    small = total_sum(jnp.stack(small_grads))
     width = current.shape[0]
     return (
         current.T,

time: 723 us -> 686 us (0.949)
  waiting for transfers between devices: 189 us -> 145 us
  matrix products: 148 us -> 166 us
  Pallas kernels: 152 us -> 139 us
  starting transfers between devices: 126 us -> 115 us
    ppermute x99 -> x97, waiting for transfers between devices: 189 us -> 145 us  [pair_swap(): return lax.ppermute(values, axis, [(i, i ^ bit) for i in range(size)])]
    pallas_call x8, Pallas kernels: 99.7 us -> 76.5 us  [per_head(): pl.pallas_call(work, grid=(heads,), in_specs=[spec for spec, _ in ins] +...]
    dot_general x24, matrix products: 57.8 us -> 69.9 us  [dot_nn(): return jnp.dot(former, latter, preferred_element_type=jnp.float32)]
    pallas_call x34 -> x36, Pallas kernels: 51.9 us -> 62.8 us  [quick_call(): pl.pallas_call(kernel, in_specs=[SCALAR] + [WHOLE] * (len(arrays) - 1) +...]
    ppermute x99 -> x97, starting transfers between devices: 126 us -> 115 us  [pair_swap(): return lax.ppermute(values, axis, [(i, i ^ bit) for i in range(size)])]
    dot_general x20, matrix products: 38.7 us -> 49 us  [dot_tn(): lax.dot_general(former, latter, (((0,), (0,)), ((), ())), preferred_eleme...]
    slice x1 -> x11, local copies, waits for them, and re-layouts: 0.03 us -> 8.47 us  [the longest x9 4.63 us: tied(): corner = after[0][(0,) * after[0].ndim].astype(jnp.float32)]
    unnamed x370 -> x416, local copies, waits for them, and re-layouts: 48.4 us -> 46.3 us
  transfers between devices with their start and end apart: 99 -> 97, of which waited for: 37 -> 36; matrix products, arithmetic and copies ran while one was open for 25% -> 31% of each run, Pallas kernels for 17% -> 17%
where the time goes in v5:
time: 686 us; the launch traced here: 675 us
  matrix products  166 us (24%)
  waiting for transfers between devices  145 us (21%)
  Pallas kernels  139 us (20%)
  starting transfers between devices  115 us (17%)
  local copies, waits for them, and re-layouts  65.8 us (10%)
  other arithmetic  34.2 us (5%)
  between operations  9.55 us (1%)
    ppermute x97, waiting for transfers between devices, pair_swap(): return lax.ppermute(values, axis, [(i, i ^ bit) for i in range(size)])  145 us
    ppermute x97, starting transfers between devices, pair_swap(): return lax.ppermute(values, axis, [(i, i ^ bit) for i in range(size)])  115 us
    pallas_call x8, Pallas kernels, per_head(): pl.pallas_call(work, grid=(heads,), in_specs=[spec for spec, _ in ins] +...  76.5 us
    dot_general x24, matrix products, dot_nn(): return jnp.dot(former, latter, preferred_element_type=jnp.float32)  69.9 us
    pallas_call x36, Pallas kernels, quick_call(): pl.pallas_call(kernel, in_specs=[SCALAR] + [WHOLE] * (len(arrays) - 1) +...  62.8 us
    dot_general x20, matrix products, dot_tn(): lax.dot_general(former, latter, (((0,), (0,)), ((), ())), preferred_eleme...  49 us
    dot_general x16, matrix products, dot_nt(): lax.dot_general(former, latter, (((1,), (1,)), ((), ())), preferred_eleme...  46.6 us
    unnamed x416, local copies, waits for them, and re-layouts  46.3 us
  transfers between devices with their start and end apart: 97, of which 36 were waited for; matrix products, arithmetic and copies ran while one was open for 31% of the time, Pallas kernels for 17%

profile of v5, /device:TPU:0, one launch (start us, length us, event | category | flops | bytes accessed | tf_op | source)
XLA Modules:
  0.0 675.1 jit_solution(17674046781235194064)
XLA Ops:
  6.2 3.7 collective-permute-start
  20.9 10.1 %collective-permute-done.3.refs_3_ = bf16[1280,256]{1,0:T(8,128)(2,1)S(1)} collective-permute-done((bf16[1280,256]{1,0:T(8,128)(2,1)S(1)}, bf16[1280,256]{1,0:T(8,128)(2,1)S(1)}, u32[]{:S(2)}, u32[]{:S(2)}) %collective-permute-start.3) | collective-permute-done | bytes 655392 | tf_op jit(solution)/shard_map/ppermute | solution.py:48
  37.9 9.0 %collective-permute-done.4.refs_3_ = bf16[2,1,80,640]{3,2,1,0:T(8,128)(2,1)S(1)} collective-permute-done((bf16[2,1,80,640]{3,2,1,0:T(8,128)(2,1)S(1)}, bf16[2,1,80,640]{3,2,1,0:T(8,128)(2,1)S(1)}, u32[]{:S(2)}, u32[]{:S(2)}) %collective-permute-start.4) | collective-permute-done | bytes 204832 | tf_op jit(solution)/shard_map/ppermute | solution.py:48
  51.1 9.2 %collective-permute-done.8.refs_3_ = bf16[2,2,80,640]{3,2,1,0:T(8,128)(2,1)S(1)} collective-permute-done((bf16[2,2,80,640]{3,2,1,0:T(8,128)(2,1)}, bf16[2,2,80,640]{3,2,1,0:T(8,128)(2,1)S(1)}, u32[]{:S(2)}, u32[]{:S(2)}) %collective-permute-start.8) | collective-permute-done | bytes 409632 | tf_op jit(solution)/shard_map/ppermute | solution.py:48
  60.3 8.0 %collective-permute-done.9.refs_4_ = bf16[1,8,80,640]{3,2,1,0:T(8,128)(2,1)} collective-permute-done((bf16[1,8,80,640]{3,2,1,0:T(8,128)(2,1)S(1)}, bf16[1,8,80,640]{3,2,1,0:T(8,128)(2,1)}, u32[]{:S(2)}, u32[]{:S(2)}) %collective-permute-start.9) | collective-permute-done | bytes 819232 | tf_op jit(solution)/shard_map/ppermute | solution.py:48
  68.6 3.6 join_halves.17
  74.8 4.5 convolution_convert_fusion.23.refs_7_.refs_2_.refs_3_
  79.3 3.7 collective-permute-done.11.refs_3_
  88.5 5.2 collective-permute-start.14
  111.0 9.8 %attention_own.2 = (f32[640,1024]{1,0:T(8,128)S(1)}, f32[8,1,1024]{2,1,0:T(1,128)S(1)}, f32[8,1,1024]{2,1,0:T(1,128)S(1)}) custom-call(s32[1,1024]{1,0:T(1,128)S(1)} %bitcast.268, bf16[640,1024]{1,0:T(8,128)(2,1)S(1)} %multiply_convert_fusion.4.refs_1_.refs_2_, bf16[640,1024]{1,0:T(8,128)(2,1)S(1)} %copy-done.4, bf16[640,1024]{1,0:T(8,128)(2,1)S(1)} %copy-done.6), custom_call_target="tpu_custom_call" | custom-call | flops 629145600 | bytes 3936256 | tf_op jit(solution)/shard_map/attention_own/pallas_call | solution.py:618
  125.7 4.7 collective-permute-start.21
  134.0 5.6 attention_far.2
  139.7 4.7 join_halves.21
  148.6 4.2 collective-permute-start.26
  159.7 6.0 collective-permute-done.24.refs_3_
  177.2 9.5 %collective-permute-done.29.refs_4_ = bf16[1,8,80,640]{3,2,1,0:T(8,128)(2,1)S(1)} collective-permute-done((bf16[1,8,80,640]{3,2,1,0:T(8,128)(2,1)S(1)}, bf16[1,8,80,640]{3,2,1,0:T(8,128)(2,1)S(1)}, u32[]{:S(2)}, u32[]{:S(2)}) %collective-permute-start.29) | collective-permute-done | bytes 819232 | tf_op jit(solution)/shard_map/ppermute | solution.py:48
  205.8 9.2 %collective-permute-done.31.refs_3_ = bf16[2,1,80,640]{3,2,1,0:T(8,128)(2,1)} collective-permute-done((bf16[2,1,80,640]{3,2,1,0:T(8,128)(2,1)S(1)}, bf16[2,1,80,640]{3,2,1,0:T(8,128)(2,1)}, u32[]{:S(2)}, u32[]{:S(2)}) %collective-permute-start.31) | collective-permute-done | bytes 204832 | tf_op jit(solution)/shard_map/ppermute | solution.py:48
  218.1 4.5 convolution_convert_fusion.21.refs_6_.refs_2_.refs_3_
  227.7 12.2 %collective-permute-done.36.refs_4_ = bf16[1,8,80,640]{3,2,1,0:T(8,128)(2,1)S(1)} collective-permute-done((bf16[1,8,80,640]{3,2,1,0:T(8,128)(2,1)S(1)}, bf16[1,8,80,640]{3,2,1,0:T(8,128)(2,1)S(1)}, u32[]{:S(2)}, u32[]{:S(2)}) %collective-permute-start.36) | collective-permute-done | bytes 819232 | tf_op jit(solution)/shard_map/ppermute | solution.py:48
  248.3 9.6 %attention_own.3 = (f32[640,1024]{1,0:T(8,128)S(1)}, f32[8,1,1024]{2,1,0:T(1,128)S(1)}, f32[8,1,1024]{2,1,0:T(1,128)S(1)}) custom-call(s32[1,1024]{1,0:T(1,128)S(1)} %bitcast.269, bf16[640,1024]{1,0:T(8,128)(2,1)S(1)} %multiply_convert_fusion.1.refs_1_.refs_2_, bf16[640,1024]{1,0:T(8,128)(2,1)S(1)} %copy-done.30, bf16[640,1024]{1,0:T(8,128)(2,1)S(1)} %copy-done.32), custom_call_target="tpu_custom_call" | custom-call | flops 629145600 | bytes 3936256 | tf_op jit(solution)/shard_map/attention_own/pallas_call | solution.py:618
  263.0 5.6 attention_far.3
  271.0 6.7 collective-permute-done.43.refs_2_
  319.6 3.9 convolution_convert_fusion.13
  328.3 3.6 copy.67
  331.9 4.2 add_halves.20
  338.4 8.7 %attention_far_back.2 = (f32[640,1024]{1,0:T(8,128)S(1)}, f32[8,1,1024]{2,1,0:T(1,128)S(1)}, bf16[2,640,512]{2,1,0:T(8,128)(2,1)}) custom-call(s32[1]{0:T(128)} %bitcast.18.refs_0_, bf16[640,1024]{1,0:T(8,128)(2,1)S(1)} %copy-done.41, bf16[640,512]{1,0:T(8,128)(2,1)S(1)} %copy-done.58, bf16[640,512]{1,0:T(8,128)(2,1)S(1)} %copy-done.60, ...), custom_call_target="tpu_custom_call" | custom-call | flops 503316480 | bytes 5275652 | tf_op jit(solution)/shard_map/attention_far_back/pallas_call | solution.py:618
  348.6 4.3 collective-permute-start.51
  353.1 3.9 convolution_convert_fusion.7
  366.2 14.3 %attention_own_back.2 = (bf16[640,1024]{1,0:T(8,128)(2,1)S(1)}, bf16[640,1024]{1,0:T(8,128)(2,1)S(1)}, bf16[640,1024]{1,0:T(8,128)(2,1)S(1)}, f32[640,1]{1,0:T(8,128)S(1)}) custom-call(s32[1,1024]{1,0:T(1,128)S(1)} %bitcast.270, f32[80,1]{1,0:T(8,128)S(1)} %copy.68.refs_1_, bf16[640,1024]{1,0:T(8,128)(2,1)S(1)} %copy-done.42, ...), custom_call_target="tpu_custom_call" | custom-call | flops 838860800 | bytes 7934272 | tf_op jit(solution)/shard_map/attention_own_back/pallas_call | solution.py:618
  387.5 6.7 collective-permute-done.53.refs_3_
  414.8 4.0 fusion.69
  422.5 6.6 multiply_reduce_fusion.1
  442.9 4.2 fusion.30
  452.5 4.4 convolution_add_fusion.2.refs_6_
  456.9 5.3 collective-permute-done.61.refs_1_
  469.6 4.7 fusion.33
  481.5 4.0 add_halves.28
  496.1 8.7 %attention_far_back.3 = (f32[640,1024]{1,0:T(8,128)S(1)}, f32[8,1,1024]{2,1,0:T(1,128)S(1)}, bf16[2,640,512]{2,1,0:T(8,128)(2,1)}) custom-call(s32[1]{0:T(128)} %bitcast.18.refs_0_, bf16[640,1024]{1,0:T(8,128)(2,1)S(1)} %copy-done.1, bf16[640,512]{1,0:T(8,128)(2,1)S(1)} %copy-done.16, bf16[640,512]{1,0:T(8,128)(2,1)S(1)} %copy-done.19, ...), custom_call_target="tpu_custom_call" | custom-call | flops 503316480 | bytes 5275652 | tf_op jit(solution)/shard_map/attention_far_back/pallas_call | solution.py:618
  506.3 4.3 collective-permute-start.73
  522.7 4.3 convolution_convert_fusion.3
  527.1 3.6 collective-permute-done.70.refs_1_
  538.3 14.2 %attention_own_back.3 = (bf16[640,1024]{1,0:T(8,128)(2,1)S(1)}, bf16[640,1024]{1,0:T(8,128)(2,1)S(1)}, bf16[640,1024]{1,0:T(8,128)(2,1)S(1)}, f32[640,1]{1,0:T(8,128)S(1)}) custom-call(s32[1,1024]{1,0:T(1,128)S(1)} %bitcast.271, f32[80,1]{1,0:T(8,128)S(1)} %copy.74.refs_1_, bf16[640,1024]{1,0:T(8,128)(2,1)S(1)} %copy-done.1, ...), custom_call_target="tpu_custom_call" | custom-call | flops 838860800 | bytes 7934272 | tf_op jit(solution)/shard_map/attention_own_back/pallas_call | solution.py:618
  600.9 5.4 multiply_reduce_fusion.3
  614.0 6.4 collective-permute-done.82.refs_4_
  629.9 6.2 collective-permute-done.84.refs_1_
  644.9 3.9 collective-permute-done.92.refs_6_
  654.2 6.2 collective-permute-done.94.refs_2_
  665.5 5.4 collective-permute-done.96.refs_2_
  (764 shorter events, 365.1 us)
Async XLA Ops:
  49.0 19.3 %collective-permute-start.9 = (bf16[1,8,80,640]{3,2,1,0:T(8,128)(2,1)S(1)}, bf16[1,8,80,640]{3,2,1,0:T(8,128)(2,1)}, u32[]{:S(2)}, u32[]{:S(2)}) collective-permute-start(bf16[1,8,80,640]{3,2,1,0:T(8,128)(2,1)S(1)} %get-tuple-element.178.refs_1_), channel_id=1, source_target_pairs={{0,2},{2,0},{4,6},{6,4},{8,10},{10,8},{12,14},{14,12},{16,18},{18,... | collective-permute-start | bytes 2457608 | tf_op jit(solution)/shard_map/ppermute | solution.py:48
  49.5 19.0 %collective-permute-start.10 = (bf16[1,8,80,640]{3,2,1,0:T(8,128)(2,1)S(1)}, bf16[1,8,80,640]{3,2,1,0:T(8,128)(2,1)}, u32[]{:S(2)}, u32[]{:S(2)}) collective-permute-start(bf16[1,8,80,640]{3,2,1,0:T(8,128)(2,1)S(1)} %get-tuple-element.179.refs_2_), channel_id=1, source_target_pairs={{0,4},{2,6},{4,0},{6,2},{8,12},{10,14},{12,8},{14,10},{16,20},{18,... | collective-permute-start | bytes 2457608 | tf_op jit(solution)/shard_map/ppermute | solution.py:48
  84.0 16.9 %collective-permute-start.15 = (bf16[1,8,80,640]{3,2,1,0:T(8,128)(2,1)S(1)}, bf16[1,8,80,640]{3,2,1,0:T(8,128)(2,1)S(1)}, u32[]{:S(2)}, u32[]{:S(2)}) collective-permute-start(bf16[1,8,80,640]{3,2,1,0:T(8,128)(2,1)S(1)} %get-tuple-element.185.refs_1_), channel_id=1, source_target_pairs={{0,2},{2,0},{4,6},{6,4},{8,10},{10,8},{12,14},{14,12},{16,18},{18,... | collective-permute-start | bytes 2457608 | tf_op jit(solution)/shard_map/ppermute | solution.py:48
  103.9 16.9 %collective-permute-start.17 = (bf16[2,1,80,640]{3,2,1,0:T(8,128)(2,1)S(1)}, bf16[2,1,80,640]{3,2,1,0:T(8,128)(2,1)S(1)}, u32[]{:S(2)}, u32[]{:S(2)}) collective-permute-start(bf16[2,1,80,640]{3,2,1,0:T(8,128)(2,1)S(1)} %get-tuple-element.195.refs_0_), channel_id=1, source_target_pairs={{0,16},{2,18},{4,20},{6,22},{8,24},{10,26},{12,28},{14,30},{16,0},... | collective-permute-start | bytes 614408 | tf_op jit(solution)/shard_map/ppermute | solution.py:48
  144.3 29.3 %collective-permute-start.27 = (bf16[2,1280,640]{2,1,0:T(8,128)(2,1)}, bf16[2,1280,640]{2,1,0:T(8,128)(2,1)}, u32[]{:S(2)}, u32[]{:S(2)}) collective-permute-start(bf16[2,1280,640]{2,1,0:T(8,128)(2,1)} %bitcast.289), channel_id=1, source_target_pairs={{0,1},{1,0},{2,3},{3,2},{4,5},{5,4},{6,7},{7,6},{8,9},{9,8},{10,11... | collective-permute-start | bytes 9830408 | tf_op jit(solution)/shard_map/ppermute | solution.py:48
  146.6 19.1 %collective-permute-start.20 = (bf16[1280,512]{1,0:T(8,128)(2,1)}, bf16[1280,512]{1,0:T(8,128)(2,1)S(1)}, u32[]{:S(2)}, u32[]{:S(2)}) collective-permute-start(bf16[1280,512]{1,0:T(8,128)(2,1)} %convolution_convert_fusion.18), channel_id=1, source_target_pairs={{0,1},{1,0},{2,3},{3,2},{4,5},{5,4},{6,7},{7,6},{8,9},{9,8},{10,11... | collective-permute-start | bytes 3932168 | tf_op jit(solution)/shard_map/ppermute | solution.py:48
  147.1 18.6 %collective-permute-start.25 = (bf16[1,4,80,640]{3,2,1,0:T(8,128)(2,1)S(1)}, bf16[1,4,80,640]{3,2,1,0:T(8,128)(2,1)S(1)}, u32[]{:S(2)}, u32[]{:S(2)}) collective-permute-start(bf16[1,4,80,640]{3,2,1,0:T(8,128)(2,1)S(1)} %get-tuple-element.206.refs_1_), channel_id=1, source_target_pairs={{0,4},{2,6},{4,0},{6,2},{8,12},{10,14},{12,8},{14,10},{16,20},{18,... | collective-permute-start | bytes 1228808 | tf_op jit(solution)/shard_map/ppermute | solution.py:48
  148.6 17.2 %collective-permute-start.26 = (bf16[1,4,80,640]{3,2,1,0:T(8,128)(2,1)S(1)}, bf16[1,4,80,640]{3,2,1,0:T(8,128)(2,1)S(1)}, u32[]{:S(2)}, u32[]{:S(2)}) collective-permute-start(bf16[1,4,80,640]{3,2,1,0:T(8,128)(2,1)S(1)} %get-tuple-element.207.refs_2_), channel_id=1, source_target_pairs={{0,2},{2,0},{4,6},{6,4},{8,10},{10,8},{12,14},{14,12},{16,18},{18,... | collective-permute-start | bytes 1228808 | tf_op jit(solution)/shard_map/ppermute | solution.py:48
  167.2 19.4 %collective-permute-start.29 = (bf16[1,8,80,640]{3,2,1,0:T(8,128)(2,1)S(1)}, bf16[1,8,80,640]{3,2,1,0:T(8,128)(2,1)S(1)}, u32[]{:S(2)}, u32[]{:S(2)}) collective-permute-start(bf16[1,8,80,640]{3,2,1,0:T(8,128)(2,1)S(1)} %get-tuple-element.209.refs_1_), channel_id=1, source_target_pairs={{0,2},{2,0},{4,6},{6,4},{8,10},{10,8},{12,14},{14,12},{16,18},{18,... | collective-permute-start | bytes 2457608 | tf_op jit(solution)/shard_map/ppermute | solution.py:48
  168.0 19.6 %collective-permute-start.30 = (bf16[1,8,80,640]{3,2,1,0:T(8,128)(2,1)S(1)}, bf16[1,8,80,640]{3,2,1,0:T(8,128)(2,1)S(1)}, u32[]{:S(2)}, u32[]{:S(2)}) collective-permute-start(bf16[1,8,80,640]{3,2,1,0:T(8,128)(2,1)S(1)} %get-tuple-element.210.refs_2_), channel_id=1, source_target_pairs={{0,4},{2,6},{4,0},{6,2},{8,12},{10,14},{12,8},{14,10},{16,20},{18,... | collective-permute-start | bytes 2457608 | tf_op jit(solution)/shard_map/ppermute | solution.py:48
  196.1 18.8 %collective-permute-start.32 = (bf16[1,4,80,640]{3,2,1,0:T(8,128)(2,1)S(1)}, bf16[1,4,80,640]{3,2,1,0:T(8,128)(2,1)S(1)}, u32[]{:S(2)}, u32[]{:S(2)}) collective-permute-start(bf16[1,4,80,640]{3,2,1,0:T(8,128)(2,1)S(1)} %get-tuple-element.213.refs_1_), channel_id=1, source_target_pairs={{0,4},{2,6},{4,0},{6,2},{8,12},{10,14},{12,8},{14,10},{16,20},{18,... | collective-permute-start | bytes 1228808 | tf_op jit(solution)/shard_map/ppermute | solution.py:48
  196.7 18.2 %collective-permute-start.33 = (bf16[1,4,80,640]{3,2,1,0:T(8,128)(2,1)S(1)}, bf16[1,4,80,640]{3,2,1,0:T(8,128)(2,1)}, u32[]{:S(2)}, u32[]{:S(2)}) collective-permute-start(bf16[1,4,80,640]{3,2,1,0:T(8,128)(2,1)S(1)} %get-tuple-element.214.refs_2_), channel_id=1, source_target_pairs={{0,2},{2,0},{4,6},{6,4},{8,10},{10,8},{12,14},{14,12},{16,18},{18,... | collective-permute-start | bytes 1228808 | tf_op jit(solution)/shard_map/ppermute | solution.py:48
  201.4 21.7 %collective-permute-start.38 = (bf16[1280,256]{1,0:T(8,128)(2,1)}, bf16[1280,256]{1,0:T(8,128)(2,1)S(1)}, u32[]{:S(2)}, u32[]{:S(2)}) collective-permute-start(bf16[1280,256]{1,0:T(8,128)(2,1)} %fusion.50), channel_id=1, source_target_pairs={{0,2},{2,0},{4,6},{6,4},{8,10},{10,8},{12,14},{14,12},{16,18},{18,... | collective-permute-start | bytes 1966088 | tf_op jit(solution)/shard_map/ppermute | solution.py:48
  216.3 23.6 %collective-permute-start.36 = (bf16[1,8,80,640]{3,2,1,0:T(8,128)(2,1)S(1)}, bf16[1,8,80,640]{3,2,1,0:T(8,128)(2,1)S(1)}, u32[]{:S(2)}, u32[]{:S(2)}) collective-permute-start(bf16[1,8,80,640]{3,2,1,0:T(8,128)(2,1)S(1)} %get-tuple-element.216.refs_1_), channel_id=1, source_target_pairs={{0,2},{2,0},{4,6},{6,4},{8,10},{10,8},{12,14},{14,12},{16,18},{18,... | collective-permute-start | bytes 2457608 | tf_op jit(solution)/shard_map/ppermute | solution.py:48
  217.5 22.4 %collective-permute-start.37 = (bf16[1,8,80,640]{3,2,1,0:T(8,128)(2,1)S(1)}, bf16[1,8,80,640]{3,2,1,0:T(8,128)(2,1)S(1)}, u32[]{:S(2)}, u32[]{:S(2)}) collective-permute-start(bf16[1,8,80,640]{3,2,1,0:T(8,128)(2,1)S(1)} %get-tuple-element.217.refs_2_), channel_id=1, source_target_pairs={{0,4},{2,6},{4,0},{6,2},{8,12},{10,14},{12,8},{14,10},{16,20},{18,... | collective-permute-start | bytes 2457608 | tf_op jit(solution)/shard_map/ppermute | solution.py:48
  223.1 37.3 %collective-permute-start.39 = (bf16[1280,256]{1,0:T(8,128)(2,1)S(1)}, bf16[1280,256]{1,0:T(8,128)(2,1)S(1)}, u32[]{:S(2)}, u32[]{:S(2)}) collective-permute-start(bf16[1280,256]{1,0:T(8,128)(2,1)S(1)} %collective-permute-done.38.refs_5_), channel_id=1, source_target_pairs={{0,1},{1,0},{2,3},{3,2},{4,5},{5,4},{6,7},{7,6},{8,9},{9,8},{10,11... | collective-permute-start | bytes 1966088 | tf_op jit(solution)/shard_map/ppermute | solution.py:48
  258.7 19.0 %collective-permute-start.43 = (bf16[1,8,80,640]{3,2,1,0:T(8,128)(2,1)S(1)}, bf16[1,8,80,640]{3,2,1,0:T(8,128)(2,1)S(1)}, u32[]{:S(2)}, u32[]{:S(2)}) collective-permute-start(bf16[1,8,80,640]{3,2,1,0:T(8,128)(2,1)S(1)} %get-tuple-element.227.refs_7_.refs_0_), channel_id=1, source_target_pairs={{0,2},{2,0},{4,6},{6,4},{8,10},{10,8},{12,14},{14,12},{16,18},{18,... | collective-permute-start | bytes 2457608 | tf_op jit(solution)/shard_map/ppermute | solution.py:48
  259.8 18.6 %collective-permute-start.44 = (bf16[1,8,80,640]{3,2,1,0:T(8,128)(2,1)S(1)}, bf16[1,8,80,640]{3,2,1,0:T(8,128)(2,1)S(1)}, u32[]{:S(2)}, u32[]{:S(2)}) collective-permute-start(bf16[1,8,80,640]{3,2,1,0:T(8,128)(2,1)S(1)} %get-tuple-element.228.refs_8_.refs_1_), channel_id=1, source_target_pairs={{0,4},{2,6},{4,0},{6,2},{8,12},{10,14},{12,8},{14,10},{16,20},{18,... | collective-permute-start | bytes 2457608 | tf_op jit(solution)/shard_map/ppermute | solution.py:48
  311.3 17.0 %collective-permute-start.47 = (bf16[1280,640]{0,1:T(8,128)(2,1)}, bf16[1280,640]{0,1:T(8,128)(2,1)}, u32[]{:S(2)}, u32[]{:S(2)}) collective-permute-start(bf16[1280,640]{0,1:T(8,128)(2,1)} %fusion.22), channel_id=1, source_target_pairs={{0,1},{1,0},{2,3},{3,2},{4,5},{5,4},{6,7},{7,6},{8,9},{9,8},{10,11... | collective-permute-start | bytes 4915208 | tf_op jit(solution)/shard_map/ppermute | solution.py:48
  313.7 18.2 %collective-permute-start.48 = (bf16[1280,640]{1,0:T(8,128)(2,1)}, bf16[1280,640]{1,0:T(8,128)(2,1)}, u32[]{:S(2)}, u32[]{:S(2)}) collective-permute-start(bf16[1280,640]{1,0:T(8,128)(2,1)} %convolution_convert_fusion.12), channel_id=1, source_target_pairs={{0,1},{1,0},{2,3},{3,2},{4,5},{5,4},{6,7},{7,6},{8,9},{9,8},{10,11... | collective-permute-start | bytes 4915208 | tf_op jit(solution)/shard_map/ppermute | solution.py:48
  336.1 21.4 %collective-permute-start.49 = (bf16[1,8,80,640]{3,2,1,0:T(8,128)(2,1)}, bf16[1,8,80,640]{3,2,1,0:T(8,128)(2,1)}, u32[]{:S(2)}, u32[]{:S(2)}) collective-permute-start(bf16[1,8,80,640]{3,2,1,0:T(8,128)(2,1)} %get-tuple-element.232.refs_8_), channel_id=1, source_target_pairs={{0,2},{2,0},{4,6},{6,4},{8,10},{10,8},{12,14},{14,12},{16,18},{18,... | collective-permute-start | bytes 2457608 | tf_op jit(solution)/shard_map/ppermute | solution.py:48
  337.0 20.5 %collective-permute-start.50 = (bf16[1,8,80,640]{3,2,1,0:T(8,128)(2,1)}, bf16[1,8,80,640]{3,2,1,0:T(8,128)(2,1)}, u32[]{:S(2)}, u32[]{:S(2)}) collective-permute-start(bf16[1,8,80,640]{3,2,1,0:T(8,128)(2,1)} %get-tuple-element.234.refs_10_), channel_id=1, source_target_pairs={{0,4},{2,6},{4,0},{6,2},{8,12},{10,14},{12,8},{14,10},{16,20},{18,... | collective-permute-start | bytes 2457608 | tf_op jit(solution)/shard_map/ppermute | solution.py:48
  348.6 46.2 %collective-permute-start.51 = (bf16[2,640,512]{2,1,0:T(8,128)(2,1)}, bf16[2,640,512]{2,1,0:T(8,128)(2,1)}, u32[]{:S(2)}, u32[]{:S(2)}) collective-permute-start(bf16[2,640,512]{2,1,0:T(8,128)(2,1)} %get-tuple-element.244), channel_id=1, source_target_pairs={{0,2},{2,0},{4,6},{6,4},{8,10},{10,8},{12,14},{14,12},{16,18},{18,... | collective-permute-start | bytes 3932168 | tf_op jit(solution)/shard_map/ppermute | solution.py:48
  359.5 28.1 %collective-permute-start.52 = (bf16[1,4,80,640]{3,2,1,0:T(8,128)(2,1)S(1)}, bf16[1,4,80,640]{3,2,1,0:T(8,128)(2,1)S(1)}, u32[]{:S(2)}, u32[]{:S(2)}) collective-permute-start(bf16[1,4,80,640]{3,2,1,0:T(8,128)(2,1)S(1)} %get-tuple-element.238.refs_10_), channel_id=1, source_target_pairs={{0,4},{2,6},{4,0},{6,2},{8,12},{10,14},{12,8},{14,10},{16,20},{18,... | collective-permute-start | bytes 1228808 | tf_op jit(solution)/shard_map/ppermute | solution.py:48
  360.6 33.7 %collective-permute-start.53 = (bf16[1,4,80,640]{3,2,1,0:T(8,128)(2,1)S(1)}, bf16[1,4,80,640]{3,2,1,0:T(8,128)(2,1)S(1)}, u32[]{:S(2)}, u32[]{:S(2)}) collective-permute-start(bf16[1,4,80,640]{3,2,1,0:T(8,128)(2,1)S(1)} %get-tuple-element.240.refs_12_), channel_id=1, source_target_pairs={{0,2},{2,0},{4,6},{6,4},{8,10},{10,8},{12,14},{14,12},{16,18},{18,... | collective-permute-start | bytes 1228808 | tf_op jit(solution)/shard_map/ppermute | solution.py:48
  385.7 34.5 %collective-permute-start.56 = (bf16[1,8,80,640]{3,2,1,0:T(8,128)(2,1)S(1)}, bf16[1,8,80,640]{3,2,1,0:T(8,128)(2,1)S(1)}, u32[]{:S(2)}, u32[]{:S(2)}) collective-permute-start(bf16[1,8,80,640]{3,2,1,0:T(8,128)(2,1)S(1)} %get-tuple-element.251), channel_id=1, source_target_pairs={{0,2},{2,0},{4,6},{6,4},{8,10},{10,8},{12,14},{14,12},{16,18},{18,... | collective-permute-start | bytes 2457608 | tf_op jit(solution)/shard_map/ppermute | solution.py:48
  386.6 33.6 %collective-permute-start.57 = (bf16[1,8,80,640]{3,2,1,0:T(8,128)(2,1)S(1)}, bf16[1,8,80,640]{3,2,1,0:T(8,128)(2,1)S(1)}, u32[]{:S(2)}, u32[]{:S(2)}) collective-permute-start(bf16[1,8,80,640]{3,2,1,0:T(8,128)(2,1)S(1)} %get-tuple-element.253), channel_id=1, source_target_pairs={{0,4},{2,6},{4,0},{6,2},{8,12},{10,14},{12,8},{14,10},{16,20},{18,... | collective-permute-start | bytes 2457608 | tf_op jit(solution)/shard_map/ppermute | solution.py:48
  394.5 24.3 %collective-permute-start.55 = (bf16[2,2,80,640]{3,2,1,0:T(8,128)(2,1)S(1)}, bf16[2,2,80,640]{3,2,1,0:T(8,128)(2,1)S(1)}, u32[]{:S(2)}, u32[]{:S(2)}) collective-permute-start(bf16[2,2,80,640]{3,2,1,0:T(8,128)(2,1)S(1)} %get-tuple-element.247.refs_1_), channel_id=1, source_target_pairs={{0,8},{2,10},{4,12},{6,14},{8,0},{10,2},{12,4},{14,6},{16,24},{18,... | collective-permute-start | bytes 1228808 | tf_op jit(solution)/shard_map/ppermute | solution.py:48
  403.1 17.1 %collective-permute-start.54 = (bf16[1280,512]{1,0:T(8,128)(2,1)}, bf16[1280,512]{1,0:T(8,128)(2,1)}, u32[]{:S(2)}, u32[]{:S(2)}) collective-permute-start(bf16[1280,512]{1,0:T(8,128)(2,1)} %fusion.17), channel_id=1, source_target_pairs={{0,1},{1,0},{2,3},{3,2},{4,5},{5,4},{6,7},{7,6},{8,9},{9,8},{10,11... | collective-permute-start | bytes 3932168 | tf_op jit(solution)/shard_map/ppermute | solution.py:48
  413.3 43.6 %collective-permute-start.62 = (bf16[1,8,80,640]{3,2,1,0:T(8,128)(2,1)S(1)}, bf16[1,8,80,640]{3,2,1,0:T(8,128)(2,1)S(1)}, u32[]{:S(2)}, u32[]{:S(2)}) collective-permute-start(bf16[1,8,80,640]{3,2,1,0:T(8,128)(2,1)S(1)} %get-tuple-element.263), channel_id=1, source_target_pairs={{0,2},{2,0},{4,6},{6,4},{8,10},{10,8},{12,14},{14,12},{16,18},{18,... | collective-permute-start | bytes 2457608 | tf_op jit(solution)/shard_map/ppermute | solution.py:48
  418.8 38.1 %collective-permute-start.63 = (bf16[1,8,80,640]{3,2,1,0:T(8,128)(2,1)S(1)}, bf16[1,8,80,640]{3,2,1,0:T(8,128)(2,1)S(1)}, u32[]{:S(2)}, u32[]{:S(2)}) collective-permute-start(bf16[1,8,80,640]{3,2,1,0:T(8,128)(2,1)S(1)} %get-tuple-element.265), channel_id=1, source_target_pairs={{0,4},{2,6},{4,0},{6,2},{8,12},{10,14},{12,8},{14,10},{16,20},{18,... | collective-permute-start | bytes 2457608 | tf_op jit(solution)/shard_map/ppermute | solution.py:48
  449.4 31.8 %collective-permute-start.65 = (bf16[1280,640]{1,0:T(8,128)(2,1)}, bf16[1280,640]{1,0:T(8,128)(2,1)}, u32[]{:S(2)}, u32[]{:S(2)}) collective-permute-start(bf16[1280,640]{1,0:T(8,128)(2,1)} %convolution_convert_fusion.10), channel_id=1, source_target_pairs={{0,1},{1,0},{2,3},{3,2},{4,5},{5,4},{6,7},{7,6},{8,9},{9,8},{10,11... | collective-permute-start | bytes 4915208 | tf_op jit(solution)/shard_map/ppermute | solution.py:48
  449.4 32.1 %collective-permute-start.66 = (bf16[1280,640]{1,0:T(8,128)(2,1)}, bf16[1280,640]{1,0:T(8,128)(2,1)}, u32[]{:S(2)}, u32[]{:S(2)}) collective-permute-start(bf16[1280,640]{1,0:T(8,128)(2,1)} %convolution_convert_fusion.8), channel_id=1, source_target_pairs={{0,1},{1,0},{2,3},{3,2},{4,5},{5,4},{6,7},{7,6},{8,9},{9,8},{10,11... | collective-permute-start | bytes 4915208 | tf_op jit(solution)/shard_map/ppermute | solution.py:48
  469.5 17.8 %collective-permute-start.64 = (bf16[1280,512]{1,0:T(8,128)(2,1)}, bf16[1280,512]{1,0:T(8,128)(2,1)S(1)}, u32[]{:S(2)}, u32[]{:S(2)}) collective-permute-start(bf16[1280,512]{1,0:T(8,128)(2,1)} %get-tuple-element.376), channel_id=1, source_target_pairs={{0,1},{1,0},{2,3},{3,2},{4,5},{5,4},{6,7},{7,6},{8,9},{9,8},{10,11... | collective-permute-start | bytes 3932168 | tf_op jit(solution)/shard_map/ppermute | solution.py:48
  485.6 41.5 %collective-permute-start.71 = (bf16[1,8,80,640]{3,2,1,0:T(8,128)(2,1)}, bf16[1,8,80,640]{3,2,1,0:T(8,128)(2,1)}, u32[]{:S(2)}, u32[]{:S(2)}) collective-permute-start(bf16[1,8,80,640]{3,2,1,0:T(8,128)(2,1)} %get-tuple-element.268.refs_8_), channel_id=1, source_target_pairs={{0,2},{2,0},{4,6},{6,4},{8,10},{10,8},{12,14},{14,12},{16,18},{18,... | collective-permute-start | bytes 2457608 | tf_op jit(solution)/shard_map/ppermute | solution.py:48
  487.2 39.8 %collective-permute-start.72 = (bf16[1,8,80,640]{3,2,1,0:T(8,128)(2,1)}, bf16[1,8,80,640]{3,2,1,0:T(8,128)(2,1)}, u32[]{:S(2)}, u32[]{:S(2)}) collective-permute-start(bf16[1,8,80,640]{3,2,1,0:T(8,128)(2,1)} %get-tuple-element.270.refs_10_), channel_id=1, source_target_pairs={{0,4},{2,6},{4,0},{6,2},{8,12},{10,14},{12,8},{14,10},{16,20},{18,... | collective-permute-start | bytes 2457608 | tf_op jit(solution)/shard_map/ppermute | solution.py:48
  506.3 62.1 %collective-permute-start.73 = (bf16[2,640,512]{2,1,0:T(8,128)(2,1)}, bf16[2,640,512]{2,1,0:T(8,128)(2,1)}, u32[]{:S(2)}, u32[]{:S(2)}) collective-permute-start(bf16[2,640,512]{2,1,0:T(8,128)(2,1)} %get-tuple-element.291), channel_id=1, source_target_pairs={{0,2},{2,0},{4,6},{6,4},{8,10},{10,8},{12,14},{14,12},{16,18},{18,... | collective-permute-start | bytes 3932168 | tf_op jit(solution)/shard_map/ppermute | solution.py:48
  533.4 30.3 %collective-permute-start.74 = (bf16[2,1,80,640]{3,2,1,0:T(8,128)(2,1)}, bf16[2,1,80,640]{3,2,1,0:T(8,128)(2,1)}, u32[]{:S(2)}, u32[]{:S(2)}) collective-permute-start(bf16[2,1,80,640]{3,2,1,0:T(8,128)(2,1)} %get-tuple-element.283.refs_10_), channel_id=1, source_target_pairs={{0,16},{2,18},{4,20},{6,22},{8,24},{10,26},{12,28},{14,30},{16,0},... | collective-permute-start | bytes 614408 | tf_op jit(solution)/shard_map/ppermute | solution.py:48
  535.5 29.6 %collective-permute-start.75 = (bf16[1,4,80,640]{3,2,1,0:T(8,128)(2,1)}, bf16[1,4,80,640]{3,2,1,0:T(8,128)(2,1)}, u32[]{:S(2)}, u32[]{:S(2)}) collective-permute-start(bf16[1,4,80,640]{3,2,1,0:T(8,128)(2,1)} %get-tuple-element.285.refs_12_), channel_id=1, source_target_pairs={{0,4},{2,6},{4,0},{6,2},{8,12},{10,14},{12,8},{14,10},{16,20},{18,... | collective-permute-start | bytes 1228808 | tf_op jit(solution)/shard_map/ppermute | solution.py:48
  536.3 28.8 %collective-permute-start.76 = (bf16[1,4,80,640]{3,2,1,0:T(8,128)(2,1)}, bf16[1,4,80,640]{3,2,1,0:T(8,128)(2,1)}, u32[]{:S(2)}, u32[]{:S(2)}) collective-permute-start(bf16[1,4,80,640]{3,2,1,0:T(8,128)(2,1)} %get-tuple-element.287.refs_14_), channel_id=1, source_target_pairs={{0,2},{2,0},{4,6},{6,4},{8,10},{10,8},{12,14},{14,12},{16,18},{18,... | collective-permute-start | bytes 1228808 | tf_op jit(solution)/shard_map/ppermute | solution.py:48
  561.6 29.6 %collective-permute-start.79 = (bf16[1,8,80,640]{3,2,1,0:T(8,128)(2,1)}, bf16[1,8,80,640]{3,2,1,0:T(8,128)(2,1)}, u32[]{:S(2)}, u32[]{:S(2)}) collective-permute-start(bf16[1,8,80,640]{3,2,1,0:T(8,128)(2,1)} %get-tuple-element.300), channel_id=1, source_target_pairs={{0,2},{2,0},{4,6},{6,4},{8,10},{10,8},{12,14},{14,12},{16,18},{18,... | collective-permute-start | bytes 2457608 | tf_op jit(solution)/shard_map/ppermute | solution.py:48
  563.8 28.2 %collective-permute-start.80 = (bf16[1,8,80,640]{3,2,1,0:T(8,128)(2,1)}, bf16[1,8,80,640]{3,2,1,0:T(8,128)(2,1)S(1)}, u32[]{:S(2)}, u32[]{:S(2)}) collective-permute-start(bf16[1,8,80,640]{3,2,1,0:T(8,128)(2,1)} %copy-done.96), channel_id=1, source_target_pairs={{0,4},{2,6},{4,0},{6,2},{8,12},{10,14},{12,8},{14,10},{16,20},{18,... | collective-permute-start | bytes 2457608 | tf_op jit(solution)/shard_map/ppermute | solution.py:48
  566.6 25.4 %collective-permute-start.78 = (bf16[2,2,80,640]{3,2,1,0:T(8,128)(2,1)S(1)}, bf16[2,2,80,640]{3,2,1,0:T(8,128)(2,1)S(1)}, u32[]{:S(2)}, u32[]{:S(2)}) collective-permute-start(bf16[2,2,80,640]{3,2,1,0:T(8,128)(2,1)S(1)} %get-tuple-element.296.refs_3_), channel_id=1, source_target_pairs={{0,8},{2,10},{4,12},{6,14},{8,0},{10,2},{12,4},{14,6},{16,24},{18,... | collective-permute-start | bytes 1228808 | tf_op jit(solution)/shard_map/ppermute | solution.py:48
  588.2 40.4 %collective-permute-start.85 = (bf16[1,8,80,640]{3,2,1,0:T(8,128)(2,1)}, bf16[1,8,80,640]{3,2,1,0:T(8,128)(2,1)}, u32[]{:S(2)}, u32[]{:S(2)}) collective-permute-start(bf16[1,8,80,640]{3,2,1,0:T(8,128)(2,1)} %get-tuple-element.312), channel_id=1, source_target_pairs={{0,2},{2,0},{4,6},{6,4},{8,10},{10,8},{12,14},{14,12},{16,18},{18,... | collective-permute-start | bytes 2457608 | tf_op jit(solution)/shard_map/ppermute | solution.py:48
  591.2 37.4 %collective-permute-start.86 = (bf16[1,8,80,640]{3,2,1,0:T(8,128)(2,1)}, bf16[1,8,80,640]{3,2,1,0:T(8,128)(2,1)}, u32[]{:S(2)}, u32[]{:S(2)}) collective-permute-start(bf16[1,8,80,640]{3,2,1,0:T(8,128)(2,1)} %get-tuple-element.314), channel_id=1, source_target_pairs={{0,4},{2,6},{4,0},{6,2},{8,12},{10,14},{12,8},{14,10},{16,20},{18,... | collective-permute-start | bytes 2457608 | tf_op jit(solution)/shard_map/ppermute | solution.py:48
  598.3 22.1 %collective-permute-start.82 = (bf16[1,4,80,640]{3,2,1,0:T(8,128)(2,1)}, bf16[1,4,80,640]{3,2,1,0:T(8,128)(2,1)}, u32[]{:S(2)}, u32[]{:S(2)}) collective-permute-start(bf16[1,4,80,640]{3,2,1,0:T(8,128)(2,1)} %get-tuple-element.307), channel_id=1, source_target_pairs={{0,4},{2,6},{4,0},{6,2},{8,12},{10,14},{12,8},{14,10},{16,20},{18,... | collective-permute-start | bytes 1228808 | tf_op jit(solution)/shard_map/ppermute | solution.py:48
  599.1 21.2 %collective-permute-start.83 = (bf16[1,4,80,640]{3,2,1,0:T(8,128)(2,1)}, bf16[1,4,80,640]{3,2,1,0:T(8,128)(2,1)}, u32[]{:S(2)}, u32[]{:S(2)}) collective-permute-start(bf16[1,4,80,640]{3,2,1,0:T(8,128)(2,1)} %get-tuple-element.308), channel_id=1, source_target_pairs={{0,2},{2,0},{4,6},{6,4},{8,10},{10,8},{12,14},{14,12},{16,18},{18,... | collective-permute-start | bytes 1228808 | tf_op jit(solution)/shard_map/ppermute | solution.py:48
  608.6 17.4 %collective-permute-start.87 = (f32[2,2640]{1,0:T(2,128)}, f32[2,2640]{1,0:T(2,128)S(1)}, u32[]{:S(2)}, u32[]{:S(2)}) collective-permute-start(f32[2,2640]{1,0:T(2,128)} %pad_maximum_fusion.24), channel_id=1, source_target_pairs={{0,1},{1,0},{2,3},{3,2},{4,5},{5,4},{6,7},{7,6},{8,9},{9,8},{10,11... | collective-permute-start | bytes 63368 | tf_op jit(solution)/shard_map/ppermute | solution.py:48
  (255 other events, 2371.3 us)

commit v6 on v5

--- a/solution.py
+++ b/solution.py
@@ -359,6 +359,16 @@
     return lowered(parts[0]), pair_swap(lowered(parts[1]), "tensor", 1)
 
 
+def exchange_sum(values, axis, bit, bits, exchange):
+    wide = bits == 2 and 2 * bit < lax.axis_size(axis)
+    came = [pair_swap(values, axis, bit * by) for by in ((1, 2, 3) if wide else (1,))]
+    after = exchange.tick(*came)
+    total = values + came[0]
+    if wide:
+        total = total + (came[1] + came[2])
+    return tied(total, after)
+
+
 def tied(gain, after):
     if not after:
         return gain
@@ -723,7 +733,7 @@
         "attention_own_back",
         heads,
         tokens * tokens * 5 // 8,
-        4,
+        76,
         [
             (same_block(1, tokens), start),
             (same_block(HD, 1), gain),
@@ -783,6 +793,7 @@
     stored = []
     terms = [inputs.T]
     ready = ()
+    grad = cotangent.T
     for layer in range(LAYERS):
         attn_gain = attention_gain[layer][:, None]
         ff_gain = feed_gain[layer][:, None]
@@ -794,6 +805,7 @@
             gather.tick(far)
             far_normed, came = gather_tokens(far)
             gather.tick(came)
+            gather.tick(grad)
             wk, wv = gather.take()
             gather.tick()
         keys = lowered(dot_tn(wk, normed))
@@ -839,7 +851,6 @@
 
     sums = Scatter(orders)
     small_grads = [None] * LAYERS
-    grad = cotangent.T
     grad_low = lowered(grad)
     for layer in reversed(range(LAYERS)):
         (
@@ -890,33 +901,41 @@
         ready = sums.tick(scale_rows)
         query_grad = lowered(dot_nt(normed, d_raw))
         sums.push(out_grad, query_grad)
-        sums.enter()
+        ready = [*ready, *sums.enter()]
         d_keys, d_values = add_back(own_dk, own_dv, back, ready)
         scale_raw = jnp.sum(scale_rows.reshape(heads, HD), 0) / (gain_q * LOG_TWO_E)
         scale_grad = scale_raw * jax.nn.sigmoid(query_scale[layer]) * LOG_TWO_E / math.sqrt(HD)
+        if not layer:
+            key_grad, value_grad = [lowered(dot_nt(normed, d)) for d in (d_keys, d_values)]
+            ready = sums.tick(key_grad, value_grad)
+            last = Scatter(orders)
+            last.push(key_grad, value_grad)
+            last.enter()
         terms = scatter_tokens(
             lambda dq, dk, dv: dot_nn(wq, dq) + dot_nn(wk, dk) + dot_nn(wv, dv),
             d_raw,
             d_keys,
             d_values,
         )
-        ready = sums.tick(terms[-1])
+        if layer:
+            ready = sums.tick(terms[-1])
+        else:
+            sums.tick(terms[-1])
+            ready = last.tick(terms[-1])
         grad, grad_low, attn_gain_grad = norm_back(
             source, inverse_attn, attn_gain, grad_middle, terms, ready
         )
-        key_grad = lowered(dot_nt(normed, d_keys))
-        value_grad = lowered(dot_nt(normed, d_values))
-        sums.push(key_grad, value_grad)
-        sums.tick(grad, key_grad, value_grad)
+        if layer:
+            key_grad, value_grad = [lowered(dot_nt(normed, d)) for d in (d_keys, d_values)]
+            sums.push(key_grad, value_grad)
+            sums.tick(grad, key_grad, value_grad)
         small_grads[layer] = jnp.concatenate([attn_gain_grad, feed_gain_grad, scale_grad])
     small = jnp.stack(small_grads)
-    for axis in ("tensor", "dp"):
+    for axis, bits in (("tensor", 1), ("dp", 2)):
         bit = 1
         while bit < lax.axis_size(axis):
-            came = pair_swap(small, axis, bit)
-            after = sums.tick(came) if axis == "dp" else ()
-            small, bit = tied(small + came, after), 2 * bit
-    done = sums.finish()
+            small, bit = exchange_sum(small, axis, bit, bits, last), bit << bits
+    done = sums.finish() + last.finish()
     layer_grads = []
     for layer in range(LAYERS):
         at = 3 * (LAYERS - 1 - layer)

time: 686 us -> 671 us (0.978)
  waiting for transfers between devices: 145 us -> 132 us
    ppermute x97 -> x99, waiting for transfers between devices: 145 us -> 132 us  [pair_swap(): return lax.ppermute(values, axis, [(i, i ^ bit) for i in range(size)])]
    ppermute x97 -> x99, starting transfers between devices: 115 us -> 120 us  [pair_swap(): return lax.ppermute(values, axis, [(i, i ^ bit) for i in range(size)])]
    unnamed x416 -> x366, local copies, waits for them, and re-layouts: 46.3 us -> 45.3 us
    pallas_call x36 -> x38, Pallas kernels: 62.8 us -> 62.6 us  [quick_call(): pl.pallas_call(kernel, in_specs=[SCALAR] + [WHOLE] * (len(arrays) - 1) +...]
  transfers between devices with their start and end apart: 97 -> 99, of which waited for: 36 -> 32; matrix products, arithmetic and copies ran while one was open for 31% -> 30% of each run, Pallas kernels for 17% -> 18%
where the time goes in v6:
time: 671 us; the launch traced here: 661 us
  matrix products  166 us (25%)
  Pallas kernels  138 us (21%)
  waiting for transfers between devices  132 us (20%)
  starting transfers between devices  120 us (18%)
  local copies, waits for them, and re-layouts  62.5 us (9%)
  other arithmetic  33.3 us (5%)
  between operations  8.89 us (1%)
    ppermute x99, waiting for transfers between devices, pair_swap(): return lax.ppermute(values, axis, [(i, i ^ bit) for i in range(size)])  132 us
    ppermute x99, starting transfers between devices, pair_swap(): return lax.ppermute(values, axis, [(i, i ^ bit) for i in range(size)])  120 us
    pallas_call x8, Pallas kernels, per_head(): pl.pallas_call(work, grid=(heads,), in_specs=[spec for spec, _ in ins] +...  75.8 us
    dot_general x24, matrix products, dot_nn(): return jnp.dot(former, latter, preferred_element_type=jnp.float32)  73.8 us
    pallas_call x38, Pallas kernels, quick_call(): pl.pallas_call(kernel, in_specs=[SCALAR] + [WHOLE] * (len(arrays) - 1) +...  62.6 us
    dot_general x20, matrix products, dot_tn(): lax.dot_general(former, latter, (((0,), (0,)), ((), ())), preferred_eleme...  47.4 us
    unnamed x366, local copies, waits for them, and re-layouts  45.3 us
    dot_general x16, matrix products, dot_nt(): lax.dot_general(former, latter, (((1,), (1,)), ((), ())), preferred_eleme...  44.4 us
  transfers between devices with their start and end apart: 99, of which 32 were waited for; matrix products, arithmetic and copies ran while one was open for 30% of the time, Pallas kernels for 18%

profile of v6, /device:TPU:0, one launch (start us, length us, event | category | flops | bytes accessed | tf_op | source)
XLA Modules:
  0.0 660.8 jit_solution(2798792285911183353)
XLA Ops:
  6.2 3.7 collective-permute-start
  20.9 10.0 %collective-permute-done.3.refs_3_ = bf16[1280,256]{1,0:T(8,128)(2,1)S(1)} collective-permute-done((bf16[1280,256]{1,0:T(8,128)(2,1)S(1)}, bf16[1280,256]{1,0:T(8,128)(2,1)S(1)}, u32[]{:S(2)}, u32[]{:S(2)}) %collective-permute-start.3) | collective-permute-done | bytes 655392 | tf_op jit(solution)/shard_map/ppermute | solution.py:48
  37.9 9.4 %collective-permute-done.4.refs_3_ = bf16[2,1,80,640]{3,2,1,0:T(8,128)(2,1)S(1)} collective-permute-done((bf16[2,1,80,640]{3,2,1,0:T(8,128)(2,1)S(1)}, bf16[2,1,80,640]{3,2,1,0:T(8,128)(2,1)S(1)}, u32[]{:S(2)}, u32[]{:S(2)}) %collective-permute-start.4) | collective-permute-done | bytes 204832 | tf_op jit(solution)/shard_map/ppermute | solution.py:48
  54.1 9.2 %collective-permute-done.8.refs_3_ = bf16[2,2,80,640]{3,2,1,0:T(8,128)(2,1)S(1)} collective-permute-done((bf16[2,2,80,640]{3,2,1,0:T(8,128)(2,1)}, bf16[2,2,80,640]{3,2,1,0:T(8,128)(2,1)S(1)}, u32[]{:S(2)}, u32[]{:S(2)}) %collective-permute-start.8) | collective-permute-done | bytes 409632 | tf_op jit(solution)/shard_map/ppermute | solution.py:48
  63.3 4.8 collective-permute-done.9.refs_4_
  68.3 3.5 join_halves.17
  73.9 4.5 convolution_convert_fusion.23.refs_7_.refs_2_.refs_3_
  78.3 4.4 collective-permute-done.11.refs_3_
  88.0 5.5 collective-permute-start.14
  107.1 3.5 multiply_convert_fusion.4.refs_1_.refs_2_
  110.6 9.8 %attention_own.2 = (f32[640,1024]{1,0:T(8,128)S(1)}, f32[8,1,1024]{2,1,0:T(1,128)S(1)}, f32[8,1,1024]{2,1,0:T(1,128)S(1)}) custom-call(s32[1,1024]{1,0:T(1,128)S(1)} %bitcast.268, bf16[640,1024]{1,0:T(8,128)(2,1)S(1)} %multiply_convert_fusion.4.refs_1_.refs_2_, bf16[640,1024]{1,0:T(8,128)(2,1)S(1)} %copy-done.14, bf16[640,1024]{1,0:T(8,128)(2,1)S(1)} %copy-done.16), custom_call_target="tpu_custom_call" | custom-call | flops 629145600 | bytes 3936256 | tf_op jit(solution)/shard_map/attention_own/pallas_call | solution.py:628
  125.0 4.9 collective-permute-start.21
  132.9 5.5 attention_far.2
  138.6 4.3 join_halves.21
  147.3 4.2 collective-permute-start.26
  157.3 6.3 collective-permute-done.24.refs_3_
  174.0 3.6 fusion.31.refs_8_
  177.6 7.8 %collective-permute-done.29.refs_4_ = bf16[1,8,80,640]{3,2,1,0:T(8,128)(2,1)S(1)} collective-permute-done((bf16[1,8,80,640]{3,2,1,0:T(8,128)(2,1)S(1)}, bf16[1,8,80,640]{3,2,1,0:T(8,128)(2,1)S(1)}, u32[]{:S(2)}, u32[]{:S(2)}) %collective-permute-start.29) | collective-permute-done | bytes 819232 | tf_op jit(solution)/shard_map/ppermute | solution.py:48
  204.7 9.2 %collective-permute-done.31.refs_3_ = bf16[2,1,80,640]{3,2,1,0:T(8,128)(2,1)} collective-permute-done((bf16[2,1,80,640]{3,2,1,0:T(8,128)(2,1)S(1)}, bf16[2,1,80,640]{3,2,1,0:T(8,128)(2,1)}, u32[]{:S(2)}, u32[]{:S(2)}) %collective-permute-start.31) | collective-permute-done | bytes 204832 | tf_op jit(solution)/shard_map/ppermute | solution.py:48
  216.1 4.5 convolution_convert_fusion.21.refs_6_.refs_2_.refs_3_
  226.6 11.4 %collective-permute-done.36.refs_4_ = bf16[1,8,80,640]{3,2,1,0:T(8,128)(2,1)S(1)} collective-permute-done((bf16[1,8,80,640]{3,2,1,0:T(8,128)(2,1)S(1)}, bf16[1,8,80,640]{3,2,1,0:T(8,128)(2,1)S(1)}, u32[]{:S(2)}, u32[]{:S(2)}) %collective-permute-start.36) | collective-permute-done | bytes 819232 | tf_op jit(solution)/shard_map/ppermute | solution.py:48
  247.1 9.5 %attention_own.3 = (f32[640,1024]{1,0:T(8,128)S(1)}, f32[8,1,1024]{2,1,0:T(1,128)S(1)}, f32[8,1,1024]{2,1,0:T(1,128)S(1)}) custom-call(s32[1,1024]{1,0:T(1,128)S(1)} %bitcast.269, bf16[640,1024]{1,0:T(8,128)(2,1)S(1)} %multiply_convert_fusion.1.refs_1_.refs_2_, bf16[640,1024]{1,0:T(8,128)(2,1)S(1)} %copy-done.18, bf16[640,1024]{1,0:T(8,128)(2,1)S(1)} %copy-done.20), custom_call_target="tpu_custom_call" | custom-call | flops 629145600 | bytes 3936256 | tf_op jit(solution)/shard_map/attention_own/pallas_call | solution.py:628
  261.3 6.0 attention_far.3
  269.7 6.7 %collective-permute-done.43.refs_2_ = bf16[1,8,80,640]{3,2,1,0:T(8,128)(2,1)S(1)} collective-permute-done((bf16[1,8,80,640]{3,2,1,0:T(8,128)(2,1)S(1)}, bf16[1,8,80,640]{3,2,1,0:T(8,128)(2,1)S(1)}, u32[]{:S(2)}, u32[]{:S(2)}) %collective-permute-start.43) | collective-permute-done | bytes 819232 | tf_op jit(solution)/shard_map/ppermute | solution.py:48
  314.5 4.0 convolution_convert_fusion.13
  318.5 4.2 fusion.33
  326.2 3.5 copy.67
  329.7 4.2 add_halves.22
  340.3 8.1 %attention_far_back.2 = (f32[640,1024]{1,0:T(8,128)S(1)}, f32[8,1,1024]{2,1,0:T(1,128)S(1)}, bf16[2,640,512]{2,1,0:T(8,128)(2,1)S(1)}) custom-call(s32[1]{0:T(128)} %bitcast.19.refs_0_, bf16[640,1024]{1,0:T(8,128)(2,1)S(1)} %copy-done.23, bf16[640,512]{1,0:T(8,128)(2,1)S(1)} %copy-done.39, bf16[640,512]{1,0:T(8,128)(2,1)S(1)} %copy-done.41, ...), custom_call_target="tpu_custom_call" | custom-call | flops 503316480 | bytes 5275652 | tf_op jit(solution)/shard_map/attention_far_back/pallas_call | solution.py:628
  348.4 4.5 collective-permute-start.51
  362.3 14.1 %attention_own_back.2 = (bf16[640,1024]{1,0:T(8,128)(2,1)S(1)}, bf16[640,1024]{1,0:T(8,128)(2,1)S(1)}, bf16[640,1024]{1,0:T(8,128)(2,1)S(1)}, f32[640,1]{1,0:T(8,128)S(1)}) custom-call(s32[1,1024]{1,0:T(1,128)S(1)} %bitcast.270, f32[80,1]{1,0:T(8,128)S(1)} %copy.68.refs_1_, bf16[640,1024]{1,0:T(8,128)(2,1)S(1)} %copy-done.24, ...), custom_call_target="tpu_custom_call" | custom-call | flops 15938355200 | bytes 7934272 | tf_op jit(solution)/shard_map/attention_own_back/pallas_call | solution.py:628
  384.6 7.6 %collective-permute-done.53.refs_3_ = bf16[1,4,80,640]{3,2,1,0:T(8,128)(2,1)} collective-permute-done((bf16[1,4,80,640]{3,2,1,0:T(8,128)(2,1)S(1)}, bf16[1,4,80,640]{3,2,1,0:T(8,128)(2,1)}, u32[]{:S(2)}, u32[]{:S(2)}) %collective-permute-start.53) | collective-permute-done | bytes 409632 | tf_op jit(solution)/shard_map/ppermute | solution.py:48
  416.2 4.1 fusion.69
  423.8 6.2 multiply_reduce_fusion.1
  443.7 4.2 fusion.30
  454.0 4.4 convolution_add_fusion.2.refs_6_
  458.4 5.1 collective-permute-done.61.refs_1_
  501.6 8.7 %attention_far_back.3 = (f32[640,1024]{1,0:T(8,128)S(1)}, f32[8,1,1024]{2,1,0:T(1,128)S(1)}, bf16[2,640,512]{2,1,0:T(8,128)(2,1)}) custom-call(s32[1]{0:T(128)} %bitcast.19.refs_0_, bf16[640,1024]{1,0:T(8,128)(2,1)S(1)} %copy-done.11, bf16[640,512]{1,0:T(8,128)(2,1)S(1)} %copy-done.6, bf16[640,512]{1,0:T(8,128)(2,1)S(1)} %copy-done.8, ...), custom_call_target="tpu_custom_call" | custom-call | flops 503316480 | bytes 5275652 | tf_op jit(solution)/shard_map/attention_far_back/pallas_call | solution.py:628
  510.3 5.1 collective-permute-start.73
  531.6 14.1 %attention_own_back.3 = (bf16[640,1024]{1,0:T(8,128)(2,1)S(1)}, bf16[640,1024]{1,0:T(8,128)(2,1)S(1)}, bf16[640,1024]{1,0:T(8,128)(2,1)S(1)}, f32[640,1]{1,0:T(8,128)S(1)}) custom-call(s32[1,1024]{1,0:T(1,128)S(1)} %bitcast.271, f32[80,1]{1,0:T(8,128)S(1)} %copy.74.refs_1_, bf16[640,1024]{1,0:T(8,128)(2,1)S(1)} %copy-done.11, ...), custom_call_target="tpu_custom_call" | custom-call | flops 15938355200 | bytes 7934272 | tf_op jit(solution)/shard_map/attention_own_back/pallas_call | solution.py:628
  545.8 3.5 convolution_convert_fusion.2
  585.5 4.2 fusion.57
  592.4 6.4 collective-permute-done.78.refs_1_
  603.5 6.8 %multiply_reduce_fusion.3 = (f32[1280]{0:T(1024)S(1)}, f32[512]{0:T(512)S(1)}, f32[1280,512]{1,0:T(8,128)}) fusion(f32[512,1280]{0,1:T(8,128)S(1)} %copy-done.84, f32[512]{0:T(512)S(1)} %copy-done.156, f32[1280]{0:T(1024)S(1)} %broadcast_add_fusion, bf16[1280,512]{1,0:T(8,128)(2,1)} %copy-done, f32[1280,512]{1,0:T(8,128)} %fusion.57, ...), kind=kOutput, calls=%fused_computation.65 | convolution fusion | flops 846723328 | bytes 14107652 | tf_op jit(solution)/shard_map/dot_general | solution.py:27
  616.8 3.9 add_bitcast_fusion
  632.6 5.6 collective-permute-done.87.refs_1_
  639.1 4.1 collective-permute-done.91.refs_1_
  649.9 6.5 collective-permute-done.97.refs_3_
  (717 shorter events, 357.0 us)
Async XLA Ops:
  48.8 19.2 %collective-permute-start.9 = (bf16[1,8,80,640]{3,2,1,0:T(8,128)(2,1)S(1)}, bf16[1,8,80,640]{3,2,1,0:T(8,128)(2,1)}, u32[]{:S(2)}, u32[]{:S(2)}) collective-permute-start(bf16[1,8,80,640]{3,2,1,0:T(8,128)(2,1)S(1)} %get-tuple-element.178.refs_1_), channel_id=1, source_target_pairs={{0,2},{2,0},{4,6},{6,4},{8,10},{10,8},{12,14},{14,12},{16,18},{18,... | collective-permute-start | bytes 2457608 | tf_op jit(solution)/shard_map/ppermute | solution.py:48
  49.3 19.0 %collective-permute-start.10 = (bf16[1,8,80,640]{3,2,1,0:T(8,128)(2,1)S(1)}, bf16[1,8,80,640]{3,2,1,0:T(8,128)(2,1)}, u32[]{:S(2)}, u32[]{:S(2)}) collective-permute-start(bf16[1,8,80,640]{3,2,1,0:T(8,128)(2,1)S(1)} %get-tuple-element.179.refs_2_), channel_id=1, source_target_pairs={{0,4},{2,6},{4,0},{6,2},{8,12},{10,14},{12,8},{14,10},{16,20},{18,... | collective-permute-start | bytes 2457608 | tf_op jit(solution)/shard_map/ppermute | solution.py:48
  103.1 17.3 %collective-permute-start.17 = (bf16[2,1,80,640]{3,2,1,0:T(8,128)(2,1)S(1)}, bf16[2,1,80,640]{3,2,1,0:T(8,128)(2,1)S(1)}, u32[]{:S(2)}, u32[]{:S(2)}) collective-permute-start(bf16[2,1,80,640]{3,2,1,0:T(8,128)(2,1)S(1)} %get-tuple-element.195.refs_0_), channel_id=1, source_target_pairs={{0,16},{2,18},{4,20},{6,22},{8,24},{10,26},{12,28},{14,30},{16,0},... | collective-permute-start | bytes 614408 | tf_op jit(solution)/shard_map/ppermute | solution.py:48
  142.9 31.1 %collective-permute-start.27 = (bf16[2,1280,640]{2,1,0:T(8,128)(2,1)}, bf16[2,1280,640]{2,1,0:T(8,128)(2,1)}, u32[]{:S(2)}, u32[]{:S(2)}) collective-permute-start(bf16[2,1280,640]{2,1,0:T(8,128)(2,1)} %bitcast.289), channel_id=1, source_target_pairs={{0,1},{1,0},{2,3},{3,2},{4,5},{5,4},{6,7},{7,6},{8,9},{9,8},{10,11... | collective-permute-start | bytes 9830408 | tf_op jit(solution)/shard_map/ppermute | solution.py:48
  145.3 18.3 %collective-permute-start.20 = (bf16[1280,512]{1,0:T(8,128)(2,1)}, bf16[1280,512]{1,0:T(8,128)(2,1)S(1)}, u32[]{:S(2)}, u32[]{:S(2)}) collective-permute-start(bf16[1280,512]{1,0:T(8,128)(2,1)} %convolution_convert_fusion.18), channel_id=1, source_target_pairs={{0,1},{1,0},{2,3},{3,2},{4,5},{5,4},{6,7},{7,6},{8,9},{9,8},{10,11... | collective-permute-start | bytes 3932168 | tf_op jit(solution)/shard_map/ppermute | solution.py:48
  145.8 17.8 %collective-permute-start.25 = (bf16[1,4,80,640]{3,2,1,0:T(8,128)(2,1)}, bf16[1,4,80,640]{3,2,1,0:T(8,128)(2,1)S(1)}, u32[]{:S(2)}, u32[]{:S(2)}) collective-permute-start(bf16[1,4,80,640]{3,2,1,0:T(8,128)(2,1)} %copy-done.52), channel_id=1, source_target_pairs={{0,4},{2,6},{4,0},{6,2},{8,12},{10,14},{12,8},{14,10},{16,20},{18,... | collective-permute-start | bytes 1228808 | tf_op jit(solution)/shard_map/ppermute | solution.py:48
  165.5 19.9 %collective-permute-start.29 = (bf16[1,8,80,640]{3,2,1,0:T(8,128)(2,1)S(1)}, bf16[1,8,80,640]{3,2,1,0:T(8,128)(2,1)S(1)}, u32[]{:S(2)}, u32[]{:S(2)}) collective-permute-start(bf16[1,8,80,640]{3,2,1,0:T(8,128)(2,1)S(1)} %get-tuple-element.209.refs_1_), channel_id=1, source_target_pairs={{0,2},{2,0},{4,6},{6,4},{8,10},{10,8},{12,14},{14,12},{16,18},{18,... | collective-permute-start | bytes 2457608 | tf_op jit(solution)/shard_map/ppermute | solution.py:48
  166.1 19.3 %collective-permute-start.30 = (bf16[1,8,80,640]{3,2,1,0:T(8,128)(2,1)S(1)}, bf16[1,8,80,640]{3,2,1,0:T(8,128)(2,1)S(1)}, u32[]{:S(2)}, u32[]{:S(2)}) collective-permute-start(bf16[1,8,80,640]{3,2,1,0:T(8,128)(2,1)S(1)} %get-tuple-element.210.refs_2_), channel_id=1, source_target_pairs={{0,4},{2,6},{4,0},{6,2},{8,12},{10,14},{12,8},{14,10},{16,20},{18,... | collective-permute-start | bytes 2457608 | tf_op jit(solution)/shard_map/ppermute | solution.py:48
  194.1 19.7 %collective-permute-start.32 = (bf16[1,4,80,640]{3,2,1,0:T(8,128)(2,1)S(1)}, bf16[1,4,80,640]{3,2,1,0:T(8,128)(2,1)S(1)}, u32[]{:S(2)}, u32[]{:S(2)}) collective-permute-start(bf16[1,4,80,640]{3,2,1,0:T(8,128)(2,1)S(1)} %get-tuple-element.213.refs_1_), channel_id=1, source_target_pairs={{0,4},{2,6},{4,0},{6,2},{8,12},{10,14},{12,8},{14,10},{16,20},{18,... | collective-permute-start | bytes 1228808 | tf_op jit(solution)/shard_map/ppermute | solution.py:48
  194.8 19.0 %collective-permute-start.33 = (bf16[1,4,80,640]{3,2,1,0:T(8,128)(2,1)S(1)}, bf16[1,4,80,640]{3,2,1,0:T(8,128)(2,1)}, u32[]{:S(2)}, u32[]{:S(2)}) collective-permute-start(bf16[1,4,80,640]{3,2,1,0:T(8,128)(2,1)S(1)} %get-tuple-element.214.refs_2_), channel_id=1, source_target_pairs={{0,2},{2,0},{4,6},{6,4},{8,10},{10,8},{12,14},{14,12},{16,18},{18,... | collective-permute-start | bytes 1228808 | tf_op jit(solution)/shard_map/ppermute | solution.py:48
  199.5 21.7 %collective-permute-start.38 = (bf16[1280,256]{1,0:T(8,128)(2,1)}, bf16[1280,256]{1,0:T(8,128)(2,1)S(1)}, u32[]{:S(2)}, u32[]{:S(2)}) collective-permute-start(bf16[1280,256]{1,0:T(8,128)(2,1)} %fusion.50), channel_id=1, source_target_pairs={{0,2},{2,0},{4,6},{6,4},{8,10},{10,8},{12,14},{14,12},{16,18},{18,... | collective-permute-start | bytes 1966088 | tf_op jit(solution)/shard_map/ppermute | solution.py:48
  215.2 22.8 %collective-permute-start.36 = (bf16[1,8,80,640]{3,2,1,0:T(8,128)(2,1)S(1)}, bf16[1,8,80,640]{3,2,1,0:T(8,128)(2,1)S(1)}, u32[]{:S(2)}, u32[]{:S(2)}) collective-permute-start(bf16[1,8,80,640]{3,2,1,0:T(8,128)(2,1)S(1)} %get-tuple-element.216.refs_1_), channel_id=1, source_target_pairs={{0,2},{2,0},{4,6},{6,4},{8,10},{10,8},{12,14},{14,12},{16,18},{18,... | collective-permute-start | bytes 2457608 | tf_op jit(solution)/shard_map/ppermute | solution.py:48
  215.6 22.4 %collective-permute-start.37 = (bf16[1,8,80,640]{3,2,1,0:T(8,128)(2,1)S(1)}, bf16[1,8,80,640]{3,2,1,0:T(8,128)(2,1)S(1)}, u32[]{:S(2)}, u32[]{:S(2)}) collective-permute-start(bf16[1,8,80,640]{3,2,1,0:T(8,128)(2,1)S(1)} %get-tuple-element.217.refs_2_), channel_id=1, source_target_pairs={{0,4},{2,6},{4,0},{6,2},{8,12},{10,14},{12,8},{14,10},{16,20},{18,... | collective-permute-start | bytes 2457608 | tf_op jit(solution)/shard_map/ppermute | solution.py:48
  221.2 37.2 %collective-permute-start.39 = (bf16[1280,256]{1,0:T(8,128)(2,1)S(1)}, bf16[1280,256]{1,0:T(8,128)(2,1)S(1)}, u32[]{:S(2)}, u32[]{:S(2)}) collective-permute-start(bf16[1280,256]{1,0:T(8,128)(2,1)S(1)} %collective-permute-done.38.refs_5_), channel_id=1, source_target_pairs={{0,1},{1,0},{2,3},{3,2},{4,5},{5,4},{6,7},{7,6},{8,9},{9,8},{10,11... | collective-permute-start | bytes 1966088 | tf_op jit(solution)/shard_map/ppermute | solution.py:48
  257.4 19.0 %collective-permute-start.43 = (bf16[1,8,80,640]{3,2,1,0:T(8,128)(2,1)S(1)}, bf16[1,8,80,640]{3,2,1,0:T(8,128)(2,1)S(1)}, u32[]{:S(2)}, u32[]{:S(2)}) collective-permute-start(bf16[1,8,80,640]{3,2,1,0:T(8,128)(2,1)S(1)} %get-tuple-element.227.refs_7_.refs_0_), channel_id=1, source_target_pairs={{0,2},{2,0},{4,6},{6,4},{8,10},{10,8},{12,14},{14,12},{16,18},{18,... | collective-permute-start | bytes 2457608 | tf_op jit(solution)/shard_map/ppermute | solution.py:48
  257.7 18.7 %collective-permute-start.44 = (bf16[1,8,80,640]{3,2,1,0:T(8,128)(2,1)S(1)}, bf16[1,8,80,640]{3,2,1,0:T(8,128)(2,1)S(1)}, u32[]{:S(2)}, u32[]{:S(2)}) collective-permute-start(bf16[1,8,80,640]{3,2,1,0:T(8,128)(2,1)S(1)} %get-tuple-element.228.refs_8_.refs_1_), channel_id=1, source_target_pairs={{0,4},{2,6},{4,0},{6,2},{8,12},{10,14},{12,8},{14,10},{16,20},{18,... | collective-permute-start | bytes 2457608 | tf_op jit(solution)/shard_map/ppermute | solution.py:48
  308.6 17.6 %collective-permute-start.47 = (bf16[1280,640]{0,1:T(8,128)(2,1)}, bf16[1280,640]{0,1:T(8,128)(2,1)}, u32[]{:S(2)}, u32[]{:S(2)}) collective-permute-start(bf16[1280,640]{0,1:T(8,128)(2,1)} %fusion.22), channel_id=1, source_target_pairs={{0,1},{1,0},{2,3},{3,2},{4,5},{5,4},{6,7},{7,6},{8,9},{9,8},{10,11... | collective-permute-start | bytes 4915208 | tf_op jit(solution)/shard_map/ppermute | solution.py:48
  308.6 21.1 %collective-permute-start.48 = (bf16[1280,640]{1,0:T(8,128)(2,1)}, bf16[1280,640]{1,0:T(8,128)(2,1)}, u32[]{:S(2)}, u32[]{:S(2)}) collective-permute-start(bf16[1280,640]{1,0:T(8,128)(2,1)} %convolution_convert_fusion.12), channel_id=1, source_target_pairs={{0,1},{1,0},{2,3},{3,2},{4,5},{5,4},{6,7},{7,6},{8,9},{9,8},{10,11... | collective-permute-start | bytes 4915208 | tf_op jit(solution)/shard_map/ppermute | solution.py:48
  333.9 21.3 %collective-permute-start.49 = (bf16[1,8,80,640]{3,2,1,0:T(8,128)(2,1)}, bf16[1,8,80,640]{3,2,1,0:T(8,128)(2,1)S(1)}, u32[]{:S(2)}, u32[]{:S(2)}) collective-permute-start(bf16[1,8,80,640]{3,2,1,0:T(8,128)(2,1)} %get-tuple-element.232.refs_8_), channel_id=1, source_target_pairs={{0,2},{2,0},{4,6},{6,4},{8,10},{10,8},{12,14},{14,12},{16,18},{18,... | collective-permute-start | bytes 2457608 | tf_op jit(solution)/shard_map/ppermute | solution.py:48
  335.5 20.1 %collective-permute-start.50 = (bf16[1,8,80,640]{3,2,1,0:T(8,128)(2,1)}, bf16[1,8,80,640]{3,2,1,0:T(8,128)(2,1)S(1)}, u32[]{:S(2)}, u32[]{:S(2)}) collective-permute-start(bf16[1,8,80,640]{3,2,1,0:T(8,128)(2,1)} %get-tuple-element.234.refs_10_), channel_id=1, source_target_pairs={{0,4},{2,6},{4,0},{6,2},{8,12},{10,14},{12,8},{14,10},{16,20},{18,... | collective-permute-start | bytes 2457608 | tf_op jit(solution)/shard_map/ppermute | solution.py:48
  348.4 45.5 %collective-permute-start.51 = (bf16[2,640,512]{2,1,0:T(8,128)(2,1)S(1)}, bf16[2,640,512]{2,1,0:T(8,128)(2,1)}, u32[]{:S(2)}, u32[]{:S(2)}) collective-permute-start(bf16[2,640,512]{2,1,0:T(8,128)(2,1)S(1)} %get-tuple-element.244), channel_id=1, source_target_pairs={{0,2},{2,0},{4,6},{6,4},{8,10},{10,8},{12,14},{14,12},{16,18},{18,... | collective-permute-start | bytes 3932168 | tf_op jit(solution)/shard_map/ppermute | solution.py:48
  356.6 28.0 %collective-permute-start.52 = (bf16[1,4,80,640]{3,2,1,0:T(8,128)(2,1)S(1)}, bf16[1,4,80,640]{3,2,1,0:T(8,128)(2,1)}, u32[]{:S(2)}, u32[]{:S(2)}) collective-permute-start(bf16[1,4,80,640]{3,2,1,0:T(8,128)(2,1)S(1)} %get-tuple-element.238.refs_10_), channel_id=1, source_target_pairs={{0,4},{2,6},{4,0},{6,2},{8,12},{10,14},{12,8},{14,10},{16,20},{18,... | collective-permute-start | bytes 1228808 | tf_op jit(solution)/shard_map/ppermute | solution.py:48
  357.2 35.0 %collective-permute-start.53 = (bf16[1,4,80,640]{3,2,1,0:T(8,128)(2,1)S(1)}, bf16[1,4,80,640]{3,2,1,0:T(8,128)(2,1)}, u32[]{:S(2)}, u32[]{:S(2)}) collective-permute-start(bf16[1,4,80,640]{3,2,1,0:T(8,128)(2,1)S(1)} %get-tuple-element.240.refs_12_), channel_id=1, source_target_pairs={{0,2},{2,0},{4,6},{6,4},{8,10},{10,8},{12,14},{14,12},{16,18},{18,... | collective-permute-start | bytes 1228808 | tf_op jit(solution)/shard_map/ppermute | solution.py:48
  381.7 39.8 %collective-permute-start.56 = (bf16[1,8,80,640]{3,2,1,0:T(8,128)(2,1)S(1)}, bf16[1,8,80,640]{3,2,1,0:T(8,128)(2,1)S(1)}, u32[]{:S(2)}, u32[]{:S(2)}) collective-permute-start(bf16[1,8,80,640]{3,2,1,0:T(8,128)(2,1)S(1)} %get-tuple-element.249.refs_3_), channel_id=1, source_target_pairs={{0,2},{2,0},{4,6},{6,4},{8,10},{10,8},{12,14},{14,12},{16,18},{18,... | collective-permute-start | bytes 2457608 | tf_op jit(solution)/shard_map/ppermute | solution.py:48
  383.1 38.4 %collective-permute-start.57 = (bf16[1,8,80,640]{3,2,1,0:T(8,128)(2,1)S(1)}, bf16[1,8,80,640]{3,2,1,0:T(8,128)(2,1)S(1)}, u32[]{:S(2)}, u32[]{:S(2)}) collective-permute-start(bf16[1,8,80,640]{3,2,1,0:T(8,128)(2,1)S(1)} %get-tuple-element.251.refs_5_), channel_id=1, source_target_pairs={{0,4},{2,6},{4,0},{6,2},{8,12},{10,14},{12,8},{14,10},{16,20},{18,... | collective-permute-start | bytes 2457608 | tf_op jit(solution)/shard_map/ppermute | solution.py:48
  393.5 26.8 %collective-permute-start.55 = (bf16[2,2,80,640]{3,2,1,0:T(8,128)(2,1)S(1)}, bf16[2,2,80,640]{3,2,1,0:T(8,128)(2,1)S(1)}, u32[]{:S(2)}, u32[]{:S(2)}) collective-permute-start(bf16[2,2,80,640]{3,2,1,0:T(8,128)(2,1)S(1)} %get-tuple-element.247.refs_1_), channel_id=1, source_target_pairs={{0,8},{2,10},{4,12},{6,14},{8,0},{10,2},{12,4},{14,6},{16,24},{18,... | collective-permute-start | bytes 1228808 | tf_op jit(solution)/shard_map/ppermute | solution.py:48
  403.6 17.9 %collective-permute-start.54 = (bf16[1280,512]{1,0:T(8,128)(2,1)}, bf16[1280,512]{1,0:T(8,128)(2,1)}, u32[]{:S(2)}, u32[]{:S(2)}) collective-permute-start(bf16[1280,512]{1,0:T(8,128)(2,1)} %fusion.17), channel_id=1, source_target_pairs={{0,1},{1,0},{2,3},{3,2},{4,5},{5,4},{6,7},{7,6},{8,9},{9,8},{10,11... | collective-permute-start | bytes 3932168 | tf_op jit(solution)/shard_map/ppermute | solution.py:48
  414.6 43.8 %collective-permute-start.62 = (bf16[1,8,80,640]{3,2,1,0:T(8,128)(2,1)}, bf16[1,8,80,640]{3,2,1,0:T(8,128)(2,1)S(1)}, u32[]{:S(2)}, u32[]{:S(2)}) collective-permute-start(bf16[1,8,80,640]{3,2,1,0:T(8,128)(2,1)} %get-tuple-element.263), channel_id=1, source_target_pairs={{0,2},{2,0},{4,6},{6,4},{8,10},{10,8},{12,14},{14,12},{16,18},{18,... | collective-permute-start | bytes 2457608 | tf_op jit(solution)/shard_map/ppermute | solution.py:48
  420.3 38.1 %collective-permute-start.63 = (bf16[1,8,80,640]{3,2,1,0:T(8,128)(2,1)S(1)}, bf16[1,8,80,640]{3,2,1,0:T(8,128)(2,1)S(1)}, u32[]{:S(2)}, u32[]{:S(2)}) collective-permute-start(bf16[1,8,80,640]{3,2,1,0:T(8,128)(2,1)S(1)} %get-tuple-element.265), channel_id=1, source_target_pairs={{0,4},{2,6},{4,0},{6,2},{8,12},{10,14},{12,8},{14,10},{16,20},{18,... | collective-permute-start | bytes 2457608 | tf_op jit(solution)/shard_map/ppermute | solution.py:48
  450.3 34.5 %collective-permute-start.65 = (bf16[1280,640]{1,0:T(8,128)(2,1)}, bf16[1280,640]{1,0:T(8,128)(2,1)}, u32[]{:S(2)}, u32[]{:S(2)}) collective-permute-start(bf16[1280,640]{1,0:T(8,128)(2,1)} %convolution_convert_fusion.10), channel_id=1, source_target_pairs={{0,1},{1,0},{2,3},{3,2},{4,5},{5,4},{6,7},{7,6},{8,9},{9,8},{10,11... | collective-permute-start | bytes 4915208 | tf_op jit(solution)/shard_map/ppermute | solution.py:48
  450.8 37.8 %collective-permute-start.66 = (bf16[1280,640]{1,0:T(8,128)(2,1)}, bf16[1280,640]{1,0:T(8,128)(2,1)}, u32[]{:S(2)}, u32[]{:S(2)}) collective-permute-start(bf16[1280,640]{1,0:T(8,128)(2,1)} %convolution_convert_fusion.8), channel_id=1, source_target_pairs={{0,1},{1,0},{2,3},{3,2},{4,5},{5,4},{6,7},{7,6},{8,9},{9,8},{10,11... | collective-permute-start | bytes 4915208 | tf_op jit(solution)/shard_map/ppermute | solution.py:48
  470.8 26.0 %collective-permute-start.64 = (bf16[1280,512]{1,0:T(8,128)(2,1)}, bf16[1280,512]{1,0:T(8,128)(2,1)S(1)}, u32[]{:S(2)}, u32[]{:S(2)}) collective-permute-start(bf16[1280,512]{1,0:T(8,128)(2,1)} %get-tuple-element.376), channel_id=1, source_target_pairs={{0,1},{1,0},{2,3},{3,2},{4,5},{5,4},{6,7},{7,6},{8,9},{9,8},{10,11... | collective-permute-start | bytes 3932168 | tf_op jit(solution)/shard_map/ppermute | solution.py:48
  479.4 17.4 %collective-permute-start.68 = (bf16[1,4,80,640]{3,2,1,0:T(8,128)(2,1)S(1)}, bf16[1,4,80,640]{3,2,1,0:T(8,128)(2,1)S(1)}, u32[]{:S(2)}, u32[]{:S(2)}) collective-permute-start(bf16[1,4,80,640]{3,2,1,0:T(8,128)(2,1)S(1)} %get-tuple-element.274), channel_id=1, source_target_pairs={{0,4},{2,6},{4,0},{6,2},{8,12},{10,14},{12,8},{14,10},{16,20},{18,... | collective-permute-start | bytes 1228808 | tf_op jit(solution)/shard_map/ppermute | solution.py:48
  491.8 25.8 %collective-permute-start.71 = (bf16[1,8,80,640]{3,2,1,0:T(8,128)(2,1)S(1)}, bf16[1,8,80,640]{3,2,1,0:T(8,128)(2,1)S(1)}, u32[]{:S(2)}, u32[]{:S(2)}) collective-permute-start(bf16[1,8,80,640]{3,2,1,0:T(8,128)(2,1)S(1)} %get-tuple-element.268.refs_8_), channel_id=1, source_target_pairs={{0,2},{2,0},{4,6},{6,4},{8,10},{10,8},{12,14},{14,12},{16,18},{18,... | collective-permute-start | bytes 2457608 | tf_op jit(solution)/shard_map/ppermute | solution.py:48
  495.8 21.8 %collective-permute-start.72 = (bf16[1,8,80,640]{3,2,1,0:T(8,128)(2,1)S(1)}, bf16[1,8,80,640]{3,2,1,0:T(8,128)(2,1)}, u32[]{:S(2)}, u32[]{:S(2)}) collective-permute-start(bf16[1,8,80,640]{3,2,1,0:T(8,128)(2,1)S(1)} %get-tuple-element.270.refs_10_), channel_id=1, source_target_pairs={{0,4},{2,6},{4,0},{6,2},{8,12},{10,14},{12,8},{14,10},{16,20},{18,... | collective-permute-start | bytes 2457608 | tf_op jit(solution)/shard_map/ppermute | solution.py:48
  497.6 20.0 %collective-permute-start.70 = (bf16[2,2,80,640]{3,2,1,0:T(8,128)(2,1)S(1)}, bf16[2,2,80,640]{3,2,1,0:T(8,128)(2,1)S(1)}, u32[]{:S(2)}, u32[]{:S(2)}) collective-permute-start(bf16[2,2,80,640]{3,2,1,0:T(8,128)(2,1)S(1)} %get-tuple-element.279.refs_14_), channel_id=1, source_target_pairs={{0,8},{2,10},{4,12},{6,14},{8,0},{10,2},{12,4},{14,6},{16,24},{18,... | collective-permute-start | bytes 1228808 | tf_op jit(solution)/shard_map/ppermute | solution.py:48
  510.3 50.7 %collective-permute-start.73 = (bf16[2,640,512]{2,1,0:T(8,128)(2,1)}, bf16[2,640,512]{2,1,0:T(8,128)(2,1)}, u32[]{:S(2)}, u32[]{:S(2)}) collective-permute-start(bf16[2,640,512]{2,1,0:T(8,128)(2,1)} %get-tuple-element.291), channel_id=1, source_target_pairs={{0,2},{2,0},{4,6},{6,4},{8,10},{10,8},{12,14},{14,12},{16,18},{18,... | collective-permute-start | bytes 3932168 | tf_op jit(solution)/shard_map/ppermute | solution.py:48
  523.3 31.8 %collective-permute-start.74 = (bf16[2,1,80,640]{3,2,1,0:T(8,128)(2,1)}, bf16[2,1,80,640]{3,2,1,0:T(8,128)(2,1)}, u32[]{:S(2)}, u32[]{:S(2)}) collective-permute-start(bf16[2,1,80,640]{3,2,1,0:T(8,128)(2,1)} %get-tuple-element.283.refs_10_), channel_id=1, source_target_pairs={{0,16},{2,18},{4,20},{6,22},{8,24},{10,26},{12,28},{14,30},{16,0},... | collective-permute-start | bytes 614408 | tf_op jit(solution)/shard_map/ppermute | solution.py:48
  526.7 29.4 %collective-permute-start.75 = (bf16[1,4,80,640]{3,2,1,0:T(8,128)(2,1)}, bf16[1,4,80,640]{3,2,1,0:T(8,128)(2,1)}, u32[]{:S(2)}, u32[]{:S(2)}) collective-permute-start(bf16[1,4,80,640]{3,2,1,0:T(8,128)(2,1)} %get-tuple-element.285.refs_12_), channel_id=1, source_target_pairs={{0,4},{2,6},{4,0},{6,2},{8,12},{10,14},{12,8},{14,10},{16,20},{18,... | collective-permute-start | bytes 1228808 | tf_op jit(solution)/shard_map/ppermute | solution.py:48
  527.8 28.3 %collective-permute-start.76 = (bf16[1,4,80,640]{3,2,1,0:T(8,128)(2,1)}, bf16[1,4,80,640]{3,2,1,0:T(8,128)(2,1)}, u32[]{:S(2)}, u32[]{:S(2)}) collective-permute-start(bf16[1,4,80,640]{3,2,1,0:T(8,128)(2,1)} %get-tuple-element.287.refs_14_), channel_id=1, source_target_pairs={{0,2},{2,0},{4,6},{6,4},{8,10},{10,8},{12,14},{14,12},{16,18},{18,... | collective-permute-start | bytes 1228808 | tf_op jit(solution)/shard_map/ppermute | solution.py:48
  552.8 25.4 %collective-permute-start.81 = (bf16[1,8,80,640]{3,2,1,0:T(8,128)(2,1)}, bf16[1,8,80,640]{3,2,1,0:T(8,128)(2,1)}, u32[]{:S(2)}, u32[]{:S(2)}) collective-permute-start(bf16[1,8,80,640]{3,2,1,0:T(8,128)(2,1)} %get-tuple-element.298.refs_5_), channel_id=1, source_target_pairs={{0,2},{2,0},{4,6},{6,4},{8,10},{10,8},{12,14},{14,12},{16,18},{18,... | collective-permute-start | bytes 2457608 | tf_op jit(solution)/shard_map/ppermute | solution.py:48
  555.1 24.3 %collective-permute-start.82 = (bf16[1,8,80,640]{3,2,1,0:T(8,128)(2,1)}, bf16[1,8,80,640]{3,2,1,0:T(8,128)(2,1)S(1)}, u32[]{:S(2)}, u32[]{:S(2)}) collective-permute-start(bf16[1,8,80,640]{3,2,1,0:T(8,128)(2,1)} %copy-done.31), channel_id=1, source_target_pairs={{0,4},{2,6},{4,0},{6,2},{8,12},{10,14},{12,8},{14,10},{16,20},{18,... | collective-permute-start | bytes 2457608 | tf_op jit(solution)/shard_map/ppermute | solution.py:48
  560.6 18.9 %collective-permute-start.80 = (bf16[2,2,80,640]{3,2,1,0:T(8,128)(2,1)S(1)}, bf16[2,2,80,640]{3,2,1,0:T(8,128)(2,1)S(1)}, u32[]{:S(2)}, u32[]{:S(2)}) collective-permute-start(bf16[2,2,80,640]{3,2,1,0:T(8,128)(2,1)S(1)} %get-tuple-element.296.refs_3_), channel_id=1, source_target_pairs={{0,8},{2,10},{4,12},{6,14},{8,0},{10,2},{12,4},{14,6},{16,24},{18,... | collective-permute-start | bytes 1228808 | tf_op jit(solution)/shard_map/ppermute | solution.py:48
  572.9 26.4 %collective-permute-start.77 = (bf16[1280,512]{1,0:T(8,128)(2,1)}, bf16[1280,512]{1,0:T(8,128)(2,1)S(1)}, u32[]{:S(2)}, u32[]{:S(2)}) collective-permute-start(bf16[1280,512]{1,0:T(8,128)(2,1)} %fusion.13), channel_id=1, source_target_pairs={{0,1},{1,0},{2,3},{3,2},{4,5},{5,4},{6,7},{7,6},{8,9},{9,8},{10,11... | collective-permute-start | bytes 3932168 | tf_op jit(solution)/shard_map/ppermute | solution.py:48
  578.1 20.7 %collective-permute-start.78 = (bf16[1,8,80,640]{3,2,1,0:T(8,128)(2,1)S(1)}, bf16[1,8,80,640]{3,2,1,0:T(8,128)(2,1)S(1)}, u32[]{:S(2)}, u32[]{:S(2)}) collective-permute-start(bf16[1,8,80,640]{3,2,1,0:T(8,128)(2,1)S(1)} %get-tuple-element.304), channel_id=1, source_target_pairs={{0,2},{2,0},{4,6},{6,4},{8,10},{10,8},{12,14},{14,12},{16,18},{18,... | collective-permute-start | bytes 2457608 | tf_op jit(solution)/shard_map/ppermute | solution.py:48
  578.2 21.1 %collective-permute-start.79 = (bf16[1,8,80,640]{3,2,1,0:T(8,128)(2,1)S(1)}, bf16[1,8,80,640]{3,2,1,0:T(8,128)(2,1)S(1)}, u32[]{:S(2)}, u32[]{:S(2)}) collective-permute-start(bf16[1,8,80,640]{3,2,1,0:T(8,128)(2,1)S(1)} %get-tuple-element.306), channel_id=1, source_target_pairs={{0,4},{2,6},{4,0},{6,2},{8,12},{10,14},{12,8},{14,10},{16,20},{18,... | collective-permute-start | bytes 2457608 | tf_op jit(solution)/shard_map/ppermute | solution.py:48
  581.1 29.2 %collective-permute-start.83 = (bf16[2,1,80,640]{3,2,1,0:T(8,128)(2,1)S(1)}, bf16[2,1,80,640]{3,2,1,0:T(8,128)(2,1)S(1)}, u32[]{:S(2)}, u32[]{:S(2)}) collective-permute-start(bf16[2,1,80,640]{3,2,1,0:T(8,128)(2,1)S(1)} %get-tuple-element.309), channel_id=1, source_target_pairs={{0,16},{2,18},{4,20},{6,22},{8,24},{10,26},{12,28},{14,30},{16,0},... | collective-permute-start | bytes 614408 | tf_op jit(solution)/shard_map/ppermute | solution.py:48
  584.5 25.8 %collective-permute-start.84 = (bf16[1,4,80,640]{3,2,1,0:T(8,128)(2,1)S(1)}, bf16[1,4,80,640]{3,2,1,0:T(8,128)(2,1)S(1)}, u32[]{:S(2)}, u32[]{:S(2)}) collective-permute-start(bf16[1,4,80,640]{3,2,1,0:T(8,128)(2,1)S(1)} %get-tuple-element.312), channel_id=1, source_target_pairs={{0,4},{2,6},{4,0},{6,2},{8,12},{10,14},{12,8},{14,10},{16,20},{18,... | collective-permute-start | bytes 1228808 | tf_op jit(solution)/shard_map/ppermute | solution.py:48
  (232 other events, 1842.9 us)

commit v7 on v6

--- a/solution.py
+++ b/solution.py
@@ -4,6 +4,7 @@
 import jax
 import jax.numpy as jnp
 from jax import lax
+from jax.experimental.layout import Layout, with_layout_constraint
 from jax.experimental import pallas as pl
 from jax.experimental.pallas import tpu as pltpu
 from jax.sharding import PartitionSpec as P
@@ -356,7 +357,8 @@
     if lax.axis_size("tensor") != 2:
         whole = lax.psum_scatter(lowered(parts[0]), "tensor", scatter_dimension=1, tiled=True)
         return whole, None
-    return lowered(parts[0]), pair_swap(lowered(parts[1]), "tensor", 1)
+    mine, theirs = [with_layout_constraint(lowered(part), Layout((0, 1))) for part in parts]
+    return mine, pair_swap(theirs, "tensor", 1)
 
 
 def exchange_sum(values, axis, bit, bits, exchange):
@@ -430,74 +432,82 @@
     return [(tile, slice(tile * TILE, tile * TILE + TILE)) for tile in range(tokens // TILE)]
 
 
-def ahead(items, first, second):
-    items = list(items)
-    held = first(items[0])
-    for place, item in enumerate(items):
-        following = first(items[place + 1]) if place + 1 < len(items) else None
-        second(item, held)
+def ahead(steps):
+    held = steps[0][0]()
+    for place, (_, second) in enumerate(steps):
+        following = steps[place + 1][0]() if place + 1 < len(steps) else None
+        second(held)
         held = following
 
 
-def own_forward(start_ref, q_ref, k_ref, v_ref, sum_ref, top_ref, total_ref):
-    keys = k_ref[...].T
-
-    def scores_of(item):
-        tile, at = item
-        query, start = q_ref[:, at], start_ref[:, at]
-        return [
-            masked(dot_nn(keys[key : key + count], query), kind, key, tile * TILE, start)
-            for key, count, kind in key_parts(tile)
-        ]
-
-    def mix(item, parts):
-        tile, at = item
-        highest = jnp.max(parts[0], axis=0, keepdims=True)
-        for scores in parts[1:]:
-            highest = jnp.maximum(highest, jnp.max(scores, axis=0, keepdims=True))
-        total, mixed = 0.0, 0.0
-        for scores, (key, count, _) in zip(parts, key_parts(tile)):
-            weights = jnp.exp2(scores - highest)
-            total = total + jnp.sum(weights, axis=0, keepdims=True)
-            mixed = mixed + dot_nn(v_ref[:, key : key + count], lowered(weights))
-        sum_ref[:, at] = mixed
-        top_ref[:, at] = highest
-        total_ref[:, at] = total
-
-    ahead(spans(q_ref), scores_of, mix)
-
-
-def far_forward(
-    side_ref, q_ref, k_ref, v_ref, sum_ref, top_ref, total_ref, out_ref, lse_ref
-):
-    keys = k_ref[...].T
-
-    def scores_of(at):
-        return dot_nn(keys, q_ref[:, at])
-
-    def mix(at, scores):
-        highest = jnp.maximum(top_ref[:, at], jnp.max(scores, axis=0, keepdims=True))
-        weights = jnp.exp2(scores - highest)
-        scale = jnp.exp2(top_ref[:, at] - highest)
-        total = total_ref[:, at] * scale + jnp.sum(weights, axis=0, keepdims=True)
-        mixed = sum_ref[:, at] * scale + dot_nn(v_ref[...], lowered(weights))
-        out_ref[:, at] = lowered(mixed / total)
-        lse_ref[:, at] = highest + jnp.log2(total)
-
+def own_forward(heads):
+    def steps(start_ref, q_ref, k_ref, v_ref, sum_ref, top_ref, total_ref):
+        keys = k_ref[...].T
+
+        def scores_of(tile, at):
+            query, start = q_ref[:, at], start_ref[:, at]
+            return [
+                masked(dot_nn(keys[key : key + count], query), kind, key, tile * TILE, start)
+                for key, count, kind in key_parts(tile)
+            ]
+
+        def mix(tile, at, parts):
+            highest = jnp.max(parts[0], axis=0, keepdims=True)
+            for scores in parts[1:]:
+                highest = jnp.maximum(highest, jnp.max(scores, axis=0, keepdims=True))
+            total, mixed = 0.0, 0.0
+            for scores, (key, count, _) in zip(parts, key_parts(tile)):
+                weights = jnp.exp2(scores - highest)
+                total = total + jnp.sum(weights, axis=0, keepdims=True)
+                mixed = mixed + dot_nn(v_ref[:, key : key + count], lowered(weights))
+            sum_ref[:, at] = mixed
+            top_ref[:, at] = highest
+            total_ref[:, at] = total
+
+        return [(partial(scores_of, *item), partial(mix, *item)) for item in spans(q_ref)]
+
+    ahead([step for refs in heads for step in steps(*refs)])
+
+
+def sides(side_ref, q_ref, run):
     tiles = [at for _, at in spans(q_ref)]
     conts = [at for tile, at in spans(q_ref) if tile * TILE >= PROMPT_DEV]
 
     @pl.when(side_ref[0] == 0)
     def _():
-        for at in tiles:
-            if at not in conts:
+        run(conts, [at for at in tiles if at not in conts])
+
+    @pl.when(side_ref[0] != 0)
+    def _():
+        run(tiles, [])
+
+
+def far_forward(heads):
+    def steps(tiles, _, q_ref, k_ref, v_ref, sum_ref, top_ref, total_ref, out_ref, lse_ref):
+        keys = k_ref[...].T
+
+        def scores_of(at):
+            return dot_nn(keys, q_ref[:, at])
+
+        def mix(at, scores):
+            highest = jnp.maximum(top_ref[:, at], jnp.max(scores, axis=0, keepdims=True))
+            weights = jnp.exp2(scores - highest)
+            scale = jnp.exp2(top_ref[:, at] - highest)
+            total = total_ref[:, at] * scale + jnp.sum(weights, axis=0, keepdims=True)
+            mixed = sum_ref[:, at] * scale + dot_nn(v_ref[...], lowered(weights))
+            out_ref[:, at] = lowered(mixed / total)
+            lse_ref[:, at] = highest + jnp.log2(total)
+
+        return [(partial(scores_of, at), partial(mix, at)) for at in tiles]
+
+    def run(tiles, others):
+        for _, _, _, _, sum_ref, top_ref, total_ref, out_ref, lse_ref in heads:
+            for at in others:
                 out_ref[:, at] = lowered(sum_ref[:, at] / total_ref[:, at])
                 lse_ref[:, at] = top_ref[:, at] + jnp.log2(total_ref[:, at])
-        ahead(conts, scores_of, mix)
-
-    @pl.when(side_ref[0] != 0)
-    def _():
-        ahead(tiles, scores_of, mix)
+        ahead([step for refs in heads for step in steps(tiles, *refs)])
+
+    sides(heads[0][0], heads[0][1], run)
 
 
 def score_grads(scores, lse, d_shares, delta):
@@ -505,19 +515,20 @@
     return lowered(shares), lowered(shares * (d_shares - delta))
 
 
-def far_backward(
-    side_ref, q_ref, k_ref, v_ref, out_ref, grad_ref, lse_ref, dq_ref, delta_ref, dkv_ref
-):
-    keys, values = k_ref[...].T, v_ref[...].T
-    delta_ref[...] = jnp.sum(
-        out_ref[...].astype(jnp.float32) * grad_ref[...].astype(jnp.float32), axis=0, keepdims=True
-    )
-
-    def begin(at):
-        return dot_nn(keys, q_ref[:, at]), dot_nn(values, grad_ref[:, at])
-
-    def close(tiles):
+def far_backward(heads):
+    def steps(
+        tiles, _, q_ref, k_ref, v_ref, out_ref, grad_ref, lse_ref, dq_ref, delta_ref, dkv_ref
+    ):
+        keys, values = k_ref[...].T, v_ref[...].T
+        delta_ref[...] = jnp.sum(
+            out_ref[...].astype(jnp.float32) * grad_ref[...].astype(jnp.float32),
+            axis=0,
+            keepdims=True,
+        )
         sums = [0.0, 0.0]
+
+        def begin(at):
+            return dot_nn(keys, q_ref[:, at]), dot_nn(values, grad_ref[:, at])
 
         def terms(at, held):
             scores, d_shares = held
@@ -525,116 +536,128 @@
             dq_ref[:, at] = dot_nn(k_ref[...], d_scores)
             sums[0] = sums[0] + dot_nt(q_ref[:, at], d_scores)
             sums[1] = sums[1] + dot_nt(grad_ref[:, at], shares)
-
-        ahead(tiles, begin, terms)
-        dkv_ref[0] = lowered(sums[0] * LN_TWO)
-        dkv_ref[1] = lowered(sums[1])
-
-    tiles = [at for _, at in spans(q_ref)]
-    conts = [at for tile, at in spans(q_ref) if tile * TILE >= PROMPT_DEV]
-
-    @pl.when(side_ref[0] == 0)
-    def _():
-        for at in tiles:
-            if at not in conts:
-                dq_ref[:, at] = jnp.zeros_like(dq_ref[:, at])
-        close(conts)
-
-    @pl.when(side_ref[0] != 0)
-    def _():
-        close(tiles)
-
-
-def own_backward(
-    start_ref,
-    gain_ref,
-    q_ref,
-    k_ref,
-    v_ref,
-    grad_ref,
-    lse_ref,
-    delta_ref,
-    far_dq_ref,
-    dq_ref,
-    dk_ref,
-    dv_ref,
-    scale_ref,
-    k_total,
-    v_total,
-):
-    keys, values = k_ref[...].T, v_ref[...].T
-    seen, dqs, scales = set(), {}, [0.0]
-
-    def begin(item):
-        (tile, at), (key, count, kind), _ = item
-        scores = dot_nn(keys[key : key + count], q_ref[:, at])
-        scores = masked(scores, kind, key, tile * TILE, start_ref[:, at])
-        return scores, dot_nn(values[key : key + count], grad_ref[:, at])
-
-    def terms(item, held):
-        (tile, at), (key, count, _), last = item
-        scores, d_shares = held
-        query, grad = q_ref[:, at], grad_ref[:, at]
-        shares, d_scores = score_grads(scores, lse_ref[:, at], d_shares, delta_ref[:, at])
-        dv = dot_nt(grad, shares)
-        dk = dot_nt(query, d_scores)
-        dq = dqs.get(tile, far_dq_ref[:, at]) + dot_nn(k_ref[:, key : key + count], d_scores)
-        dqs[tile] = dq
-        for offset in range(0, count, TILE):
-            there = slice(key + offset, key + offset + TILE)
-            here = slice(offset, offset + TILE)
-            if key + offset in seen:
-                k_total[:, there] += dk[:, here]
-                v_total[:, there] += dv[:, here]
-            else:
-                seen.add(key + offset)
-                k_total[:, there] = dk[:, here]
-                v_total[:, there] = dv[:, here]
-        if last:
-            dq_ref[:, at] = lowered(dq * gain_ref[...])
-            product = jnp.sum(dq * query.astype(jnp.float32), axis=1, keepdims=True)
-            scales[0] = scales[0] + product
-
-    items = []
-    for tile, at in spans(q_ref):
-        parts = key_parts(tile)
-        items += [((tile, at), part, part is parts[-1]) for part in parts]
-    ahead(items, begin, terms)
-    dk_ref[...] = lowered(k_total[...] * LN_TWO)
-    dv_ref[...] = lowered(v_total[...])
-    scale_ref[...] = scales[0]
-
-
-def rows_block(count):
-    return pl.BlockSpec((HD, count), lambda head: (head, 0))
-
-
-def flat_block(count):
-    return pl.BlockSpec((None, 1, count), lambda head: (head, 0, 0))
-
-
-def same_block(*shape):
-    return pl.BlockSpec(shape, lambda head: (0, 0))
+            if at is tiles[-1]:
+                dkv_ref[0] = lowered(sums[0] * LN_TWO)
+                dkv_ref[1] = lowered(sums[1])
+
+        return [(partial(begin, at), partial(terms, at)) for at in tiles]
+
+    def run(tiles, others):
+        for refs in heads:
+            for at in others:
+                refs[7][:, at] = jnp.zeros_like(refs[7][:, at])
+        ahead([step for refs in heads for step in steps(tiles, *refs)])
+
+    sides(heads[0][0], heads[0][1], run)
+
+
+def own_backward(heads):
+    def steps(
+        start_ref,
+        gain_ref,
+        q_ref,
+        k_ref,
+        v_ref,
+        grad_ref,
+        lse_ref,
+        delta_ref,
+        far_dq_ref,
+        dq_ref,
+        dk_ref,
+        dv_ref,
+        scale_ref,
+        k_total,
+        v_total,
+    ):
+        keys, values = k_ref[...].T, v_ref[...].T
+        seen, dqs, scales = set(), {}, [0.0]
+        final = spans(q_ref)[-1][0]
+
+        def begin(tile, at, part, last):
+            key, count, kind = part
+            scores = dot_nn(keys[key : key + count], q_ref[:, at])
+            scores = masked(scores, kind, key, tile * TILE, start_ref[:, at])
+            return scores, dot_nn(values[key : key + count], grad_ref[:, at])
+
+        def terms(tile, at, part, last, held):
+            key, count, _ = part
+            scores, d_shares = held
+            query, grad = q_ref[:, at], grad_ref[:, at]
+            shares, d_scores = score_grads(scores, lse_ref[:, at], d_shares, delta_ref[:, at])
+            dv = dot_nt(grad, shares)
+            dk = dot_nt(query, d_scores)
+            dq = dqs.get(tile, far_dq_ref[:, at])
+            dqs[tile] = dq = dq + dot_nn(k_ref[:, key : key + count], d_scores)
+            for offset in range(0, count, TILE):
+                there = slice(key + offset, key + offset + TILE)
+                here = slice(offset, offset + TILE)
+                if key + offset in seen:
+                    k_total[:, there] += dk[:, here]
+                    v_total[:, there] += dv[:, here]
+                else:
+                    seen.add(key + offset)
+                    k_total[:, there] = dk[:, here]
+                    v_total[:, there] = dv[:, here]
+            if last:
+                dq_ref[:, at] = lowered(dq * gain_ref[...])
+                product = jnp.sum(dq * query.astype(jnp.float32), axis=1, keepdims=True)
+                scales[0] = scales[0] + product
+                if tile == final:
+                    dk_ref[...] = lowered(k_total[...] * LN_TWO)
+                    dv_ref[...] = lowered(v_total[...])
+                    scale_ref[...] = scales[0]
+
+        items = []
+        for tile, at in spans(q_ref):
+            parts = key_parts(tile)
+            items += [(tile, at, part, part is parts[-1]) for part in parts]
+        return [(partial(begin, *item), partial(terms, *item)) for item in items]
+
+    ahead([step for refs in heads for step in steps(*refs)])
 
 
 def per_head(kernel, name, heads, area, products, ins, outs, after=(), scratch=()):
-    flops = 40 * area * heads * products
+    group = 2 - heads % 2
     moved = sum(array.size * array.dtype.itemsize for _, array in ins)
+
+    def spec(kind, shape):
+        if kind == "rows":
+            return pl.BlockSpec((group * HD, shape[1]), lambda step: (step, 0))
+        if kind == "flat":
+            return pl.BlockSpec((group, 1, shape[2]), lambda step: (step, 0, 0))
+        if kind == "pair":
+            return pl.BlockSpec((2, group * HD, shape[2]), lambda step: (0, step, 0))
+        return pl.BlockSpec(shape, lambda step: (0, 0)) if kind == "same" else SCALAR
+
+    def view(kind, ref, head):
+        rows = pl.ds(head * HD, HD)
+        if kind == "rows":
+            return ref.at[rows]
+        if kind == "flat":
+            return ref.at[head]
+        return ref.at[:, rows] if kind == "pair" else ref
+
     count = len(ins)
+    kinds = [kind for kind, _ in ins] + [out[0] for out in outs] + ["rows"] * len(scratch)
 
     def work(*refs):
-        kernel(*refs[:count], *refs[count + len(after) :])
+        refs = refs[:count] + refs[count + len(after) :]
+        kernel(
+            [[view(kind, ref, head) for kind, ref in zip(kinds, refs)] for head in range(group)]
+        )
 
     return pl.pallas_call(
         work,
-        grid=(heads,),
-        in_specs=[spec for spec, _ in ins] + [UNREAD] * len(after),
-        out_specs=[spec for spec, _, _ in outs],
+        grid=(heads // group,),
+        in_specs=[spec(kind, array.shape) for kind, array in ins] + [UNREAD] * len(after),
+        out_specs=[spec(kind, shape) for kind, shape, _ in outs],
         out_shape=[jax.ShapeDtypeStruct(shape, kind) for _, shape, kind in outs],
-        scratch_shapes=list(scratch),
-        compiler_params=pltpu.CompilerParams(vmem_limit_bytes=32 << 20),
+        scratch_shapes=[pltpu.VMEM((group * HD, tokens), jnp.float32) for tokens in scratch],
+        compiler_params=pltpu.CompilerParams(vmem_limit_bytes=40 << 20),
         cost_estimate=pl.CostEstimate(
-            flops=flops, bytes_accessed=moved, transcendentals=area * heads
+            flops=40 * area * heads * products,
+            bytes_accessed=moved,
+            transcendentals=area * heads,
         ),
         name=name,
     )(*[array for _, array in ins], *after)
@@ -643,24 +666,15 @@
 def attention_own(start, queries, keys, values, after):
     width, tokens = queries.shape
     heads = width // HD
-    all_rows, flat = rows_block(tokens), flat_block(tokens)
+    flat = ("flat", (heads, 1, tokens), jnp.float32)
     return per_head(
         own_forward,
         "attention_own",
         heads,
         tokens * tokens * 5 // 8,
         3,
-        [
-            (same_block(1, tokens), start),
-            (all_rows, queries),
-            (all_rows, keys),
-            (all_rows, values),
-        ],
-        [
-            (all_rows, (width, tokens), jnp.float32),
-            (flat, (heads, 1, tokens), jnp.float32),
-            (flat, (heads, 1, tokens), jnp.float32),
-        ],
+        [("same", start), ("rows", queries), ("rows", keys), ("rows", values)],
+        [("rows", (width, tokens), jnp.float32), flat, flat],
         after,
     )
 
@@ -668,7 +682,6 @@
 def attention_far(side, queries, keys, values, partial_sum, top, total, after):
     width, tokens = queries.shape
     heads = width // HD
-    all_rows, flat, far_rows = rows_block(tokens), flat_block(tokens), rows_block(PROMPT_DEV)
     return per_head(
         far_forward,
         "attention_far",
@@ -676,17 +689,17 @@
         tokens * PROMPT_DEV,
         2,
         [
-            (SCALAR, side),
-            (all_rows, queries),
-            (far_rows, keys),
-            (far_rows, values),
-            (all_rows, partial_sum),
-            (flat, top),
-            (flat, total),
+            ("scalar", side),
+            ("rows", queries),
+            ("rows", keys),
+            ("rows", values),
+            ("rows", partial_sum),
+            ("flat", top),
+            ("flat", total),
         ],
         [
-            (all_rows, (width, tokens), jnp.bfloat16),
-            (flat, (heads, 1, tokens), jnp.float32),
+            ("rows", (width, tokens), jnp.bfloat16),
+            ("flat", (heads, 1, tokens), jnp.float32),
         ],
         after,
     )
@@ -695,7 +708,6 @@
 def attention_far_back(side, queries, keys, values, mixed, grads, lse, after):
     width, tokens = queries.shape
     heads = width // HD
-    all_rows, flat, far_rows = rows_block(tokens), flat_block(tokens), rows_block(PROMPT_DEV)
     return per_head(
         far_backward,
         "attention_far_back",
@@ -703,22 +715,18 @@
         tokens * PROMPT_DEV,
         3,
         [
-            (SCALAR, side),
-            (all_rows, queries),
-            (far_rows, keys),
-            (far_rows, values),
-            (all_rows, mixed),
-            (all_rows, grads),
-            (flat, lse),
+            ("scalar", side),
+            ("rows", queries),
+            ("rows", keys),
+            ("rows", values),
+            ("rows", mixed),
+            ("rows", grads),
+            ("flat", lse),
         ],
         [
-            (all_rows, (width, tokens), jnp.float32),
-            (flat, (heads, 1, tokens), jnp.float32),
-            (
-                pl.BlockSpec((2, HD, PROMPT_DEV), lambda head: (0, head, 0)),
-                (2, width, PROMPT_DEV),
-                jnp.bfloat16,
-            ),
+            ("rows", (width, tokens), jnp.float32),
+            ("flat", (heads, 1, tokens), jnp.float32),
+            ("pair", (2, width, PROMPT_DEV), jnp.bfloat16),
         ],
         after,
     )
@@ -727,7 +735,6 @@
 def attention_own_back(start, gain, queries, keys, values, grads, lse, delta, far_dq, after):
     width, tokens = queries.shape
     heads = width // HD
-    all_rows, flat = rows_block(tokens), flat_block(tokens)
     return per_head(
         own_backward,
         "attention_own_back",
@@ -735,24 +742,24 @@
         tokens * tokens * 5 // 8,
         76,
         [
-            (same_block(1, tokens), start),
-            (same_block(HD, 1), gain),
-            (all_rows, queries),
-            (all_rows, keys),
-            (all_rows, values),
-            (all_rows, grads),
-            (flat, lse),
-            (flat, delta),
-            (all_rows, far_dq),
+            ("same", start),
+            ("same", gain),
+            ("rows", queries),
+            ("rows", keys),
+            ("rows", values),
+            ("rows", grads),
+            ("flat", lse),
+            ("flat", delta),
+            ("rows", far_dq),
         ],
         [
-            (all_rows, (width, tokens), jnp.bfloat16),
-            (all_rows, (width, tokens), jnp.bfloat16),
-            (all_rows, (width, tokens), jnp.bfloat16),
-            (pl.BlockSpec((HD, 1), lambda head: (head, 0)), (width, 1), jnp.float32),
+            ("rows", (width, tokens), jnp.bfloat16),
+            ("rows", (width, tokens), jnp.bfloat16),
+            ("rows", (width, tokens), jnp.bfloat16),
+            ("rows", (width, 1), jnp.float32),
         ],
         after,
-        [pltpu.VMEM((HD, tokens), jnp.float32)] * 2,
+        (tokens, tokens),
     )
 
 

time: 671 us -> 659 us (0.982)
  Pallas kernels: 138 us -> 128 us
    pallas_call x8, Pallas kernels: 75.8 us -> 64.7 us  [per_head(): pl.pallas_call(work, grid=(heads // group,), in_specs=[spec(kind, array.s...]
    unnamed x366 -> x368, local copies, waits for them, and re-layouts: 45.3 us -> 47.2 us
  transfers between devices with their start and end apart: 99 -> 99, of which waited for: 32 -> 32; matrix products, arithmetic and copies ran while one was open for 30% -> 30% of each run, Pallas kernels for 18% -> 17%
where the time goes in v7:
time: 659 us; the launch traced here: 649 us
  matrix products  164 us (25%)
  waiting for transfers between devices  133 us (20%)
  Pallas kernels  128 us (19%)
  starting transfers between devices  123 us (19%)
  local copies, waits for them, and re-layouts  58.9 us (9%)
  other arithmetic  33.2 us (5%)
  between operations  8.53 us (1%)
    ppermute x99, waiting for transfers between devices, pair_swap(): return lax.ppermute(values, axis, [(i, i ^ bit) for i in range(size)])  133 us
    ppermute x99, starting transfers between devices, pair_swap(): return lax.ppermute(values, axis, [(i, i ^ bit) for i in range(size)])  123 us
    dot_general x24, matrix products, dot_nn(): return jnp.dot(former, latter, preferred_element_type=jnp.float32)  74.4 us
    pallas_call x8, Pallas kernels, per_head(): pl.pallas_call(work, grid=(heads // group,), in_specs=[spec(kind, array.s...  64.7 us
    pallas_call x38, Pallas kernels, quick_call(): pl.pallas_call(kernel, in_specs=[SCALAR] + [WHOLE] * (len(arrays) - 1) +...  63.7 us
    dot_general x20, matrix products, dot_tn(): lax.dot_general(former, latter, (((0,), (0,)), ((), ())), preferred_eleme...  48.4 us
    unnamed x368, local copies, waits for them, and re-layouts  47.2 us
    dot_general x16, matrix products, dot_nt(): lax.dot_general(former, latter, (((1,), (1,)), ((), ())), preferred_eleme...  41.2 us
  transfers between devices with their start and end apart: 99, of which 32 were waited for; matrix products, arithmetic and copies ran while one was open for 30% of the time, Pallas kernels for 17%

profile of v7, /device:TPU:0, one launch (start us, length us, event | category | flops | bytes accessed | tf_op | source)
XLA Modules:
  0.0 648.9 jit_solution(17438717774367143844)
XLA Ops:
  6.2 3.7 collective-permute-start
  20.9 9.9 %collective-permute-done.3.refs_3_ = bf16[1280,256]{1,0:T(8,128)(2,1)S(1)} collective-permute-done((bf16[1280,256]{1,0:T(8,128)(2,1)S(1)}, bf16[1280,256]{1,0:T(8,128)(2,1)S(1)}, u32[]{:S(2)}, u32[]{:S(2)}) %collective-permute-start.3) | collective-permute-done | bytes 655392 | tf_op jit(solution)/shard_map/ppermute | solution.py:49
  38.5 8.8 %collective-permute-done.4.refs_3_ = bf16[2,1,80,640]{3,2,1,0:T(8,128)(2,1)S(1)} collective-permute-done((bf16[2,1,80,640]{3,2,1,0:T(8,128)(2,1)S(1)}, bf16[2,1,80,640]{3,2,1,0:T(8,128)(2,1)S(1)}, u32[]{:S(2)}, u32[]{:S(2)}) %collective-permute-start.4) | collective-permute-done | bytes 204832 | tf_op jit(solution)/shard_map/ppermute | solution.py:49
  54.1 9.2 %collective-permute-done.8.refs_3_ = bf16[2,2,80,640]{3,2,1,0:T(8,128)(2,1)S(1)} collective-permute-done((bf16[2,2,80,640]{3,2,1,0:T(8,128)(2,1)}, bf16[2,2,80,640]{3,2,1,0:T(8,128)(2,1)S(1)}, u32[]{:S(2)}, u32[]{:S(2)}) %collective-permute-start.8) | collective-permute-done | bytes 409632 | tf_op jit(solution)/shard_map/ppermute | solution.py:49
  63.3 4.8 collective-permute-done.9.refs_4_
  68.3 3.5 join_halves.17
  73.8 4.4 convolution_convert_fusion.23.refs_7_.refs_2_.refs_3_
  78.3 4.4 collective-permute-done.11.refs_3_
  87.9 5.5 collective-permute-start.14
  96.4 3.5 collective-permute-done.14.refs_3_
  110.5 8.4 %attention_own.2 = (f32[640,1024]{1,0:T(8,128)S(1)}, f32[8,1,1024]{2,1,0:T(1,128)S(1)}, f32[8,1,1024]{2,1,0:T(1,128)S(1)}) custom-call(s32[1,1024]{1,0:T(1,128)S(1)} %bitcast.268, bf16[640,1024]{1,0:T(8,128)(2,1)S(1)} %multiply_convert_fusion.4.refs_1_.refs_2_, bf16[640,1024]{1,0:T(8,128)(2,1)S(1)} %copy-done.12, bf16[640,1024]{1,0:T(8,128)(2,1)S(1)} %copy-done.14), custom_call_target="tpu_custom_call" | custom-call | flops 629145600 | bytes 3936256 | tf_op jit(solution)/shard_map/attention_own/pallas_call | solution.py:649
  124.9 4.9 collective-permute-start.21
  132.9 4.4 attention_far.2
  138.6 4.0 join_halves.21
  146.2 3.6 collective-permute-start.26
  155.7 6.2 collective-permute-done.24.refs_3_
  173.9 3.5 fusion.30.refs_8_
  177.5 6.6 %collective-permute-done.29.refs_4_ = bf16[1,8,80,640]{3,2,1,0:T(8,128)(2,1)S(1)} collective-permute-done((bf16[1,8,80,640]{3,2,1,0:T(8,128)(2,1)S(1)}, bf16[1,8,80,640]{3,2,1,0:T(8,128)(2,1)S(1)}, u32[]{:S(2)}, u32[]{:S(2)}) %collective-permute-start.29) | collective-permute-done | bytes 819232 | tf_op jit(solution)/shard_map/ppermute | solution.py:49
  203.8 9.2 %collective-permute-done.31.refs_3_ = bf16[2,1,80,640]{3,2,1,0:T(8,128)(2,1)} collective-permute-done((bf16[2,1,80,640]{3,2,1,0:T(8,128)(2,1)S(1)}, bf16[2,1,80,640]{3,2,1,0:T(8,128)(2,1)}, u32[]{:S(2)}, u32[]{:S(2)}) %collective-permute-start.31) | collective-permute-done | bytes 204832 | tf_op jit(solution)/shard_map/ppermute | solution.py:49
  216.6 4.5 convolution_convert_fusion.21.refs_6_.refs_2_.refs_3_
  226.0 13.0 %collective-permute-done.36.refs_4_ = bf16[1,8,80,640]{3,2,1,0:T(8,128)(2,1)S(1)} collective-permute-done((bf16[1,8,80,640]{3,2,1,0:T(8,128)(2,1)S(1)}, bf16[1,8,80,640]{3,2,1,0:T(8,128)(2,1)S(1)}, u32[]{:S(2)}, u32[]{:S(2)}) %collective-permute-start.36) | collective-permute-done | bytes 819232 | tf_op jit(solution)/shard_map/ppermute | solution.py:49
  246.9 8.1 %attention_own.3 = (f32[640,1024]{1,0:T(8,128)S(1)}, f32[8,1,1024]{2,1,0:T(1,128)S(1)}, f32[8,1,1024]{2,1,0:T(1,128)S(1)}) custom-call(s32[1,1024]{1,0:T(1,128)S(1)} %bitcast.269, bf16[640,1024]{1,0:T(8,128)(2,1)S(1)} %multiply_convert_fusion.1.refs_1_.refs_2_, bf16[640,1024]{1,0:T(8,128)(2,1)S(1)} %copy-done.16, bf16[640,1024]{1,0:T(8,128)(2,1)S(1)} %copy-done.18), custom_call_target="tpu_custom_call" | custom-call | flops 629145600 | bytes 3936256 | tf_op jit(solution)/shard_map/attention_own/pallas_call | solution.py:649
  260.5 4.7 attention_far.3
  267.6 7.1 %collective-permute-done.43.refs_2_ = bf16[1,8,80,640]{3,2,1,0:T(8,128)(2,1)S(1)} collective-permute-done((bf16[1,8,80,640]{3,2,1,0:T(8,128)(2,1)S(1)}, bf16[1,8,80,640]{3,2,1,0:T(8,128)(2,1)S(1)}, u32[]{:S(2)}, u32[]{:S(2)}) %collective-permute-start.43) | collective-permute-done | bytes 819232 | tf_op jit(solution)/shard_map/ppermute | solution.py:49
  309.0 4.2 fusion.32
  322.1 3.7 convolution_convert_fusion.7
  329.2 6.9 %attention_far_back.2 = (f32[640,1024]{1,0:T(8,128)S(1)}, f32[8,1,1024]{2,1,0:T(1,128)S(1)}, bf16[2,640,512]{2,1,0:T(8,128)(2,1)}) custom-call(s32[1]{0:T(128)} %bitcast.19.refs_0_, bf16[640,1024]{1,0:T(8,128)(2,1)S(1)} %copy-done.21, bf16[640,512]{1,0:T(8,128)(2,1)S(1)} %convolution_convert_fusion.27.refs_2_, bf16[640,512]{1,0:T(8,128)(2,1)S(1)} %copy-done.39, ...), custom_call_target="tpu_custom_call" | custom-call | flops 503316480 | bytes 5275652 | tf_op jit(solution)/shard_map/attention_far_back/pallas_call | solution.py:649
  336.1 5.3 collective-permute-start.51
  348.3 12.7 %attention_own_back.2 = (bf16[640,1024]{1,0:T(8,128)(2,1)S(1)}, bf16[640,1024]{1,0:T(8,128)(2,1)S(1)}, bf16[640,1024]{1,0:T(8,128)(2,1)S(1)}, f32[640,1]{1,0:T(8,128)S(1)}) custom-call(s32[1,1024]{1,0:T(1,128)S(1)} %bitcast.270, f32[80,1]{1,0:T(8,128)S(1)} %copy.62.refs_1_, bf16[640,1024]{1,0:T(8,128)(2,1)S(1)} %copy-done.22, ...), custom_call_target="tpu_custom_call" | custom-call | flops 15938355200 | bytes 7934272 | tf_op jit(solution)/shard_map/attention_own_back/pallas_call | solution.py:649
  361.0 3.5 convolution_convert_fusion.6
  369.8 10.3 %collective-permute-done.53.refs_3_ = bf16[1,4,80,640]{3,2,1,0:T(8,128)(2,1)} collective-permute-done((bf16[1,4,80,640]{3,2,1,0:T(8,128)(2,1)S(1)}, bf16[1,4,80,640]{3,2,1,0:T(8,128)(2,1)}, u32[]{:S(2)}, u32[]{:S(2)}) %collective-permute-start.53) | collective-permute-done | bytes 409632 | tf_op jit(solution)/shard_map/ppermute | solution.py:49
  404.8 4.1 fusion.68
  411.9 6.8 %multiply_reduce_fusion.1 = (f32[1280]{0:T(1024)}, f32[512]{0:T(512)S(1)}, f32[1280,512]{1,0:T(8,128)S(1)}) fusion(f32[1280,512]{1,0:T(8,128)} %copy-done.84, f32[512]{0:T(512)S(1)} %add_rsqrt_fusion.1, f32[1280]{0:T(1024)S(1)} %add_reduce_fusion.1, bf16[1280,512]{1,0:T(8,128)(2,1)} %collective-permute-done.54.refs_6_, f32[1280,512]{1,0:T(8,128)} %fusion.66, ...), kind=kOutput, calls=%fused_computation.62 | convolution fusion | flops 846723328 | bytes 14107652 | tf_op jit(solution)/shard_map/dot_general | solution.py:28
  431.4 4.2 fusion.29
  442.1 4.4 convolution_add_fusion.2.refs_6_
  446.5 5.0 collective-permute-done.61.refs_1_
  491.4 6.9 %attention_far_back.3 = (f32[640,1024]{1,0:T(8,128)S(1)}, f32[8,1,1024]{2,1,0:T(1,128)S(1)}, bf16[2,640,512]{2,1,0:T(8,128)(2,1)}) custom-call(s32[1]{0:T(128)} %bitcast.19.refs_0_, bf16[640,1024]{1,0:T(8,128)(2,1)S(1)} %copy-done.9, bf16[640,512]{1,0:T(8,128)(2,1)S(1)} %copy-done.4, bf16[640,512]{1,0:T(8,128)(2,1)S(1)} %copy-done.6, ...), custom_call_target="tpu_custom_call" | custom-call | flops 503316480 | bytes 5275652 | tf_op jit(solution)/shard_map/attention_far_back/pallas_call | solution.py:649
  498.3 5.2 collective-permute-start.73
  519.4 12.7 %attention_own_back.3 = (bf16[640,1024]{1,0:T(8,128)(2,1)S(1)}, bf16[640,1024]{1,0:T(8,128)(2,1)S(1)}, bf16[640,1024]{1,0:T(8,128)(2,1)S(1)}, f32[640,1]{1,0:T(8,128)S(1)}) custom-call(s32[1,1024]{1,0:T(1,128)S(1)} %bitcast.271, f32[80,1]{1,0:T(8,128)S(1)} %copy.68.refs_1_, bf16[640,1024]{1,0:T(8,128)(2,1)S(1)} %copy-done.9, ...), custom_call_target="tpu_custom_call" | custom-call | flops 15938355200 | bytes 7934272 | tf_op jit(solution)/shard_map/attention_own_back/pallas_call | solution.py:649
  532.2 3.5 convolution_convert_fusion.2
  567.9 4.7 collective-permute-start.83
  573.6 4.2 fusion.56
  580.5 4.9 collective-permute-done.78.refs_1_
  590.3 6.8 %multiply_reduce_fusion.3 = (f32[1280]{0:T(1024)S(1)}, f32[512]{0:T(512)S(1)}, f32[1280,512]{1,0:T(8,128)}) fusion(f32[512,1280]{0,1:T(8,128)S(1)} %copy-done.83, f32[512]{0:T(512)S(1)} %copy-done.154, f32[1280]{0:T(1024)S(1)} %broadcast_add_fusion, bf16[1280,512]{1,0:T(8,128)(2,1)} %copy-done, f32[1280,512]{1,0:T(8,128)} %fusion.56, ...), kind=kOutput, calls=%fused_computation.64 | convolution fusion | flops 846723328 | bytes 14107652 | tf_op jit(solution)/shard_map/dot_general | solution.py:28
  603.3 4.0 add_bitcast_fusion
  620.8 4.4 collective-permute-done.87.refs_1_
  626.0 5.3 collective-permute-done.91.refs_1_
  638.0 6.5 %collective-permute-done.97.refs_3_ = f32[2,2640]{1,0:T(2,128)S(1)} collective-permute-done((f32[2,2640]{1,0:T(2,128)S(1)}, f32[2,2640]{1,0:T(2,128)S(1)}, u32[]{:S(2)}, u32[]{:S(2)}) %collective-permute-start.97) | collective-permute-done | bytes 21152 | tf_op jit(solution)/shard_map/ppermute | solution.py:49
  (717 shorter events, 354.2 us)
Async XLA Ops:
  14.0 16.9 %collective-permute-start.3 = (bf16[1280,256]{1,0:T(8,128)(2,1)S(1)}, bf16[1280,256]{1,0:T(8,128)(2,1)S(1)}, u32[]{:S(2)}, u32[]{:S(2)}) collective-permute-start(bf16[1280,256]{1,0:T(8,128)(2,1)S(1)} %fusion.50), channel_id=1, source_target_pairs={{0,2},{2,0},{4,6},{6,4},{8,10},{10,8},{12,14},{14,12},{16,18},{18,... | collective-permute-start | bytes 1966088 | tf_op jit(solution)/shard_map/ppermute | solution.py:49
  30.9 16.4 %collective-permute-start.7 = (bf16[1280,256]{1,0:T(8,128)(2,1)S(1)}, bf16[1280,256]{1,0:T(8,128)(2,1)S(1)}, u32[]{:S(2)}, u32[]{:S(2)}) collective-permute-start(bf16[1280,256]{1,0:T(8,128)(2,1)S(1)} %collective-permute-done.3.refs_3_), channel_id=1, source_target_pairs={{0,1},{1,0},{2,3},{3,2},{4,5},{5,4},{6,7},{7,6},{8,9},{9,8},{10,11... | collective-permute-start | bytes 1966088 | tf_op jit(solution)/shard_map/ppermute | solution.py:49
  48.8 19.2 %collective-permute-start.9 = (bf16[1,8,80,640]{3,2,1,0:T(8,128)(2,1)S(1)}, bf16[1,8,80,640]{3,2,1,0:T(8,128)(2,1)}, u32[]{:S(2)}, u32[]{:S(2)}) collective-permute-start(bf16[1,8,80,640]{3,2,1,0:T(8,128)(2,1)S(1)} %get-tuple-element.178.refs_1_), channel_id=1, source_target_pairs={{0,2},{2,0},{4,6},{6,4},{8,10},{10,8},{12,14},{14,12},{16,18},{18,... | collective-permute-start | bytes 2457608 | tf_op jit(solution)/shard_map/ppermute | solution.py:49
  49.3 19.0 %collective-permute-start.10 = (bf16[1,8,80,640]{3,2,1,0:T(8,128)(2,1)S(1)}, bf16[1,8,80,640]{3,2,1,0:T(8,128)(2,1)}, u32[]{:S(2)}, u32[]{:S(2)}) collective-permute-start(bf16[1,8,80,640]{3,2,1,0:T(8,128)(2,1)S(1)} %get-tuple-element.179.refs_2_), channel_id=1, source_target_pairs={{0,4},{2,6},{4,0},{6,2},{8,12},{10,14},{12,8},{14,10},{16,20},{18,... | collective-permute-start | bytes 2457608 | tf_op jit(solution)/shard_map/ppermute | solution.py:49
  83.5 16.4 %collective-permute-start.15 = (bf16[1,8,80,640]{3,2,1,0:T(8,128)(2,1)S(1)}, bf16[1,8,80,640]{3,2,1,0:T(8,128)(2,1)S(1)}, u32[]{:S(2)}, u32[]{:S(2)}) collective-permute-start(bf16[1,8,80,640]{3,2,1,0:T(8,128)(2,1)S(1)} %get-tuple-element.185.refs_1_), channel_id=1, source_target_pairs={{0,2},{2,0},{4,6},{6,4},{8,10},{10,8},{12,14},{14,12},{16,18},{18,... | collective-permute-start | bytes 2457608 | tf_op jit(solution)/shard_map/ppermute | solution.py:49
  103.1 17.4 %collective-permute-start.17 = (bf16[2,1,80,640]{3,2,1,0:T(8,128)(2,1)S(1)}, bf16[2,1,80,640]{3,2,1,0:T(8,128)(2,1)S(1)}, u32[]{:S(2)}, u32[]{:S(2)}) collective-permute-start(bf16[2,1,80,640]{3,2,1,0:T(8,128)(2,1)S(1)} %get-tuple-element.195.refs_0_), channel_id=1, source_target_pairs={{0,16},{2,18},{4,20},{6,22},{8,24},{10,26},{12,28},{14,30},{16,0},... | collective-permute-start | bytes 614408 | tf_op jit(solution)/shard_map/ppermute | solution.py:49
  142.6 31.3 %collective-permute-start.27 = (bf16[2,1280,640]{2,1,0:T(8,128)(2,1)}, bf16[2,1280,640]{2,1,0:T(8,128)(2,1)}, u32[]{:S(2)}, u32[]{:S(2)}) collective-permute-start(bf16[2,1280,640]{2,1,0:T(8,128)(2,1)} %bitcast.288), channel_id=1, source_target_pairs={{0,1},{1,0},{2,3},{3,2},{4,5},{5,4},{6,7},{7,6},{8,9},{9,8},{10,11... | collective-permute-start | bytes 9830408 | tf_op jit(solution)/shard_map/ppermute | solution.py:49
  145.0 16.9 %collective-permute-start.20 = (bf16[1280,512]{1,0:T(8,128)(2,1)}, bf16[1280,512]{1,0:T(8,128)(2,1)S(1)}, u32[]{:S(2)}, u32[]{:S(2)}) collective-permute-start(bf16[1280,512]{1,0:T(8,128)(2,1)} %convolution_convert_fusion.18), channel_id=1, source_target_pairs={{0,1},{1,0},{2,3},{3,2},{4,5},{5,4},{6,7},{7,6},{8,9},{9,8},{10,11... | collective-permute-start | bytes 3932168 | tf_op jit(solution)/shard_map/ppermute | solution.py:49
  165.3 18.8 %collective-permute-start.29 = (bf16[1,8,80,640]{3,2,1,0:T(8,128)(2,1)S(1)}, bf16[1,8,80,640]{3,2,1,0:T(8,128)(2,1)S(1)}, u32[]{:S(2)}, u32[]{:S(2)}) collective-permute-start(bf16[1,8,80,640]{3,2,1,0:T(8,128)(2,1)S(1)} %get-tuple-element.209.refs_1_), channel_id=1, source_target_pairs={{0,2},{2,0},{4,6},{6,4},{8,10},{10,8},{12,14},{14,12},{16,18},{18,... | collective-permute-start | bytes 2457608 | tf_op jit(solution)/shard_map/ppermute | solution.py:49
  166.1 18.5 %collective-permute-start.30 = (bf16[1,8,80,640]{3,2,1,0:T(8,128)(2,1)S(1)}, bf16[1,8,80,640]{3,2,1,0:T(8,128)(2,1)S(1)}, u32[]{:S(2)}, u32[]{:S(2)}) collective-permute-start(bf16[1,8,80,640]{3,2,1,0:T(8,128)(2,1)S(1)} %get-tuple-element.210.refs_2_), channel_id=1, source_target_pairs={{0,4},{2,6},{4,0},{6,2},{8,12},{10,14},{12,8},{14,10},{16,20},{18,... | collective-permute-start | bytes 2457608 | tf_op jit(solution)/shard_map/ppermute | solution.py:49
  194.2 18.7 %collective-permute-start.32 = (bf16[1,4,80,640]{3,2,1,0:T(8,128)(2,1)}, bf16[1,4,80,640]{3,2,1,0:T(8,128)(2,1)}, u32[]{:S(2)}, u32[]{:S(2)}) collective-permute-start(bf16[1,4,80,640]{3,2,1,0:T(8,128)(2,1)} %get-tuple-element.213.refs_1_), channel_id=1, source_target_pairs={{0,4},{2,6},{4,0},{6,2},{8,12},{10,14},{12,8},{14,10},{16,20},{18,... | collective-permute-start | bytes 1228808 | tf_op jit(solution)/shard_map/ppermute | solution.py:49
  195.7 17.3 %collective-permute-start.33 = (bf16[1,4,80,640]{3,2,1,0:T(8,128)(2,1)}, bf16[1,4,80,640]{3,2,1,0:T(8,128)(2,1)}, u32[]{:S(2)}, u32[]{:S(2)}) collective-permute-start(bf16[1,4,80,640]{3,2,1,0:T(8,128)(2,1)} %get-tuple-element.214.refs_2_), channel_id=1, source_target_pairs={{0,2},{2,0},{4,6},{6,4},{8,10},{10,8},{12,14},{14,12},{16,18},{18,... | collective-permute-start | bytes 1228808 | tf_op jit(solution)/shard_map/ppermute | solution.py:49
  199.5 22.7 %collective-permute-start.38 = (bf16[1280,256]{1,0:T(8,128)(2,1)}, bf16[1280,256]{1,0:T(8,128)(2,1)S(1)}, u32[]{:S(2)}, u32[]{:S(2)}) collective-permute-start(bf16[1280,256]{1,0:T(8,128)(2,1)} %fusion.49), channel_id=1, source_target_pairs={{0,2},{2,0},{4,6},{6,4},{8,10},{10,8},{12,14},{14,12},{16,18},{18,... | collective-permute-start | bytes 1966088 | tf_op jit(solution)/shard_map/ppermute | solution.py:49
  214.6 24.4 %collective-permute-start.36 = (bf16[1,8,80,640]{3,2,1,0:T(8,128)(2,1)S(1)}, bf16[1,8,80,640]{3,2,1,0:T(8,128)(2,1)S(1)}, u32[]{:S(2)}, u32[]{:S(2)}) collective-permute-start(bf16[1,8,80,640]{3,2,1,0:T(8,128)(2,1)S(1)} %get-tuple-element.216.refs_1_), channel_id=1, source_target_pairs={{0,2},{2,0},{4,6},{6,4},{8,10},{10,8},{12,14},{14,12},{16,18},{18,... | collective-permute-start | bytes 2457608 | tf_op jit(solution)/shard_map/ppermute | solution.py:49
  215.2 23.8 %collective-permute-start.37 = (bf16[1,8,80,640]{3,2,1,0:T(8,128)(2,1)S(1)}, bf16[1,8,80,640]{3,2,1,0:T(8,128)(2,1)S(1)}, u32[]{:S(2)}, u32[]{:S(2)}) collective-permute-start(bf16[1,8,80,640]{3,2,1,0:T(8,128)(2,1)S(1)} %get-tuple-element.217.refs_2_), channel_id=1, source_target_pairs={{0,4},{2,6},{4,0},{6,2},{8,12},{10,14},{12,8},{14,10},{16,20},{18,... | collective-permute-start | bytes 2457608 | tf_op jit(solution)/shard_map/ppermute | solution.py:49
  222.2 35.7 %collective-permute-start.39 = (bf16[1280,256]{1,0:T(8,128)(2,1)S(1)}, bf16[1280,256]{1,0:T(8,128)(2,1)S(1)}, u32[]{:S(2)}, u32[]{:S(2)}) collective-permute-start(bf16[1280,256]{1,0:T(8,128)(2,1)S(1)} %collective-permute-done.38.refs_5_), channel_id=1, source_target_pairs={{0,1},{1,0},{2,3},{3,2},{4,5},{5,4},{6,7},{7,6},{8,9},{9,8},{10,11... | collective-permute-start | bytes 1966088 | tf_op jit(solution)/shard_map/ppermute | solution.py:49
  255.7 19.0 %collective-permute-start.43 = (bf16[1,8,80,640]{3,2,1,0:T(8,128)(2,1)S(1)}, bf16[1,8,80,640]{3,2,1,0:T(8,128)(2,1)S(1)}, u32[]{:S(2)}, u32[]{:S(2)}) collective-permute-start(bf16[1,8,80,640]{3,2,1,0:T(8,128)(2,1)S(1)} %get-tuple-element.227.refs_7_.refs_0_), channel_id=1, source_target_pairs={{0,2},{2,0},{4,6},{6,4},{8,10},{10,8},{12,14},{14,12},{16,18},{18,... | collective-permute-start | bytes 2457608 | tf_op jit(solution)/shard_map/ppermute | solution.py:49
  256.5 18.6 %collective-permute-start.44 = (bf16[1,8,80,640]{3,2,1,0:T(8,128)(2,1)S(1)}, bf16[1,8,80,640]{3,2,1,0:T(8,128)(2,1)S(1)}, u32[]{:S(2)}, u32[]{:S(2)}) collective-permute-start(bf16[1,8,80,640]{3,2,1,0:T(8,128)(2,1)S(1)} %get-tuple-element.228.refs_8_.refs_1_), channel_id=1, source_target_pairs={{0,4},{2,6},{4,0},{6,2},{8,12},{10,14},{12,8},{14,10},{16,20},{18,... | collective-permute-start | bytes 2457608 | tf_op jit(solution)/shard_map/ppermute | solution.py:49
  319.4 22.0 %collective-permute-start.49 = (bf16[1,8,80,640]{3,2,1,0:T(8,128)(2,1)S(1)}, bf16[1,8,80,640]{3,2,1,0:T(8,128)(2,1)S(1)}, u32[]{:S(2)}, u32[]{:S(2)}) collective-permute-start(bf16[1,8,80,640]{3,2,1,0:T(8,128)(2,1)S(1)} %get-tuple-element.232.refs_8_), channel_id=1, source_target_pairs={{0,2},{2,0},{4,6},{6,4},{8,10},{10,8},{12,14},{14,12},{16,18},{18,... | collective-permute-start | bytes 2457608 | tf_op jit(solution)/shard_map/ppermute | solution.py:49
  320.7 20.7 %collective-permute-start.50 = (bf16[1,8,80,640]{3,2,1,0:T(8,128)(2,1)S(1)}, bf16[1,8,80,640]{3,2,1,0:T(8,128)(2,1)S(1)}, u32[]{:S(2)}, u32[]{:S(2)}) collective-permute-start(bf16[1,8,80,640]{3,2,1,0:T(8,128)(2,1)S(1)} %get-tuple-element.234.refs_10_), channel_id=1, source_target_pairs={{0,4},{2,6},{4,0},{6,2},{8,12},{10,14},{12,8},{14,10},{16,20},{18,... | collective-permute-start | bytes 2457608 | tf_op jit(solution)/shard_map/ppermute | solution.py:49
  336.1 45.7 %collective-permute-start.51 = (bf16[2,640,512]{2,1,0:T(8,128)(2,1)}, bf16[2,640,512]{2,1,0:T(8,128)(2,1)}, u32[]{:S(2)}, u32[]{:S(2)}) collective-permute-start(bf16[2,640,512]{2,1,0:T(8,128)(2,1)} %get-tuple-element.244), channel_id=1, source_target_pairs={{0,2},{2,0},{4,6},{6,4},{8,10},{10,8},{12,14},{14,12},{16,18},{18,... | collective-permute-start | bytes 3932168 | tf_op jit(solution)/shard_map/ppermute | solution.py:49
  342.3 27.4 %collective-permute-start.52 = (bf16[1,4,80,640]{3,2,1,0:T(8,128)(2,1)S(1)}, bf16[1,4,80,640]{3,2,1,0:T(8,128)(2,1)}, u32[]{:S(2)}, u32[]{:S(2)}) collective-permute-start(bf16[1,4,80,640]{3,2,1,0:T(8,128)(2,1)S(1)} %get-tuple-element.238.refs_10_), channel_id=1, source_target_pairs={{0,4},{2,6},{4,0},{6,2},{8,12},{10,14},{12,8},{14,10},{16,20},{18,... | collective-permute-start | bytes 1228808 | tf_op jit(solution)/shard_map/ppermute | solution.py:49
  343.1 37.0 %collective-permute-start.53 = (bf16[1,4,80,640]{3,2,1,0:T(8,128)(2,1)S(1)}, bf16[1,4,80,640]{3,2,1,0:T(8,128)(2,1)}, u32[]{:S(2)}, u32[]{:S(2)}) collective-permute-start(bf16[1,4,80,640]{3,2,1,0:T(8,128)(2,1)S(1)} %get-tuple-element.240.refs_12_), channel_id=1, source_target_pairs={{0,2},{2,0},{4,6},{6,4},{8,10},{10,8},{12,14},{14,12},{16,18},{18,... | collective-permute-start | bytes 1228808 | tf_op jit(solution)/shard_map/ppermute | solution.py:49
  367.2 42.5 %collective-permute-start.56 = (bf16[1,8,80,640]{3,2,1,0:T(8,128)(2,1)}, bf16[1,8,80,640]{3,2,1,0:T(8,128)(2,1)S(1)}, u32[]{:S(2)}, u32[]{:S(2)}) collective-permute-start(bf16[1,8,80,640]{3,2,1,0:T(8,128)(2,1)} %get-tuple-element.249.refs_3_), channel_id=1, source_target_pairs={{0,2},{2,0},{4,6},{6,4},{8,10},{10,8},{12,14},{14,12},{16,18},{18,... | collective-permute-start | bytes 2457608 | tf_op jit(solution)/shard_map/ppermute | solution.py:49
  368.4 41.2 %collective-permute-start.57 = (bf16[1,8,80,640]{3,2,1,0:T(8,128)(2,1)S(1)}, bf16[1,8,80,640]{3,2,1,0:T(8,128)(2,1)S(1)}, u32[]{:S(2)}, u32[]{:S(2)}) collective-permute-start(bf16[1,8,80,640]{3,2,1,0:T(8,128)(2,1)S(1)} %get-tuple-element.251.refs_5_), channel_id=1, source_target_pairs={{0,4},{2,6},{4,0},{6,2},{8,12},{10,14},{12,8},{14,10},{16,20},{18,... | collective-permute-start | bytes 2457608 | tf_op jit(solution)/shard_map/ppermute | solution.py:49
  381.4 27.5 %collective-permute-start.55 = (bf16[2,2,80,640]{3,2,1,0:T(8,128)(2,1)S(1)}, bf16[2,2,80,640]{3,2,1,0:T(8,128)(2,1)S(1)}, u32[]{:S(2)}, u32[]{:S(2)}) collective-permute-start(bf16[2,2,80,640]{3,2,1,0:T(8,128)(2,1)S(1)} %get-tuple-element.247.refs_1_), channel_id=1, source_target_pairs={{0,8},{2,10},{4,12},{6,14},{8,0},{10,2},{12,4},{14,6},{16,24},{18,... | collective-permute-start | bytes 1228808 | tf_op jit(solution)/shard_map/ppermute | solution.py:49
  391.5 18.2 %collective-permute-start.54 = (bf16[1280,512]{1,0:T(8,128)(2,1)}, bf16[1280,512]{1,0:T(8,128)(2,1)}, u32[]{:S(2)}, u32[]{:S(2)}) collective-permute-start(bf16[1280,512]{1,0:T(8,128)(2,1)} %fusion.17), channel_id=1, source_target_pairs={{0,1},{1,0},{2,3},{3,2},{4,5},{5,4},{6,7},{7,6},{8,9},{9,8},{10,11... | collective-permute-start | bytes 3932168 | tf_op jit(solution)/shard_map/ppermute | solution.py:49
  402.8 43.7 %collective-permute-start.62 = (bf16[1,8,80,640]{3,2,1,0:T(8,128)(2,1)}, bf16[1,8,80,640]{3,2,1,0:T(8,128)(2,1)S(1)}, u32[]{:S(2)}, u32[]{:S(2)}) collective-permute-start(bf16[1,8,80,640]{3,2,1,0:T(8,128)(2,1)} %get-tuple-element.263), channel_id=1, source_target_pairs={{0,2},{2,0},{4,6},{6,4},{8,10},{10,8},{12,14},{14,12},{16,18},{18,... | collective-permute-start | bytes 2457608 | tf_op jit(solution)/shard_map/ppermute | solution.py:49
  409.0 37.5 %collective-permute-start.63 = (bf16[1,8,80,640]{3,2,1,0:T(8,128)(2,1)}, bf16[1,8,80,640]{3,2,1,0:T(8,128)(2,1)S(1)}, u32[]{:S(2)}, u32[]{:S(2)}) collective-permute-start(bf16[1,8,80,640]{3,2,1,0:T(8,128)(2,1)} %get-tuple-element.265), channel_id=1, source_target_pairs={{0,4},{2,6},{4,0},{6,2},{8,12},{10,14},{12,8},{14,10},{16,20},{18,... | collective-permute-start | bytes 2457608 | tf_op jit(solution)/shard_map/ppermute | solution.py:49
  438.0 36.0 %collective-permute-start.65 = (bf16[1280,640]{1,0:T(8,128)(2,1)}, bf16[1280,640]{1,0:T(8,128)(2,1)}, u32[]{:S(2)}, u32[]{:S(2)}) collective-permute-start(bf16[1280,640]{1,0:T(8,128)(2,1)} %convolution_convert_fusion.10), channel_id=1, source_target_pairs={{0,1},{1,0},{2,3},{3,2},{4,5},{5,4},{6,7},{7,6},{8,9},{9,8},{10,11... | collective-permute-start | bytes 4915208 | tf_op jit(solution)/shard_map/ppermute | solution.py:49
  438.7 38.6 %collective-permute-start.66 = (bf16[1280,640]{1,0:T(8,128)(2,1)}, bf16[1280,640]{1,0:T(8,128)(2,1)}, u32[]{:S(2)}, u32[]{:S(2)}) collective-permute-start(bf16[1280,640]{1,0:T(8,128)(2,1)} %convolution_convert_fusion.8), channel_id=1, source_target_pairs={{0,1},{1,0},{2,3},{3,2},{4,5},{5,4},{6,7},{7,6},{8,9},{9,8},{10,11... | collective-permute-start | bytes 4915208 | tf_op jit(solution)/shard_map/ppermute | solution.py:49
  459.9 26.1 %collective-permute-start.64 = (bf16[1280,512]{1,0:T(8,128)(2,1)}, bf16[1280,512]{1,0:T(8,128)(2,1)S(1)}, u32[]{:S(2)}, u32[]{:S(2)}) collective-permute-start(bf16[1280,512]{1,0:T(8,128)(2,1)} %get-tuple-element.376), channel_id=1, source_target_pairs={{0,1},{1,0},{2,3},{3,2},{4,5},{5,4},{6,7},{7,6},{8,9},{9,8},{10,11... | collective-permute-start | bytes 3932168 | tf_op jit(solution)/shard_map/ppermute | solution.py:49
  468.5 17.5 %collective-permute-start.68 = (bf16[1,4,80,640]{3,2,1,0:T(8,128)(2,1)}, bf16[1,4,80,640]{3,2,1,0:T(8,128)(2,1)S(1)}, u32[]{:S(2)}, u32[]{:S(2)}) collective-permute-start(bf16[1,4,80,640]{3,2,1,0:T(8,128)(2,1)} %copy-done.76), channel_id=1, source_target_pairs={{0,4},{2,6},{4,0},{6,2},{8,12},{10,14},{12,8},{14,10},{16,20},{18,... | collective-permute-start | bytes 1228808 | tf_op jit(solution)/shard_map/ppermute | solution.py:49
  480.6 25.1 %collective-permute-start.71 = (bf16[1,8,80,640]{3,2,1,0:T(8,128)(2,1)S(1)}, bf16[1,8,80,640]{3,2,1,0:T(8,128)(2,1)S(1)}, u32[]{:S(2)}, u32[]{:S(2)}) collective-permute-start(bf16[1,8,80,640]{3,2,1,0:T(8,128)(2,1)S(1)} %get-tuple-element.268.refs_8_), channel_id=1, source_target_pairs={{0,2},{2,0},{4,6},{6,4},{8,10},{10,8},{12,14},{14,12},{16,18},{18,... | collective-permute-start | bytes 2457608 | tf_op jit(solution)/shard_map/ppermute | solution.py:49
  485.0 21.7 %collective-permute-start.72 = (bf16[1,8,80,640]{3,2,1,0:T(8,128)(2,1)S(1)}, bf16[1,8,80,640]{3,2,1,0:T(8,128)(2,1)}, u32[]{:S(2)}, u32[]{:S(2)}) collective-permute-start(bf16[1,8,80,640]{3,2,1,0:T(8,128)(2,1)S(1)} %get-tuple-element.270.refs_10_), channel_id=1, source_target_pairs={{0,4},{2,6},{4,0},{6,2},{8,12},{10,14},{12,8},{14,10},{16,20},{18,... | collective-permute-start | bytes 2457608 | tf_op jit(solution)/shard_map/ppermute | solution.py:49
  487.5 19.1 %collective-permute-start.70 = (bf16[2,2,80,640]{3,2,1,0:T(8,128)(2,1)}, bf16[2,2,80,640]{3,2,1,0:T(8,128)(2,1)S(1)}, u32[]{:S(2)}, u32[]{:S(2)}) collective-permute-start(bf16[2,2,80,640]{3,2,1,0:T(8,128)(2,1)} %get-tuple-element.279.refs_14_), channel_id=1, source_target_pairs={{0,8},{2,10},{4,12},{6,14},{8,0},{10,2},{12,4},{14,6},{16,24},{18,... | collective-permute-start | bytes 1228808 | tf_op jit(solution)/shard_map/ppermute | solution.py:49
  498.3 49.3 %collective-permute-start.73 = (bf16[2,640,512]{2,1,0:T(8,128)(2,1)}, bf16[2,640,512]{2,1,0:T(8,128)(2,1)}, u32[]{:S(2)}, u32[]{:S(2)}) collective-permute-start(bf16[2,640,512]{2,1,0:T(8,128)(2,1)} %get-tuple-element.291), channel_id=1, source_target_pairs={{0,2},{2,0},{4,6},{6,4},{8,10},{10,8},{12,14},{14,12},{16,18},{18,... | collective-permute-start | bytes 3932168 | tf_op jit(solution)/shard_map/ppermute | solution.py:49
  511.0 30.6 %collective-permute-start.74 = (bf16[2,1,80,640]{3,2,1,0:T(8,128)(2,1)}, bf16[2,1,80,640]{3,2,1,0:T(8,128)(2,1)}, u32[]{:S(2)}, u32[]{:S(2)}) collective-permute-start(bf16[2,1,80,640]{3,2,1,0:T(8,128)(2,1)} %get-tuple-element.283.refs_10_), channel_id=1, source_target_pairs={{0,16},{2,18},{4,20},{6,22},{8,24},{10,26},{12,28},{14,30},{16,0},... | collective-permute-start | bytes 614408 | tf_op jit(solution)/shard_map/ppermute | solution.py:49
  514.3 28.4 %collective-permute-start.75 = (bf16[1,4,80,640]{3,2,1,0:T(8,128)(2,1)}, bf16[1,4,80,640]{3,2,1,0:T(8,128)(2,1)}, u32[]{:S(2)}, u32[]{:S(2)}) collective-permute-start(bf16[1,4,80,640]{3,2,1,0:T(8,128)(2,1)} %get-tuple-element.285.refs_12_), channel_id=1, source_target_pairs={{0,4},{2,6},{4,0},{6,2},{8,12},{10,14},{12,8},{14,10},{16,20},{18,... | collective-permute-start | bytes 1228808 | tf_op jit(solution)/shard_map/ppermute | solution.py:49
  515.3 27.4 %collective-permute-start.76 = (bf16[1,4,80,640]{3,2,1,0:T(8,128)(2,1)}, bf16[1,4,80,640]{3,2,1,0:T(8,128)(2,1)}, u32[]{:S(2)}, u32[]{:S(2)}) collective-permute-start(bf16[1,4,80,640]{3,2,1,0:T(8,128)(2,1)} %get-tuple-element.287.refs_14_), channel_id=1, source_target_pairs={{0,2},{2,0},{4,6},{6,4},{8,10},{10,8},{12,14},{14,12},{16,18},{18,... | collective-permute-start | bytes 1228808 | tf_op jit(solution)/shard_map/ppermute | solution.py:49
  539.3 25.8 %collective-permute-start.81 = (bf16[1,8,80,640]{3,2,1,0:T(8,128)(2,1)}, bf16[1,8,80,640]{3,2,1,0:T(8,128)(2,1)}, u32[]{:S(2)}, u32[]{:S(2)}) collective-permute-start(bf16[1,8,80,640]{3,2,1,0:T(8,128)(2,1)} %get-tuple-element.298.refs_5_), channel_id=1, source_target_pairs={{0,2},{2,0},{4,6},{6,4},{8,10},{10,8},{12,14},{14,12},{16,18},{18,... | collective-permute-start | bytes 2457608 | tf_op jit(solution)/shard_map/ppermute | solution.py:49
  541.6 24.6 %collective-permute-start.82 = (bf16[1,8,80,640]{3,2,1,0:T(8,128)(2,1)}, bf16[1,8,80,640]{3,2,1,0:T(8,128)(2,1)S(1)}, u32[]{:S(2)}, u32[]{:S(2)}) collective-permute-start(bf16[1,8,80,640]{3,2,1,0:T(8,128)(2,1)} %copy-done.29), channel_id=1, source_target_pairs={{0,4},{2,6},{4,0},{6,2},{8,12},{10,14},{12,8},{14,10},{16,20},{18,... | collective-permute-start | bytes 2457608 | tf_op jit(solution)/shard_map/ppermute | solution.py:49
  547.1 19.0 %collective-permute-start.80 = (bf16[2,2,80,640]{3,2,1,0:T(8,128)(2,1)S(1)}, bf16[2,2,80,640]{3,2,1,0:T(8,128)(2,1)S(1)}, u32[]{:S(2)}, u32[]{:S(2)}) collective-permute-start(bf16[2,2,80,640]{3,2,1,0:T(8,128)(2,1)S(1)} %get-tuple-element.296.refs_3_), channel_id=1, source_target_pairs={{0,8},{2,10},{4,12},{6,14},{8,0},{10,2},{12,4},{14,6},{16,24},{18,... | collective-permute-start | bytes 1228808 | tf_op jit(solution)/shard_map/ppermute | solution.py:49
  559.5 26.6 %collective-permute-start.77 = (bf16[1280,512]{1,0:T(8,128)(2,1)}, bf16[1280,512]{1,0:T(8,128)(2,1)S(1)}, u32[]{:S(2)}, u32[]{:S(2)}) collective-permute-start(bf16[1280,512]{1,0:T(8,128)(2,1)} %fusion.13), channel_id=1, source_target_pairs={{0,1},{1,0},{2,3},{3,2},{4,5},{5,4},{6,7},{7,6},{8,9},{9,8},{10,11... | collective-permute-start | bytes 3932168 | tf_op jit(solution)/shard_map/ppermute | solution.py:49
  564.8 20.7 %collective-permute-start.78 = (bf16[1,8,80,640]{3,2,1,0:T(8,128)(2,1)S(1)}, bf16[1,8,80,640]{3,2,1,0:T(8,128)(2,1)S(1)}, u32[]{:S(2)}, u32[]{:S(2)}) collective-permute-start(bf16[1,8,80,640]{3,2,1,0:T(8,128)(2,1)S(1)} %get-tuple-element.304), channel_id=1, source_target_pairs={{0,2},{2,0},{4,6},{6,4},{8,10},{10,8},{12,14},{14,12},{16,18},{18,... | collective-permute-start | bytes 2457608 | tf_op jit(solution)/shard_map/ppermute | solution.py:49
  565.1 21.1 %collective-permute-start.79 = (bf16[1,8,80,640]{3,2,1,0:T(8,128)(2,1)S(1)}, bf16[1,8,80,640]{3,2,1,0:T(8,128)(2,1)S(1)}, u32[]{:S(2)}, u32[]{:S(2)}) collective-permute-start(bf16[1,8,80,640]{3,2,1,0:T(8,128)(2,1)S(1)} %get-tuple-element.306), channel_id=1, source_target_pairs={{0,4},{2,6},{4,0},{6,2},{8,12},{10,14},{12,8},{14,10},{16,20},{18,... | collective-permute-start | bytes 2457608 | tf_op jit(solution)/shard_map/ppermute | solution.py:49
  567.9 29.3 %collective-permute-start.83 = (bf16[2,1,80,640]{3,2,1,0:T(8,128)(2,1)S(1)}, bf16[2,1,80,640]{3,2,1,0:T(8,128)(2,1)S(1)}, u32[]{:S(2)}, u32[]{:S(2)}) collective-permute-start(bf16[2,1,80,640]{3,2,1,0:T(8,128)(2,1)S(1)} %get-tuple-element.309), channel_id=1, source_target_pairs={{0,16},{2,18},{4,20},{6,22},{8,24},{10,26},{12,28},{14,30},{16,0},... | collective-permute-start | bytes 614408 | tf_op jit(solution)/shard_map/ppermute | solution.py:49
  572.6 24.6 %collective-permute-start.84 = (bf16[1,4,80,640]{3,2,1,0:T(8,128)(2,1)S(1)}, bf16[1,4,80,640]{3,2,1,0:T(8,128)(2,1)S(1)}, u32[]{:S(2)}, u32[]{:S(2)}) collective-permute-start(bf16[1,4,80,640]{3,2,1,0:T(8,128)(2,1)S(1)} %get-tuple-element.312), channel_id=1, source_target_pairs={{0,4},{2,6},{4,0},{6,2},{8,12},{10,14},{12,8},{14,10},{16,20},{18,... | collective-permute-start | bytes 1228808 | tf_op jit(solution)/shard_map/ppermute | solution.py:49
  (233 other events, 1674.8 us)

commit v8 on v7

--- a/solution.py
+++ b/solution.py
@@ -386,6 +386,8 @@
 
 def norm_back(source, inverse, gain, grad, terms, after=()):
     incoming = sum(term.astype(jnp.float32) for term in terms)
+    if len(terms) > 1:
+        incoming = lax.optimization_barrier(lowered(incoming)).astype(jnp.float32)
     unit = source * inverse
     gain_grad = jnp.sum(incoming * unit, axis=1)
     scaled = incoming * tied(gain, after)
@@ -851,10 +853,10 @@
                 (wk, wv, wq, wo, ups, downs),
             )
         )
-        terms = [middle, sum(dot_nn(w, hidden) for w, hidden in zip(downs, hiddens))]
         if layer + 1 < LAYERS:
+            terms = [middle, sum(dot_nn(w, hidden) for w, hidden in zip(downs, hiddens))]
             wk, wv = following
-    current = terms[0] + terms[1]
+    final = (middle, downs, hiddens)
 
     sums = Scatter(orders)
     small_grads = [None] * LAYERS
@@ -929,6 +931,8 @@
         else:
             sums.tick(terms[-1])
             ready = last.tick(terms[-1])
+            hiddens = [lowered(tied(h.astype(jnp.float32), ready)) for h in final[2]]
+            current = final[0] + sum(dot_nn(w, h) for w, h in zip(final[1], hiddens))
         grad, grad_low, attn_gain_grad = norm_back(
             source, inverse_attn, attn_gain, grad_middle, terms, ready
         )

time: 659 us -> 648 us (0.983)
  matrix products: 164 us -> 149 us
    dot_general x24, matrix products: 74.4 us -> 58.4 us  [dot_nn(): return jnp.dot(former, latter, preferred_element_type=jnp.float32)]
    unnamed x368 -> x376, local copies, waits for them, and re-layouts: 47.2 us -> 48.6 us
  transfers between devices with their start and end apart: 99 -> 99, of which waited for: 32 -> 32; matrix products, arithmetic and copies ran while one was open for 30% -> 29% of each run, Pallas kernels for 17% -> 17%
where the time goes in v8:
time: 648 us; the launch traced here: 638 us
  matrix products  149 us (23%)
  waiting for transfers between devices  135 us (21%)
  Pallas kernels  128 us (20%)
  starting transfers between devices  121 us (19%)
  local copies, waits for them, and re-layouts  60.2 us (9%)
  other arithmetic  35.3 us (5%)
  between operations  9.18 us (1%)
    ppermute x99, waiting for transfers between devices, pair_swap(): return lax.ppermute(values, axis, [(i, i ^ bit) for i in range(size)])  135 us
    ppermute x99, starting transfers between devices, pair_swap(): return lax.ppermute(values, axis, [(i, i ^ bit) for i in range(size)])  121 us
    pallas_call x8, Pallas kernels, per_head(): pl.pallas_call(work, grid=(heads // group,), in_specs=[spec(kind, array.s...  64.7 us
    pallas_call x38, Pallas kernels, quick_call(): pl.pallas_call(kernel, in_specs=[SCALAR] + [WHOLE] * (len(arrays) - 1) +...  63.6 us
    dot_general x24, matrix products, dot_nn(): return jnp.dot(former, latter, preferred_element_type=jnp.float32)  58.4 us
    unnamed x376, local copies, waits for them, and re-layouts  48.6 us
    dot_general x20, matrix products, dot_tn(): lax.dot_general(former, latter, (((0,), (0,)), ((), ())), preferred_eleme...  46.5 us
    dot_general x16, matrix products, dot_nt(): lax.dot_general(former, latter, (((1,), (1,)), ((), ())), preferred_eleme...  44 us
  transfers between devices with their start and end apart: 99, of which 32 were waited for; matrix products, arithmetic and copies ran while one was open for 29% of the time, Pallas kernels for 17%

profile of v8, /device:TPU:0, one launch (start us, length us, event | category | flops | bytes accessed | tf_op | source)
XLA Modules:
  0.0 638.1 jit_solution(2937201673396586763)
XLA Ops:
  6.2 3.7 collective-permute-start
  20.9 9.9 %collective-permute-done.3.refs_3_ = bf16[1280,256]{1,0:T(8,128)(2,1)S(1)} collective-permute-done((bf16[1280,256]{1,0:T(8,128)(2,1)S(1)}, bf16[1280,256]{1,0:T(8,128)(2,1)S(1)}, u32[]{:S(2)}, u32[]{:S(2)}) %collective-permute-start.3) | collective-permute-done | bytes 655392 | tf_op jit(solution)/shard_map/ppermute | solution.py:49
  38.5 8.8 %collective-permute-done.4.refs_3_ = bf16[2,1,80,640]{3,2,1,0:T(8,128)(2,1)S(1)} collective-permute-done((bf16[2,1,80,640]{3,2,1,0:T(8,128)(2,1)S(1)}, bf16[2,1,80,640]{3,2,1,0:T(8,128)(2,1)S(1)}, u32[]{:S(2)}, u32[]{:S(2)}) %collective-permute-start.4) | collective-permute-done | bytes 204832 | tf_op jit(solution)/shard_map/ppermute | solution.py:49
  54.0 9.2 %collective-permute-done.8.refs_3_ = bf16[2,2,80,640]{3,2,1,0:T(8,128)(2,1)S(1)} collective-permute-done((bf16[2,2,80,640]{3,2,1,0:T(8,128)(2,1)}, bf16[2,2,80,640]{3,2,1,0:T(8,128)(2,1)S(1)}, u32[]{:S(2)}, u32[]{:S(2)}) %collective-permute-start.8) | collective-permute-done | bytes 409632 | tf_op jit(solution)/shard_map/ppermute | solution.py:49
  63.3 4.8 collective-permute-done.9.refs_4_
  68.3 3.5 join_halves.17
  73.8 4.5 convolution_convert_fusion.23.refs_7_.refs_2_.refs_3_
  78.3 4.4 collective-permute-done.11.refs_3_
  87.9 5.5 collective-permute-start.14
  96.4 3.5 collective-permute-done.14.refs_3_
  110.8 8.4 %attention_own.2 = (f32[640,1024]{1,0:T(8,128)S(1)}, f32[8,1,1024]{2,1,0:T(1,128)S(1)}, f32[8,1,1024]{2,1,0:T(1,128)S(1)}) custom-call(s32[1,1024]{1,0:T(1,128)S(1)} %bitcast.268, bf16[640,1024]{1,0:T(8,128)(2,1)S(1)} %multiply_convert_fusion.4.refs_1_.refs_2_, bf16[640,1024]{1,0:T(8,128)(2,1)S(1)} %copy-done.12, bf16[640,1024]{1,0:T(8,128)(2,1)S(1)} %copy-done.14), custom_call_target="tpu_custom_call" | custom-call | flops 629145600 | bytes 3936256 | tf_op jit(solution)/shard_map/attention_own/pallas_call | solution.py:651
  125.1 4.9 collective-permute-start.21
  133.1 4.4 attention_far.2
  138.8 4.0 join_halves.21
  146.4 3.6 collective-permute-start.26
  155.9 6.2 collective-permute-done.24.refs_3_
  174.1 3.5 fusion.45.refs_8_
  177.7 6.6 %collective-permute-done.29.refs_4_ = bf16[1,8,80,640]{3,2,1,0:T(8,128)(2,1)S(1)} collective-permute-done((bf16[1,8,80,640]{3,2,1,0:T(8,128)(2,1)S(1)}, bf16[1,8,80,640]{3,2,1,0:T(8,128)(2,1)S(1)}, u32[]{:S(2)}, u32[]{:S(2)}) %collective-permute-start.29) | collective-permute-done | bytes 819232 | tf_op jit(solution)/shard_map/ppermute | solution.py:49
  204.0 9.2 %collective-permute-done.31.refs_3_ = bf16[2,1,80,640]{3,2,1,0:T(8,128)(2,1)} collective-permute-done((bf16[2,1,80,640]{3,2,1,0:T(8,128)(2,1)S(1)}, bf16[2,1,80,640]{3,2,1,0:T(8,128)(2,1)}, u32[]{:S(2)}, u32[]{:S(2)}) %collective-permute-start.31) | collective-permute-done | bytes 204832 | tf_op jit(solution)/shard_map/ppermute | solution.py:49
  216.9 4.5 convolution_convert_fusion.21.refs_6_.refs_2_.refs_3_
  226.2 13.0 %collective-permute-done.36.refs_4_ = bf16[1,8,80,640]{3,2,1,0:T(8,128)(2,1)S(1)} collective-permute-done((bf16[1,8,80,640]{3,2,1,0:T(8,128)(2,1)S(1)}, bf16[1,8,80,640]{3,2,1,0:T(8,128)(2,1)S(1)}, u32[]{:S(2)}, u32[]{:S(2)}) %collective-permute-start.36) | collective-permute-done | bytes 819232 | tf_op jit(solution)/shard_map/ppermute | solution.py:49
  247.1 8.1 %attention_own.3 = (f32[640,1024]{1,0:T(8,128)S(1)}, f32[8,1,1024]{2,1,0:T(1,128)S(1)}, f32[8,1,1024]{2,1,0:T(1,128)S(1)}) custom-call(s32[1,1024]{1,0:T(1,128)S(1)} %bitcast.269, bf16[640,1024]{1,0:T(8,128)(2,1)S(1)} %multiply_convert_fusion.1.refs_1_.refs_2_, bf16[640,1024]{1,0:T(8,128)(2,1)S(1)} %copy-done.16, bf16[640,1024]{1,0:T(8,128)(2,1)S(1)} %copy-done.18), custom_call_target="tpu_custom_call" | custom-call | flops 629145600 | bytes 3936256 | tf_op jit(solution)/shard_map/attention_own/pallas_call | solution.py:651
  260.8 4.7 attention_far.3
  266.8 8.1 %collective-permute-done.43.refs_2_ = bf16[1,8,80,640]{3,2,1,0:T(8,128)(2,1)S(1)} collective-permute-done((bf16[1,8,80,640]{3,2,1,0:T(8,128)(2,1)S(1)}, bf16[1,8,80,640]{3,2,1,0:T(8,128)(2,1)S(1)}, u32[]{:S(2)}, u32[]{:S(2)}) %collective-permute-start.43) | collective-permute-done | bytes 819232 | tf_op jit(solution)/shard_map/ppermute | solution.py:49
  300.8 4.5 convolution_convert_fusion.13
  308.5 3.7 add_halves.22
  320.5 6.9 %attention_far_back.2 = (f32[640,1024]{1,0:T(8,128)S(1)}, f32[8,1,1024]{2,1,0:T(1,128)S(1)}, bf16[2,640,512]{2,1,0:T(8,128)(2,1)}) custom-call(s32[1]{0:T(128)} %bitcast.19.refs_0_, bf16[640,1024]{1,0:T(8,128)(2,1)S(1)} %copy-done.21, bf16[640,512]{1,0:T(8,128)(2,1)S(1)} %convolution_convert_fusion.27.refs_2_, bf16[640,512]{1,0:T(8,128)(2,1)S(1)} %copy-done.39, ...), custom_call_target="tpu_custom_call" | custom-call | flops 503316480 | bytes 5275652 | tf_op jit(solution)/shard_map/attention_far_back/pallas_call | solution.py:651
  329.0 5.3 collective-permute-start.51
  341.5 12.7 %attention_own_back.2 = (bf16[640,1024]{1,0:T(8,128)(2,1)S(1)}, bf16[640,1024]{1,0:T(8,128)(2,1)S(1)}, bf16[640,1024]{1,0:T(8,128)(2,1)S(1)}, f32[640,1]{1,0:T(8,128)S(1)}) custom-call(s32[1,1024]{1,0:T(1,128)S(1)} %bitcast.270, f32[80,1]{1,0:T(8,128)S(1)} %copy.56.refs_1_, bf16[640,1024]{1,0:T(8,128)(2,1)S(1)} %copy-done.22, ...), custom_call_target="tpu_custom_call" | custom-call | flops 15938355200 | bytes 7934272 | tf_op jit(solution)/shard_map/attention_own_back/pallas_call | solution.py:651
  362.6 10.4 %collective-permute-done.53.refs_3_ = bf16[1,4,80,640]{3,2,1,0:T(8,128)(2,1)} collective-permute-done((bf16[1,4,80,640]{3,2,1,0:T(8,128)(2,1)S(1)}, bf16[1,4,80,640]{3,2,1,0:T(8,128)(2,1)}, u32[]{:S(2)}, u32[]{:S(2)}) %collective-permute-start.53) | collective-permute-done | bytes 409632 | tf_op jit(solution)/shard_map/ppermute | solution.py:49
  374.7 3.5 add_back.2
  386.7 3.5 convolution_convert_fusion.4.refs_8_
  404.2 3.5 fusion.35
  407.8 4.2 fusion.119
  423.0 4.2 fusion.44
  433.5 4.4 convolution_add_fusion.3.refs_6_
  437.9 5.0 collective-permute-done.61.refs_1_
  463.9 5.0 collective-permute-done.67.refs_1_
  475.2 6.9 %attention_far_back.3 = (f32[640,1024]{1,0:T(8,128)S(1)}, f32[8,1,1024]{2,1,0:T(1,128)S(1)}, bf16[2,640,512]{2,1,0:T(8,128)(2,1)}) custom-call(s32[1]{0:T(128)} %bitcast.19.refs_0_, bf16[640,1024]{1,0:T(8,128)(2,1)S(1)} %copy-done.9, bf16[640,512]{1,0:T(8,128)(2,1)S(1)} %copy-done.4, bf16[640,512]{1,0:T(8,128)(2,1)S(1)} %copy-done.6, ...), custom_call_target="tpu_custom_call" | custom-call | flops 503316480 | bytes 5275652 | tf_op jit(solution)/shard_map/attention_far_back/pallas_call | solution.py:651
  482.1 5.2 collective-permute-start.73
  501.9 12.7 %attention_own_back.3 = (bf16[640,1024]{1,0:T(8,128)(2,1)S(1)}, bf16[640,1024]{1,0:T(8,128)(2,1)S(1)}, bf16[640,1024]{1,0:T(8,128)(2,1)S(1)}, f32[640,1]{1,0:T(8,128)S(1)}) custom-call(s32[1,1024]{1,0:T(1,128)S(1)} %bitcast.271, f32[80,1]{1,0:T(8,128)S(1)} %copy.59.refs_1_, bf16[640,1024]{1,0:T(8,128)(2,1)S(1)} %copy-done.9, ...), custom_call_target="tpu_custom_call" | custom-call | flops 15938355200 | bytes 7934272 | tf_op jit(solution)/shard_map/attention_own_back/pallas_call | solution.py:651
  514.7 3.5 convolution_convert_fusion.2
  556.2 4.3 fusion.66
  563.2 6.2 collective-permute-done.77.refs_1_
  575.8 4.3 fusion.20
  610.4 4.8 collective-permute-done.87.refs_1_
  616.2 4.0 collective-permute-done.91.refs_1_
  627.8 5.8 collective-permute-done.97.refs_3_
  (727 shorter events, 347.5 us)
Async XLA Ops:
  48.8 19.2 %collective-permute-start.9 = (bf16[1,8,80,640]{3,2,1,0:T(8,128)(2,1)S(1)}, bf16[1,8,80,640]{3,2,1,0:T(8,128)(2,1)}, u32[]{:S(2)}, u32[]{:S(2)}) collective-permute-start(bf16[1,8,80,640]{3,2,1,0:T(8,128)(2,1)S(1)} %get-tuple-element.178.refs_1_), channel_id=1, source_target_pairs={{0,2},{2,0},{4,6},{6,4},{8,10},{10,8},{12,14},{14,12},{16,18},{18,... | collective-permute-start | bytes 2457608 | tf_op jit(solution)/shard_map/ppermute | solution.py:49
  49.3 19.0 %collective-permute-start.10 = (bf16[1,8,80,640]{3,2,1,0:T(8,128)(2,1)S(1)}, bf16[1,8,80,640]{3,2,1,0:T(8,128)(2,1)}, u32[]{:S(2)}, u32[]{:S(2)}) collective-permute-start(bf16[1,8,80,640]{3,2,1,0:T(8,128)(2,1)S(1)} %get-tuple-element.179.refs_2_), channel_id=1, source_target_pairs={{0,4},{2,6},{4,0},{6,2},{8,12},{10,14},{12,8},{14,10},{16,20},{18,... | collective-permute-start | bytes 2457608 | tf_op jit(solution)/shard_map/ppermute | solution.py:49
  103.3 17.4 %collective-permute-start.17 = (bf16[2,1,80,640]{3,2,1,0:T(8,128)(2,1)S(1)}, bf16[2,1,80,640]{3,2,1,0:T(8,128)(2,1)S(1)}, u32[]{:S(2)}, u32[]{:S(2)}) collective-permute-start(bf16[2,1,80,640]{3,2,1,0:T(8,128)(2,1)S(1)} %get-tuple-element.195.refs_0_), channel_id=1, source_target_pairs={{0,16},{2,18},{4,20},{6,22},{8,24},{10,26},{12,28},{14,30},{16,0},... | collective-permute-start | bytes 614408 | tf_op jit(solution)/shard_map/ppermute | solution.py:49
  142.8 31.3 %collective-permute-start.27 = (bf16[2,1280,640]{2,1,0:T(8,128)(2,1)}, bf16[2,1280,640]{2,1,0:T(8,128)(2,1)}, u32[]{:S(2)}, u32[]{:S(2)}) collective-permute-start(bf16[2,1280,640]{2,1,0:T(8,128)(2,1)} %bitcast.288), channel_id=1, source_target_pairs={{0,1},{1,0},{2,3},{3,2},{4,5},{5,4},{6,7},{7,6},{8,9},{9,8},{10,11... | collective-permute-start | bytes 9830408 | tf_op jit(solution)/shard_map/ppermute | solution.py:49
  165.5 18.8 %collective-permute-start.29 = (bf16[1,8,80,640]{3,2,1,0:T(8,128)(2,1)S(1)}, bf16[1,8,80,640]{3,2,1,0:T(8,128)(2,1)S(1)}, u32[]{:S(2)}, u32[]{:S(2)}) collective-permute-start(bf16[1,8,80,640]{3,2,1,0:T(8,128)(2,1)S(1)} %get-tuple-element.209.refs_1_), channel_id=1, source_target_pairs={{0,2},{2,0},{4,6},{6,4},{8,10},{10,8},{12,14},{14,12},{16,18},{18,... | collective-permute-start | bytes 2457608 | tf_op jit(solution)/shard_map/ppermute | solution.py:49
  166.3 18.5 %collective-permute-start.30 = (bf16[1,8,80,640]{3,2,1,0:T(8,128)(2,1)S(1)}, bf16[1,8,80,640]{3,2,1,0:T(8,128)(2,1)S(1)}, u32[]{:S(2)}, u32[]{:S(2)}) collective-permute-start(bf16[1,8,80,640]{3,2,1,0:T(8,128)(2,1)S(1)} %get-tuple-element.210.refs_2_), channel_id=1, source_target_pairs={{0,4},{2,6},{4,0},{6,2},{8,12},{10,14},{12,8},{14,10},{16,20},{18,... | collective-permute-start | bytes 2457608 | tf_op jit(solution)/shard_map/ppermute | solution.py:49
  194.3 18.8 %collective-permute-start.32 = (bf16[1,4,80,640]{3,2,1,0:T(8,128)(2,1)}, bf16[1,4,80,640]{3,2,1,0:T(8,128)(2,1)}, u32[]{:S(2)}, u32[]{:S(2)}) collective-permute-start(bf16[1,4,80,640]{3,2,1,0:T(8,128)(2,1)} %get-tuple-element.213.refs_1_), channel_id=1, source_target_pairs={{0,4},{2,6},{4,0},{6,2},{8,12},{10,14},{12,8},{14,10},{16,20},{18,... | collective-permute-start | bytes 1228808 | tf_op jit(solution)/shard_map/ppermute | solution.py:49
  195.8 17.3 %collective-permute-start.33 = (bf16[1,4,80,640]{3,2,1,0:T(8,128)(2,1)}, bf16[1,4,80,640]{3,2,1,0:T(8,128)(2,1)}, u32[]{:S(2)}, u32[]{:S(2)}) collective-permute-start(bf16[1,4,80,640]{3,2,1,0:T(8,128)(2,1)} %get-tuple-element.214.refs_2_), channel_id=1, source_target_pairs={{0,2},{2,0},{4,6},{6,4},{8,10},{10,8},{12,14},{14,12},{16,18},{18,... | collective-permute-start | bytes 1228808 | tf_op jit(solution)/shard_map/ppermute | solution.py:49
  199.7 22.7 %collective-permute-start.38 = (bf16[1280,256]{1,0:T(8,128)(2,1)}, bf16[1280,256]{1,0:T(8,128)(2,1)S(1)}, u32[]{:S(2)}, u32[]{:S(2)}) collective-permute-start(bf16[1280,256]{1,0:T(8,128)(2,1)} %fusion.64), channel_id=1, source_target_pairs={{0,2},{2,0},{4,6},{6,4},{8,10},{10,8},{12,14},{14,12},{16,18},{18,... | collective-permute-start | bytes 1966088 | tf_op jit(solution)/shard_map/ppermute | solution.py:49
  214.8 24.4 %collective-permute-start.36 = (bf16[1,8,80,640]{3,2,1,0:T(8,128)(2,1)S(1)}, bf16[1,8,80,640]{3,2,1,0:T(8,128)(2,1)S(1)}, u32[]{:S(2)}, u32[]{:S(2)}) collective-permute-start(bf16[1,8,80,640]{3,2,1,0:T(8,128)(2,1)S(1)} %get-tuple-element.216.refs_1_), channel_id=1, source_target_pairs={{0,2},{2,0},{4,6},{6,4},{8,10},{10,8},{12,14},{14,12},{16,18},{18,... | collective-permute-start | bytes 2457608 | tf_op jit(solution)/shard_map/ppermute | solution.py:49
  215.4 23.7 %collective-permute-start.37 = (bf16[1,8,80,640]{3,2,1,0:T(8,128)(2,1)S(1)}, bf16[1,8,80,640]{3,2,1,0:T(8,128)(2,1)S(1)}, u32[]{:S(2)}, u32[]{:S(2)}) collective-permute-start(bf16[1,8,80,640]{3,2,1,0:T(8,128)(2,1)S(1)} %get-tuple-element.217.refs_2_), channel_id=1, source_target_pairs={{0,4},{2,6},{4,0},{6,2},{8,12},{10,14},{12,8},{14,10},{16,20},{18,... | collective-permute-start | bytes 2457608 | tf_op jit(solution)/shard_map/ppermute | solution.py:49
  222.4 35.8 %collective-permute-start.39 = (bf16[1280,256]{1,0:T(8,128)(2,1)S(1)}, bf16[1280,256]{1,0:T(8,128)(2,1)S(1)}, u32[]{:S(2)}, u32[]{:S(2)}) collective-permute-start(bf16[1280,256]{1,0:T(8,128)(2,1)S(1)} %collective-permute-done.38.refs_5_), channel_id=1, source_target_pairs={{0,1},{1,0},{2,3},{3,2},{4,5},{5,4},{6,7},{7,6},{8,9},{9,8},{10,11... | collective-permute-start | bytes 1966088 | tf_op jit(solution)/shard_map/ppermute | solution.py:49
  255.9 19.0 %collective-permute-start.43 = (bf16[1,8,80,640]{3,2,1,0:T(8,128)(2,1)S(1)}, bf16[1,8,80,640]{3,2,1,0:T(8,128)(2,1)S(1)}, u32[]{:S(2)}, u32[]{:S(2)}) collective-permute-start(bf16[1,8,80,640]{3,2,1,0:T(8,128)(2,1)S(1)} %get-tuple-element.227.refs_7_.refs_0_), channel_id=1, source_target_pairs={{0,2},{2,0},{4,6},{6,4},{8,10},{10,8},{12,14},{14,12},{16,18},{18,... | collective-permute-start | bytes 2457608 | tf_op jit(solution)/shard_map/ppermute | solution.py:49
  256.7 18.6 %collective-permute-start.44 = (bf16[1,8,80,640]{3,2,1,0:T(8,128)(2,1)S(1)}, bf16[1,8,80,640]{3,2,1,0:T(8,128)(2,1)S(1)}, u32[]{:S(2)}, u32[]{:S(2)}) collective-permute-start(bf16[1,8,80,640]{3,2,1,0:T(8,128)(2,1)S(1)} %get-tuple-element.228.refs_8_.refs_1_), channel_id=1, source_target_pairs={{0,4},{2,6},{4,0},{6,2},{8,12},{10,14},{12,8},{14,10},{16,20},{18,... | collective-permute-start | bytes 2457608 | tf_op jit(solution)/shard_map/ppermute | solution.py:49
  312.2 22.1 %collective-permute-start.49 = (bf16[1,8,80,640]{3,2,1,0:T(8,128)(2,1)S(1)}, bf16[1,8,80,640]{3,2,1,0:T(8,128)(2,1)S(1)}, u32[]{:S(2)}, u32[]{:S(2)}) collective-permute-start(bf16[1,8,80,640]{3,2,1,0:T(8,128)(2,1)S(1)} %get-tuple-element.232.refs_8_), channel_id=1, source_target_pairs={{0,2},{2,0},{4,6},{6,4},{8,10},{10,8},{12,14},{14,12},{16,18},{18,... | collective-permute-start | bytes 2457608 | tf_op jit(solution)/shard_map/ppermute | solution.py:49
  313.5 20.8 %collective-permute-start.50 = (bf16[1,8,80,640]{3,2,1,0:T(8,128)(2,1)S(1)}, bf16[1,8,80,640]{3,2,1,0:T(8,128)(2,1)S(1)}, u32[]{:S(2)}, u32[]{:S(2)}) collective-permute-start(bf16[1,8,80,640]{3,2,1,0:T(8,128)(2,1)S(1)} %get-tuple-element.234.refs_10_), channel_id=1, source_target_pairs={{0,4},{2,6},{4,0},{6,2},{8,12},{10,14},{12,8},{14,10},{16,20},{18,... | collective-permute-start | bytes 2457608 | tf_op jit(solution)/shard_map/ppermute | solution.py:49
  329.0 45.7 %collective-permute-start.51 = (bf16[2,640,512]{2,1,0:T(8,128)(2,1)}, bf16[2,640,512]{2,1,0:T(8,128)(2,1)}, u32[]{:S(2)}, u32[]{:S(2)}) collective-permute-start(bf16[2,640,512]{2,1,0:T(8,128)(2,1)} %get-tuple-element.244), channel_id=1, source_target_pairs={{0,2},{2,0},{4,6},{6,4},{8,10},{10,8},{12,14},{14,12},{16,18},{18,... | collective-permute-start | bytes 3932168 | tf_op jit(solution)/shard_map/ppermute | solution.py:49
  335.3 27.3 %collective-permute-start.52 = (bf16[1,4,80,640]{3,2,1,0:T(8,128)(2,1)S(1)}, bf16[1,4,80,640]{3,2,1,0:T(8,128)(2,1)}, u32[]{:S(2)}, u32[]{:S(2)}) collective-permute-start(bf16[1,4,80,640]{3,2,1,0:T(8,128)(2,1)S(1)} %get-tuple-element.238.refs_10_), channel_id=1, source_target_pairs={{0,4},{2,6},{4,0},{6,2},{8,12},{10,14},{12,8},{14,10},{16,20},{18,... | collective-permute-start | bytes 1228808 | tf_op jit(solution)/shard_map/ppermute | solution.py:49
  336.3 36.7 %collective-permute-start.53 = (bf16[1,4,80,640]{3,2,1,0:T(8,128)(2,1)S(1)}, bf16[1,4,80,640]{3,2,1,0:T(8,128)(2,1)}, u32[]{:S(2)}, u32[]{:S(2)}) collective-permute-start(bf16[1,4,80,640]{3,2,1,0:T(8,128)(2,1)S(1)} %get-tuple-element.240.refs_12_), channel_id=1, source_target_pairs={{0,2},{2,0},{4,6},{6,4},{8,10},{10,8},{12,14},{14,12},{16,18},{18,... | collective-permute-start | bytes 1228808 | tf_op jit(solution)/shard_map/ppermute | solution.py:49
  360.3 41.3 %collective-permute-start.56 = (bf16[1,8,80,640]{3,2,1,0:T(8,128)(2,1)}, bf16[1,8,80,640]{3,2,1,0:T(8,128)(2,1)S(1)}, u32[]{:S(2)}, u32[]{:S(2)}) collective-permute-start(bf16[1,8,80,640]{3,2,1,0:T(8,128)(2,1)} %get-tuple-element.249.refs_3_), channel_id=1, source_target_pairs={{0,2},{2,0},{4,6},{6,4},{8,10},{10,8},{12,14},{14,12},{16,18},{18,... | collective-permute-start | bytes 2457608 | tf_op jit(solution)/shard_map/ppermute | solution.py:49
  361.5 40.1 %collective-permute-start.57 = (bf16[1,8,80,640]{3,2,1,0:T(8,128)(2,1)S(1)}, bf16[1,8,80,640]{3,2,1,0:T(8,128)(2,1)S(1)}, u32[]{:S(2)}, u32[]{:S(2)}) collective-permute-start(bf16[1,8,80,640]{3,2,1,0:T(8,128)(2,1)S(1)} %get-tuple-element.251.refs_5_), channel_id=1, source_target_pairs={{0,4},{2,6},{4,0},{6,2},{8,12},{10,14},{12,8},{14,10},{16,20},{18,... | collective-permute-start | bytes 2457608 | tf_op jit(solution)/shard_map/ppermute | solution.py:49
  374.3 27.2 %collective-permute-start.55 = (bf16[2,2,80,640]{3,2,1,0:T(8,128)(2,1)S(1)}, bf16[2,2,80,640]{3,2,1,0:T(8,128)(2,1)S(1)}, u32[]{:S(2)}, u32[]{:S(2)}) collective-permute-start(bf16[2,2,80,640]{3,2,1,0:T(8,128)(2,1)S(1)} %get-tuple-element.247.refs_1_), channel_id=1, source_target_pairs={{0,8},{2,10},{4,12},{6,14},{8,0},{10,2},{12,4},{14,6},{16,24},{18,... | collective-permute-start | bytes 1228808 | tf_op jit(solution)/shard_map/ppermute | solution.py:49
  391.9 46.0 %collective-permute-start.62 = (bf16[1,8,80,640]{3,2,1,0:T(8,128)(2,1)S(1)}, bf16[1,8,80,640]{3,2,1,0:T(8,128)(2,1)S(1)}, u32[]{:S(2)}, u32[]{:S(2)}) collective-permute-start(bf16[1,8,80,640]{3,2,1,0:T(8,128)(2,1)S(1)} %get-tuple-element.263), channel_id=1, source_target_pairs={{0,2},{2,0},{4,6},{6,4},{8,10},{10,8},{12,14},{14,12},{16,18},{18,... | collective-permute-start | bytes 2457608 | tf_op jit(solution)/shard_map/ppermute | solution.py:49
  398.1 39.8 %collective-permute-start.63 = (bf16[1,8,80,640]{3,2,1,0:T(8,128)(2,1)S(1)}, bf16[1,8,80,640]{3,2,1,0:T(8,128)(2,1)S(1)}, u32[]{:S(2)}, u32[]{:S(2)}) collective-permute-start(bf16[1,8,80,640]{3,2,1,0:T(8,128)(2,1)S(1)} %get-tuple-element.265), channel_id=1, source_target_pairs={{0,4},{2,6},{4,0},{6,2},{8,12},{10,14},{12,8},{14,10},{16,20},{18,... | collective-permute-start | bytes 2457608 | tf_op jit(solution)/shard_map/ppermute | solution.py:49
  429.6 26.9 %collective-permute-start.65 = (bf16[1280,640]{1,0:T(8,128)(2,1)}, bf16[1280,640]{1,0:T(8,128)(2,1)}, u32[]{:S(2)}, u32[]{:S(2)}) collective-permute-start(bf16[1280,640]{1,0:T(8,128)(2,1)} %convolution_convert_fusion.10), channel_id=1, source_target_pairs={{0,1},{1,0},{2,3},{3,2},{4,5},{5,4},{6,7},{7,6},{8,9},{9,8},{10,11... | collective-permute-start | bytes 4915208 | tf_op jit(solution)/shard_map/ppermute | solution.py:49
  430.1 29.4 %collective-permute-start.66 = (bf16[1280,640]{1,0:T(8,128)(2,1)}, bf16[1280,640]{1,0:T(8,128)(2,1)}, u32[]{:S(2)}, u32[]{:S(2)}) collective-permute-start(bf16[1280,640]{1,0:T(8,128)(2,1)} %convolution_convert_fusion.8), channel_id=1, source_target_pairs={{0,1},{1,0},{2,3},{3,2},{4,5},{5,4},{6,7},{7,6},{8,9},{9,8},{10,11... | collective-permute-start | bytes 4915208 | tf_op jit(solution)/shard_map/ppermute | solution.py:49
  450.4 19.5 %collective-permute-start.64 = (bf16[1280,512]{1,0:T(8,128)(2,1)}, bf16[1280,512]{1,0:T(8,128)(2,1)S(1)}, u32[]{:S(2)}, u32[]{:S(2)}) collective-permute-start(bf16[1280,512]{1,0:T(8,128)(2,1)} %get-tuple-element.376), channel_id=1, source_target_pairs={{0,1},{1,0},{2,3},{3,2},{4,5},{5,4},{6,7},{7,6},{8,9},{9,8},{10,11... | collective-permute-start | bytes 3932168 | tf_op jit(solution)/shard_map/ppermute | solution.py:49
  450.8 19.1 %collective-permute-start.68 = (bf16[1,4,80,640]{3,2,1,0:T(8,128)(2,1)}, bf16[1,4,80,640]{3,2,1,0:T(8,128)(2,1)S(1)}, u32[]{:S(2)}, u32[]{:S(2)}) collective-permute-start(bf16[1,4,80,640]{3,2,1,0:T(8,128)(2,1)} %copy-done.76), channel_id=1, source_target_pairs={{0,4},{2,6},{4,0},{6,2},{8,12},{10,14},{12,8},{14,10},{16,20},{18,... | collective-permute-start | bytes 1228808 | tf_op jit(solution)/shard_map/ppermute | solution.py:49
  451.9 18.0 %collective-permute-start.69 = (bf16[1,4,80,640]{3,2,1,0:T(8,128)(2,1)}, bf16[1,4,80,640]{3,2,1,0:T(8,128)(2,1)S(1)}, u32[]{:S(2)}, u32[]{:S(2)}) collective-permute-start(bf16[1,4,80,640]{3,2,1,0:T(8,128)(2,1)} %copy-done.75), channel_id=1, source_target_pairs={{0,2},{2,0},{4,6},{6,4},{8,10},{10,8},{12,14},{14,12},{16,18},{18,... | collective-permute-start | bytes 1228808 | tf_op jit(solution)/shard_map/ppermute | solution.py:49
  462.7 26.8 %collective-permute-start.71 = (bf16[1,8,80,640]{3,2,1,0:T(8,128)(2,1)S(1)}, bf16[1,8,80,640]{3,2,1,0:T(8,128)(2,1)S(1)}, u32[]{:S(2)}, u32[]{:S(2)}) collective-permute-start(bf16[1,8,80,640]{3,2,1,0:T(8,128)(2,1)S(1)} %get-tuple-element.268.refs_8_), channel_id=1, source_target_pairs={{0,2},{2,0},{4,6},{6,4},{8,10},{10,8},{12,14},{14,12},{16,18},{18,... | collective-permute-start | bytes 2457608 | tf_op jit(solution)/shard_map/ppermute | solution.py:49
  468.8 21.7 %collective-permute-start.72 = (bf16[1,8,80,640]{3,2,1,0:T(8,128)(2,1)S(1)}, bf16[1,8,80,640]{3,2,1,0:T(8,128)(2,1)}, u32[]{:S(2)}, u32[]{:S(2)}) collective-permute-start(bf16[1,8,80,640]{3,2,1,0:T(8,128)(2,1)S(1)} %get-tuple-element.270.refs_10_), channel_id=1, source_target_pairs={{0,4},{2,6},{4,0},{6,2},{8,12},{10,14},{12,8},{14,10},{16,20},{18,... | collective-permute-start | bytes 2457608 | tf_op jit(solution)/shard_map/ppermute | solution.py:49
  471.4 19.2 %collective-permute-start.70 = (bf16[2,2,80,640]{3,2,1,0:T(8,128)(2,1)}, bf16[2,2,80,640]{3,2,1,0:T(8,128)(2,1)S(1)}, u32[]{:S(2)}, u32[]{:S(2)}) collective-permute-start(bf16[2,2,80,640]{3,2,1,0:T(8,128)(2,1)} %get-tuple-element.279.refs_14_), channel_id=1, source_target_pairs={{0,8},{2,10},{4,12},{6,14},{8,0},{10,2},{12,4},{14,6},{16,24},{18,... | collective-permute-start | bytes 1228808 | tf_op jit(solution)/shard_map/ppermute | solution.py:49
  482.1 49.5 %collective-permute-start.73 = (bf16[2,640,512]{2,1,0:T(8,128)(2,1)}, bf16[2,640,512]{2,1,0:T(8,128)(2,1)}, u32[]{:S(2)}, u32[]{:S(2)}) collective-permute-start(bf16[2,640,512]{2,1,0:T(8,128)(2,1)} %get-tuple-element.290), channel_id=1, source_target_pairs={{0,2},{2,0},{4,6},{6,4},{8,10},{10,8},{12,14},{14,12},{16,18},{18,... | collective-permute-start | bytes 3932168 | tf_op jit(solution)/shard_map/ppermute | solution.py:49
  494.9 29.2 %collective-permute-start.74 = (bf16[2,1,80,640]{3,2,1,0:T(8,128)(2,1)}, bf16[2,1,80,640]{3,2,1,0:T(8,128)(2,1)}, u32[]{:S(2)}, u32[]{:S(2)}) collective-permute-start(bf16[2,1,80,640]{3,2,1,0:T(8,128)(2,1)} %get-tuple-element.283.refs_10_), channel_id=1, source_target_pairs={{0,16},{2,18},{4,20},{6,22},{8,24},{10,26},{12,28},{14,30},{16,0},... | collective-permute-start | bytes 614408 | tf_op jit(solution)/shard_map/ppermute | solution.py:49
  497.0 28.3 %collective-permute-start.75 = (bf16[1,4,80,640]{3,2,1,0:T(8,128)(2,1)}, bf16[1,4,80,640]{3,2,1,0:T(8,128)(2,1)}, u32[]{:S(2)}, u32[]{:S(2)}) collective-permute-start(bf16[1,4,80,640]{3,2,1,0:T(8,128)(2,1)} %get-tuple-element.285.refs_12_), channel_id=1, source_target_pairs={{0,4},{2,6},{4,0},{6,2},{8,12},{10,14},{12,8},{14,10},{16,20},{18,... | collective-permute-start | bytes 1228808 | tf_op jit(solution)/shard_map/ppermute | solution.py:49
  497.8 27.5 %collective-permute-start.76 = (bf16[1,4,80,640]{3,2,1,0:T(8,128)(2,1)}, bf16[1,4,80,640]{3,2,1,0:T(8,128)(2,1)}, u32[]{:S(2)}, u32[]{:S(2)}) collective-permute-start(bf16[1,4,80,640]{3,2,1,0:T(8,128)(2,1)} %get-tuple-element.287.refs_14_), channel_id=1, source_target_pairs={{0,2},{2,0},{4,6},{6,4},{8,10},{10,8},{12,14},{14,12},{16,18},{18,... | collective-permute-start | bytes 1228808 | tf_op jit(solution)/shard_map/ppermute | solution.py:49
  521.8 28.8 %collective-permute-start.81 = (bf16[1,8,80,640]{3,2,1,0:T(8,128)(2,1)}, bf16[1,8,80,640]{3,2,1,0:T(8,128)(2,1)}, u32[]{:S(2)}, u32[]{:S(2)}) collective-permute-start(bf16[1,8,80,640]{3,2,1,0:T(8,128)(2,1)} %get-tuple-element.298.refs_5_), channel_id=1, source_target_pairs={{0,2},{2,0},{4,6},{6,4},{8,10},{10,8},{12,14},{14,12},{16,18},{18,... | collective-permute-start | bytes 2457608 | tf_op jit(solution)/shard_map/ppermute | solution.py:49
  524.1 27.8 %collective-permute-start.82 = (bf16[1,8,80,640]{3,2,1,0:T(8,128)(2,1)}, bf16[1,8,80,640]{3,2,1,0:T(8,128)(2,1)S(1)}, u32[]{:S(2)}, u32[]{:S(2)}) collective-permute-start(bf16[1,8,80,640]{3,2,1,0:T(8,128)(2,1)} %copy-done.29), channel_id=1, source_target_pairs={{0,4},{2,6},{4,0},{6,2},{8,12},{10,14},{12,8},{14,10},{16,20},{18,... | collective-permute-start | bytes 2457608 | tf_op jit(solution)/shard_map/ppermute | solution.py:49
  529.8 22.1 %collective-permute-start.80 = (bf16[2,2,80,640]{3,2,1,0:T(8,128)(2,1)S(1)}, bf16[2,2,80,640]{3,2,1,0:T(8,128)(2,1)S(1)}, u32[]{:S(2)}, u32[]{:S(2)}) collective-permute-start(bf16[2,2,80,640]{3,2,1,0:T(8,128)(2,1)S(1)} %get-tuple-element.295.refs_3_), channel_id=1, source_target_pairs={{0,8},{2,10},{4,12},{6,14},{8,0},{10,2},{12,4},{14,6},{16,24},{18,... | collective-permute-start | bytes 1228808 | tf_op jit(solution)/shard_map/ppermute | solution.py:49
  543.5 28.1 %collective-permute-start.79 = (bf16[1280,512]{1,0:T(8,128)(2,1)}, bf16[1280,512]{1,0:T(8,128)(2,1)S(1)}, u32[]{:S(2)}, u32[]{:S(2)}) collective-permute-start(bf16[1280,512]{1,0:T(8,128)(2,1)} %fusion.21), channel_id=1, source_target_pairs={{0,1},{1,0},{2,3},{3,2},{4,5},{5,4},{6,7},{7,6},{8,9},{9,8},{10,11... | collective-permute-start | bytes 3932168 | tf_op jit(solution)/shard_map/ppermute | solution.py:49
  548.8 20.7 %collective-permute-start.77 = (bf16[1,8,80,640]{3,2,1,0:T(8,128)(2,1)S(1)}, bf16[1,8,80,640]{3,2,1,0:T(8,128)(2,1)S(1)}, u32[]{:S(2)}, u32[]{:S(2)}) collective-permute-start(bf16[1,8,80,640]{3,2,1,0:T(8,128)(2,1)S(1)} %get-tuple-element.304), channel_id=1, source_target_pairs={{0,2},{2,0},{4,6},{6,4},{8,10},{10,8},{12,14},{14,12},{16,18},{18,... | collective-permute-start | bytes 2457608 | tf_op jit(solution)/shard_map/ppermute | solution.py:49
  550.6 21.1 %collective-permute-start.78 = (bf16[1,8,80,640]{3,2,1,0:T(8,128)(2,1)S(1)}, bf16[1,8,80,640]{3,2,1,0:T(8,128)(2,1)S(1)}, u32[]{:S(2)}, u32[]{:S(2)}) collective-permute-start(bf16[1,8,80,640]{3,2,1,0:T(8,128)(2,1)S(1)} %get-tuple-element.306), channel_id=1, source_target_pairs={{0,4},{2,6},{4,0},{6,2},{8,12},{10,14},{12,8},{14,10},{16,20},{18,... | collective-permute-start | bytes 2457608 | tf_op jit(solution)/shard_map/ppermute | solution.py:49
  553.6 27.8 %collective-permute-start.83 = (bf16[2,1,80,640]{3,2,1,0:T(8,128)(2,1)S(1)}, bf16[2,1,80,640]{3,2,1,0:T(8,128)(2,1)S(1)}, u32[]{:S(2)}, u32[]{:S(2)}) collective-permute-start(bf16[2,1,80,640]{3,2,1,0:T(8,128)(2,1)S(1)} %get-tuple-element.309), channel_id=1, source_target_pairs={{0,16},{2,18},{4,20},{6,22},{8,24},{10,26},{12,28},{14,30},{16,0},... | collective-permute-start | bytes 614408 | tf_op jit(solution)/shard_map/ppermute | solution.py:49
  555.0 26.3 %collective-permute-start.84 = (bf16[1,4,80,640]{3,2,1,0:T(8,128)(2,1)S(1)}, bf16[1,4,80,640]{3,2,1,0:T(8,128)(2,1)S(1)}, u32[]{:S(2)}, u32[]{:S(2)}) collective-permute-start(bf16[1,4,80,640]{3,2,1,0:T(8,128)(2,1)S(1)} %get-tuple-element.312), channel_id=1, source_target_pairs={{0,4},{2,6},{4,0},{6,2},{8,12},{10,14},{12,8},{14,10},{16,20},{18,... | collective-permute-start | bytes 1228808 | tf_op jit(solution)/shard_map/ppermute | solution.py:49
  583.0 18.9 %collective-permute-start.86 = (bf16[2,2,80,640]{3,2,1,0:T(8,128)(2,1)}, bf16[2,2,80,640]{3,2,1,0:T(8,128)(2,1)S(1)}, u32[]{:S(2)}, u32[]{:S(2)}) collective-permute-start(bf16[2,2,80,640]{3,2,1,0:T(8,128)(2,1)} %get-tuple-element.315), channel_id=1, source_target_pairs={{0,8},{2,10},{4,12},{6,14},{8,0},{10,2},{12,4},{14,6},{16,24},{18,... | collective-permute-start | bytes 1228808 | tf_op jit(solution)/shard_map/ppermute | solution.py:49
  583.0 22.0 %collective-permute-start.88 = (bf16[1,4,80,640]{3,2,1,0:T(8,128)(2,1)}, bf16[1,4,80,640]{3,2,1,0:T(8,128)(2,1)S(1)}, u32[]{:S(2)}, u32[]{:S(2)}) collective-permute-start(bf16[1,4,80,640]{3,2,1,0:T(8,128)(2,1)} %get-tuple-element.320), channel_id=1, source_target_pairs={{0,4},{2,6},{4,0},{6,2},{8,12},{10,14},{12,8},{14,10},{16,20},{18,... | collective-permute-start | bytes 1228808 | tf_op jit(solution)/shard_map/ppermute | solution.py:49
  584.2 20.8 %collective-permute-start.89 = (bf16[1,4,80,640]{3,2,1,0:T(8,128)(2,1)S(1)}, bf16[1,4,80,640]{3,2,1,0:T(8,128)(2,1)S(1)}, u32[]{:S(2)}, u32[]{:S(2)}) collective-permute-start(bf16[1,4,80,640]{3,2,1,0:T(8,128)(2,1)S(1)} %get-tuple-element.321), channel_id=1, source_target_pairs={{0,2},{2,0},{4,6},{6,4},{8,10},{10,8},{12,14},{14,12},{16,18},{18,... | collective-permute-start | bytes 1228808 | tf_op jit(solution)/shard_map/ppermute | solution.py:49
  585.0 20.0 %collective-permute-start.90 = (f32[2,2640]{1,0:T(2,128)S(1)}, f32[2,2640]{1,0:T(2,128)S(1)}, u32[]{:S(2)}, u32[]{:S(2)}) collective-permute-start(f32[2,2640]{1,0:T(2,128)S(1)} %pad_maximum_fusion.24), channel_id=1, source_target_pairs={{0,1},{1,0},{2,3},{3,2},{4,5},{5,4},{6,7},{7,6},{8,9},{9,8},{10,11... | collective-permute-start | bytes 63368 | tf_op jit(solution)/shard_map/ppermute | solution.py:49
  (237 other events, 1770.2 us)

commit v9 on v8

--- a/solution.py
+++ b/solution.py
@@ -907,11 +907,16 @@
             far_dq,
             ready,
         )
-        ready = sums.tick(scale_rows)
         query_grad = lowered(dot_nt(normed, d_raw))
-        sums.push(out_grad, query_grad)
-        ready = [*ready, *sums.enter()]
-        d_keys, d_values = add_back(own_dk, own_dv, back, ready)
+        if layer:
+            d_keys, d_values = add_back(own_dk, own_dv, back, ())
+            sums.tick(d_keys)
+            sums.push(out_grad, query_grad)
+            sums.enter()
+        else:
+            ready = sums.tick(scale_rows)
+            sums.push(out_grad, query_grad)
+            d_keys, d_values = add_back(own_dk, own_dv, back, [*ready, *sums.enter()])
         scale_raw = jnp.sum(scale_rows.reshape(heads, HD), 0) / (gain_q * LOG_TWO_E)
         scale_grad = scale_raw * jax.nn.sigmoid(query_scale[layer]) * LOG_TWO_E / math.sqrt(HD)
         if not layer:

time: 648 us -> 640 us (0.988)
  waiting for transfers between devices: 135 us -> 127 us
    ppermute x99, waiting for transfers between devices: 135 us -> 127 us  [pair_swap(): return lax.ppermute(values, axis, [(i, i ^ bit) for i in range(size)])]
    unnamed x376 -> x366, local copies, waits for them, and re-layouts: 48.6 us -> 49 us
  transfers between devices with their start and end apart: 99 -> 99, of which waited for: 32 -> 31; matrix products, arithmetic and copies ran while one was open for 29% -> 30% of each run, Pallas kernels for 17% -> 17%
where the time goes in v9:
time: 640 us; the launch traced here: 630 us
  matrix products  150 us (23%)
  Pallas kernels  128 us (20%)
  waiting for transfers between devices  127 us (20%)
  starting transfers between devices  119 us (19%)
  local copies, waits for them, and re-layouts  60.6 us (9%)
  other arithmetic  37.2 us (6%)
  between operations  8.97 us (1%)
    ppermute x99, waiting for transfers between devices, pair_swap(): return lax.ppermute(values, axis, [(i, i ^ bit) for i in range(size)])  127 us
    ppermute x99, starting transfers between devices, pair_swap(): return lax.ppermute(values, axis, [(i, i ^ bit) for i in range(size)])  119 us
    pallas_call x8, Pallas kernels, per_head(): pl.pallas_call(work, grid=(heads // group,), in_specs=[spec(kind, array.s...  64.8 us
    pallas_call x38, Pallas kernels, quick_call(): pl.pallas_call(kernel, in_specs=[SCALAR] + [WHOLE] * (len(arrays) - 1) +...  63 us
    dot_general x24, matrix products, dot_nn(): return jnp.dot(former, latter, preferred_element_type=jnp.float32)  57.4 us
    unnamed x366, local copies, waits for them, and re-layouts  49 us
    dot_general x16, matrix products, dot_nt(): lax.dot_general(former, latter, (((1,), (1,)), ((), ())), preferred_eleme...  46.8 us
    dot_general x20, matrix products, dot_tn(): lax.dot_general(former, latter, (((0,), (0,)), ((), ())), preferred_eleme...  45.6 us
  transfers between devices with their start and end apart: 99, of which 31 were waited for; matrix products, arithmetic and copies ran while one was open for 30% of the time, Pallas kernels for 17%

profile of v9, /device:TPU:0, one launch (start us, length us, event | category | flops | bytes accessed | tf_op | source)
XLA Modules:
  0.0 630.3 jit_solution(16567576427908467000)
XLA Ops:
  6.2 3.7 collective-permute-start
  20.9 10.0 %collective-permute-done.3.refs_3_ = bf16[1280,256]{1,0:T(8,128)(2,1)S(1)} collective-permute-done((bf16[1280,256]{1,0:T(8,128)(2,1)S(1)}, bf16[1280,256]{1,0:T(8,128)(2,1)S(1)}, u32[]{:S(2)}, u32[]{:S(2)}) %collective-permute-start.3) | collective-permute-done | bytes 655392 | tf_op jit(solution)/shard_map/ppermute | solution.py:49
  38.5 8.8 %collective-permute-done.4.refs_3_ = bf16[2,1,80,640]{3,2,1,0:T(8,128)(2,1)S(1)} collective-permute-done((bf16[2,1,80,640]{3,2,1,0:T(8,128)(2,1)S(1)}, bf16[2,1,80,640]{3,2,1,0:T(8,128)(2,1)S(1)}, u32[]{:S(2)}, u32[]{:S(2)}) %collective-permute-start.4) | collective-permute-done | bytes 204832 | tf_op jit(solution)/shard_map/ppermute | solution.py:49
  54.1 9.2 %collective-permute-done.8.refs_3_ = bf16[2,2,80,640]{3,2,1,0:T(8,128)(2,1)S(1)} collective-permute-done((bf16[2,2,80,640]{3,2,1,0:T(8,128)(2,1)}, bf16[2,2,80,640]{3,2,1,0:T(8,128)(2,1)S(1)}, u32[]{:S(2)}, u32[]{:S(2)}) %collective-permute-start.8) | collective-permute-done | bytes 409632 | tf_op jit(solution)/shard_map/ppermute | solution.py:49
  63.3 4.8 collective-permute-done.9.refs_4_
  68.3 3.5 join_halves.17
  73.8 4.4 convolution_convert_fusion.23.refs_7_.refs_2_.refs_3_
  78.3 4.4 collective-permute-done.11.refs_3_
  87.9 5.5 collective-permute-start.14
  96.4 3.5 collective-permute-done.14.refs_3_
  107.3 3.5 multiply_convert_fusion.4.refs_1_.refs_2_
  110.8 8.4 %attention_own.2 = (f32[640,1024]{1,0:T(8,128)S(1)}, f32[8,1,1024]{2,1,0:T(1,128)S(1)}, f32[8,1,1024]{2,1,0:T(1,128)S(1)}) custom-call(s32[1,1024]{1,0:T(1,128)S(1)} %bitcast.268, bf16[640,1024]{1,0:T(8,128)(2,1)S(1)} %multiply_convert_fusion.4.refs_1_.refs_2_, bf16[640,1024]{1,0:T(8,128)(2,1)S(1)} %copy-done.10, bf16[640,1024]{1,0:T(8,128)(2,1)S(1)} %copy-done.12), custom_call_target="tpu_custom_call" | custom-call | flops 629145600 | bytes 3936256 | tf_op jit(solution)/shard_map/attention_own/pallas_call | solution.py:651
  125.2 4.9 collective-permute-start.21
  133.1 4.4 attention_far.2
  138.8 4.0 join_halves.21
  146.4 3.6 collective-permute-start.26
  155.9 6.2 collective-permute-done.24.refs_3_
  174.2 3.5 fusion.45.refs_8_
  177.7 6.6 %collective-permute-done.29.refs_4_ = bf16[1,8,80,640]{3,2,1,0:T(8,128)(2,1)S(1)} collective-permute-done((bf16[1,8,80,640]{3,2,1,0:T(8,128)(2,1)S(1)}, bf16[1,8,80,640]{3,2,1,0:T(8,128)(2,1)S(1)}, u32[]{:S(2)}, u32[]{:S(2)}) %collective-permute-start.29) | collective-permute-done | bytes 819232 | tf_op jit(solution)/shard_map/ppermute | solution.py:49
  204.0 9.2 %collective-permute-done.31.refs_3_ = bf16[2,1,80,640]{3,2,1,0:T(8,128)(2,1)} collective-permute-done((bf16[2,1,80,640]{3,2,1,0:T(8,128)(2,1)S(1)}, bf16[2,1,80,640]{3,2,1,0:T(8,128)(2,1)}, u32[]{:S(2)}, u32[]{:S(2)}) %collective-permute-start.31) | collective-permute-done | bytes 204832 | tf_op jit(solution)/shard_map/ppermute | solution.py:49
  216.9 4.5 convolution_convert_fusion.21.refs_6_.refs_2_.refs_3_
  226.2 13.0 %collective-permute-done.36.refs_4_ = bf16[1,8,80,640]{3,2,1,0:T(8,128)(2,1)S(1)} collective-permute-done((bf16[1,8,80,640]{3,2,1,0:T(8,128)(2,1)S(1)}, bf16[1,8,80,640]{3,2,1,0:T(8,128)(2,1)S(1)}, u32[]{:S(2)}, u32[]{:S(2)}) %collective-permute-start.36) | collective-permute-done | bytes 819232 | tf_op jit(solution)/shard_map/ppermute | solution.py:49
  247.1 8.1 %attention_own.3 = (f32[640,1024]{1,0:T(8,128)S(1)}, f32[8,1,1024]{2,1,0:T(1,128)S(1)}, f32[8,1,1024]{2,1,0:T(1,128)S(1)}) custom-call(s32[1,1024]{1,0:T(1,128)S(1)} %bitcast.269, bf16[640,1024]{1,0:T(8,128)(2,1)S(1)} %multiply_convert_fusion.1.refs_1_.refs_2_, bf16[640,1024]{1,0:T(8,128)(2,1)S(1)} %copy-done.14, bf16[640,1024]{1,0:T(8,128)(2,1)S(1)} %copy-done.16), custom_call_target="tpu_custom_call" | custom-call | flops 629145600 | bytes 3936256 | tf_op jit(solution)/shard_map/attention_own/pallas_call | solution.py:651
  260.8 4.7 attention_far.3
  266.8 8.1 %collective-permute-done.43.refs_2_ = bf16[1,8,80,640]{3,2,1,0:T(8,128)(2,1)S(1)} collective-permute-done((bf16[1,8,80,640]{3,2,1,0:T(8,128)(2,1)S(1)}, bf16[1,8,80,640]{3,2,1,0:T(8,128)(2,1)S(1)}, u32[]{:S(2)}, u32[]{:S(2)}) %collective-permute-start.43) | collective-permute-done | bytes 819232 | tf_op jit(solution)/shard_map/ppermute | solution.py:49
  300.8 4.5 convolution_convert_fusion.13
  309.6 3.7 add_halves.22
  316.0 3.7 convolution_convert_fusion.7
  323.1 6.9 %attention_far_back.2 = (f32[640,1024]{1,0:T(8,128)S(1)}, f32[8,1,1024]{2,1,0:T(1,128)S(1)}, bf16[2,640,512]{2,1,0:T(8,128)(2,1)}) custom-call(s32[1]{0:T(128)} %bitcast.19.refs_0_, bf16[640,1024]{1,0:T(8,128)(2,1)S(1)} %copy-done.19, bf16[640,512]{1,0:T(8,128)(2,1)S(1)} %convolution_convert_fusion.27.refs_2_, bf16[640,512]{1,0:T(8,128)(2,1)S(1)} %copy-done.37, ...), custom_call_target="tpu_custom_call" | custom-call | flops 503316480 | bytes 5275652 | tf_op jit(solution)/shard_map/attention_far_back/pallas_call | solution.py:651
  330.0 5.3 collective-permute-start.51
  344.4 12.7 %attention_own_back.2 = (bf16[640,1024]{1,0:T(8,128)(2,1)S(1)}, bf16[640,1024]{1,0:T(8,128)(2,1)S(1)}, bf16[640,1024]{1,0:T(8,128)(2,1)S(1)}, f32[640,1]{1,0:T(8,128)S(1)}) custom-call(s32[1,1024]{1,0:T(1,128)S(1)} %bitcast.270, f32[80,1]{1,0:T(8,128)S(1)} %copy.56.refs_1_, bf16[640,1024]{1,0:T(8,128)(2,1)S(1)} %copy-done.20, ...), custom_call_target="tpu_custom_call" | custom-call | flops 15938355200 | bytes 7934272 | tf_op jit(solution)/shard_map/attention_own_back/pallas_call | solution.py:651
  376.3 3.6 convolution_convert_fusion.5.refs_7_
  397.2 3.5 fusion.35
  400.8 4.0 fusion.119
  415.5 4.2 fusion.44
  425.1 4.4 convolution_add_fusion.3.refs_6_
  429.6 5.3 collective-permute-done.61.refs_1_
  456.3 5.8 collective-permute-done.67.refs_1_
  468.5 6.9 %attention_far_back.3 = (f32[640,1024]{1,0:T(8,128)S(1)}, f32[8,1,1024]{2,1,0:T(1,128)S(1)}, bf16[2,640,512]{2,1,0:T(8,128)(2,1)}) custom-call(s32[1]{0:T(128)} %bitcast.19.refs_0_, bf16[640,1024]{1,0:T(8,128)(2,1)S(1)} %copy-done.9, bf16[640,512]{1,0:T(8,128)(2,1)S(1)} %copy-done.4, bf16[640,512]{1,0:T(8,128)(2,1)S(1)} %copy-done.6, ...), custom_call_target="tpu_custom_call" | custom-call | flops 503316480 | bytes 5275652 | tf_op jit(solution)/shard_map/attention_far_back/pallas_call | solution.py:651
  475.4 4.9 collective-permute-start.73
  494.5 12.7 %attention_own_back.3 = (bf16[640,1024]{1,0:T(8,128)(2,1)S(1)}, bf16[640,1024]{1,0:T(8,128)(2,1)S(1)}, bf16[640,1024]{1,0:T(8,128)(2,1)S(1)}, f32[640,1]{1,0:T(8,128)S(1)}) custom-call(s32[1,1024]{1,0:T(1,128)S(1)} %bitcast.271, f32[80,1]{1,0:T(8,128)S(1)} %copy.59.refs_1_, bf16[640,1024]{1,0:T(8,128)(2,1)S(1)} %copy-done.9, ...), custom_call_target="tpu_custom_call" | custom-call | flops 15938355200 | bytes 7934272 | tf_op jit(solution)/shard_map/attention_own_back/pallas_call | solution.py:651
  507.2 3.5 convolution_convert_fusion.2
  525.3 3.5 add_back.3
  549.1 4.3 fusion.66
  556.1 7.3 %collective-permute-done.77.refs_1_ = bf16[1,8,80,640]{3,2,1,0:T(8,128)(2,1)S(1)} collective-permute-done((bf16[1,8,80,640]{3,2,1,0:T(8,128)(2,1)S(1)}, bf16[1,8,80,640]{3,2,1,0:T(8,128)(2,1)S(1)}, u32[]{:S(2)}, u32[]{:S(2)}) %collective-permute-start.77) | collective-permute-done | bytes 819232 | tf_op jit(solution)/shard_map/ppermute | solution.py:49
  569.8 4.3 fusion.20
  603.1 5.0 collective-permute-done.87.refs_1_
  621.1 4.8 collective-permute-done.97.refs_3_
  (717 shorter events, 345.9 us)
Async XLA Ops:
  48.8 19.2 %collective-permute-start.9 = (bf16[1,8,80,640]{3,2,1,0:T(8,128)(2,1)S(1)}, bf16[1,8,80,640]{3,2,1,0:T(8,128)(2,1)}, u32[]{:S(2)}, u32[]{:S(2)}) collective-permute-start(bf16[1,8,80,640]{3,2,1,0:T(8,128)(2,1)S(1)} %get-tuple-element.178.refs_1_), channel_id=1, source_target_pairs={{0,2},{2,0},{4,6},{6,4},{8,10},{10,8},{12,14},{14,12},{16,18},{18,... | collective-permute-start | bytes 2457608 | tf_op jit(solution)/shard_map/ppermute | solution.py:49
  49.3 19.0 %collective-permute-start.10 = (bf16[1,8,80,640]{3,2,1,0:T(8,128)(2,1)S(1)}, bf16[1,8,80,640]{3,2,1,0:T(8,128)(2,1)}, u32[]{:S(2)}, u32[]{:S(2)}) collective-permute-start(bf16[1,8,80,640]{3,2,1,0:T(8,128)(2,1)S(1)} %get-tuple-element.179.refs_2_), channel_id=1, source_target_pairs={{0,4},{2,6},{4,0},{6,2},{8,12},{10,14},{12,8},{14,10},{16,20},{18,... | collective-permute-start | bytes 2457608 | tf_op jit(solution)/shard_map/ppermute | solution.py:49
  103.3 17.4 %collective-permute-start.17 = (bf16[2,1,80,640]{3,2,1,0:T(8,128)(2,1)S(1)}, bf16[2,1,80,640]{3,2,1,0:T(8,128)(2,1)S(1)}, u32[]{:S(2)}, u32[]{:S(2)}) collective-permute-start(bf16[2,1,80,640]{3,2,1,0:T(8,128)(2,1)S(1)} %get-tuple-element.195.refs_0_), channel_id=1, source_target_pairs={{0,16},{2,18},{4,20},{6,22},{8,24},{10,26},{12,28},{14,30},{16,0},... | collective-permute-start | bytes 614408 | tf_op jit(solution)/shard_map/ppermute | solution.py:49
  142.8 31.3 %collective-permute-start.27 = (bf16[2,1280,640]{2,1,0:T(8,128)(2,1)}, bf16[2,1280,640]{2,1,0:T(8,128)(2,1)}, u32[]{:S(2)}, u32[]{:S(2)}) collective-permute-start(bf16[2,1280,640]{2,1,0:T(8,128)(2,1)} %bitcast.288), channel_id=1, source_target_pairs={{0,1},{1,0},{2,3},{3,2},{4,5},{5,4},{6,7},{7,6},{8,9},{9,8},{10,11... | collective-permute-start | bytes 9830408 | tf_op jit(solution)/shard_map/ppermute | solution.py:49
  165.6 18.8 %collective-permute-start.29 = (bf16[1,8,80,640]{3,2,1,0:T(8,128)(2,1)S(1)}, bf16[1,8,80,640]{3,2,1,0:T(8,128)(2,1)S(1)}, u32[]{:S(2)}, u32[]{:S(2)}) collective-permute-start(bf16[1,8,80,640]{3,2,1,0:T(8,128)(2,1)S(1)} %get-tuple-element.209.refs_1_), channel_id=1, source_target_pairs={{0,2},{2,0},{4,6},{6,4},{8,10},{10,8},{12,14},{14,12},{16,18},{18,... | collective-permute-start | bytes 2457608 | tf_op jit(solution)/shard_map/ppermute | solution.py:49
  166.3 18.5 %collective-permute-start.30 = (bf16[1,8,80,640]{3,2,1,0:T(8,128)(2,1)S(1)}, bf16[1,8,80,640]{3,2,1,0:T(8,128)(2,1)S(1)}, u32[]{:S(2)}, u32[]{:S(2)}) collective-permute-start(bf16[1,8,80,640]{3,2,1,0:T(8,128)(2,1)S(1)} %get-tuple-element.210.refs_2_), channel_id=1, source_target_pairs={{0,4},{2,6},{4,0},{6,2},{8,12},{10,14},{12,8},{14,10},{16,20},{18,... | collective-permute-start | bytes 2457608 | tf_op jit(solution)/shard_map/ppermute | solution.py:49
  194.4 18.8 %collective-permute-start.32 = (bf16[1,4,80,640]{3,2,1,0:T(8,128)(2,1)}, bf16[1,4,80,640]{3,2,1,0:T(8,128)(2,1)}, u32[]{:S(2)}, u32[]{:S(2)}) collective-permute-start(bf16[1,4,80,640]{3,2,1,0:T(8,128)(2,1)} %get-tuple-element.213.refs_1_), channel_id=1, source_target_pairs={{0,4},{2,6},{4,0},{6,2},{8,12},{10,14},{12,8},{14,10},{16,20},{18,... | collective-permute-start | bytes 1228808 | tf_op jit(solution)/shard_map/ppermute | solution.py:49
  199.7 22.7 %collective-permute-start.38 = (bf16[1280,256]{1,0:T(8,128)(2,1)}, bf16[1280,256]{1,0:T(8,128)(2,1)S(1)}, u32[]{:S(2)}, u32[]{:S(2)}) collective-permute-start(bf16[1280,256]{1,0:T(8,128)(2,1)} %fusion.64), channel_id=1, source_target_pairs={{0,2},{2,0},{4,6},{6,4},{8,10},{10,8},{12,14},{14,12},{16,18},{18,... | collective-permute-start | bytes 1966088 | tf_op jit(solution)/shard_map/ppermute | solution.py:49
  214.8 24.4 %collective-permute-start.36 = (bf16[1,8,80,640]{3,2,1,0:T(8,128)(2,1)S(1)}, bf16[1,8,80,640]{3,2,1,0:T(8,128)(2,1)S(1)}, u32[]{:S(2)}, u32[]{:S(2)}) collective-permute-start(bf16[1,8,80,640]{3,2,1,0:T(8,128)(2,1)S(1)} %get-tuple-element.216.refs_1_), channel_id=1, source_target_pairs={{0,2},{2,0},{4,6},{6,4},{8,10},{10,8},{12,14},{14,12},{16,18},{18,... | collective-permute-start | bytes 2457608 | tf_op jit(solution)/shard_map/ppermute | solution.py:49
  215.5 23.7 %collective-permute-start.37 = (bf16[1,8,80,640]{3,2,1,0:T(8,128)(2,1)S(1)}, bf16[1,8,80,640]{3,2,1,0:T(8,128)(2,1)S(1)}, u32[]{:S(2)}, u32[]{:S(2)}) collective-permute-start(bf16[1,8,80,640]{3,2,1,0:T(8,128)(2,1)S(1)} %get-tuple-element.217.refs_2_), channel_id=1, source_target_pairs={{0,4},{2,6},{4,0},{6,2},{8,12},{10,14},{12,8},{14,10},{16,20},{18,... | collective-permute-start | bytes 2457608 | tf_op jit(solution)/shard_map/ppermute | solution.py:49
  222.4 35.8 %collective-permute-start.39 = (bf16[1280,256]{1,0:T(8,128)(2,1)S(1)}, bf16[1280,256]{1,0:T(8,128)(2,1)S(1)}, u32[]{:S(2)}, u32[]{:S(2)}) collective-permute-start(bf16[1280,256]{1,0:T(8,128)(2,1)S(1)} %collective-permute-done.38.refs_5_), channel_id=1, source_target_pairs={{0,1},{1,0},{2,3},{3,2},{4,5},{5,4},{6,7},{7,6},{8,9},{9,8},{10,11... | collective-permute-start | bytes 1966088 | tf_op jit(solution)/shard_map/ppermute | solution.py:49
  255.9 19.0 %collective-permute-start.43 = (bf16[1,8,80,640]{3,2,1,0:T(8,128)(2,1)S(1)}, bf16[1,8,80,640]{3,2,1,0:T(8,128)(2,1)S(1)}, u32[]{:S(2)}, u32[]{:S(2)}) collective-permute-start(bf16[1,8,80,640]{3,2,1,0:T(8,128)(2,1)S(1)} %get-tuple-element.227.refs_7_.refs_0_), channel_id=1, source_target_pairs={{0,2},{2,0},{4,6},{6,4},{8,10},{10,8},{12,14},{14,12},{16,18},{18,... | collective-permute-start | bytes 2457608 | tf_op jit(solution)/shard_map/ppermute | solution.py:49
  256.8 18.6 %collective-permute-start.44 = (bf16[1,8,80,640]{3,2,1,0:T(8,128)(2,1)S(1)}, bf16[1,8,80,640]{3,2,1,0:T(8,128)(2,1)S(1)}, u32[]{:S(2)}, u32[]{:S(2)}) collective-permute-start(bf16[1,8,80,640]{3,2,1,0:T(8,128)(2,1)S(1)} %get-tuple-element.228.refs_8_.refs_1_), channel_id=1, source_target_pairs={{0,4},{2,6},{4,0},{6,2},{8,12},{10,14},{12,8},{14,10},{16,20},{18,... | collective-permute-start | bytes 2457608 | tf_op jit(solution)/shard_map/ppermute | solution.py:49
  313.2 22.0 %collective-permute-start.49 = (bf16[1,8,80,640]{3,2,1,0:T(8,128)(2,1)S(1)}, bf16[1,8,80,640]{3,2,1,0:T(8,128)(2,1)S(1)}, u32[]{:S(2)}, u32[]{:S(2)}) collective-permute-start(bf16[1,8,80,640]{3,2,1,0:T(8,128)(2,1)S(1)} %get-tuple-element.232.refs_8_), channel_id=1, source_target_pairs={{0,2},{2,0},{4,6},{6,4},{8,10},{10,8},{12,14},{14,12},{16,18},{18,... | collective-permute-start | bytes 2457608 | tf_op jit(solution)/shard_map/ppermute | solution.py:49
  314.6 20.8 %collective-permute-start.50 = (bf16[1,8,80,640]{3,2,1,0:T(8,128)(2,1)S(1)}, bf16[1,8,80,640]{3,2,1,0:T(8,128)(2,1)S(1)}, u32[]{:S(2)}, u32[]{:S(2)}) collective-permute-start(bf16[1,8,80,640]{3,2,1,0:T(8,128)(2,1)S(1)} %get-tuple-element.234.refs_10_), channel_id=1, source_target_pairs={{0,4},{2,6},{4,0},{6,2},{8,12},{10,14},{12,8},{14,10},{16,20},{18,... | collective-permute-start | bytes 2457608 | tf_op jit(solution)/shard_map/ppermute | solution.py:49
  330.0 35.7 %collective-permute-start.51 = (bf16[2,640,512]{2,1,0:T(8,128)(2,1)}, bf16[2,640,512]{2,1,0:T(8,128)(2,1)}, u32[]{:S(2)}, u32[]{:S(2)}) collective-permute-start(bf16[2,640,512]{2,1,0:T(8,128)(2,1)} %get-tuple-element.244), channel_id=1, source_target_pairs={{0,2},{2,0},{4,6},{6,4},{8,10},{10,8},{12,14},{14,12},{16,18},{18,... | collective-permute-start | bytes 3932168 | tf_op jit(solution)/shard_map/ppermute | solution.py:49
  336.9 35.8 %collective-permute-start.53 = (bf16[1,4,80,640]{3,2,1,0:T(8,128)(2,1)}, bf16[1,4,80,640]{3,2,1,0:T(8,128)(2,1)}, u32[]{:S(2)}, u32[]{:S(2)}) collective-permute-start(bf16[1,4,80,640]{3,2,1,0:T(8,128)(2,1)} %get-tuple-element.238.refs_10_), channel_id=1, source_target_pairs={{0,4},{2,6},{4,0},{6,2},{8,12},{10,14},{12,8},{14,10},{16,20},{18,... | collective-permute-start | bytes 1228808 | tf_op jit(solution)/shard_map/ppermute | solution.py:49
  337.9 36.0 %collective-permute-start.54 = (bf16[1,4,80,640]{3,2,1,0:T(8,128)(2,1)S(1)}, bf16[1,4,80,640]{3,2,1,0:T(8,128)(2,1)}, u32[]{:S(2)}, u32[]{:S(2)}) collective-permute-start(bf16[1,4,80,640]{3,2,1,0:T(8,128)(2,1)S(1)} %get-tuple-element.240.refs_12_), channel_id=1, source_target_pairs={{0,2},{2,0},{4,6},{6,4},{8,10},{10,8},{12,14},{14,12},{16,18},{18,... | collective-permute-start | bytes 1228808 | tf_op jit(solution)/shard_map/ppermute | solution.py:49
  363.5 31.5 %collective-permute-start.56 = (bf16[1,8,80,640]{3,2,1,0:T(8,128)(2,1)}, bf16[1,8,80,640]{3,2,1,0:T(8,128)(2,1)S(1)}, u32[]{:S(2)}, u32[]{:S(2)}) collective-permute-start(bf16[1,8,80,640]{3,2,1,0:T(8,128)(2,1)} %get-tuple-element.250), channel_id=1, source_target_pairs={{0,2},{2,0},{4,6},{6,4},{8,10},{10,8},{12,14},{14,12},{16,18},{18,... | collective-permute-start | bytes 2457608 | tf_op jit(solution)/shard_map/ppermute | solution.py:49
  364.7 30.2 %collective-permute-start.57 = (bf16[1,8,80,640]{3,2,1,0:T(8,128)(2,1)}, bf16[1,8,80,640]{3,2,1,0:T(8,128)(2,1)S(1)}, u32[]{:S(2)}, u32[]{:S(2)}) collective-permute-start(bf16[1,8,80,640]{3,2,1,0:T(8,128)(2,1)} %get-tuple-element.252), channel_id=1, source_target_pairs={{0,4},{2,6},{4,0},{6,2},{8,12},{10,14},{12,8},{14,10},{16,20},{18,... | collective-permute-start | bytes 2457608 | tf_op jit(solution)/shard_map/ppermute | solution.py:49
  372.7 18.3 %collective-permute-start.52 = (bf16[1280,512]{1,0:T(8,128)(2,1)}, bf16[1280,512]{1,0:T(8,128)(2,1)}, u32[]{:S(2)}, u32[]{:S(2)}) collective-permute-start(bf16[1280,512]{1,0:T(8,128)(2,1)} %fusion.22), channel_id=1, source_target_pairs={{0,1},{1,0},{2,3},{3,2},{4,5},{5,4},{6,7},{7,6},{8,9},{9,8},{10,11... | collective-permute-start | bytes 3932168 | tf_op jit(solution)/shard_map/ppermute | solution.py:49
  376.0 19.0 %collective-permute-start.55 = (bf16[2,2,80,640]{3,2,1,0:T(8,128)(2,1)}, bf16[2,2,80,640]{3,2,1,0:T(8,128)(2,1)S(1)}, u32[]{:S(2)}, u32[]{:S(2)}) collective-permute-start(bf16[2,2,80,640]{3,2,1,0:T(8,128)(2,1)} %get-tuple-element.248), channel_id=1, source_target_pairs={{0,8},{2,10},{4,12},{6,14},{8,0},{10,2},{12,4},{14,6},{16,24},{18,... | collective-permute-start | bytes 1228808 | tf_op jit(solution)/shard_map/ppermute | solution.py:49
  385.1 44.5 %collective-permute-start.62 = (bf16[1,8,80,640]{3,2,1,0:T(8,128)(2,1)S(1)}, bf16[1,8,80,640]{3,2,1,0:T(8,128)(2,1)S(1)}, u32[]{:S(2)}, u32[]{:S(2)}) collective-permute-start(bf16[1,8,80,640]{3,2,1,0:T(8,128)(2,1)S(1)} %get-tuple-element.262), channel_id=1, source_target_pairs={{0,2},{2,0},{4,6},{6,4},{8,10},{10,8},{12,14},{14,12},{16,18},{18,... | collective-permute-start | bytes 2457608 | tf_op jit(solution)/shard_map/ppermute | solution.py:49
  391.1 38.5 %collective-permute-start.63 = (bf16[1,8,80,640]{3,2,1,0:T(8,128)(2,1)S(1)}, bf16[1,8,80,640]{3,2,1,0:T(8,128)(2,1)S(1)}, u32[]{:S(2)}, u32[]{:S(2)}) collective-permute-start(bf16[1,8,80,640]{3,2,1,0:T(8,128)(2,1)S(1)} %get-tuple-element.264), channel_id=1, source_target_pairs={{0,4},{2,6},{4,0},{6,2},{8,12},{10,14},{12,8},{14,10},{16,20},{18,... | collective-permute-start | bytes 2457608 | tf_op jit(solution)/shard_map/ppermute | solution.py:49
  422.1 27.7 %collective-permute-start.65 = (bf16[1280,640]{1,0:T(8,128)(2,1)}, bf16[1280,640]{1,0:T(8,128)(2,1)}, u32[]{:S(2)}, u32[]{:S(2)}) collective-permute-start(bf16[1280,640]{1,0:T(8,128)(2,1)} %convolution_convert_fusion.10), channel_id=1, source_target_pairs={{0,1},{1,0},{2,3},{3,2},{4,5},{5,4},{6,7},{7,6},{8,9},{9,8},{10,11... | collective-permute-start | bytes 4915208 | tf_op jit(solution)/shard_map/ppermute | solution.py:49
  422.1 30.6 %collective-permute-start.66 = (bf16[1280,640]{1,0:T(8,128)(2,1)}, bf16[1280,640]{1,0:T(8,128)(2,1)}, u32[]{:S(2)}, u32[]{:S(2)}) collective-permute-start(bf16[1280,640]{1,0:T(8,128)(2,1)} %convolution_convert_fusion.8), channel_id=1, source_target_pairs={{0,1},{1,0},{2,3},{3,2},{4,5},{5,4},{6,7},{7,6},{8,9},{9,8},{10,11... | collective-permute-start | bytes 4915208 | tf_op jit(solution)/shard_map/ppermute | solution.py:49
  442.3 20.9 %collective-permute-start.64 = (bf16[1280,512]{1,0:T(8,128)(2,1)}, bf16[1280,512]{1,0:T(8,128)(2,1)S(1)}, u32[]{:S(2)}, u32[]{:S(2)}) collective-permute-start(bf16[1280,512]{1,0:T(8,128)(2,1)} %get-tuple-element.376), channel_id=1, source_target_pairs={{0,1},{1,0},{2,3},{3,2},{4,5},{5,4},{6,7},{7,6},{8,9},{9,8},{10,11... | collective-permute-start | bytes 3932168 | tf_op jit(solution)/shard_map/ppermute | solution.py:49
  443.6 19.5 %collective-permute-start.68 = (bf16[1,4,80,640]{3,2,1,0:T(8,128)(2,1)}, bf16[1,4,80,640]{3,2,1,0:T(8,128)(2,1)S(1)}, u32[]{:S(2)}, u32[]{:S(2)}) collective-permute-start(bf16[1,4,80,640]{3,2,1,0:T(8,128)(2,1)} %copy-done.73), channel_id=1, source_target_pairs={{0,4},{2,6},{4,0},{6,2},{8,12},{10,14},{12,8},{14,10},{16,20},{18,... | collective-permute-start | bytes 1228808 | tf_op jit(solution)/shard_map/ppermute | solution.py:49
  444.7 18.5 %collective-permute-start.69 = (bf16[1,4,80,640]{3,2,1,0:T(8,128)(2,1)}, bf16[1,4,80,640]{3,2,1,0:T(8,128)(2,1)S(1)}, u32[]{:S(2)}, u32[]{:S(2)}) collective-permute-start(bf16[1,4,80,640]{3,2,1,0:T(8,128)(2,1)} %copy-done.72), channel_id=1, source_target_pairs={{0,2},{2,0},{4,6},{6,4},{8,10},{10,8},{12,14},{14,12},{16,18},{18,... | collective-permute-start | bytes 1228808 | tf_op jit(solution)/shard_map/ppermute | solution.py:49
  456.0 26.6 %collective-permute-start.71 = (bf16[1,8,80,640]{3,2,1,0:T(8,128)(2,1)S(1)}, bf16[1,8,80,640]{3,2,1,0:T(8,128)(2,1)S(1)}, u32[]{:S(2)}, u32[]{:S(2)}) collective-permute-start(bf16[1,8,80,640]{3,2,1,0:T(8,128)(2,1)S(1)} %get-tuple-element.267.refs_8_), channel_id=1, source_target_pairs={{0,2},{2,0},{4,6},{6,4},{8,10},{10,8},{12,14},{14,12},{16,18},{18,... | collective-permute-start | bytes 2457608 | tf_op jit(solution)/shard_map/ppermute | solution.py:49
  462.1 21.4 %collective-permute-start.72 = (bf16[1,8,80,640]{3,2,1,0:T(8,128)(2,1)S(1)}, bf16[1,8,80,640]{3,2,1,0:T(8,128)(2,1)}, u32[]{:S(2)}, u32[]{:S(2)}) collective-permute-start(bf16[1,8,80,640]{3,2,1,0:T(8,128)(2,1)S(1)} %get-tuple-element.269.refs_10_), channel_id=1, source_target_pairs={{0,4},{2,6},{4,0},{6,2},{8,12},{10,14},{12,8},{14,10},{16,20},{18,... | collective-permute-start | bytes 2457608 | tf_op jit(solution)/shard_map/ppermute | solution.py:49
  464.6 18.8 %collective-permute-start.70 = (bf16[2,2,80,640]{3,2,1,0:T(8,128)(2,1)}, bf16[2,2,80,640]{3,2,1,0:T(8,128)(2,1)S(1)}, u32[]{:S(2)}, u32[]{:S(2)}) collective-permute-start(bf16[2,2,80,640]{3,2,1,0:T(8,128)(2,1)} %get-tuple-element.278.refs_14_), channel_id=1, source_target_pairs={{0,8},{2,10},{4,12},{6,14},{8,0},{10,2},{12,4},{14,6},{16,24},{18,... | collective-permute-start | bytes 1228808 | tf_op jit(solution)/shard_map/ppermute | solution.py:49
  475.4 49.9 %collective-permute-start.73 = (bf16[2,640,512]{2,1,0:T(8,128)(2,1)}, bf16[2,640,512]{2,1,0:T(8,128)(2,1)}, u32[]{:S(2)}, u32[]{:S(2)}) collective-permute-start(bf16[2,640,512]{2,1,0:T(8,128)(2,1)} %get-tuple-element.289), channel_id=1, source_target_pairs={{0,2},{2,0},{4,6},{6,4},{8,10},{10,8},{12,14},{14,12},{16,18},{18,... | collective-permute-start | bytes 3932168 | tf_op jit(solution)/shard_map/ppermute | solution.py:49
  487.8 28.7 %collective-permute-start.74 = (bf16[2,1,80,640]{3,2,1,0:T(8,128)(2,1)}, bf16[2,1,80,640]{3,2,1,0:T(8,128)(2,1)}, u32[]{:S(2)}, u32[]{:S(2)}) collective-permute-start(bf16[2,1,80,640]{3,2,1,0:T(8,128)(2,1)} %get-tuple-element.282.refs_10_), channel_id=1, source_target_pairs={{0,16},{2,18},{4,20},{6,22},{8,24},{10,26},{12,28},{14,30},{16,0},... | collective-permute-start | bytes 614408 | tf_op jit(solution)/shard_map/ppermute | solution.py:49
  489.8 28.3 %collective-permute-start.75 = (bf16[1,4,80,640]{3,2,1,0:T(8,128)(2,1)}, bf16[1,4,80,640]{3,2,1,0:T(8,128)(2,1)}, u32[]{:S(2)}, u32[]{:S(2)}) collective-permute-start(bf16[1,4,80,640]{3,2,1,0:T(8,128)(2,1)} %get-tuple-element.284.refs_12_), channel_id=1, source_target_pairs={{0,4},{2,6},{4,0},{6,2},{8,12},{10,14},{12,8},{14,10},{16,20},{18,... | collective-permute-start | bytes 1228808 | tf_op jit(solution)/shard_map/ppermute | solution.py:49
  490.4 28.5 %collective-permute-start.76 = (bf16[1,4,80,640]{3,2,1,0:T(8,128)(2,1)}, bf16[1,4,80,640]{3,2,1,0:T(8,128)(2,1)}, u32[]{:S(2)}, u32[]{:S(2)}) collective-permute-start(bf16[1,4,80,640]{3,2,1,0:T(8,128)(2,1)} %get-tuple-element.286.refs_14_), channel_id=1, source_target_pairs={{0,2},{2,0},{4,6},{6,4},{8,10},{10,8},{12,14},{14,12},{16,18},{18,... | collective-permute-start | bytes 1228808 | tf_op jit(solution)/shard_map/ppermute | solution.py:49
  514.2 30.3 %collective-permute-start.81 = (bf16[1,8,80,640]{3,2,1,0:T(8,128)(2,1)}, bf16[1,8,80,640]{3,2,1,0:T(8,128)(2,1)}, u32[]{:S(2)}, u32[]{:S(2)}) collective-permute-start(bf16[1,8,80,640]{3,2,1,0:T(8,128)(2,1)} %get-tuple-element.297.refs_5_), channel_id=1, source_target_pairs={{0,2},{2,0},{4,6},{6,4},{8,10},{10,8},{12,14},{14,12},{16,18},{18,... | collective-permute-start | bytes 2457608 | tf_op jit(solution)/shard_map/ppermute | solution.py:49
  516.6 28.6 %collective-permute-start.82 = (bf16[1,8,80,640]{3,2,1,0:T(8,128)(2,1)}, bf16[1,8,80,640]{3,2,1,0:T(8,128)(2,1)S(1)}, u32[]{:S(2)}, u32[]{:S(2)}) collective-permute-start(bf16[1,8,80,640]{3,2,1,0:T(8,128)(2,1)} %copy-done.27), channel_id=1, source_target_pairs={{0,4},{2,6},{4,0},{6,2},{8,12},{10,14},{12,8},{14,10},{16,20},{18,... | collective-permute-start | bytes 2457608 | tf_op jit(solution)/shard_map/ppermute | solution.py:49
  523.3 21.8 %collective-permute-start.80 = (bf16[2,2,80,640]{3,2,1,0:T(8,128)(2,1)S(1)}, bf16[2,2,80,640]{3,2,1,0:T(8,128)(2,1)S(1)}, u32[]{:S(2)}, u32[]{:S(2)}) collective-permute-start(bf16[2,2,80,640]{3,2,1,0:T(8,128)(2,1)S(1)} %get-tuple-element.294.refs_3_), channel_id=1, source_target_pairs={{0,8},{2,10},{4,12},{6,14},{8,0},{10,2},{12,4},{14,6},{16,24},{18,... | collective-permute-start | bytes 1228808 | tf_op jit(solution)/shard_map/ppermute | solution.py:49
  537.2 28.4 %collective-permute-start.79 = (bf16[1280,512]{1,0:T(8,128)(2,1)}, bf16[1280,512]{1,0:T(8,128)(2,1)S(1)}, u32[]{:S(2)}, u32[]{:S(2)}) collective-permute-start(bf16[1280,512]{1,0:T(8,128)(2,1)} %fusion.21), channel_id=1, source_target_pairs={{0,1},{1,0},{2,3},{3,2},{4,5},{5,4},{6,7},{7,6},{8,9},{9,8},{10,11... | collective-permute-start | bytes 3932168 | tf_op jit(solution)/shard_map/ppermute | solution.py:49
  542.5 21.0 %collective-permute-start.77 = (bf16[1,8,80,640]{3,2,1,0:T(8,128)(2,1)S(1)}, bf16[1,8,80,640]{3,2,1,0:T(8,128)(2,1)S(1)}, u32[]{:S(2)}, u32[]{:S(2)}) collective-permute-start(bf16[1,8,80,640]{3,2,1,0:T(8,128)(2,1)S(1)} %get-tuple-element.303), channel_id=1, source_target_pairs={{0,2},{2,0},{4,6},{6,4},{8,10},{10,8},{12,14},{14,12},{16,18},{18,... | collective-permute-start | bytes 2457608 | tf_op jit(solution)/shard_map/ppermute | solution.py:49
  544.6 21.1 %collective-permute-start.78 = (bf16[1,8,80,640]{3,2,1,0:T(8,128)(2,1)S(1)}, bf16[1,8,80,640]{3,2,1,0:T(8,128)(2,1)S(1)}, u32[]{:S(2)}, u32[]{:S(2)}) collective-permute-start(bf16[1,8,80,640]{3,2,1,0:T(8,128)(2,1)S(1)} %get-tuple-element.305), channel_id=1, source_target_pairs={{0,4},{2,6},{4,0},{6,2},{8,12},{10,14},{12,8},{14,10},{16,20},{18,... | collective-permute-start | bytes 2457608 | tf_op jit(solution)/shard_map/ppermute | solution.py:49
  546.8 28.5 %collective-permute-start.83 = (bf16[2,1,80,640]{3,2,1,0:T(8,128)(2,1)S(1)}, bf16[2,1,80,640]{3,2,1,0:T(8,128)(2,1)S(1)}, u32[]{:S(2)}, u32[]{:S(2)}) collective-permute-start(bf16[2,1,80,640]{3,2,1,0:T(8,128)(2,1)S(1)} %get-tuple-element.308), channel_id=1, source_target_pairs={{0,16},{2,18},{4,20},{6,22},{8,24},{10,26},{12,28},{14,30},{16,0},... | collective-permute-start | bytes 614408 | tf_op jit(solution)/shard_map/ppermute | solution.py:49
  547.7 27.7 %collective-permute-start.84 = (bf16[1,4,80,640]{3,2,1,0:T(8,128)(2,1)S(1)}, bf16[1,4,80,640]{3,2,1,0:T(8,128)(2,1)S(1)}, u32[]{:S(2)}, u32[]{:S(2)}) collective-permute-start(bf16[1,4,80,640]{3,2,1,0:T(8,128)(2,1)S(1)} %get-tuple-element.311), channel_id=1, source_target_pairs={{0,4},{2,6},{4,0},{6,2},{8,12},{10,14},{12,8},{14,10},{16,20},{18,... | collective-permute-start | bytes 1228808 | tf_op jit(solution)/shard_map/ppermute | solution.py:49
  577.0 18.1 %collective-permute-start.86 = (bf16[2,2,80,640]{3,2,1,0:T(8,128)(2,1)}, bf16[2,2,80,640]{3,2,1,0:T(8,128)(2,1)S(1)}, u32[]{:S(2)}, u32[]{:S(2)}) collective-permute-start(bf16[2,2,80,640]{3,2,1,0:T(8,128)(2,1)} %get-tuple-element.314), channel_id=1, source_target_pairs={{0,8},{2,10},{4,12},{6,14},{8,0},{10,2},{12,4},{14,6},{16,24},{18,... | collective-permute-start | bytes 1228808 | tf_op jit(solution)/shard_map/ppermute | solution.py:49
  577.0 20.7 %collective-permute-start.88 = (bf16[1,4,80,640]{3,2,1,0:T(8,128)(2,1)}, bf16[1,4,80,640]{3,2,1,0:T(8,128)(2,1)S(1)}, u32[]{:S(2)}, u32[]{:S(2)}) collective-permute-start(bf16[1,4,80,640]{3,2,1,0:T(8,128)(2,1)} %get-tuple-element.319), channel_id=1, source_target_pairs={{0,4},{2,6},{4,0},{6,2},{8,12},{10,14},{12,8},{14,10},{16,20},{18,... | collective-permute-start | bytes 1228808 | tf_op jit(solution)/shard_map/ppermute | solution.py:49
  577.5 20.2 %collective-permute-start.89 = (bf16[1,4,80,640]{3,2,1,0:T(8,128)(2,1)S(1)}, bf16[1,4,80,640]{3,2,1,0:T(8,128)(2,1)S(1)}, u32[]{:S(2)}, u32[]{:S(2)}) collective-permute-start(bf16[1,4,80,640]{3,2,1,0:T(8,128)(2,1)S(1)} %get-tuple-element.320), channel_id=1, source_target_pairs={{0,2},{2,0},{4,6},{6,4},{8,10},{10,8},{12,14},{14,12},{16,18},{18,... | collective-permute-start | bytes 1228808 | tf_op jit(solution)/shard_map/ppermute | solution.py:49
  578.3 19.4 %collective-permute-start.90 = (f32[2,2640]{1,0:T(2,128)S(1)}, f32[2,2640]{1,0:T(2,128)S(1)}, u32[]{:S(2)}, u32[]{:S(2)}) collective-permute-start(f32[2,2640]{1,0:T(2,128)S(1)} %pad_maximum_fusion.24), channel_id=1, source_target_pairs={{0,1},{1,0},{2,3},{3,2},{4,5},{5,4},{6,7},{7,6},{8,9},{9,8},{10,11... | collective-permute-start | bytes 63368 | tf_op jit(solution)/shard_map/ppermute | solution.py:49
  (232 other events, 1755.8 us)

commit v10 on v8

--- a/solution.py
+++ b/solution.py
@@ -907,11 +907,11 @@
             far_dq,
             ready,
         )
-        ready = sums.tick(scale_rows)
         query_grad = lowered(dot_nt(normed, d_raw))
+        d_keys, d_values = add_back(own_dk, own_dv, back, ())
+        sums.tick(d_keys)
         sums.push(out_grad, query_grad)
-        ready = [*ready, *sums.enter()]
-        d_keys, d_values = add_back(own_dk, own_dv, back, ready)
+        sums.enter()
         scale_raw = jnp.sum(scale_rows.reshape(heads, HD), 0) / (gain_q * LOG_TWO_E)
         scale_grad = scale_raw * jax.nn.sigmoid(query_scale[layer]) * LOG_TWO_E / math.sqrt(HD)
         if not layer:

time: 648 us -> 646 us (level)
  waiting for transfers between devices: 135 us -> 144 us
  starting transfers between devices: 121 us -> 114 us
    ppermute x99, waiting for transfers between devices: 135 us -> 144 us  [pair_swap(): return lax.ppermute(values, axis, [(i, i ^ bit) for i in range(size)])]
    unnamed x376 -> x356, local copies, waits for them, and re-layouts: 48.6 us -> 48.6 us
  transfers between devices with their start and end apart: 99 -> 99, of which waited for: 32 -> 32; matrix products, arithmetic and copies ran while one was open for 29% -> 29% of each run, Pallas kernels for 17% -> 16%
where the time goes in v10:
time: 646 us; the launch traced here: 637 us
  waiting for transfers between devices  144 us (22%)
  matrix products  144 us (22%)
  Pallas kernels  127 us (20%)
  starting transfers between devices  114 us (18%)
  local copies, waits for them, and re-layouts  60.2 us (9%)
  other arithmetic  37.8 us (6%)
  between operations  9.38 us (1%)
    ppermute x99, waiting for transfers between devices, pair_swap(): return lax.ppermute(values, axis, [(i, i ^ bit) for i in range(size)])  144 us
    ppermute x99, starting transfers between devices, pair_swap(): return lax.ppermute(values, axis, [(i, i ^ bit) for i in range(size)])  114 us
    pallas_call x8, Pallas kernels, per_head(): pl.pallas_call(work, grid=(heads // group,), in_specs=[spec(kind, array.s...  64.7 us
    pallas_call x38, Pallas kernels, quick_call(): pl.pallas_call(kernel, in_specs=[SCALAR] + [WHOLE] * (len(arrays) - 1) +...  62.3 us
    dot_general x24, matrix products, dot_nn(): return jnp.dot(former, latter, preferred_element_type=jnp.float32)  53.1 us
    unnamed x356, local copies, waits for them, and re-layouts  48.6 us
    dot_general x20, matrix products, dot_tn(): lax.dot_general(former, latter, (((0,), (0,)), ((), ())), preferred_eleme...  45.6 us
    dot_general x16, matrix products, dot_nt(): lax.dot_general(former, latter, (((1,), (1,)), ((), ())), preferred_eleme...  45.3 us
  transfers between devices with their start and end apart: 99, of which 32 were waited for; matrix products, arithmetic and copies ran while one was open for 29% of the time, Pallas kernels for 16%

profile of v10, /device:TPU:0, one launch (start us, length us, event | category | flops | bytes accessed | tf_op | source)
XLA Modules:
  0.0 636.5 jit_solution(4773174717561534600)
XLA Ops:
  6.2 3.7 collective-permute-start
  20.9 9.9 %collective-permute-done.3.refs_3_ = bf16[1280,256]{1,0:T(8,128)(2,1)S(1)} collective-permute-done((bf16[1280,256]{1,0:T(8,128)(2,1)S(1)}, bf16[1280,256]{1,0:T(8,128)(2,1)S(1)}, u32[]{:S(2)}, u32[]{:S(2)}) %collective-permute-start.3) | collective-permute-done | bytes 655392 | tf_op jit(solution)/shard_map/ppermute | solution.py:49
  38.5 8.8 %collective-permute-done.4.refs_3_ = bf16[2,1,80,640]{3,2,1,0:T(8,128)(2,1)S(1)} collective-permute-done((bf16[2,1,80,640]{3,2,1,0:T(8,128)(2,1)S(1)}, bf16[2,1,80,640]{3,2,1,0:T(8,128)(2,1)S(1)}, u32[]{:S(2)}, u32[]{:S(2)}) %collective-permute-start.4) | collective-permute-done | bytes 204832 | tf_op jit(solution)/shard_map/ppermute | solution.py:49
  54.2 9.0 %collective-permute-done.8.refs_3_ = bf16[2,2,80,640]{3,2,1,0:T(8,128)(2,1)S(1)} collective-permute-done((bf16[2,2,80,640]{3,2,1,0:T(8,128)(2,1)S(1)}, bf16[2,2,80,640]{3,2,1,0:T(8,128)(2,1)S(1)}, u32[]{:S(2)}, u32[]{:S(2)}) %collective-permute-start.8) | collective-permute-done | bytes 409632 | tf_op jit(solution)/shard_map/ppermute | solution.py:49
  63.2 5.0 collective-permute-done.9.refs_4_
  68.6 3.8 join_halves.17
  74.5 4.4 convolution_convert_fusion.23.refs_7_.refs_2_.refs_3_
  78.9 4.3 collective-permute-done.11.refs_3_
  88.5 5.5 collective-permute-start.14
  97.0 3.5 collective-permute-done.14.refs_3_
  107.7 3.5 multiply_convert_fusion.4.refs_1_.refs_2_
  111.2 8.4 %attention_own.2 = (f32[640,1024]{1,0:T(8,128)S(1)}, f32[8,1,1024]{2,1,0:T(1,128)S(1)}, f32[8,1,1024]{2,1,0:T(1,128)S(1)}) custom-call(s32[1,1024]{1,0:T(1,128)S(1)} %bitcast.268, bf16[640,1024]{1,0:T(8,128)(2,1)S(1)} %multiply_convert_fusion.4.refs_1_.refs_2_, bf16[640,1024]{1,0:T(8,128)(2,1)S(1)} %copy-done.12, bf16[640,1024]{1,0:T(8,128)(2,1)S(1)} %copy-done.14), custom_call_target="tpu_custom_call" | custom-call | flops 629145600 | bytes 3936256 | tf_op jit(solution)/shard_map/attention_own/pallas_call | solution.py:651
  125.7 4.9 collective-permute-start.21
  133.6 4.4 attention_far.2
  139.3 4.0 join_halves.21
  156.2 6.2 collective-permute-done.24.refs_3_
  174.4 3.5 fusion.45.refs_8_
  178.0 6.9 %collective-permute-done.29.refs_4_ = bf16[1,8,80,640]{3,2,1,0:T(8,128)(2,1)S(1)} collective-permute-done((bf16[1,8,80,640]{3,2,1,0:T(8,128)(2,1)S(1)}, bf16[1,8,80,640]{3,2,1,0:T(8,128)(2,1)S(1)}, u32[]{:S(2)}, u32[]{:S(2)}) %collective-permute-start.29) | collective-permute-done | bytes 819232 | tf_op jit(solution)/shard_map/ppermute | solution.py:49
  204.3 9.2 %collective-permute-done.31.refs_3_ = bf16[2,1,80,640]{3,2,1,0:T(8,128)(2,1)} collective-permute-done((bf16[2,1,80,640]{3,2,1,0:T(8,128)(2,1)S(1)}, bf16[2,1,80,640]{3,2,1,0:T(8,128)(2,1)}, u32[]{:S(2)}, u32[]{:S(2)}) %collective-permute-start.31) | collective-permute-done | bytes 204832 | tf_op jit(solution)/shard_map/ppermute | solution.py:49
  217.1 4.5 convolution_convert_fusion.21.refs_6_.refs_2_.refs_3_
  226.5 12.9 %collective-permute-done.36.refs_4_ = bf16[1,8,80,640]{3,2,1,0:T(8,128)(2,1)S(1)} collective-permute-done((bf16[1,8,80,640]{3,2,1,0:T(8,128)(2,1)S(1)}, bf16[1,8,80,640]{3,2,1,0:T(8,128)(2,1)S(1)}, u32[]{:S(2)}, u32[]{:S(2)}) %collective-permute-start.36) | collective-permute-done | bytes 819232 | tf_op jit(solution)/shard_map/ppermute | solution.py:49
  244.1 3.5 multiply_convert_fusion.1.refs_1_.refs_2_
  247.6 8.1 %attention_own.3 = (f32[640,1024]{1,0:T(8,128)S(1)}, f32[8,1,1024]{2,1,0:T(1,128)S(1)}, f32[8,1,1024]{2,1,0:T(1,128)S(1)}) custom-call(s32[1,1024]{1,0:T(1,128)S(1)} %bitcast.269, bf16[640,1024]{1,0:T(8,128)(2,1)S(1)} %multiply_convert_fusion.1.refs_1_.refs_2_, bf16[640,1024]{1,0:T(8,128)(2,1)S(1)} %copy-done.16, bf16[640,1024]{1,0:T(8,128)(2,1)S(1)} %copy-done.18), custom_call_target="tpu_custom_call" | custom-call | flops 629145600 | bytes 3936256 | tf_op jit(solution)/shard_map/attention_own/pallas_call | solution.py:651
  261.0 4.7 attention_far.3
  267.1 8.3 %collective-permute-done.43.refs_2_ = bf16[1,8,80,640]{3,2,1,0:T(8,128)(2,1)S(1)} collective-permute-done((bf16[1,8,80,640]{3,2,1,0:T(8,128)(2,1)S(1)}, bf16[1,8,80,640]{3,2,1,0:T(8,128)(2,1)S(1)}, u32[]{:S(2)}, u32[]{:S(2)}) %collective-permute-start.43) | collective-permute-done | bytes 819232 | tf_op jit(solution)/shard_map/ppermute | solution.py:49
  301.1 4.5 convolution_convert_fusion.13
  308.8 3.7 add_halves.22
  321.1 6.9 %attention_far_back.2 = (f32[640,1024]{1,0:T(8,128)S(1)}, f32[8,1,1024]{2,1,0:T(1,128)S(1)}, bf16[2,640,512]{2,1,0:T(8,128)(2,1)}) custom-call(s32[1]{0:T(128)} %bitcast.19.refs_0_, bf16[640,1024]{1,0:T(8,128)(2,1)S(1)} %copy-done.21, bf16[640,512]{1,0:T(8,128)(2,1)S(1)} %convolution_convert_fusion.27.refs_2_, bf16[640,512]{1,0:T(8,128)(2,1)S(1)} %copy-done.33, ...), custom_call_target="tpu_custom_call" | custom-call | flops 503316480 | bytes 5275652 | tf_op jit(solution)/shard_map/attention_far_back/pallas_call | solution.py:651
  329.4 5.1 collective-permute-start.51
  343.6 12.7 %attention_own_back.2 = (bf16[640,1024]{1,0:T(8,128)(2,1)S(1)}, bf16[640,1024]{1,0:T(8,128)(2,1)S(1)}, bf16[640,1024]{1,0:T(8,128)(2,1)S(1)}, f32[640,1]{1,0:T(8,128)S(1)}) custom-call(s32[1,1024]{1,0:T(1,128)S(1)} %bitcast.270, f32[80,1]{1,0:T(8,128)S(1)} %copy.56.refs_1_, bf16[640,1024]{1,0:T(8,128)(2,1)S(1)} %copy-done.22, ...), custom_call_target="tpu_custom_call" | custom-call | flops 15938355200 | bytes 7934272 | tf_op jit(solution)/shard_map/attention_own_back/pallas_call | solution.py:651
  373.6 3.7 convolution_convert_fusion.5.refs_7_
  388.7 4.3 fusion.26
  401.3 4.1 fusion.119
  427.2 6.9 %collective-permute-done.61.refs_1_ = bf16[2,2,80,640]{3,2,1,0:T(8,128)(2,1)S(1)} collective-permute-done((bf16[2,2,80,640]{3,2,1,0:T(8,128)(2,1)S(1)}, bf16[2,2,80,640]{3,2,1,0:T(8,128)(2,1)S(1)}, u32[]{:S(2)}, u32[]{:S(2)}) %collective-permute-start.61) | collective-permute-done | bytes 409632 | tf_op jit(solution)/shard_map/ppermute | solution.py:49
  450.9 4.1 add_halves.30
  455.8 4.5 collective-permute-done.67.refs_1_
  465.9 6.9 %attention_far_back.3 = (f32[640,1024]{1,0:T(8,128)S(1)}, f32[8,1,1024]{2,1,0:T(1,128)S(1)}, bf16[2,640,512]{2,1,0:T(8,128)(2,1)}) custom-call(s32[1]{0:T(128)} %bitcast.19.refs_0_, bf16[640,1024]{1,0:T(8,128)(2,1)S(1)} %copy-done.9, bf16[640,512]{1,0:T(8,128)(2,1)S(1)} %copy-done.4, bf16[640,512]{1,0:T(8,128)(2,1)S(1)} %copy-done.6, ...), custom_call_target="tpu_custom_call" | custom-call | flops 503316480 | bytes 5275652 | tf_op jit(solution)/shard_map/attention_far_back/pallas_call | solution.py:651
  472.8 5.0 collective-permute-start.73
  490.2 12.7 %attention_own_back.3 = (bf16[640,1024]{1,0:T(8,128)(2,1)S(1)}, bf16[640,1024]{1,0:T(8,128)(2,1)S(1)}, bf16[640,1024]{1,0:T(8,128)(2,1)S(1)}, f32[640,1]{1,0:T(8,128)S(1)}) custom-call(s32[1,1024]{1,0:T(1,128)S(1)} %bitcast.271, f32[80,1]{1,0:T(8,128)S(1)} %copy.59.refs_1_, bf16[640,1024]{1,0:T(8,128)(2,1)S(1)} %copy-done.9, ...), custom_call_target="tpu_custom_call" | custom-call | flops 15938355200 | bytes 7934272 | tf_op jit(solution)/shard_map/attention_own_back/pallas_call | solution.py:651
  503.0 3.5 convolution_convert_fusion
  536.1 4.2 fusion.66
  543.0 9.2 %collective-permute-done.82.refs_5_ = bf16[1,8,80,640]{3,2,1,0:T(8,128)(2,1)S(1)} collective-permute-done((bf16[1,8,80,640]{3,2,1,0:T(8,128)(2,1)S(1)}, bf16[1,8,80,640]{3,2,1,0:T(8,128)(2,1)S(1)}, u32[]{:S(2)}, u32[]{:S(2)}) %collective-permute-start.82) | collective-permute-done | bytes 819232 | tf_op jit(solution)/shard_map/ppermute | solution.py:49
  556.1 13.7 %collective-permute-done.75.refs_3_ = bf16[1,8,80,640]{3,2,1,0:T(8,128)(2,1)S(1)} collective-permute-done((bf16[1,8,80,640]{3,2,1,0:T(8,128)(2,1)S(1)}, bf16[1,8,80,640]{3,2,1,0:T(8,128)(2,1)S(1)}, u32[]{:S(2)}, u32[]{:S(2)}) %collective-permute-start.75) | collective-permute-done | bytes 819232 | tf_op jit(solution)/shard_map/ppermute | solution.py:49
  573.8 4.8 fusion.20
  583.8 4.0 fusion.31
  608.1 6.2 collective-permute-done.87.refs_1_
  615.1 3.6 collective-permute-done.91.refs_1_
  626.0 6.1 collective-permute-done.97.refs_3_
  (707 shorter events, 336.1 us)
Async XLA Ops:
  48.9 19.2 %collective-permute-start.9 = (bf16[1,8,80,640]{3,2,1,0:T(8,128)(2,1)S(1)}, bf16[1,8,80,640]{3,2,1,0:T(8,128)(2,1)}, u32[]{:S(2)}, u32[]{:S(2)}) collective-permute-start(bf16[1,8,80,640]{3,2,1,0:T(8,128)(2,1)S(1)} %get-tuple-element.178.refs_1_), channel_id=1, source_target_pairs={{0,2},{2,0},{4,6},{6,4},{8,10},{10,8},{12,14},{14,12},{16,18},{18,... | collective-permute-start | bytes 2457608 | tf_op jit(solution)/shard_map/ppermute | solution.py:49
  49.5 19.2 %collective-permute-start.10 = (bf16[1,8,80,640]{3,2,1,0:T(8,128)(2,1)}, bf16[1,8,80,640]{3,2,1,0:T(8,128)(2,1)}, u32[]{:S(2)}, u32[]{:S(2)}) collective-permute-start(bf16[1,8,80,640]{3,2,1,0:T(8,128)(2,1)} %get-tuple-element.179.refs_2_), channel_id=1, source_target_pairs={{0,4},{2,6},{4,0},{6,2},{8,12},{10,14},{12,8},{14,10},{16,20},{18,... | collective-permute-start | bytes 2457608 | tf_op jit(solution)/shard_map/ppermute | solution.py:49
  103.3 17.8 %collective-permute-start.17 = (bf16[2,1,80,640]{3,2,1,0:T(8,128)(2,1)S(1)}, bf16[2,1,80,640]{3,2,1,0:T(8,128)(2,1)S(1)}, u32[]{:S(2)}, u32[]{:S(2)}) collective-permute-start(bf16[2,1,80,640]{3,2,1,0:T(8,128)(2,1)S(1)} %get-tuple-element.195.refs_0_), channel_id=1, source_target_pairs={{0,16},{2,18},{4,20},{6,22},{8,24},{10,26},{12,28},{14,30},{16,0},... | collective-permute-start | bytes 614408 | tf_op jit(solution)/shard_map/ppermute | solution.py:49
  143.3 31.1 %collective-permute-start.27 = (bf16[2,1280,640]{2,1,0:T(8,128)(2,1)}, bf16[2,1280,640]{2,1,0:T(8,128)(2,1)}, u32[]{:S(2)}, u32[]{:S(2)}) collective-permute-start(bf16[2,1280,640]{2,1,0:T(8,128)(2,1)} %bitcast.288), channel_id=1, source_target_pairs={{0,1},{1,0},{2,3},{3,2},{4,5},{5,4},{6,7},{7,6},{8,9},{9,8},{10,11... | collective-permute-start | bytes 9830408 | tf_op jit(solution)/shard_map/ppermute | solution.py:49
  166.0 18.8 %collective-permute-start.29 = (bf16[1,8,80,640]{3,2,1,0:T(8,128)(2,1)S(1)}, bf16[1,8,80,640]{3,2,1,0:T(8,128)(2,1)S(1)}, u32[]{:S(2)}, u32[]{:S(2)}) collective-permute-start(bf16[1,8,80,640]{3,2,1,0:T(8,128)(2,1)S(1)} %get-tuple-element.209.refs_1_), channel_id=1, source_target_pairs={{0,2},{2,0},{4,6},{6,4},{8,10},{10,8},{12,14},{14,12},{16,18},{18,... | collective-permute-start | bytes 2457608 | tf_op jit(solution)/shard_map/ppermute | solution.py:49
  166.6 18.5 %collective-permute-start.30 = (bf16[1,8,80,640]{3,2,1,0:T(8,128)(2,1)S(1)}, bf16[1,8,80,640]{3,2,1,0:T(8,128)(2,1)S(1)}, u32[]{:S(2)}, u32[]{:S(2)}) collective-permute-start(bf16[1,8,80,640]{3,2,1,0:T(8,128)(2,1)S(1)} %get-tuple-element.210.refs_2_), channel_id=1, source_target_pairs={{0,4},{2,6},{4,0},{6,2},{8,12},{10,14},{12,8},{14,10},{16,20},{18,... | collective-permute-start | bytes 2457608 | tf_op jit(solution)/shard_map/ppermute | solution.py:49
  194.6 18.8 %collective-permute-start.32 = (bf16[1,4,80,640]{3,2,1,0:T(8,128)(2,1)}, bf16[1,4,80,640]{3,2,1,0:T(8,128)(2,1)}, u32[]{:S(2)}, u32[]{:S(2)}) collective-permute-start(bf16[1,4,80,640]{3,2,1,0:T(8,128)(2,1)} %get-tuple-element.213.refs_1_), channel_id=1, source_target_pairs={{0,4},{2,6},{4,0},{6,2},{8,12},{10,14},{12,8},{14,10},{16,20},{18,... | collective-permute-start | bytes 1228808 | tf_op jit(solution)/shard_map/ppermute | solution.py:49
  199.9 22.7 %collective-permute-start.38 = (bf16[1280,256]{1,0:T(8,128)(2,1)}, bf16[1280,256]{1,0:T(8,128)(2,1)S(1)}, u32[]{:S(2)}, u32[]{:S(2)}) collective-permute-start(bf16[1280,256]{1,0:T(8,128)(2,1)} %fusion.64), channel_id=1, source_target_pairs={{0,2},{2,0},{4,6},{6,4},{8,10},{10,8},{12,14},{14,12},{16,18},{18,... | collective-permute-start | bytes 1966088 | tf_op jit(solution)/shard_map/ppermute | solution.py:49
  215.1 24.3 %collective-permute-start.36 = (bf16[1,8,80,640]{3,2,1,0:T(8,128)(2,1)S(1)}, bf16[1,8,80,640]{3,2,1,0:T(8,128)(2,1)S(1)}, u32[]{:S(2)}, u32[]{:S(2)}) collective-permute-start(bf16[1,8,80,640]{3,2,1,0:T(8,128)(2,1)S(1)} %get-tuple-element.216.refs_1_), channel_id=1, source_target_pairs={{0,2},{2,0},{4,6},{6,4},{8,10},{10,8},{12,14},{14,12},{16,18},{18,... | collective-permute-start | bytes 2457608 | tf_op jit(solution)/shard_map/ppermute | solution.py:49
  215.7 23.8 %collective-permute-start.37 = (bf16[1,8,80,640]{3,2,1,0:T(8,128)(2,1)S(1)}, bf16[1,8,80,640]{3,2,1,0:T(8,128)(2,1)S(1)}, u32[]{:S(2)}, u32[]{:S(2)}) collective-permute-start(bf16[1,8,80,640]{3,2,1,0:T(8,128)(2,1)S(1)} %get-tuple-element.217.refs_2_), channel_id=1, source_target_pairs={{0,4},{2,6},{4,0},{6,2},{8,12},{10,14},{12,8},{14,10},{16,20},{18,... | collective-permute-start | bytes 2457608 | tf_op jit(solution)/shard_map/ppermute | solution.py:49
  222.7 35.7 %collective-permute-start.39 = (bf16[1280,256]{1,0:T(8,128)(2,1)S(1)}, bf16[1280,256]{1,0:T(8,128)(2,1)S(1)}, u32[]{:S(2)}, u32[]{:S(2)}) collective-permute-start(bf16[1280,256]{1,0:T(8,128)(2,1)S(1)} %collective-permute-done.38.refs_5_), channel_id=1, source_target_pairs={{0,1},{1,0},{2,3},{3,2},{4,5},{5,4},{6,7},{7,6},{8,9},{9,8},{10,11... | collective-permute-start | bytes 1966088 | tf_op jit(solution)/shard_map/ppermute | solution.py:49
  256.4 19.0 %collective-permute-start.43 = (bf16[1,8,80,640]{3,2,1,0:T(8,128)(2,1)S(1)}, bf16[1,8,80,640]{3,2,1,0:T(8,128)(2,1)S(1)}, u32[]{:S(2)}, u32[]{:S(2)}) collective-permute-start(bf16[1,8,80,640]{3,2,1,0:T(8,128)(2,1)S(1)} %get-tuple-element.227.refs_7_.refs_0_), channel_id=1, source_target_pairs={{0,2},{2,0},{4,6},{6,4},{8,10},{10,8},{12,14},{14,12},{16,18},{18,... | collective-permute-start | bytes 2457608 | tf_op jit(solution)/shard_map/ppermute | solution.py:49
  257.0 18.6 %collective-permute-start.44 = (bf16[1,8,80,640]{3,2,1,0:T(8,128)(2,1)S(1)}, bf16[1,8,80,640]{3,2,1,0:T(8,128)(2,1)S(1)}, u32[]{:S(2)}, u32[]{:S(2)}) collective-permute-start(bf16[1,8,80,640]{3,2,1,0:T(8,128)(2,1)S(1)} %get-tuple-element.228.refs_8_.refs_1_), channel_id=1, source_target_pairs={{0,4},{2,6},{4,0},{6,2},{8,12},{10,14},{12,8},{14,10},{16,20},{18,... | collective-permute-start | bytes 2457608 | tf_op jit(solution)/shard_map/ppermute | solution.py:49
  312.5 22.0 %collective-permute-start.49 = (bf16[1,8,80,640]{3,2,1,0:T(8,128)(2,1)S(1)}, bf16[1,8,80,640]{3,2,1,0:T(8,128)(2,1)S(1)}, u32[]{:S(2)}, u32[]{:S(2)}) collective-permute-start(bf16[1,8,80,640]{3,2,1,0:T(8,128)(2,1)S(1)} %get-tuple-element.232.refs_8_), channel_id=1, source_target_pairs={{0,2},{2,0},{4,6},{6,4},{8,10},{10,8},{12,14},{14,12},{16,18},{18,... | collective-permute-start | bytes 2457608 | tf_op jit(solution)/shard_map/ppermute | solution.py:49
  314.0 20.5 %collective-permute-start.50 = (bf16[1,8,80,640]{3,2,1,0:T(8,128)(2,1)S(1)}, bf16[1,8,80,640]{3,2,1,0:T(8,128)(2,1)S(1)}, u32[]{:S(2)}, u32[]{:S(2)}) collective-permute-start(bf16[1,8,80,640]{3,2,1,0:T(8,128)(2,1)S(1)} %get-tuple-element.234.refs_10_), channel_id=1, source_target_pairs={{0,4},{2,6},{4,0},{6,2},{8,12},{10,14},{12,8},{14,10},{16,20},{18,... | collective-permute-start | bytes 2457608 | tf_op jit(solution)/shard_map/ppermute | solution.py:49
  329.4 35.5 %collective-permute-start.51 = (bf16[2,640,512]{2,1,0:T(8,128)(2,1)}, bf16[2,640,512]{2,1,0:T(8,128)(2,1)}, u32[]{:S(2)}, u32[]{:S(2)}) collective-permute-start(bf16[2,640,512]{2,1,0:T(8,128)(2,1)} %get-tuple-element.244), channel_id=1, source_target_pairs={{0,2},{2,0},{4,6},{6,4},{8,10},{10,8},{12,14},{14,12},{16,18},{18,... | collective-permute-start | bytes 3932168 | tf_op jit(solution)/shard_map/ppermute | solution.py:49
  336.1 35.8 %collective-permute-start.53 = (bf16[1,4,80,640]{3,2,1,0:T(8,128)(2,1)}, bf16[1,4,80,640]{3,2,1,0:T(8,128)(2,1)S(1)}, u32[]{:S(2)}, u32[]{:S(2)}) collective-permute-start(bf16[1,4,80,640]{3,2,1,0:T(8,128)(2,1)} %get-tuple-element.238.refs_10_), channel_id=1, source_target_pairs={{0,4},{2,6},{4,0},{6,2},{8,12},{10,14},{12,8},{14,10},{16,20},{18,... | collective-permute-start | bytes 1228808 | tf_op jit(solution)/shard_map/ppermute | solution.py:49
  337.4 35.7 %collective-permute-start.54 = (bf16[1,4,80,640]{3,2,1,0:T(8,128)(2,1)S(1)}, bf16[1,4,80,640]{3,2,1,0:T(8,128)(2,1)S(1)}, u32[]{:S(2)}, u32[]{:S(2)}) collective-permute-start(bf16[1,4,80,640]{3,2,1,0:T(8,128)(2,1)S(1)} %get-tuple-element.240.refs_12_), channel_id=1, source_target_pairs={{0,2},{2,0},{4,6},{6,4},{8,10},{10,8},{12,14},{14,12},{16,18},{18,... | collective-permute-start | bytes 1228808 | tf_op jit(solution)/shard_map/ppermute | solution.py:49
  362.7 30.3 %collective-permute-start.56 = (bf16[1,8,80,640]{3,2,1,0:T(8,128)(2,1)}, bf16[1,8,80,640]{3,2,1,0:T(8,128)(2,1)S(1)}, u32[]{:S(2)}, u32[]{:S(2)}) collective-permute-start(bf16[1,8,80,640]{3,2,1,0:T(8,128)(2,1)} %get-tuple-element.250), channel_id=1, source_target_pairs={{0,2},{2,0},{4,6},{6,4},{8,10},{10,8},{12,14},{14,12},{16,18},{18,... | collective-permute-start | bytes 2457608 | tf_op jit(solution)/shard_map/ppermute | solution.py:49
  364.1 29.8 %collective-permute-start.57 = (bf16[1,8,80,640]{3,2,1,0:T(8,128)(2,1)}, bf16[1,8,80,640]{3,2,1,0:T(8,128)(2,1)}, u32[]{:S(2)}, u32[]{:S(2)}) collective-permute-start(bf16[1,8,80,640]{3,2,1,0:T(8,128)(2,1)} %get-tuple-element.252), channel_id=1, source_target_pairs={{0,4},{2,6},{4,0},{6,2},{8,12},{10,14},{12,8},{14,10},{16,20},{18,... | collective-permute-start | bytes 2457608 | tf_op jit(solution)/shard_map/ppermute | solution.py:49
  373.3 20.7 %collective-permute-start.55 = (bf16[2,2,80,640]{3,2,1,0:T(8,128)(2,1)S(1)}, bf16[2,2,80,640]{3,2,1,0:T(8,128)(2,1)S(1)}, u32[]{:S(2)}, u32[]{:S(2)}) collective-permute-start(bf16[2,2,80,640]{3,2,1,0:T(8,128)(2,1)S(1)} %get-tuple-element.248), channel_id=1, source_target_pairs={{0,8},{2,10},{4,12},{6,14},{8,0},{10,2},{12,4},{14,6},{16,24},{18,... | collective-permute-start | bytes 1228808 | tf_op jit(solution)/shard_map/ppermute | solution.py:49
  383.5 43.6 %collective-permute-start.62 = (bf16[1,8,80,640]{3,2,1,0:T(8,128)(2,1)}, bf16[1,8,80,640]{3,2,1,0:T(8,128)(2,1)S(1)}, u32[]{:S(2)}, u32[]{:S(2)}) collective-permute-start(bf16[1,8,80,640]{3,2,1,0:T(8,128)(2,1)} %get-tuple-element.262), channel_id=1, source_target_pairs={{0,2},{2,0},{4,6},{6,4},{8,10},{10,8},{12,14},{14,12},{16,18},{18,... | collective-permute-start | bytes 2457608 | tf_op jit(solution)/shard_map/ppermute | solution.py:49
  388.0 39.1 %collective-permute-start.63 = (bf16[1,8,80,640]{3,2,1,0:T(8,128)(2,1)S(1)}, bf16[1,8,80,640]{3,2,1,0:T(8,128)(2,1)S(1)}, u32[]{:S(2)}, u32[]{:S(2)}) collective-permute-start(bf16[1,8,80,640]{3,2,1,0:T(8,128)(2,1)S(1)} %get-tuple-element.264), channel_id=1, source_target_pairs={{0,4},{2,6},{4,0},{6,2},{8,12},{10,14},{12,8},{14,10},{16,20},{18,... | collective-permute-start | bytes 2457608 | tf_op jit(solution)/shard_map/ppermute | solution.py:49
  421.2 26.8 %collective-permute-start.65 = (bf16[1280,640]{1,0:T(8,128)(2,1)}, bf16[1280,640]{1,0:T(8,128)(2,1)}, u32[]{:S(2)}, u32[]{:S(2)}) collective-permute-start(bf16[1280,640]{1,0:T(8,128)(2,1)} %convolution_convert_fusion.10), channel_id=1, source_target_pairs={{0,1},{1,0},{2,3},{3,2},{4,5},{5,4},{6,7},{7,6},{8,9},{9,8},{10,11... | collective-permute-start | bytes 4915208 | tf_op jit(solution)/shard_map/ppermute | solution.py:49
  421.3 29.6 %collective-permute-start.66 = (bf16[1280,640]{1,0:T(8,128)(2,1)}, bf16[1280,640]{1,0:T(8,128)(2,1)}, u32[]{:S(2)}, u32[]{:S(2)}) collective-permute-start(bf16[1280,640]{1,0:T(8,128)(2,1)} %convolution_convert_fusion.8), channel_id=1, source_target_pairs={{0,1},{1,0},{2,3},{3,2},{4,5},{5,4},{6,7},{7,6},{8,9},{9,8},{10,11... | collective-permute-start | bytes 4915208 | tf_op jit(solution)/shard_map/ppermute | solution.py:49
  441.6 19.7 %collective-permute-start.64 = (bf16[1280,512]{1,0:T(8,128)(2,1)}, bf16[1280,512]{1,0:T(8,128)(2,1)S(1)}, u32[]{:S(2)}, u32[]{:S(2)}) collective-permute-start(bf16[1280,512]{1,0:T(8,128)(2,1)} %get-tuple-element.376), channel_id=1, source_target_pairs={{0,1},{1,0},{2,3},{3,2},{4,5},{5,4},{6,7},{7,6},{8,9},{9,8},{10,11... | collective-permute-start | bytes 3932168 | tf_op jit(solution)/shard_map/ppermute | solution.py:49
  442.0 19.3 %collective-permute-start.68 = (bf16[1,4,80,640]{3,2,1,0:T(8,128)(2,1)}, bf16[1,4,80,640]{3,2,1,0:T(8,128)(2,1)S(1)}, u32[]{:S(2)}, u32[]{:S(2)}) collective-permute-start(bf16[1,4,80,640]{3,2,1,0:T(8,128)(2,1)} %copy-done.70), channel_id=1, source_target_pairs={{0,4},{2,6},{4,0},{6,2},{8,12},{10,14},{12,8},{14,10},{16,20},{18,... | collective-permute-start | bytes 1228808 | tf_op jit(solution)/shard_map/ppermute | solution.py:49
  443.0 18.3 %collective-permute-start.69 = (bf16[1,4,80,640]{3,2,1,0:T(8,128)(2,1)}, bf16[1,4,80,640]{3,2,1,0:T(8,128)(2,1)S(1)}, u32[]{:S(2)}, u32[]{:S(2)}) collective-permute-start(bf16[1,4,80,640]{3,2,1,0:T(8,128)(2,1)} %copy-done.69), channel_id=1, source_target_pairs={{0,2},{2,0},{4,6},{6,4},{8,10},{10,8},{12,14},{14,12},{16,18},{18,... | collective-permute-start | bytes 1228808 | tf_op jit(solution)/shard_map/ppermute | solution.py:49
  455.0 25.0 %collective-permute-start.71 = (bf16[1,8,80,640]{3,2,1,0:T(8,128)(2,1)}, bf16[1,8,80,640]{3,2,1,0:T(8,128)(2,1)}, u32[]{:S(2)}, u32[]{:S(2)}) collective-permute-start(bf16[1,8,80,640]{3,2,1,0:T(8,128)(2,1)} %get-tuple-element.267.refs_8_), channel_id=1, source_target_pairs={{0,2},{2,0},{4,6},{6,4},{8,10},{10,8},{12,14},{14,12},{16,18},{18,... | collective-permute-start | bytes 2457608 | tf_op jit(solution)/shard_map/ppermute | solution.py:49
  460.3 19.7 %collective-permute-start.72 = (bf16[1,8,80,640]{3,2,1,0:T(8,128)(2,1)S(1)}, bf16[1,8,80,640]{3,2,1,0:T(8,128)(2,1)}, u32[]{:S(2)}, u32[]{:S(2)}) collective-permute-start(bf16[1,8,80,640]{3,2,1,0:T(8,128)(2,1)S(1)} %get-tuple-element.269.refs_10_), channel_id=1, source_target_pairs={{0,4},{2,6},{4,0},{6,2},{8,12},{10,14},{12,8},{14,10},{16,20},{18,... | collective-permute-start | bytes 2457608 | tf_op jit(solution)/shard_map/ppermute | solution.py:49
  462.1 17.9 %collective-permute-start.70 = (bf16[2,2,80,640]{3,2,1,0:T(8,128)(2,1)S(1)}, bf16[2,2,80,640]{3,2,1,0:T(8,128)(2,1)S(1)}, u32[]{:S(2)}, u32[]{:S(2)}) collective-permute-start(bf16[2,2,80,640]{3,2,1,0:T(8,128)(2,1)S(1)} %get-tuple-element.278.refs_14_), channel_id=1, source_target_pairs={{0,8},{2,10},{4,12},{6,14},{8,0},{10,2},{12,4},{14,6},{16,24},{18,... | collective-permute-start | bytes 1228808 | tf_op jit(solution)/shard_map/ppermute | solution.py:49
  472.8 42.3 %collective-permute-start.73 = (bf16[2,640,512]{2,1,0:T(8,128)(2,1)}, bf16[2,640,512]{2,1,0:T(8,128)(2,1)}, u32[]{:S(2)}, u32[]{:S(2)}) collective-permute-start(bf16[2,640,512]{2,1,0:T(8,128)(2,1)} %get-tuple-element.289), channel_id=1, source_target_pairs={{0,2},{2,0},{4,6},{6,4},{8,10},{10,8},{12,14},{14,12},{16,18},{18,... | collective-permute-start | bytes 3932168 | tf_op jit(solution)/shard_map/ppermute | solution.py:49
  482.6 48.5 %collective-permute-start.77 = (bf16[2,1,80,640]{3,2,1,0:T(8,128)(2,1)}, bf16[2,1,80,640]{3,2,1,0:T(8,128)(2,1)}, u32[]{:S(2)}, u32[]{:S(2)}) collective-permute-start(bf16[2,1,80,640]{3,2,1,0:T(8,128)(2,1)} %get-tuple-element.282.refs_10_), channel_id=1, source_target_pairs={{0,16},{2,18},{4,20},{6,22},{8,24},{10,26},{12,28},{14,30},{16,0},... | collective-permute-start | bytes 614408 | tf_op jit(solution)/shard_map/ppermute | solution.py:49
  484.8 47.4 %collective-permute-start.78 = (bf16[1,4,80,640]{3,2,1,0:T(8,128)(2,1)}, bf16[1,4,80,640]{3,2,1,0:T(8,128)(2,1)}, u32[]{:S(2)}, u32[]{:S(2)}) collective-permute-start(bf16[1,4,80,640]{3,2,1,0:T(8,128)(2,1)} %get-tuple-element.284.refs_12_), channel_id=1, source_target_pairs={{0,4},{2,6},{4,0},{6,2},{8,12},{10,14},{12,8},{14,10},{16,20},{18,... | collective-permute-start | bytes 1228808 | tf_op jit(solution)/shard_map/ppermute | solution.py:49
  485.8 46.4 %collective-permute-start.79 = (bf16[1,4,80,640]{3,2,1,0:T(8,128)(2,1)}, bf16[1,4,80,640]{3,2,1,0:T(8,128)(2,1)}, u32[]{:S(2)}, u32[]{:S(2)}) collective-permute-start(bf16[1,4,80,640]{3,2,1,0:T(8,128)(2,1)} %get-tuple-element.286.refs_14_), channel_id=1, source_target_pairs={{0,2},{2,0},{4,6},{6,4},{8,10},{10,8},{12,14},{14,12},{16,18},{18,... | collective-permute-start | bytes 1228808 | tf_op jit(solution)/shard_map/ppermute | solution.py:49
  511.8 23.1 %collective-permute-start.81 = (bf16[1,8,80,640]{3,2,1,0:T(8,128)(2,1)}, bf16[1,8,80,640]{3,2,1,0:T(8,128)(2,1)}, u32[]{:S(2)}, u32[]{:S(2)}) collective-permute-start(bf16[1,8,80,640]{3,2,1,0:T(8,128)(2,1)} %get-tuple-element.301), channel_id=1, source_target_pairs={{0,2},{2,0},{4,6},{6,4},{8,10},{10,8},{12,14},{14,12},{16,18},{18,... | collective-permute-start | bytes 2457608 | tf_op jit(solution)/shard_map/ppermute | solution.py:49
  525.8 44.0 %collective-permute-start.76 = (bf16[1280,512]{1,0:T(8,128)(2,1)}, bf16[1280,512]{1,0:T(8,128)(2,1)S(1)}, u32[]{:S(2)}, u32[]{:S(2)}) collective-permute-start(bf16[1280,512]{1,0:T(8,128)(2,1)} %fusion.21), channel_id=1, source_target_pairs={{0,1},{1,0},{2,3},{3,2},{4,5},{5,4},{6,7},{7,6},{8,9},{9,8},{10,11... | collective-permute-start | bytes 3932168 | tf_op jit(solution)/shard_map/ppermute | solution.py:49
  531.1 21.1 %collective-permute-start.82 = (bf16[1,8,80,640]{3,2,1,0:T(8,128)(2,1)S(1)}, bf16[1,8,80,640]{3,2,1,0:T(8,128)(2,1)S(1)}, u32[]{:S(2)}, u32[]{:S(2)}) collective-permute-start(bf16[1,8,80,640]{3,2,1,0:T(8,128)(2,1)S(1)} %copy-done.68), channel_id=1, source_target_pairs={{0,4},{2,6},{4,0},{6,2},{8,12},{10,14},{12,8},{14,10},{16,20},{18,... | collective-permute-start | bytes 2457608 | tf_op jit(solution)/shard_map/ppermute | solution.py:49
  532.2 23.8 %collective-permute-start.74 = (bf16[1,8,80,640]{3,2,1,0:T(8,128)(2,1)S(1)}, bf16[1,8,80,640]{3,2,1,0:T(8,128)(2,1)S(1)}, u32[]{:S(2)}, u32[]{:S(2)}) collective-permute-start(bf16[1,8,80,640]{3,2,1,0:T(8,128)(2,1)S(1)} %get-tuple-element.293), channel_id=1, source_target_pairs={{0,2},{2,0},{4,6},{6,4},{8,10},{10,8},{12,14},{14,12},{16,18},{18,... | collective-permute-start | bytes 2457608 | tf_op jit(solution)/shard_map/ppermute | solution.py:49
  532.2 37.6 %collective-permute-start.75 = (bf16[1,8,80,640]{3,2,1,0:T(8,128)(2,1)S(1)}, bf16[1,8,80,640]{3,2,1,0:T(8,128)(2,1)S(1)}, u32[]{:S(2)}, u32[]{:S(2)}) collective-permute-start(bf16[1,8,80,640]{3,2,1,0:T(8,128)(2,1)S(1)} %get-tuple-element.295), channel_id=1, source_target_pairs={{0,4},{2,6},{4,0},{6,2},{8,12},{10,14},{12,8},{14,10},{16,20},{18,... | collective-permute-start | bytes 2457608 | tf_op jit(solution)/shard_map/ppermute | solution.py:49
  534.9 17.3 %collective-permute-start.80 = (bf16[2,2,80,640]{3,2,1,0:T(8,128)(2,1)S(1)}, bf16[2,2,80,640]{3,2,1,0:T(8,128)(2,1)S(1)}, u32[]{:S(2)}, u32[]{:S(2)}) collective-permute-start(bf16[2,2,80,640]{3,2,1,0:T(8,128)(2,1)S(1)} %get-tuple-element.299), channel_id=1, source_target_pairs={{0,8},{2,10},{4,12},{6,14},{8,0},{10,2},{12,4},{14,6},{16,24},{18,... | collective-permute-start | bytes 1228808 | tf_op jit(solution)/shard_map/ppermute | solution.py:49
  553.9 25.8 %collective-permute-start.83 = (bf16[2,1,80,640]{3,2,1,0:T(8,128)(2,1)S(1)}, bf16[2,1,80,640]{3,2,1,0:T(8,128)(2,1)S(1)}, u32[]{:S(2)}, u32[]{:S(2)}) collective-permute-start(bf16[2,1,80,640]{3,2,1,0:T(8,128)(2,1)S(1)} %get-tuple-element.305), channel_id=1, source_target_pairs={{0,16},{2,18},{4,20},{6,22},{8,24},{10,26},{12,28},{14,30},{16,0},... | collective-permute-start | bytes 614408 | tf_op jit(solution)/shard_map/ppermute | solution.py:49
  555.0 24.8 %collective-permute-start.84 = (bf16[1,4,80,640]{3,2,1,0:T(8,128)(2,1)S(1)}, bf16[1,4,80,640]{3,2,1,0:T(8,128)(2,1)S(1)}, u32[]{:S(2)}, u32[]{:S(2)}) collective-permute-start(bf16[1,4,80,640]{3,2,1,0:T(8,128)(2,1)S(1)} %get-tuple-element.308), channel_id=1, source_target_pairs={{0,4},{2,6},{4,0},{6,2},{8,12},{10,14},{12,8},{14,10},{16,20},{18,... | collective-permute-start | bytes 1228808 | tf_op jit(solution)/shard_map/ppermute | solution.py:49
  556.0 23.7 %collective-permute-start.85 = (bf16[1,4,80,640]{3,2,1,0:T(8,128)(2,1)S(1)}, bf16[1,4,80,640]{3,2,1,0:T(8,128)(2,1)S(1)}, u32[]{:S(2)}, u32[]{:S(2)}) collective-permute-start(bf16[1,4,80,640]{3,2,1,0:T(8,128)(2,1)S(1)} %get-tuple-element.309), channel_id=1, source_target_pairs={{0,2},{2,0},{4,6},{6,4},{8,10},{10,8},{12,14},{14,12},{16,18},{18,... | collective-permute-start | bytes 1228808 | tf_op jit(solution)/shard_map/ppermute | solution.py:49
  581.4 19.8 %collective-permute-start.86 = (bf16[2,2,80,640]{3,2,1,0:T(8,128)(2,1)}, bf16[2,2,80,640]{3,2,1,0:T(8,128)(2,1)S(1)}, u32[]{:S(2)}, u32[]{:S(2)}) collective-permute-start(bf16[2,2,80,640]{3,2,1,0:T(8,128)(2,1)} %get-tuple-element.311), channel_id=1, source_target_pairs={{0,8},{2,10},{4,12},{6,14},{8,0},{10,2},{12,4},{14,6},{16,24},{18,... | collective-permute-start | bytes 1228808 | tf_op jit(solution)/shard_map/ppermute | solution.py:49
  582.1 20.7 %collective-permute-start.88 = (bf16[1,4,80,640]{3,2,1,0:T(8,128)(2,1)}, bf16[1,4,80,640]{3,2,1,0:T(8,128)(2,1)S(1)}, u32[]{:S(2)}, u32[]{:S(2)}) collective-permute-start(bf16[1,4,80,640]{3,2,1,0:T(8,128)(2,1)} %get-tuple-element.316), channel_id=1, source_target_pairs={{0,4},{2,6},{4,0},{6,2},{8,12},{10,14},{12,8},{14,10},{16,20},{18,... | collective-permute-start | bytes 1228808 | tf_op jit(solution)/shard_map/ppermute | solution.py:49
  582.7 20.1 %collective-permute-start.89 = (bf16[1,4,80,640]{3,2,1,0:T(8,128)(2,1)}, bf16[1,4,80,640]{3,2,1,0:T(8,128)(2,1)S(1)}, u32[]{:S(2)}, u32[]{:S(2)}) collective-permute-start(bf16[1,4,80,640]{3,2,1,0:T(8,128)(2,1)} %get-tuple-element.317), channel_id=1, source_target_pairs={{0,2},{2,0},{4,6},{6,4},{8,10},{10,8},{12,14},{14,12},{16,18},{18,... | collective-permute-start | bytes 1228808 | tf_op jit(solution)/shard_map/ppermute | solution.py:49
  583.7 19.1 %collective-permute-start.90 = (f32[2,2640]{1,0:T(2,128)S(1)}, f32[2,2640]{1,0:T(2,128)S(1)}, u32[]{:S(2)}, u32[]{:S(2)}) collective-permute-start(f32[2,2640]{1,0:T(2,128)S(1)} %pad_maximum_fusion.24), channel_id=1, source_target_pairs={{0,1},{1,0},{2,3},{3,2},{4,5},{5,4},{6,7},{7,6},{8,9},{9,8},{10,11... | collective-permute-start | bytes 63368 | tf_op jit(solution)/shard_map/ppermute | solution.py:49
  (227 other events, 1686.5 us)
